TPU v7x, 32 devices: a whole 2x2x4 slice. The times are simulated.
32 devices in a mesh: dp: 16 (over z, y, x), tensor: 2 (over core).
Axes of the slice: x: 2, y: 2, z: 4, core: 2. Of those that a mesh axis runs over, the one named last changes fastest.
Arguments:
- hidden_in: bfloat16 [8192, 1536], P('dp'), may hold values from -6 to 6
- attn_gain: float32 [1536], replicated, may hold values from 0.5 to 1.5
- w_query: bfloat16 [1536, 1536], P(None, 'tensor'), may hold values from -0.4375 to 0.4375
- key_weight: bfloat16 [1536, 512], P(None, 'tensor'), may hold values from -0.4375 to 0.4375
- value_weight: bfloat16 [1536, 512], P(None, 'tensor'), may hold values from -0.15625 to 0.15625
- w_output: bfloat16 [1536, 1536], P('tensor'), may hold values from -4 to 4
- moe_gain: float32 [1536], replicated, may hold values from 0.5 to 1.5
- w_router: bfloat16 [1536, 16], replicated, may hold values from -0.0625 to 0.0625
- w_gate: bfloat16 [16, 1536, 512], P('dp'), may hold values from -0.15625 to 0.15625
- w_up: bfloat16 [16, 1536, 512], P('dp'), may hold values from -0.15625 to 0.15625
- w_down: bfloat16 [16, 512, 1536], P('dp'), may hold values from -4 to 4
- expert_ids: int32 [8192, 8], P('dp'), may hold values from 0 to 15, all different within a row; in each aligned block of 512 rows (0 to 511, 512 to 1023, ...) at most 320 rows name the same one
- segment_ids: int32 [16, 512], P('dp'), may hold values from 0 to 7, never falling along the last dimension, each value on 1 to 256 neighbouring positions
- out_grad: bfloat16 [8192, 1536], P('dp'), may hold values from -6 to 6
Outputs:
- block_out: bfloat16 [8192, 1536], P('dp')
- input_grad: float32 [8192, 1536], P('dp')
- attn_gain_grad: float32 [1536], replicated
- query_grad: float32 [1536, 1536], P(None, 'tensor')
- key_grad: float32 [1536, 512], P(None, 'tensor')
- value_grad: float32 [1536, 512], P(None, 'tensor')
- w_output_grad: float32 [1536, 1536], P('tensor')
- moe_gain_grad: float32 [1536], replicated
- router_grad: float32 [1536, 16], replicated
- gate_grad: float32 [16, 1536, 512], P('dp')
- up_grad: float32 [16, 1536, 512], P('dp')
- down_grad: float32 [16, 512, 1536], P('dp')
Inputs may be any that keep to these rules, and one draw needn't show every extreme that they name: `expert_ids`: each row names 8 different experts. Among the rows of one index of dp no expert is named by more than 320 rows, and in every draw some expert is named by exactly 320 rows of some index. `segment_ids`: within each sequence the ids never fall; a document spans 1 to 256 positions, and some document exactly 256.
All inputs are finite; a program needn't handle non-finite values.
Results may differ from a plain program's by a relative error of at most 0.015.
Values may be sent and summed in bfloat16 or wider, within the bound.
A program may use at most 384 MiB of HBM per device.

v0:
```python
import jax
import jax.numpy as jnp
from jax import lax
from jax.sharding import PartitionSpec as P

HEAD_DIM = 64


epsilon = 1e-06
residual_scale = 0.22
attn_scale = 0.015625
rope_base = 10000.0
masked_score = -1e30
block_limit = 512


def positions_of(segment):
    position_index = jnp.arange(segment.shape[0], dtype=jnp.int32)
    earlier = jnp.concatenate([segment[:1] - 1, segment[:-1]])
    starts = lax.cummax(jnp.where(segment != earlier, position_index, 0), axis=0)
    return position_index - starts


def rope_tables(segment, head_size):
    position = positions_of(segment).astype(jnp.float32)
    frequency = rope_base ** (-jnp.arange(head_size // 2, dtype=jnp.float32) * 2.0 / head_size)
    angle = position[:, None] * frequency[None, :]
    return (jnp.cos(angle)[:, None, :], jnp.sin(angle)[:, None, :])


def apply_rotation(heads_in, cosine_table, sine_values):
    middle_index = heads_in.shape[-1] // 2
    first_half = heads_in[..., :middle_index]
    second_half = heads_in[..., middle_index:]
    return jnp.concatenate(
        [
            first_half * cosine_table - second_half * sine_values,
            second_half * cosine_table + first_half * sine_values,
        ],
        axis=-1,
    )


def unrotate(heads_in, cosine_table, sine_values):
    middle_index = heads_in.shape[-1] // 2
    first_half = heads_in[..., :middle_index]
    second_half = heads_in[..., middle_index:]
    return jnp.concatenate(
        [
            first_half * cosine_table + second_half * sine_values,
            second_half * cosine_table - first_half * sine_values,
        ],
        axis=-1,
    )


def block_scores(query_block, key_heads, segment_block, segment, first_row):
    kv_count = key_heads.shape[1]
    grouped = query_block.reshape(
        query_block.shape[0], kv_count, query_block.shape[1] // kv_count, query_block.shape[2]
    )
    raw_scores = (
        jnp.einsum("qhgd,khd->hgqk", grouped, key_heads, preferred_element_type=jnp.float32)
        * attn_scale
    )
    row_index = first_row + jnp.arange(query_block.shape[0], dtype=jnp.int32)[:, None]
    col_index = jnp.arange(key_heads.shape[0], dtype=jnp.int32)[None, :]
    allowed = (row_index >= col_index) & (segment_block[:, None] == segment[None, :])
    return (jnp.where(allowed, raw_scores, masked_score), grouped)


def attend_forward(seq_item, w_query, key_weight, value_weight, head_size):
    normed_seq, segment = seq_item
    sequence_length = normed_seq.shape[0]
    cosine_table, sine_values = rope_tables(segment, head_size)
    query_rows = jnp.dot(normed_seq, w_query, preferred_element_type=jnp.float32).reshape(
        sequence_length, -1, head_size
    )
    key_rows = jnp.dot(normed_seq, key_weight, preferred_element_type=jnp.float32).reshape(
        sequence_length, -1, head_size
    )
    value_proj = jnp.dot(normed_seq, value_weight, preferred_element_type=jnp.float32).reshape(
        sequence_length, -1, head_size
    )
    query_heads = apply_rotation(query_rows, cosine_table, sine_values).astype(jnp.bfloat16)
    key_heads = apply_rotation(key_rows, cosine_table, sine_values).astype(jnp.bfloat16)
    value_head_rows = value_proj.astype(jnp.bfloat16)
    block_size = min(block_limit, sequence_length)
    block_count = sequence_length // block_size
    query_blocks = query_heads.reshape(block_count, block_size, query_heads.shape[1], head_size)
    segment_blocks = segment.reshape(block_count, block_size)
    first_rows = jnp.arange(block_count, dtype=jnp.int32) * block_size

    def one_block(block_item):
        query_block, segment_block, first_row = block_item
        scores, grouped = block_scores(query_block, key_heads, segment_block, segment, first_row)
        largest = jnp.max(scores, axis=-1, keepdims=True)
        weights_raw = jnp.exp(scores - largest)
        totals = jnp.sum(weights_raw, axis=-1, keepdims=True)
        probs_low = (weights_raw / totals).astype(jnp.bfloat16)
        head_out = jnp.einsum(
            "hgqk,khd->qhgd", probs_low, value_head_rows, preferred_element_type=jnp.float32
        )
        return (
            head_out.reshape(block_size, -1).astype(jnp.bfloat16),
            (largest + jnp.log(totals))[..., 0],
        )

    head_blocks, log_sums = lax.map(one_block, (query_blocks, segment_blocks, first_rows))
    return (
        head_blocks.reshape(sequence_length, -1),
        query_heads,
        key_heads,
        value_head_rows,
        log_sums,
    )


def attend_backward(seq_item, head_size):
    query_heads, key_heads, value_head_rows, log_sums, heads_grad, segment = seq_item
    sequence_length = query_heads.shape[0]
    cosine_table, sine_values = rope_tables(segment, head_size)
    block_size = min(block_limit, sequence_length)
    block_count = sequence_length // block_size
    query_blocks = query_heads.reshape(block_count, block_size, query_heads.shape[1], head_size)
    grad_blocks = heads_grad.reshape(block_count, block_size, query_heads.shape[1], head_size)
    segment_blocks = segment.reshape(block_count, block_size)
    first_rows = jnp.arange(block_count, dtype=jnp.int32) * block_size

    def one_block(running, block_item):
        key_sum, value_sum = running
        query_block, grad_block, segment_block, first_row, log_sum = block_item
        scores, grouped = block_scores(query_block, key_heads, segment_block, segment, first_row)
        probability = jnp.exp(scores - log_sum[..., None])
        probs_low = probability.astype(jnp.bfloat16)
        grad_grouped = grad_block.reshape(grouped.shape)
        prob_grad = jnp.einsum(
            "qhgd,khd->hgqk", grad_grouped, value_head_rows, preferred_element_type=jnp.float32
        )
        weighted = jnp.sum(probability * prob_grad, axis=-1, keepdims=True)
        score_low = (probability * (prob_grad - weighted)).astype(jnp.bfloat16)
        query_part = (
            jnp.einsum("hgqk,khd->qhgd", score_low, key_heads, preferred_element_type=jnp.float32)
            * attn_scale
        )
        key_sum = (
            key_sum
            + jnp.einsum("hgqk,qhgd->khd", score_low, grouped, preferred_element_type=jnp.float32)
            * attn_scale
        )
        value_sum = value_sum + jnp.einsum(
            "hgqk,qhgd->khd", probs_low, grad_grouped, preferred_element_type=jnp.float32
        )
        return ((key_sum, value_sum), query_part.reshape(block_size, -1, head_size))

    empty_heads = jnp.zeros(key_heads.shape, jnp.float32)
    sums_kv, query_parts = lax.scan(
        one_block,
        (empty_heads, empty_heads),
        (query_blocks, grad_blocks, segment_blocks, first_rows, log_sums),
    )
    query_low = (
        unrotate(query_parts.reshape(sequence_length, -1, head_size), cosine_table, sine_values)
        .astype(jnp.bfloat16)
        .reshape(sequence_length, -1)
    )
    key_low = (
        unrotate(sums_kv[0], cosine_table, sine_values)
        .astype(jnp.bfloat16)
        .reshape(sequence_length, -1)
    )
    value_low = sums_kv[1].astype(jnp.bfloat16).reshape(sequence_length, -1)
    return (query_low, key_low, value_low)


def route_slots(expert_ids, capacity, expert_total):
    flat_ids = expert_ids.reshape(-1)
    onehot = (flat_ids[:, None] == jnp.arange(expert_total, dtype=jnp.int32)[None, :]).astype(
        jnp.int32
    )
    ranking = jnp.sum((jnp.cumsum(onehot, axis=0) - 1) * onehot, axis=1)
    return flat_ids * capacity + ranking


def expert_forward(arrived, w_gate, w_up, w_down):
    gate_act = jnp.einsum("secd,edf->secf", arrived, w_gate, preferred_element_type=jnp.float32)
    up_act = jnp.einsum("secd,edf->secf", arrived, w_up, preferred_element_type=jnp.float32)
    hidden_low = (jax.nn.silu(gate_act) * up_act).astype(jnp.bfloat16)
    expert_out = jnp.einsum(
        "secf,efd->secd", hidden_low, w_down, preferred_element_type=jnp.float32
    )
    return (gate_act, up_act, hidden_low, expert_out)


def expert_backward(arrived, arrived_grad, gate_act, up_act, hidden_low, w_gate, w_up, w_down):
    down_in = jnp.einsum("secd,efd->secf", arrived_grad, w_down, preferred_element_type=jnp.float32)
    sigmoid_gate = jax.nn.sigmoid(gate_act)
    gate_low = (down_in * up_act * sigmoid_gate * (1.0 + gate_act * (1.0 - sigmoid_gate))).astype(
        jnp.bfloat16
    )
    up_low = (down_in * gate_act * sigmoid_gate).astype(jnp.bfloat16)
    down_grad = jnp.einsum(
        "secf,secd->efd", hidden_low, arrived_grad, preferred_element_type=jnp.float32
    )
    gate_grad = jnp.einsum("secd,secf->edf", arrived, gate_low, preferred_element_type=jnp.float32)
    up_grad = jnp.einsum("secd,secf->edf", arrived, up_low, preferred_element_type=jnp.float32)
    rows_grad = jnp.einsum("secf,edf->secd", gate_low, w_gate, preferred_element_type=jnp.float32)
    rows_grad = rows_grad + jnp.einsum(
        "secf,edf->secd", up_low, w_up, preferred_element_type=jnp.float32
    )
    return (gate_grad, up_grad, down_grad, rows_grad)


def per_device(
    hidden_in,
    attn_gain,
    w_query,
    key_weight,
    value_weight,
    w_output,
    moe_gain,
    w_router,
    w_gate,
    w_up,
    w_down,
    expert_ids,
    segment_ids,
    out_grad,
):
    tokens_here = hidden_in.shape[0]
    model_width = hidden_in.shape[1]
    head_size = HEAD_DIM
    top_count = expert_ids.shape[1]
    local_experts = w_gate.shape[0]
    data_size = lax.axis_size("dp")
    tensor_size = lax.axis_size("tensor")
    expert_total = local_experts * data_size
    capacity = (
        min(tokens_here, 5 * tokens_here * top_count // (4 * expert_total))
        // tensor_size
        * tensor_size
    )
    seq_count = segment_ids.shape[0]
    sequence_length = segment_ids.shape[1]
    inputs = hidden_in.astype(jnp.float32)
    scale_in = lax.rsqrt(jnp.mean(inputs * inputs, axis=-1, keepdims=True) + epsilon)
    normed_low = (inputs * scale_in * attn_gain).astype(jnp.bfloat16)
    heads_low, query_heads, key_heads, value_head_rows, log_sums = lax.map(
        lambda seq_item: attend_forward(seq_item, w_query, key_weight, value_weight, head_size),
        (normed_low.reshape(seq_count, sequence_length, model_width), segment_ids),
    )
    heads_flat = heads_low.reshape(tokens_here, -1)
    attn_part = jnp.dot(heads_flat, w_output, preferred_element_type=jnp.float32)
    attn_total = lax.psum(attn_part, "tensor")
    middle = inputs + residual_scale * attn_total
    scale_mid = lax.rsqrt(jnp.mean(middle * middle, axis=-1, keepdims=True) + epsilon)
    routed_low = (middle * scale_mid * moe_gain).astype(jnp.bfloat16)
    logits = jnp.dot(routed_low, w_router, preferred_element_type=jnp.float32)
    pick_mask = expert_ids[:, :, None] == jnp.arange(expert_total, dtype=jnp.int32)[None, None, :]
    chosen = jnp.sum(jnp.where(pick_mask, logits[:, None, :], 0.0), axis=-1)
    gate_weights = jax.nn.softmax(chosen, axis=-1)
    slot_index = route_slots(expert_ids, capacity, expert_total)
    token_rows = jnp.repeat(routed_low, top_count, axis=0)
    dispatch_low = (
        jnp.zeros((expert_total * capacity, model_width), jnp.bfloat16)
        .at[slot_index]
        .set(token_rows)
    )
    dispatch_low = dispatch_low.reshape(data_size, local_experts, capacity, model_width)
    grad_top = out_grad.astype(jnp.float32)
    scaled_grad = residual_scale * grad_top
    slot_grad = (
        (gate_weights[:, :, None] * scaled_grad[:, None, :])
        .reshape(-1, model_width)
        .astype(jnp.bfloat16)
    )
    back_low = (
        jnp.zeros((expert_total * capacity, model_width), jnp.bfloat16)
        .at[slot_index]
        .set(slot_grad)
    )
    back_low = back_low.reshape(data_size, local_experts, capacity, model_width)
    arrived = lax.all_to_all(dispatch_low, "dp", split_axis=0, concat_axis=0, tiled=True)
    gate_act, up_act, hidden_low, expert_out = expert_forward(arrived, w_gate, w_up, w_down)
    returned = lax.all_to_all(expert_out, "dp", split_axis=0, concat_axis=0, tiled=True).reshape(
        expert_total * capacity, model_width
    )
    picked_out = returned[slot_index].reshape(tokens_here, top_count, model_width)
    moe_total = jnp.sum(gate_weights[:, :, None] * picked_out, axis=1)
    gate_sum = jnp.sum(picked_out * scaled_grad[:, None, :], axis=-1)
    arrived_grad = lax.all_to_all(back_low, "dp", split_axis=0, concat_axis=0, tiled=True)
    gate_grad, up_grad, down_grad, rows_grad = expert_backward(
        arrived, arrived_grad, gate_act, up_act, hidden_low, w_gate, w_up, w_down
    )
    rows_back = lax.all_to_all(rows_grad, "dp", split_axis=0, concat_axis=0, tiled=True).reshape(
        expert_total * capacity, model_width
    )
    picked_grad = rows_back[slot_index].reshape(tokens_here, top_count, model_width)
    routed_grad = jnp.sum(picked_grad, axis=1)
    block_out = (middle + residual_scale * moe_total).astype(jnp.bfloat16)
    chosen_grad = gate_weights * (
        gate_sum - jnp.sum(gate_weights * gate_sum, axis=-1, keepdims=True)
    )
    logit_grad = jnp.sum(jnp.where(pick_mask, chosen_grad[:, :, None], 0.0), axis=1).astype(
        jnp.bfloat16
    )
    router_grad = jnp.einsum(
        "td,te->de", routed_low, logit_grad, preferred_element_type=jnp.float32
    )
    routed_grad = routed_grad + jnp.einsum(
        "te,de->td", logit_grad, w_router, preferred_element_type=jnp.float32
    )
    gained = moe_gain * routed_grad
    moe_gain_grad = jnp.sum(routed_grad * middle * scale_mid, axis=0)
    middle_grad = (
        grad_top
        + scale_mid * gained
        - middle
        * (scale_mid * scale_mid * scale_mid)
        * jnp.mean(middle * gained, axis=-1, keepdims=True)
    )
    branch_low = (residual_scale * middle_grad).astype(jnp.bfloat16)
    w_output_grad = jnp.einsum(
        "tc,td->cd", heads_flat, branch_low, preferred_element_type=jnp.float32
    )
    heads_grad = jnp.einsum(
        "td,cd->tc", branch_low, w_output, preferred_element_type=jnp.float32
    ).astype(jnp.bfloat16)
    heads_grad = heads_grad.reshape(seq_count, sequence_length, -1, head_size)
    query_low, key_low, value_low = lax.map(
        lambda seq_item: attend_backward(seq_item, head_size),
        (query_heads, key_heads, value_head_rows, log_sums, heads_grad, segment_ids),
    )
    query_low = query_low.reshape(tokens_here, -1)
    key_low = key_low.reshape(tokens_here, -1)
    value_low = value_low.reshape(tokens_here, -1)
    query_grad = jnp.einsum("td,tc->dc", normed_low, query_low, preferred_element_type=jnp.float32)
    key_grad = jnp.einsum("td,tc->dc", normed_low, key_low, preferred_element_type=jnp.float32)
    value_grad = jnp.einsum("td,tc->dc", normed_low, value_low, preferred_element_type=jnp.float32)
    normed_part = jnp.einsum("tc,dc->td", query_low, w_query, preferred_element_type=jnp.float32)
    normed_part = normed_part + jnp.einsum(
        "tc,dc->td", key_low, key_weight, preferred_element_type=jnp.float32
    )
    normed_part = normed_part + jnp.einsum(
        "tc,dc->td", value_low, value_weight, preferred_element_type=jnp.float32
    )
    normed_grad = lax.psum(normed_part, "tensor")
    gained_in = attn_gain * normed_grad
    attn_gain_grad = jnp.sum(normed_grad * inputs * scale_in, axis=0)
    input_grad = (
        middle_grad
        + scale_in * gained_in
        - inputs
        * (scale_in * scale_in * scale_in)
        * jnp.mean(inputs * gained_in, axis=-1, keepdims=True)
    )
    reduced = lax.psum(
        (
            query_grad,
            key_grad,
            value_grad,
            w_output_grad,
            router_grad,
            attn_gain_grad,
            moe_gain_grad,
        ),
        "dp",
    )
    return (
        block_out,
        input_grad,
        reduced[5],
        reduced[0],
        reduced[1],
        reduced[2],
        reduced[3],
        reduced[6],
        reduced[4],
        gate_grad,
        up_grad,
        down_grad,
    )


def solution(mesh):
    placed = (
        P("dp", None),
        P(),
        P(None, "tensor"),
        P(None, "tensor"),
        P(None, "tensor"),
        P("tensor", None),
        P(),
        P(),
        P("dp", None, None),
        P("dp", None, None),
        P("dp", None, None),
        P("dp", None),
        P("dp", None),
        P("dp", None),
    )
    return jax.shard_map(
        per_device,
        mesh=mesh,
        in_specs=placed,
        out_specs=(
            P("dp", None),
            P("dp", None),
            P(),
            P(None, "tensor"),
            P(None, "tensor"),
            P(None, "tensor"),
            P("tensor", None),
            P(),
            P(),
            P("dp", None, None),
            P("dp", None, None),
            P("dp", None, None),
        ),
        check_vma=False,
    )
```

profile of v0, /device:TPU:0, one launch (start us, length us, event | category | flops | bytes accessed | tf_op | source)
XLA Modules:
  0.0 2863.3 jit_solution(14487730348080219610)
XLA Ops:
  7.3 1.3 slice.62
  10.7 1.9 fusion.67
  14.2 3.2 convolution_convert_fusion.1
  18.2 1.6 fusion.118
  20.8 2.0 fusion.50
  22.9 2.6 fusion.24
  25.5 1.9 copy-done.1
  27.6 3.8 fusion.81
  32.3 3.1 fusion.123
  36.9 4.6 reduce-window.19
  42.6 18.9 all-reduce.6.cloned.1.call-done
  61.5 2.9 multiply_reduce_fusion.2
  66.1 1.5 multiply_convert_fusion.1
  67.6 36.4 %scatter_custom_fusion = bf16[5120,1536]{1,0:T(8,128)(2,1)} fusion(s32[4096]{0:T(1024)S(1)} %bitcast.324, bf16[]{:T(256)} %constant.165.clone.1, bf16[512,1536]{1,0:T(8,128)(2,1)} %multiply_convert_fusion.1), kind=kCustom, calls=%fused_computation.31 | custom fusion | bytes 17301506 | tf_op jit(solution)/shard_map/scatter | solution.py:267
  104.0 6.8 all-to-all-start
  110.8 3.6 convert_multiply_fusion.5
  116.6 29.2 %scatter_custom_fusion.1 = bf16[5120,1536]{1,0:T(8,128)(2,1)} fusion(s32[4096]{0:T(1024)S(1)} %bitcast.325, f32[512,1536]{1,0:T(8,128)} %convert_multiply_fusion.5, f32[4096]{0:T(1024)S(1)} %div.69, bf16[]{:T(256)} %constant.165.clone.1), kind=kCustom, calls=%fused_computation.25 | custom fusion | flops 12582912 | bytes 18890754 | tf_op jit(solution)/shard_map/scatter | solution.py:280
  145.7 261.4 %all-to-all-done = bf16[16,1,320,1536]{3,2,1,0:T(8,128)(2,1)} async-done(((bf16[16,1,320,1536]{3,2,1,0:T(8,128)(2,1)}), bf16[16,1,320,1536]{3,2,1,0:T(8,128)(2,1)}, u32[]{:S(2)}, u32[]{:S(2)}) %all-to-all-start) | async-done | bytes 15728672 | tf_op jit(solution)/shard_map/all_to_all | solution.py:283
  407.1 69.9 %all-to-all-start.2 = ((bf16[16,1,320,1536]{3,2,1,0:T(8,128)(2,1)}), bf16[16,1,320,1536]{3,2,1,0:T(8,128)(2,1)}, u32[]{:S(2)}, u32[]{:S(2)}) async-start(bf16[16,1,320,1536]{3,2,1,0:T(8,128)(2,1)} %bitcast.300), calls=%async_computation.2 | async-start | bytes 31457280 | tf_op jit(solution)/shard_map/all_to_all | solution.py:291
  477.1 14.6 fusion.11
  491.7 14.2 fusion.13
  505.9 266.1 %all-to-all-done.2 = bf16[16,1,320,1536]{3,2,1,0:T(8,128)(2,1)} async-done(((bf16[16,1,320,1536]{3,2,1,0:T(8,128)(2,1)}), bf16[16,1,320,1536]{3,2,1,0:T(8,128)(2,1)}, u32[]{:S(2)}, u32[]{:S(2)}) %all-to-all-start.2) | async-done | bytes 15728672 | tf_op jit(solution)/shard_map/all_to_all | solution.py:291
  771.9 24.3 fusion.29
  796.3 16.9 fusion.46
  813.1 26.6 add_bitcast_fusion
  839.8 67.2 %all-to-all-start.3 = ((f32[16,1,320,1536]{3,2,1,0:T(8,128)}), f32[16,1,320,1536]{3,2,1,0:T(8,128)}, u32[]{:S(2)}, u32[]{:S(2)}) async-start(f32[16,1,320,1536]{3,2,1,0:T(8,128)} %add_bitcast_fusion), calls=%async_computation.3 | async-start | bytes 62914560 | tf_op jit(solution)/shard_map/all_to_all | solution.py:295
  907.0 16.5 convolution_bitcast_fusion
  923.5 571.2 %all-to-all-done.3 = f32[16,1,320,1536]{3,2,1,0:T(8,128)} async-done(((f32[16,1,320,1536]{3,2,1,0:T(8,128)}), f32[16,1,320,1536]{3,2,1,0:T(8,128)}, u32[]{:S(2)}, u32[]{:S(2)}) %all-to-all-start.3) | async-done | bytes 31457312 | tf_op jit(solution)/shard_map/all_to_all | solution.py:295
  1494.7 135.8 %all-to-all-start.1 = ((f32[16,1,320,1536]{3,2,1,0:T(8,128)}), f32[16,1,320,1536]{3,2,1,0:T(8,128)}, u32[]{:S(2)}, u32[]{:S(2)}) async-start(f32[16,1,320,1536]{3,2,1,0:T(8,128)} %convolution_bitcast_fusion), calls=%async_computation.1 | async-start | bytes 62914560 | tf_op jit(solution)/shard_map/all_to_all | solution.py:285
  1631.2 37.4 %gather_fusion.1 = f32[4096,1536]{1,0:T(8,128)} fusion(f32[5120,1536]{1,0:T(8,128)} %bitcast.61, s32[4096]{0:T(1024)S(1)} %broadcast_clamp_fusion), kind=kCustom, calls=%fused_computation.1 | custom fusion | bytes 50348032 | tf_op jit(solution)/shard_map/gather | solution.py:298
  1668.6 14.7 bitcast_reduce_fusion
  1683.2 533.8 %all-to-all-done.1 = f32[16,1,320,1536]{3,2,1,0:T(8,128)} async-done(((f32[16,1,320,1536]{3,2,1,0:T(8,128)}), f32[16,1,320,1536]{3,2,1,0:T(8,128)}, u32[]{:S(2)}, u32[]{:S(2)}) %all-to-all-start.1) | async-done | bytes 31457312 | tf_op jit(solution)/shard_map/all_to_all | solution.py:285
  2217.0 37.2 %gather_fusion = f32[4096,1536]{1,0:T(8,128)} fusion(f32[5120,1536]{1,0:T(8,128)} %bitcast.43, s32[4096]{0:T(1024)S(1)} %broadcast_clamp_fusion), kind=kCustom, calls=%fused_computation | custom fusion | bytes 50348032 | tf_op jit(solution)/shard_map/gather | solution.py:288
  2254.3 16.8 fusion.2
  2271.4 4.0 multiply_reduce_fusion
  2276.4 2.1 fusion.66
  2278.5 1.7 copy-done.6
  2280.2 2.3 convolution_convert_fusion
  2282.5 1.4 copy.88
  2284.0 6.4 fusion.87
  2290.4 9.8 fusion.17
  2300.3 6.9 fusion.19
  2307.3 2.0 fusion.86
  2309.3 1.2 convolution_multiply_fusion
  2311.0 1.2 copy-done.66
  2312.2 1.4 fusion.125
  2314.8 2.3 convolution_add_fusion.1
  2317.2 2.5 fusion.126
  2319.7 3.3 fusion.112
  2323.0 2.0 fusion.114
  2325.0 3.8 fusion.116
  2328.8 3.6 fusion.91
  2332.4 14.9 fusion.61
  2347.3 13.0 fusion.56
  2360.3 12.9 fusion.51
  2373.2 95.5 %all-reduce.8.cloned.1.call-done = f32[512,1536]{1,0:T(8,128)} async-done(((f32[512,1536]{1,0:T(8,128)}), f32[512,1536]{1,0:T(8,128)}) %all-reduce.8.cloned.1.call-update) | async-done | bytes 3145744 | tf_op jit(solution)/shard_map/psum | solution.py:347
  2468.7 3.4 fusion.74
  2472.0 109.7 %all-reduce = (f32[1536]{0:T(1024)}, f32[1536]{0:T(1024)}) all-reduce(f32[1536]{0:T(1024)S(1)} %get-tuple-element.145, f32[1536]{0:T(1024)S(1)} %get-tuple-element.143), channel_id=1, replica_groups=mesh['dp'=16,'tensor'=2] {'dp'}, use_global_device_ids=true, to_apply=%region_25.26 | all-reduce | flops 3072 | bytes 24576 | tf_op jit(solution)/shard_map/psum | solution.py:357
  2581.7 5.8 fusion.71
  2587.5 257.8 %all-reduce.10.cloned.1.call-done = (f32[1536,768]{1,0:T(8,128)}, f32[1536,256]{1,0:T(8,128)}, f32[1536,256]{1,0:T(8,128)}, f32[768,1536]{1,0:T(8,128)}, f32[1536,16]{0,1:T(8,128)}) async-done(((f32[1536,768]{1,0:T(8,128)}, f32[1536,256]{1,0:T(8,128)}, f32[1536,256]{1,0:T(8,128)}, f32[768,1536]{1,0:T(8,128)}, f32[1536,16]{0,1:T(8,128)}), (f32[1536,768]{1,0:T(8,128)}, f32[1536,256]{1,0:T(8,128)}, ...) | async-done | bytes 12681232 | tf_op jit(solution)/shard_map/psum | solution.py:357
  2845.4 5.0 copy.110
  2850.3 1.1 copy.111
  2852.3 1.1 copy.112
  2853.5 2.2 copy.113
  (212 shorter events, 17.3 us)
Async XLA Ops:
  7.2 25.1 copy-start
  7.2 10.2 copy-start.44
  7.2 10.2 copy-start.27
  7.2 54.3 %all-reduce.6.cloned.1.call-start = ((), (), s32[]{:S(2)}) async-start(), calls=%async_computation.4 | async-start | bytes 6291456 | tf_op jit(solution)/shard_map/psum | solution.py:254
  10.5 6.9 copy-start.4
  13.2 5.0 copy-start.55
  14.2 11.3 copy-start.10
  14.2 4.0 copy-start.65
  22.8 4.5 copy-start.1
  22.8 4.7 copy-start.46
  22.9 4.7 copy-start.30
  25.4 6.0 copy-start.48
  42.5 74.0 %copy-start.53 = (s32[4096,1]{0,1:T(1,128)}, s32[4096,1]{0,1:T(1,128)S(1)}, u32[]{:S(2)}) copy-start(s32[4096,1]{0,1:T(1,128)S(1)} %compare_select_fusion) | copy-start | bytes 49156
  42.5 23.5 copy-start.51
  65.1 38.9 %copy-start.59 = (f32[512]{0:T(512)}, f32[512]{0:T(512)S(1)}, u32[]{:S(2)}) copy-start(f32[512]{0:T(512)S(1)} %get-tuple-element.184) | copy-start | bytes 6148
  104.0 303.2 %all-to-all-start = ((bf16[16,1,320,1536]{3,2,1,0:T(8,128)(2,1)}), bf16[16,1,320,1536]{3,2,1,0:T(8,128)(2,1)}, u32[]{:S(2)}, u32[]{:S(2)}) async-start(bf16[16,1,320,1536]{3,2,1,0:T(8,128)(2,1)} %bitcast.299), calls=%async_computation | async-start | bytes 31457280 | tf_op jit(solution)/shard_map/all_to_all | solution.py:283
  110.8 3.7 copy-start.8
  110.8 3.6 copy-start.42
  116.4 29.3 %copy-start.15 = (f32[512,8]{1,0:T(8,128)}, f32[512,8]{1,0:T(8,128)S(1)}, u32[]{:S(2)}) copy-start(f32[512,8]{1,0:T(8,128)S(1)} %copy.79) | copy-start | bytes 49156
  407.1 364.8 %all-to-all-start.2 = ((bf16[16,1,320,1536]{3,2,1,0:T(8,128)(2,1)}), bf16[16,1,320,1536]{3,2,1,0:T(8,128)(2,1)}, u32[]{:S(2)}, u32[]{:S(2)}) async-start(bf16[16,1,320,1536]{3,2,1,0:T(8,128)(2,1)} %bitcast.300), calls=%async_computation.2 | async-start | bytes 31457280 | tf_op jit(solution)/shard_map/all_to_all | solution.py:291
  477.1 14.7 copy-start.67
  771.9 24.3 copy-start.68
  796.3 16.9 copy-start.69
  839.8 654.9 %all-to-all-start.3 = ((f32[16,1,320,1536]{3,2,1,0:T(8,128)}), f32[16,1,320,1536]{3,2,1,0:T(8,128)}, u32[]{:S(2)}, u32[]{:S(2)}) async-start(f32[16,1,320,1536]{3,2,1,0:T(8,128)} %add_bitcast_fusion), calls=%async_computation.3 | async-start | bytes 62914560 | tf_op jit(solution)/shard_map/all_to_all | solution.py:295
  923.5 707.0 %copy-start.54 = (s32[4096,1]{0,1:T(1,128)S(1)}, s32[4096,1]{0,1:T(1,128)}, u32[]{:S(2)}) copy-start(s32[4096,1]{0,1:T(1,128)} %copy-done.53) | copy-start | bytes 49156
  923.5 707.1 %copy-start.47 = (f32[4,3,512]{2,1,0:T(4,128)S(1)}, f32[4,3,512]{2,1,0:T(4,128)}, u32[]{:S(2)}) copy-start(f32[4,3,512]{2,1,0:T(4,128)} %copy-done.46) | copy-start | bytes 73732
  923.5 707.1 %copy-start.49 = (f32[4,3,512]{2,1,0:T(4,128)S(1)}, f32[4,3,512]{2,1,0:T(4,128)}, u32[]{:S(2)}) copy-start(f32[4,3,512]{2,1,0:T(4,128)} %copy-done.48) | copy-start | bytes 73732
  1494.7 722.3 %all-to-all-start.1 = ((f32[16,1,320,1536]{3,2,1,0:T(8,128)}), f32[16,1,320,1536]{3,2,1,0:T(8,128)}, u32[]{:S(2)}, u32[]{:S(2)}) async-start(f32[16,1,320,1536]{3,2,1,0:T(8,128)} %convolution_bitcast_fusion), calls=%async_computation.1 | async-start | bytes 62914560 | tf_op jit(solution)/shard_map/all_to_all | solution.py:285
  1630.5 838.2 %all-reduce.8.cloned.1.call-start = ((), (), s32[]{:S(2)}) async-start(), calls=%async_computation.5 | async-start | bytes 6291456 | tf_op jit(solution)/shard_map/psum | solution.py:347
  2217.0 37.2 %copy-start.16 = (f32[512,8]{1,0:T(8,128)S(1)}, f32[512,8]{1,0:T(8,128)}, u32[]{:S(2)}) copy-start(f32[512,8]{1,0:T(8,128)} %copy-done.15) | copy-start | bytes 49156
  2254.2 16.9 copy-start.33
  2254.2 16.9 copy-start.58
  2254.2 16.9 copy-start.62
  2254.3 17.0 copy-start.41
  2254.3 17.0 copy-start.43
  2254.3 17.0 copy-start.52
  2254.3 17.0 copy-start.60
  2271.3 4.1 copy-start.3
  2271.3 4.7 copy-start.9
  2271.3 5.1 copy-start.12
  2271.3 5.1 copy-start.64
  2280.2 3.7 copy-start.11
  2280.2 3.7 copy-start.38
  2283.9 6.5 copy-start.31
  2284.0 16.3 slice-start
  2284.0 16.3 slice-start.1
  2290.4 23.9 copy-start.39
  2290.4 9.8 slice-start.2
  2300.3 7.0 copy-start.24
  2300.3 7.0 copy-start.26
  2317.1 2.6 copy-start.45
  2317.1 2.6 copy-start.56
  2317.1 528.2 %all-reduce.10.cloned.1.call-start = ((), (), s32[]{:S(2)}) async-start(), calls=%async_computation.6 | async-start | bytes 25362432 | tf_op jit(solution)/shard_map/psum | solution.py:357
  2317.2 5.8 copy-start.5
  2325.0 3.8 copy-start.7
  2325.0 3.8 copy-start.14
  2332.4 14.9 slice-start.5
  2332.4 14.9 slice-start.6
  2332.4 27.9 slice-start.7
  2347.3 13.0 slice-start.8
  2373.2 208.6 %copy-start.63 = (f32[512]{0:T(512)S(1)}, f32[512]{0:T(512)}, u32[]{:S(2)}) copy-start(f32[512]{0:T(512)} %get-tuple-element.181) | copy-start | bytes 6148
  2845.3 8.1 slice-start.3
  2845.4 5.0 copy-start.22
  2845.4 8.1 slice-start.4
  (22 other events, 32.7 us)
Sparse Core Ops, SparseCore 0:
  35.5 25.8 all-reduce.5
  2317.3 151.3 all-reduce.7
  2476.3 369.0 all-reduce.9
where the time goes:
time: 2870 us; the launch traced here: 2860 us
  waiting for transfers between devices  2000 us (70%)
  starting transfers between devices  280 us (10%)
  matrix products  214 us (7%)
  local copies, waits for them, and re-layouts  137 us (5%)
  blocking collectives  110 us (4%)
  other arithmetic  102 us (4%)
    all_to_all x1, waiting for transfers between devices, per_device(): lax.all_to_all(rows_grad, 'dp', split_axis=0, concat_axis=0, tiled=True)  571 us
    all_to_all x1, waiting for transfers between devices, per_device(): lax.all_to_all(expert_out, 'dp', split_axis=0, concat_axis=0, tiled=True)  534 us
    all_to_all x1, waiting for transfers between devices, per_device(): lax.all_to_all(back_low, 'dp', split_axis=0, concat_axis=0, tiled=True)  266 us
    all_to_all x1, waiting for transfers between devices, per_device(): lax.all_to_all(dispatch_low, 'dp', split_axis=0, concat_axis=0, tiled=True)  261 us
    psum x1, waiting for transfers between devices, per_device(): lax.psum((query_grad, key_grad, value_grad, w_output_grad, router_grad, a...  258 us
    all_to_all x1, starting transfers between devices, per_device(): lax.all_to_all(expert_out, 'dp', split_axis=0, concat_axis=0, tiled=True)  136 us
    psum x1, blocking collectives, per_device(): lax.psum((query_grad, key_grad, value_grad, w_output_grad, router_grad, a...  110 us
    psum x1, waiting for transfers between devices, per_device(): normed_grad = lax.psum(normed_part, 'tensor')  95.5 us
  transfers between devices with their start and end apart: 7, of which 7 were waited for; matrix products, arithmetic and copies ran while one was open for 7% of the time, Pallas kernels for 0%

commit v1 on v0

v1 whole, which is shorter than its diff:
```python
import jax
import jax.numpy as jnp
from jax import lax
from jax.sharding import PartitionSpec as P

HEAD_DIM = 64

bf16 = jnp.bfloat16
f32 = jnp.float32
epsilon = 1e-06
residual_scale = 0.22
attn_scale = 0.015625
rope_base = 10000.0
masked_score = -1e30


def positions_of(segment):
    position_index = jnp.arange(segment.shape[0], dtype=jnp.int32)
    earlier = jnp.concatenate([segment[:1] - 1, segment[:-1]])
    starts = lax.cummax(jnp.where(segment != earlier, position_index, 0), axis=0)
    return position_index - starts


def rope_tables(segment, head_size):
    position = positions_of(segment).astype(f32)
    frequency = rope_base ** (-jnp.arange(head_size // 2, dtype=f32) * 2.0 / head_size)
    angle = position[:, None] * frequency[None, :]
    return (jnp.cos(angle)[:, None, :], jnp.sin(angle)[:, None, :])


def apply_rotation(heads_in, cosine_table, sine_values):
    middle_index = heads_in.shape[-1] // 2
    first_half = heads_in[..., :middle_index]
    second_half = heads_in[..., middle_index:]
    return jnp.concatenate(
        [
            first_half * cosine_table - second_half * sine_values,
            second_half * cosine_table + first_half * sine_values,
        ],
        axis=-1,
    )


def block_scores(query_heads, key_heads, segment):
    kv_count = key_heads.shape[1]
    length = query_heads.shape[0]
    grouped = query_heads.reshape(length, kv_count, -1, query_heads.shape[2])
    raw_scores = (
        jnp.einsum("qhgd,khd->hgqk", grouped, key_heads, preferred_element_type=f32) * attn_scale
    )
    index = jnp.arange(length, dtype=jnp.int32)
    allowed = (index[:, None] >= index[None, :]) & (segment[:, None] == segment[None, :])
    return (jnp.where(allowed, raw_scores, masked_score), grouped)


def attend_forward(normed, segment, tables, w_query, key_weight, value_weight, head_size):
    length = normed.shape[0]

    def heads(weight):
        return jnp.dot(normed, weight, preferred_element_type=f32).reshape(length, -1, head_size)

    query_heads = apply_rotation(heads(w_query), *tables).astype(bf16)
    key_heads = apply_rotation(heads(key_weight), *tables).astype(bf16)
    value_heads = heads(value_weight).astype(bf16)
    scores, _ = block_scores(query_heads, key_heads, segment)
    largest = jnp.max(scores, axis=-1, keepdims=True)
    weights_raw = jnp.exp(scores - largest)
    totals = jnp.sum(weights_raw, axis=-1, keepdims=True)
    probs_low = (weights_raw / totals).astype(bf16)
    head_out = jnp.einsum("hgqk,khd->qhgd", probs_low, value_heads, preferred_element_type=f32)
    return (
        head_out.reshape(length, -1).astype(bf16),
        query_heads,
        key_heads,
        value_heads,
        (largest + jnp.log(totals))[..., 0],
    )


def attend_backward(query_heads, key_heads, value_heads, log_sums, heads_grad, segment, tables):
    length = query_heads.shape[0]
    cosine_table, sine_values = tables
    scores, grouped = block_scores(query_heads, key_heads, segment)
    probability = jnp.exp(scores - log_sums[..., None])
    probs_low = probability.astype(bf16)
    grad_grouped = heads_grad.reshape(grouped.shape)
    prob_grad = jnp.einsum(
        "qhgd,khd->hgqk", grad_grouped, value_heads, preferred_element_type=f32
    )
    weighted = jnp.sum(probability * prob_grad, axis=-1, keepdims=True)
    score_low = (probability * (prob_grad - weighted)).astype(bf16)
    query_part = (
        jnp.einsum("hgqk,khd->qhgd", score_low, key_heads, preferred_element_type=f32) * attn_scale
    ).reshape(query_heads.shape)
    key_sum = (
        jnp.einsum("hgqk,qhgd->khd", score_low, grouped, preferred_element_type=f32) * attn_scale
    )
    value_sum = jnp.einsum(
        "hgqk,qhgd->khd", probs_low, grad_grouped, preferred_element_type=f32
    )
    query_low = apply_rotation(query_part, cosine_table, -sine_values).astype(bf16)
    key_low = apply_rotation(key_sum, cosine_table, -sine_values).astype(bf16)
    return (
        query_low.reshape(length, -1),
        key_low.reshape(length, -1),
        value_sum.astype(bf16).reshape(length, -1),
    )


def bit_masks(size):
    masks = []
    while size > 1:
        size //= 2
        masks.append(size)
    return masks[::-1]


def swap(x, axis, mask):
    return lax.ppermute(x, axis, [(i, i ^ mask) for i in range(lax.axis_size(axis))])


def bit_of(axis, mask):
    return (lax.axis_index(axis) // mask) % 2


def halves_by_bit(x, axis, mask, dim=0):
    half = x.shape[dim] // 2
    bit = bit_of(axis, mask)
    mine = lax.dynamic_slice_in_dim(x, bit * half, half, dim)
    other = lax.dynamic_slice_in_dim(x, (1 - bit) * half, half, dim)
    return mine, other


def join_by_bit(mine, other, axis, mask, dim=0):
    return jnp.where(
        bit_of(axis, mask) == 0,
        jnp.concatenate([mine, other], dim),
        jnp.concatenate([other, mine], dim),
    )


def scatter_sum(x, axis, masks, kind, dim=0):
    x = x.astype(f32)
    for mask in masks:
        mine, other = halves_by_bit(x, axis, mask, dim)
        x = mine + swap(other.astype(kind), axis, mask).astype(f32)
    return x


def gather_blocks(x, axis, masks, dim=0):
    for mask in reversed(masks):
        x = join_by_bit(x, swap(x, axis, mask), axis, mask, dim)
    return x


def sum_all(x, axis):
    for mask in bit_masks(lax.axis_size(axis)):
        x = x + swap(x, axis, mask)
    return x


def rotated(masks, j):
    j = j % len(masks)
    return masks[j:] + masks[:j]


def row_parts(rows, count):
    units = rows // 16
    sizes = [16 * (units // count + (1 if i < units % count else 0)) for i in range(count)]
    starts = [sum(sizes[:i]) for i in range(count)]
    return list(zip(starts, sizes))


def cube_orders(masks, count):
    orders = []
    for j in range(count):
        order = [0]
        for mask in rotated(masks, j):
            order = order + [o ^ mask for o in order]
        orders.append(order)
    return orders


def cube_gather(x, masks):
    bufs = [x[s : s + n] for s, n in row_parts(x.shape[0], len(masks))]
    for phase in range(len(masks)):
        got = [swap(b, "dp", rotated(masks, j)[phase]) for j, b in enumerate(bufs)]
        bufs = [jnp.concatenate([b, g], 0) for b, g in zip(bufs, got)]
    return jnp.concatenate(bufs, 0)


def cube_scatter_sum(x, masks):
    devices = 2 ** len(masks)
    parts = row_parts(x.shape[0] // devices, len(masks))
    bufs = [x[devices * s : devices * (s + n)] for s, n in parts]
    for phase in reversed(range(len(masks))):
        got = [
            swap(b[b.shape[0] // 2 :].astype(bf16), "dp", rotated(masks, j)[phase])
            for j, b in enumerate(bufs)
        ]
        bufs = [b[: b.shape[0] // 2].astype(f32) + g.astype(f32) for b, g in zip(bufs, got)]
    return jnp.concatenate(bufs, 0)


def vector_gather(x, masks):
    x = x[None]
    for mask in masks:
        x = jnp.concatenate([x, swap(x, "dp", mask)], 0)
    return x


def vector_scatter(x, masks):
    for mask in reversed(masks):
        half = x.shape[0] // 2
        x = x[:half] + swap(x[half:], "dp", mask)
    return x[0]


def to_cube_rows(x, masks):
    parts = row_parts(x.shape[1], len(masks))
    orders = cube_orders(masks, len(masks))
    return jnp.concatenate(
        [x[o, s : s + n] for (s, n), order in zip(parts, orders) for o in order]
    )


def from_cube_rows(x, masks):
    devices = 2 ** len(masks)
    parts = row_parts(x.shape[0] // devices, len(masks))
    orders = cube_orders(masks, len(masks))
    found = {}
    for j, ((s, n), order) in enumerate(zip(parts, orders)):
        for place, o in enumerate(order):
            first = devices * s + place * n
            found[o, j] = x[first : first + n]
    return jnp.stack(
        [jnp.concatenate([found[o, j] for j in range(len(masks))]) for o in range(devices)]
    )


def dot(a, b, spec):
    return jnp.einsum(spec, a, b, preferred_element_type=f32)


def expert_passes(rows, grads, column, w_gate, w_up, w_down):
    gate_act = dot(rows, w_gate, "td,df->tf")
    up_act = dot(rows, w_up, "td,df->tf")
    sigmoid_gate = jax.nn.sigmoid(gate_act)
    silu_gate = gate_act * sigmoid_gate
    hidden = silu_gate * up_act
    weighted_low = (hidden * column[:, None]).astype(bf16)
    down_in = residual_scale * dot(grads, w_down, "td,fd->tf")
    gate_deriv = jnp.sum(hidden * down_in, axis=1)
    down_in = down_in * column[:, None]
    gate_low = (down_in * up_act * sigmoid_gate * (1.0 + gate_act * (1.0 - sigmoid_gate))).astype(
        bf16
    )
    up_low = (down_in * silu_gate).astype(bf16)
    return weighted_low, gate_deriv, gate_low, up_low


def summed_over_dp(x, kind):
    masks = bit_masks(lax.axis_size("dp"))
    inner, last = masks[:-1], masks[-1:]
    count = 3
    size = x.shape[0] // count
    outs = []
    for j in range(count):
        order = rotated(inner, j) + last
        part = scatter_sum(x[j * size : (j + 1) * size], "dp", order, kind)
        outs.append(gather_blocks(part.astype(kind), "dp", order))
    return jnp.concatenate(outs, 0).astype(f32)


def per_device(
    hidden_in,
    attn_gain,
    w_query,
    key_weight,
    value_weight,
    w_output,
    moe_gain,
    w_router,
    w_gate,
    w_up,
    w_down,
    expert_ids,
    segment_ids,
    out_grad,
):
    tokens_here, model_width = hidden_in.shape
    head_size = HEAD_DIM
    dp_size = lax.axis_size("dp")
    tensor_size = lax.axis_size("tensor")
    experts = w_gate.shape[0] * dp_size
    dp_index = lax.axis_index("dp")
    tensor_index = lax.axis_index("tensor")
    masks = bit_masks(dp_size)
    cube, pair = masks[:-1], masks[-1]
    tensor_masks = bit_masks(tensor_size)
    tensor_down = tensor_masks[::-1]
    rows_here = tokens_here // tensor_size

    def my_rows(x):
        return lax.dynamic_slice_in_dim(x, tensor_index * rows_here, rows_here, 0)

    block = w_gate.shape[2] // tensor_size

    def my_units(x, dim):
        return lax.dynamic_slice_in_dim(x, tensor_index * block, block, dim)

    def relative_gather(x, dim):
        for mask in tensor_masks:
            x = jnp.concatenate([x, swap(x, "tensor", mask)], dim)
        return x

    def relative_scatter(x, dim):
        x = x.astype(f32)
        for mask in reversed(tensor_masks):
            half = x.shape[dim] // 2
            keep = lax.slice_in_dim(x, 0, half, axis=dim)
            give = lax.slice_in_dim(x, half, 2 * half, axis=dim)
            x = keep + swap(give.astype(bf16), "tensor", mask).astype(f32)
        return x

    far_gate = relative_gather(swap(my_units(w_gate[0], 1), "dp", pair), 1)
    far_up = relative_gather(swap(my_units(w_up[0], 1), "dp", pair), 1)
    far_down = relative_gather(swap(my_units(w_down[0], 0), "dp", pair), 0)

    grad_mine = my_rows(out_grad)
    grads = cube_gather(grad_mine, cube)

    inputs = hidden_in.astype(f32)
    scale_in = lax.rsqrt(jnp.mean(inputs * inputs, axis=-1, keepdims=True) + epsilon)
    normed_low = (inputs * scale_in * attn_gain).astype(bf16)
    segment = segment_ids[0]
    tables = rope_tables(segment, head_size)
    heads_flat, query_heads, key_heads, value_heads, log_sums = attend_forward(
        normed_low, segment, tables, w_query, key_weight, value_weight, head_size
    )
    attn_part = jnp.dot(heads_flat, w_output, preferred_element_type=f32)
    attn_total = scatter_sum(attn_part, "tensor", tensor_down, f32)

    inputs_mine = my_rows(hidden_in).astype(f32)
    scale_in_mine = my_rows(scale_in)
    middle = inputs_mine + residual_scale * attn_total
    scale_mid = lax.rsqrt(jnp.mean(middle * middle, axis=-1, keepdims=True) + epsilon)
    routed_low = (middle * scale_mid * moe_gain).astype(bf16)
    rows = cube_gather(routed_low, cube)

    logits = dot(w_router, routed_low, "de,td->et")
    ids_mine = my_rows(expert_ids).T
    expert_range = jnp.arange(experts, dtype=jnp.int32)
    picked = jnp.any(ids_mine[None, :, :] == expert_range[:, None, None], axis=1)
    largest = jnp.max(jnp.where(picked, logits, -jnp.inf), axis=0, keepdims=True)
    raised = jnp.where(picked, jnp.exp(jnp.where(picked, logits - largest, 0.0)), 0.0)
    gate_weights = raised / jnp.sum(raised, axis=0, keepdims=True)
    all_weights = vector_gather(gate_weights, cube)
    near, far = dp_index, dp_index ^ pair

    def column_of(expert):
        picked_row = lax.dynamic_index_in_dim(all_weights, expert, 1, keepdims=False)
        return to_cube_rows(picked_row, cube)

    near_set = (w_gate[0], w_up[0], w_down[0])
    far_set = (far_gate, far_up, far_down)
    near_low, near_deriv, near_gate_low, near_up_low = expert_passes(
        rows, grads, column_of(near), *near_set
    )
    far_low, far_deriv, far_gate_low, far_up_low = expert_passes(
        rows, grads, column_of(far), *far_set
    )
    moe_part = dot(near_low, w_down[0], "tf,fd->td") + dot(far_low, far_down, "tf,fd->td")
    moe_total = cube_scatter_sum(moe_part.astype(bf16), cube)

    one_near = (expert_range == near).astype(f32)[None, :, None]
    one_far = (expert_range == far).astype(f32)[None, :, None]
    deriv_part = (
        one_near * from_cube_rows(near_deriv, cube)[:, None, :]
        + one_far * from_cube_rows(far_deriv, cube)[:, None, :]
    )
    gate_deriv = vector_scatter(deriv_part, cube)

    routed_part = (
        dot(near_gate_low, w_gate[0], "tf,df->td")
        + dot(near_up_low, w_up[0], "tf,df->td")
        + dot(far_gate_low, far_gate, "tf,df->td")
        + dot(far_up_low, far_up, "tf,df->td")
    )
    routed_grad = cube_scatter_sum(routed_part.astype(bf16), cube)

    far_gate_grad = relative_scatter(dot(rows, far_gate_low, "td,tf->df"), 1)
    far_up_grad = relative_scatter(dot(rows, far_up_low, "td,tf->df"), 1)
    far_down_grad = relative_scatter(residual_scale * dot(far_low, grads, "tf,td->fd"), 0)
    near_gate_grad = scatter_sum(
        dot(rows, near_gate_low, "td,tf->df"), "tensor", tensor_down, bf16, 1
    )
    near_up_grad = scatter_sum(dot(rows, near_up_low, "td,tf->df"), "tensor", tensor_down, bf16, 1)
    near_down_grad = scatter_sum(
        residual_scale * dot(near_low, grads, "tf,td->fd"), "tensor", tensor_down, bf16, 0
    )

    def returned(mine, away, dim):
        whole = mine + swap(away.astype(bf16), "dp", pair).astype(f32)
        return gather_blocks(whole, "tensor", tensor_down, dim)[None]

    gate_grad = returned(near_gate_grad, far_gate_grad, 1)
    up_grad = returned(near_up_grad, far_up_grad, 1)
    down_grad = returned(near_down_grad, far_down_grad, 0)

    block_mine = (middle + residual_scale * moe_total).astype(bf16)
    block_out = gather_blocks(block_mine, "tensor", tensor_down)

    chosen_grad = gate_weights * (
        gate_deriv - jnp.sum(gate_weights * gate_deriv, axis=0, keepdims=True)
    )
    logit_grad = chosen_grad.astype(bf16)
    router_part = dot(logit_grad, routed_low, "et,td->ed")
    routed_grad = routed_grad + dot(logit_grad, w_router, "et,de->td")
    gained = moe_gain * routed_grad
    moe_gain_part = jnp.sum(routed_grad * middle * scale_mid, axis=0)
    grad_top = grad_mine.astype(f32)
    middle_grad = (
        grad_top
        + scale_mid * gained
        - middle
        * (scale_mid * scale_mid * scale_mid)
        * jnp.mean(middle * gained, axis=-1, keepdims=True)
    )
    branch_low = gather_blocks(
        (residual_scale * middle_grad).astype(bf16), "tensor", tensor_down
    )
    w_output_grad = summed_over_dp(dot(heads_flat, branch_low, "tc,td->cd"), bf16)
    heads_grad = dot(branch_low, w_output, "td,cd->tc").astype(bf16)
    query_low, key_low, value_low = attend_backward(
        query_heads, key_heads, value_heads, log_sums, heads_grad, segment, tables
    )
    width_q, width_k = query_low.shape[1], key_low.shape[1]
    qkv_low = jnp.concatenate([query_low, key_low, value_low], axis=1)
    qkv_grad = summed_over_dp(dot(normed_low, qkv_low, "td,tc->dc"), bf16)
    qkv_weight = jnp.concatenate([w_query, key_weight, value_weight], axis=1)
    normed_part = dot(qkv_low, qkv_weight, "tc,dc->td")
    normed_grad = scatter_sum(normed_part, "tensor", tensor_down, f32)
    gained_in = attn_gain * normed_grad
    attn_gain_part = jnp.sum(normed_grad * inputs_mine * scale_in_mine, axis=0)
    input_mine = (
        middle_grad
        + scale_in_mine * gained_in
        - inputs_mine
        * (scale_in_mine * scale_in_mine * scale_in_mine)
        * jnp.mean(inputs_mine * gained_in, axis=-1, keepdims=True)
    )
    input_grad = gather_blocks(input_mine, "tensor", tensor_down)

    early = sum_all(
        sum_all(jnp.concatenate([router_part, moe_gain_part[None]], 0), "tensor"), "dp"
    )
    attn_gain_grad = sum_all(sum_all(attn_gain_part[None], "tensor"), "dp")[0]
    return (
        block_out,
        input_grad,
        attn_gain_grad,
        qkv_grad[:, :width_q],
        qkv_grad[:, width_q : width_q + width_k],
        qkv_grad[:, width_q + width_k :],
        w_output_grad,
        early[experts],
        early[:experts].T,
        gate_grad,
        up_grad,
        down_grad,
    )


def solution(mesh):
    placed = (
        P("dp", None),
        P(),
        P(None, "tensor"),
        P(None, "tensor"),
        P(None, "tensor"),
        P("tensor", None),
        P(),
        P(),
        P("dp", None, None),
        P("dp", None, None),
        P("dp", None, None),
        P("dp", None),
        P("dp", None),
        P("dp", None),
    )
    return jax.shard_map(
        per_device,
        mesh=mesh,
        in_specs=placed,
        out_specs=(
            P("dp", None),
            P("dp", None),
            P(),
            P(None, "tensor"),
            P(None, "tensor"),
            P(None, "tensor"),
            P("tensor", None),
            P(),
            P(),
            P("dp", None, None),
            P("dp", None, None),
            P("dp", None, None),
        ),
        check_vma=False,
    )
```

time: 2870 us -> 982 us (0.34)
  waiting for transfers between devices: 2000 us -> 476 us
  starting transfers between devices: 280 us -> 156 us
  blocking collectives: 110 us -> 0 us
  local copies, waits for them, and re-layouts: 137 us -> 78.8 us
  matrix products: 214 us -> 180 us
    all_to_all x4 -> x0, waiting for transfers between devices: 1630 us -> none  [the longest x1 571 us: per_device(): lax.all_to_all(rows_grad, 'dp', split_axis=0, concat_axis=0, tiled=True)]
    ppermute x0 -> x123, waiting for transfers between devices: none -> 476 us  [swap(): lax.ppermute(x, axis, [(i, i ^ mask) for i in range(lax.axis_size(axis))])]
    psum x3 -> x0, waiting for transfers between devices: 372 us -> none  [the longest x1 258 us: per_device(): lax.psum((query_grad, key_grad, value_grad, w_output_grad, router_grad, a...]
    all_to_all x4 -> x0, starting transfers between devices: 280 us -> none  [the longest x1 136 us: per_device(): lax.all_to_all(expert_out, 'dp', split_axis=0, concat_axis=0, tiled=True)]
    ppermute x0 -> x123, starting transfers between devices: none -> 156 us  [swap(): lax.ppermute(x, axis, [(i, i ^ mask) for i in range(lax.axis_size(axis))])]
    psum x1 -> x0, blocking collectives: 110 us -> none  [per_device(): lax.psum((query_grad, key_grad, value_grad, w_output_grad, router_grad, a...]
    gather x2 -> x0, local copies, waits for them, and re-layouts: 74.6 us -> none  [the longest x1 37.4 us: per_device(): rows_back[slot_index].reshape(tokens_here, top_count, model_width)]
    scatter x1 -> x0, local copies, waits for them, and re-layouts: 36.4 us -> none  [per_device(): dispatch_low = jnp.zeros((expert_total * capacity, model_width), jnp.bflo...]
  transfers between devices with their start and end apart: 7 -> 123, of which waited for: 7 -> 66; matrix products, arithmetic and copies ran while one was open for 7% -> 23% of each run, Pallas kernels for 0% -> 0%
where the time goes in v1:
time: 982 us; the launch traced here: 974 us
  waiting for transfers between devices  476 us (48%)
  matrix products  180 us (18%)
  starting transfers between devices  156 us (16%)
  local copies, waits for them, and re-layouts  78.8 us (8%)
  other arithmetic  78.8 us (8%)
    ppermute x123, waiting for transfers between devices, swap(): lax.ppermute(x, axis, [(i, i ^ mask) for i in range(lax.axis_size(axis))])  476 us
    ppermute x123, starting transfers between devices, swap(): lax.ppermute(x, axis, [(i, i ^ mask) for i in range(lax.axis_size(axis))])  156 us
    dot_general x25, matrix products, dot(): return jnp.einsum(spec, a, b, preferred_element_type=f32)  147 us
    unnamed x244, local copies, waits for them, and re-layouts  43.9 us
    select_n x29, other arithmetic, join_by_bit(): jnp.where(bit_of(axis, mask) == 0, jnp.concatenate([mine, other], dim), j...  24.4 us
  transfers between devices with their start and end apart: 123, of which 66 were waited for; matrix products, arithmetic and copies ran while one was open for 23% of the time, Pallas kernels for 0%

profile of v1, /device:TPU:0, one launch (start us, length us, event | category | flops | bytes accessed | tf_op | source)
XLA Modules:
  0.0 973.6 jit_solution(8882935600174818447)
XLA Ops:
  2.9 4.0 collective-permute-start.17
  48.3 60.8 %collective-permute-done.13 = bf16[1536,256]{1,0:T(8,128)(2,1)} collective-permute-done((bf16[1536,256]{1,0:T(8,128)(2,1)}, bf16[1536,256]{1,0:T(8,128)(2,1)}, u32[]{:S(2)}, u32[]{:S(2)}) %collective-permute-start.13) | collective-permute-done | bytes 786464 | tf_op jit(solution)/shard_map/ppermute | solution.py:119
  130.3 15.0 %collective-permute-done.12 = f32[4,16,256]{2,1,0:T(8,128)S(1)} collective-permute-done((f32[4,16,256]{2,1,0:T(8,128)S(1)}, f32[4,16,256]{2,1,0:T(8,128)S(1)}, u32[]{:S(2)}, u32[]{:S(2)}) %collective-permute-start.12) | collective-permute-done | bytes 65568 | tf_op jit(solution)/shard_map/ppermute | solution.py:119
  157.0 13.0 %collective-permute-done.32 = bf16[80,1536]{1,0:T(8,128)(2,1)} collective-permute-done((bf16[80,1536]{1,0:T(8,128)(2,1)}, bf16[80,1536]{1,0:T(8,128)(2,1)}, u32[]{:S(2)}, u32[]{:S(2)}) %collective-permute-start.32) | collective-permute-done | bytes 245792 | tf_op jit(solution)/shard_map/ppermute | solution.py:119
  179.7 5.6 collective-permute-done.33
  188.9 19.4 %collective-permute-done.3 = bf16[384,1536]{1,0:T(8,128)(2,1)S(1)} collective-permute-done((bf16[384,1536]{1,0:T(8,128)(2,1)S(1)}, bf16[384,1536]{1,0:T(8,128)(2,1)S(1)}, u32[]{:S(2)}, u32[]{:S(2)}) %collective-permute-start.3) | collective-permute-done | bytes 1179680 | tf_op jit(solution)/shard_map/ppermute | solution.py:119
  226.3 5.8 collective-permute-done.5
  236.3 5.4 collective-permute-done.36
  244.7 13.6 %collective-permute-done.6 = bf16[320,1536]{1,0:T(8,128)(2,1)S(1)} collective-permute-done((bf16[320,1536]{1,0:T(8,128)(2,1)S(1)}, bf16[320,1536]{1,0:T(8,128)(2,1)S(1)}, u32[]{:S(2)}, u32[]{:S(2)}) %collective-permute-start.6) | collective-permute-done | bytes 983072 | tf_op jit(solution)/shard_map/ppermute | solution.py:119
  262.6 7.9 fusion.37
  270.5 6.6 fusion.94
  277.2 5.5 fusion.31
  282.7 5.0 fusion.95
  287.7 11.2 %multiply_convert_fusion.1 = (bf16[2048,512]{0,1:T(8,128)(2,1)S(1)}, f32[2048]{0:T(1024)S(1)}, bf16[2048,512]{0,1:T(8,128)(2,1)S(1)}, bf16[2048,512]{0,1:T(8,128)(2,1)}) fusion(f32[2048,512]{0,1:T(8,128)} %fusion.94, f32[2048,512]{0,1:T(8,128)} %fusion.95, f32[2048]{0:T(1024)S(1)} %broadcast_multiply_fusion, f32[2048]{0:T(1024)S(1)} %concatenate.424, ...), kind=kOutput, calls=%fused_computation.20 | convolution fusion | flops 3242194944 | bytes 22568960 | tf_op jit(solution)/shard_map/td,df->tf/dot_general | solution.py:242
  299.0 12.0 %multiply_convert_fusion.3 = (bf16[2048,512]{0,1:T(8,128)(2,1)S(1)}, f32[2048]{0:T(1024)S(1)}, bf16[2048,512]{0,1:T(8,128)(2,1)}, bf16[2048,512]{0,1:T(8,128)(2,1)}) fusion(f32[2048,512]{0,1:T(8,128)} %fusion.37, f32[2048,512]{0,1:T(8,128)} %fusion.31, f32[2048]{0:T(1024)S(1)} %broadcast_multiply_fusion.1, f32[2048]{0:T(1024)S(1)} %concatenate.421, ...), kind=kOutput, calls=%fused_computation.22 | convolution fusion | flops 3242194944 | bytes 22568960 | tf_op jit(solution)/shard_map/td,df->tf/dot_general | solution.py:242
  311.1 7.9 fusion.99
  319.0 6.6 fusion.96
  325.7 8.0 fusion.100
  333.7 6.5 fusion.35
  340.2 5.1 fusion.98
  345.3 6.5 fusion.39
  351.8 5.1 convolution_multiply_fusion.1
  356.9 6.4 fusion.33
  363.3 5.1 fusion.101
  368.4 5.1 convolution_multiply_fusion
  378.6 18.0 %add_convert_fusion = bf16[2048,1536]{1,0:T(8,128)(2,1)} fusion(f32[2048,1536]{1,0:T(8,128)} %fusion.96, f32[2048,1536]{1,0:T(8,128)} %fusion.39, f32[2048,1536]{1,0:T(8,128)} %fusion.35, bf16[2048,512]{0,1:T(8,128)(2,1)} %copy-done.29, bf16[1536,512]{1,0:T(8,128)(2,1)} %constant_dynamic-update-slice_fusion.14), kind=kOutput, calls=%fused_computation.7 | convolution fusion | flops 3233808384 | bytes 47710208 | tf_op jit(solution)/shard_map/tf,df->td/dot_general | solution.py:242
  398.4 9.3 add_convert_fusion.1
  426.5 17.0 %collective-permute-done.41 = bf16[320,1536]{1,0:T(8,128)(2,1)S(1)} collective-permute-done((bf16[320,1536]{1,0:T(8,128)(2,1)S(1)}, bf16[320,1536]{1,0:T(8,128)(2,1)S(1)}, u32[]{:S(2)}, u32[]{:S(2)}) %collective-permute-start.41) | collective-permute-done | bytes 983072 | tf_op jit(solution)/shard_map/ppermute | solution.py:119
  447.5 15.3 %collective-permute-done.22 = bf16[320,1536]{1,0:T(8,128)(2,1)S(1)} collective-permute-done((bf16[320,1536]{1,0:T(8,128)(2,1)S(1)}, bf16[320,1536]{1,0:T(8,128)(2,1)S(1)}, u32[]{:S(2)}, u32[]{:S(2)}) %collective-permute-start.22) | collective-permute-done | bytes 983072 | tf_op jit(solution)/shard_map/ppermute | solution.py:119
  466.4 7.8 collective-permute-done.38
  474.2 9.9 %collective-permute-start.121 = (bf16[256,1536]{1,0:T(8,128)(2,1)}, bf16[256,1536]{1,0:T(8,128)(2,1)S(1)}, u32[]{:S(2)}, u32[]{:S(2)}) collective-permute-start(bf16[256,1536]{1,0:T(8,128)(2,1)} %fusion.26), channel_id=1, source_target_pairs={{0,16},{2,18},{4,20},{6,22},{8,24},{10,26},{12,28},{14,30},{16,0},... | collective-permute-start | bytes 2359304 | tf_op jit(solution)/shard_map/ppermute | solution.py:119
  484.5 29.6 %collective-permute-done.19 = bf16[384,1536]{1,0:T(8,128)(2,1)S(1)} collective-permute-done((bf16[384,1536]{1,0:T(8,128)(2,1)S(1)}, bf16[384,1536]{1,0:T(8,128)(2,1)S(1)}, u32[]{:S(2)}, u32[]{:S(2)}) %collective-permute-start.19) | collective-permute-done | bytes 1179680 | tf_op jit(solution)/shard_map/ppermute | solution.py:119
  515.9 9.7 collective-permute-done.45
  525.7 10.5 %collective-permute-done.42 = bf16[160,1536]{1,0:T(8,128)(2,1)S(1)} collective-permute-done((bf16[160,1536]{1,0:T(8,128)(2,1)S(1)}, bf16[160,1536]{1,0:T(8,128)(2,1)S(1)}, u32[]{:S(2)}, u32[]{:S(2)}) %collective-permute-start.42) | collective-permute-done | bytes 491552 | tf_op jit(solution)/shard_map/ppermute | solution.py:119
  538.4 8.1 collective-permute-done.26
  547.2 9.5 collective-permute-done.23
  556.7 4.7 collective-permute-start.117
  565.5 43.7 %collective-permute-done.117 = bf16[1536,256]{0,1:T(8,128)(2,1)S(1)} collective-permute-done((bf16[1536,256]{0,1:T(8,128)(2,1)S(1)}, bf16[1536,256]{0,1:T(8,128)(2,1)S(1)}, u32[]{:S(2)}, u32[]{:S(2)}) %collective-permute-start.117) | collective-permute-done | bytes 786464 | tf_op jit(solution)/shard_map/ppermute | solution.py:119
  610.6 17.4 %collective-permute-done.46 = bf16[80,1536]{1,0:T(8,128)(2,1)S(1)} collective-permute-done((bf16[80,1536]{1,0:T(8,128)(2,1)S(1)}, bf16[80,1536]{1,0:T(8,128)(2,1)S(1)}, u32[]{:S(2)}, u32[]{:S(2)}) %collective-permute-start.46) | collective-permute-done | bytes 245792 | tf_op jit(solution)/shard_map/ppermute | solution.py:119
  629.1 6.7 collective-permute-done.43
  635.9 7.0 collective-permute-done.27
  644.4 4.7 collective-permute-done.24
  650.4 5.4 collective-permute-done.40
  660.7 7.8 collective-permute-done.21
  669.8 3.8 collective-permute-done.107
  674.8 4.1 collective-permute-done.108
  688.0 6.7 collective-permute-done.110
  700.7 6.4 fusion.49
  707.1 9.5 fusion
  716.8 7.1 fusion.2
  748.9 5.3 maximum_select_fusion.2
  754.3 5.4 maximum_select_fusion.1
  768.0 5.3 maximum_select_fusion.3
  779.9 14.7 %collective-permute-done.91 = bf16[64,1536]{1,0:T(8,128)(2,1)S(1)} collective-permute-done((bf16[64,1536]{1,0:T(8,128)(2,1)S(1)}, bf16[64,1536]{1,0:T(8,128)(2,1)S(1)}, u32[]{:S(2)}, u32[]{:S(2)}) %collective-permute-start.91) | collective-permute-done | bytes 196640 | tf_op jit(solution)/shard_map/ppermute | solution.py:119
  795.5 5.5 collective-permute-done.99
  802.1 4.5 collective-permute-done.83
  851.3 4.7 collective-permute-done.103
  858.7 4.6 collective-permute-done.87
  878.4 3.9 collective-permute-done.69
  910.3 4.1 collective-permute-done.71
  915.4 4.3 collective-permute-done.79
  919.7 3.9 collective-permute-start.63
  949.9 8.4 collective-permute-done.57
  960.1 5.5 collective-permute-done.65
  (709 shorter events, 356.1 us)
Async XLA Ops:
  2.9 107.4 %collective-permute-start.17 = (bf16[256,1536]{1,0:T(8,128)(2,1)}, bf16[256,1536]{1,0:T(8,128)(2,1)}, u32[]{:S(2)}, u32[]{:S(2)}) collective-permute-start(bf16[256,1536]{1,0:T(8,128)(2,1)} %dynamic-slice_bitcast_fusion), channel_id=1, source_target_pairs={{0,16},{2,18},{4,20},{6,22},{8,24},{10,26},{12,28},{14,30},{16,0},... | collective-permute-start | bytes 2359304 | tf_op jit(solution)/shard_map/ppermute | solution.py:119
  7.9 103.0 %collective-permute-start.15 = (bf16[1536,256]{1,0:T(8,128)(2,1)}, bf16[1536,256]{1,0:T(8,128)(2,1)}, u32[]{:S(2)}, u32[]{:S(2)}) collective-permute-start(bf16[1536,256]{1,0:T(8,128)(2,1)} %dynamic-slice_bitcast_fusion.1), channel_id=1, source_target_pairs={{0,16},{2,18},{4,20},{6,22},{8,24},{10,26},{12,28},{14,30},{16,0},... | collective-permute-start | bytes 2359304 | tf_op jit(solution)/shard_map/ppermute | solution.py:119
  8.8 100.2 %collective-permute-start.13 = (bf16[1536,256]{1,0:T(8,128)(2,1)}, bf16[1536,256]{1,0:T(8,128)(2,1)}, u32[]{:S(2)}, u32[]{:S(2)}) collective-permute-start(bf16[1536,256]{1,0:T(8,128)(2,1)} %dynamic-slice_bitcast_fusion.2), channel_id=1, source_target_pairs={{0,16},{2,18},{4,20},{6,22},{8,24},{10,26},{12,28},{14,30},{16,0},... | collective-permute-start | bytes 2359304 | tf_op jit(solution)/shard_map/ppermute | solution.py:119
  13.5 32.4 %collective-permute-start.29 = (bf16[96,1536]{1,0:T(8,128)(2,1)S(1)}, bf16[96,1536]{1,0:T(8,128)(2,1)S(1)}, u32[]{:S(2)}, u32[]{:S(2)}) collective-permute-start(bf16[96,1536]{1,0:T(8,128)(2,1)S(1)} %get-tuple-element.60), channel_id=1, source_target_pairs={{0,2},{2,0},{4,6},{6,4},{8,10},{10,8},{12,14},{14,12},{16,18},{18,... | collective-permute-start | bytes 884744 | tf_op jit(solution)/shard_map/ppermute | solution.py:119
  43.8 73.2 %collective-permute-start = (f32[256,1536]{1,0:T(8,128)}, f32[256,1536]{1,0:T(8,128)}, u32[]{:S(2)}, u32[]{:S(2)}) collective-permute-start(f32[256,1536]{1,0:T(8,128)} %constant_dynamic-slice_fusion.7), channel_id=1, source_target_pairs={{0,1},{1,0},{2,3},{3,2},{4,5},{5,4},{6,7},{7,6},{8,9},{9,8},{10,11... | collective-permute-start | bytes 4718600 | tf_op jit(solution)/shard_map/ppermute | solution.py:119
  46.0 68.4 %collective-permute-start.30 = (bf16[192,1536]{1,0:T(8,128)(2,1)S(1)}, bf16[192,1536]{1,0:T(8,128)(2,1)S(1)}, u32[]{:S(2)}, u32[]{:S(2)}) collective-permute-start(bf16[192,1536]{1,0:T(8,128)(2,1)S(1)} %pad_maximum_fusion.10), channel_id=1, source_target_pairs={{0,4},{2,6},{4,0},{6,2},{8,12},{10,14},{12,8},{14,10},{16,20},{18,... | collective-permute-start | bytes 1769480 | tf_op jit(solution)/shard_map/ppermute | solution.py:119
  109.1 13.7 %collective-permute-start.14 = (bf16[1536,256]{1,0:T(8,128)(2,1)}, bf16[1536,256]{1,0:T(8,128)(2,1)S(1)}, u32[]{:S(2)}, u32[]{:S(2)}) collective-permute-start(bf16[1536,256]{1,0:T(8,128)(2,1)} %collective-permute-done.13), channel_id=1, source_target_pairs={{0,1},{1,0},{2,3},{3,2},{4,5},{5,4},{6,7},{7,6},{8,9},{9,8},{10,11... | collective-permute-start | bytes 2359304 | tf_op jit(solution)/shard_map/ppermute | solution.py:119
  110.3 20.0 %collective-permute-start.18 = (bf16[256,1536]{1,0:T(8,128)(2,1)}, bf16[256,1536]{1,0:T(8,128)(2,1)S(1)}, u32[]{:S(2)}, u32[]{:S(2)}) collective-permute-start(bf16[256,1536]{1,0:T(8,128)(2,1)} %collective-permute-done.17), channel_id=1, source_target_pairs={{0,1},{1,0},{2,3},{3,2},{4,5},{5,4},{6,7},{7,6},{8,9},{9,8},{10,11... | collective-permute-start | bytes 2359304 | tf_op jit(solution)/shard_map/ppermute | solution.py:119
  110.9 15.7 %collective-permute-start.16 = (bf16[1536,256]{1,0:T(8,128)(2,1)}, bf16[1536,256]{1,0:T(8,128)(2,1)S(1)}, u32[]{:S(2)}, u32[]{:S(2)}) collective-permute-start(bf16[1536,256]{1,0:T(8,128)(2,1)} %collective-permute-done.15), channel_id=1, source_target_pairs={{0,1},{1,0},{2,3},{3,2},{4,5},{5,4},{6,7},{7,6},{8,9},{9,8},{10,11... | collective-permute-start | bytes 2359304 | tf_op jit(solution)/shard_map/ppermute | solution.py:119
  115.4 35.7 %collective-permute-start.31 = (bf16[384,1536]{1,0:T(8,128)(2,1)}, bf16[384,1536]{1,0:T(8,128)(2,1)}, u32[]{:S(2)}, u32[]{:S(2)}) collective-permute-start(bf16[384,1536]{1,0:T(8,128)(2,1)} %pad_maximum_fusion.2), channel_id=1, source_target_pairs={{0,8},{2,10},{4,12},{6,14},{8,0},{10,2},{12,4},{14,6},{16,24},{18,... | collective-permute-start | bytes 3538952 | tf_op jit(solution)/shard_map/ppermute | solution.py:119
  122.8 24.9 %collective-permute-start.1 = (bf16[96,1536]{1,0:T(8,128)(2,1)S(1)}, bf16[96,1536]{1,0:T(8,128)(2,1)}, u32[]{:S(2)}, u32[]{:S(2)}) collective-permute-start(bf16[96,1536]{1,0:T(8,128)(2,1)S(1)} %get-tuple-element.95), channel_id=1, source_target_pairs={{0,2},{2,0},{4,6},{6,4},{8,10},{10,8},{12,14},{14,12},{16,18},{18,... | collective-permute-start | bytes 884744 | tf_op jit(solution)/shard_map/ppermute | solution.py:119
  128.9 16.4 %collective-permute-start.12 = (f32[4,16,256]{2,1,0:T(8,128)S(1)}, f32[4,16,256]{2,1,0:T(8,128)S(1)}, u32[]{:S(2)}, u32[]{:S(2)}) collective-permute-start(f32[4,16,256]{2,1,0:T(8,128)S(1)} %pad_maximum_fusion.22), channel_id=1, source_target_pairs={{0,8},{2,10},{4,12},{6,14},{8,0},{10,2},{12,4},{14,6},{16,24},{18,... | collective-permute-start | bytes 196616 | tf_op jit(solution)/shard_map/ppermute | solution.py:119
  149.5 22.4 %collective-permute-start.2 = (bf16[192,1536]{1,0:T(8,128)(2,1)}, bf16[192,1536]{1,0:T(8,128)(2,1)}, u32[]{:S(2)}, u32[]{:S(2)}) collective-permute-start(bf16[192,1536]{1,0:T(8,128)(2,1)} %pad_maximum_fusion.9), channel_id=1, source_target_pairs={{0,4},{2,6},{4,0},{6,2},{8,12},{10,14},{12,8},{14,10},{16,20},{18,... | collective-permute-start | bytes 1769480 | tf_op jit(solution)/shard_map/ppermute | solution.py:119
  155.2 14.8 %collective-permute-start.32 = (bf16[80,1536]{1,0:T(8,128)(2,1)}, bf16[80,1536]{1,0:T(8,128)(2,1)}, u32[]{:S(2)}, u32[]{:S(2)}) collective-permute-start(bf16[80,1536]{1,0:T(8,128)(2,1)} %get-tuple-element.58), channel_id=1, source_target_pairs={{0,4},{2,6},{4,0},{6,2},{8,12},{10,14},{12,8},{14,10},{16,20},{18,... | collective-permute-start | bytes 737288 | tf_op jit(solution)/shard_map/ppermute | solution.py:119
  171.1 14.2 %collective-permute-start.33 = (bf16[160,1536]{1,0:T(8,128)(2,1)S(1)}, bf16[160,1536]{1,0:T(8,128)(2,1)S(1)}, u32[]{:S(2)}, u32[]{:S(2)}) collective-permute-start(bf16[160,1536]{1,0:T(8,128)(2,1)S(1)} %pad_maximum_fusion.17), channel_id=1, source_target_pairs={{0,8},{2,10},{4,12},{6,14},{8,0},{10,2},{12,4},{14,6},{16,24},{18,... | collective-permute-start | bytes 1474568 | tf_op jit(solution)/shard_map/ppermute | solution.py:119
  173.1 35.2 %collective-permute-start.3 = (bf16[384,1536]{1,0:T(8,128)(2,1)S(1)}, bf16[384,1536]{1,0:T(8,128)(2,1)S(1)}, u32[]{:S(2)}, u32[]{:S(2)}) collective-permute-start(bf16[384,1536]{1,0:T(8,128)(2,1)S(1)} %pad_maximum_fusion.1), channel_id=1, source_target_pairs={{0,8},{2,10},{4,12},{6,14},{8,0},{10,2},{12,4},{14,6},{16,24},{18,... | collective-permute-start | bytes 3538952 | tf_op jit(solution)/shard_map/ppermute | solution.py:119
  186.4 26.0 %collective-permute-start.34 = (bf16[320,1536]{1,0:T(8,128)(2,1)S(1)}, bf16[320,1536]{1,0:T(8,128)(2,1)S(1)}, u32[]{:S(2)}, u32[]{:S(2)}) collective-permute-start(bf16[320,1536]{1,0:T(8,128)(2,1)S(1)} %pad_maximum_fusion.5), channel_id=1, source_target_pairs={{0,2},{2,0},{4,6},{6,4},{8,10},{10,8},{12,14},{14,12},{16,18},{18,... | collective-permute-start | bytes 2949128 | tf_op jit(solution)/shard_map/ppermute | solution.py:119
  217.7 16.1 %collective-permute-start.8 = (bf16[160,1536]{1,0:T(8,128)(2,1)S(1)}, bf16[160,1536]{1,0:T(8,128)(2,1)S(1)}, u32[]{:S(2)}, u32[]{:S(2)}) collective-permute-start(bf16[160,1536]{1,0:T(8,128)(2,1)S(1)} %pad_maximum_fusion.16), channel_id=1, source_target_pairs={{0,2},{2,0},{4,6},{6,4},{8,10},{10,8},{12,14},{14,12},{16,18},{18,... | collective-permute-start | bytes 1474568 | tf_op jit(solution)/shard_map/ppermute | solution.py:119
  219.5 12.7 %collective-permute-start.5 = (bf16[160,1536]{1,0:T(8,128)(2,1)S(1)}, bf16[160,1536]{1,0:T(8,128)(2,1)S(1)}, u32[]{:S(2)}, u32[]{:S(2)}) collective-permute-start(bf16[160,1536]{1,0:T(8,128)(2,1)S(1)} %pad_maximum_fusion.15), channel_id=1, source_target_pairs={{0,8},{2,10},{4,12},{6,14},{8,0},{10,2},{12,4},{14,6},{16,24},{18,... | collective-permute-start | bytes 1474568 | tf_op jit(solution)/shard_map/ppermute | solution.py:119
  224.0 17.7 %collective-permute-start.36 = (bf16[160,1536]{1,0:T(8,128)(2,1)S(1)}, bf16[160,1536]{1,0:T(8,128)(2,1)S(1)}, u32[]{:S(2)}, u32[]{:S(2)}) collective-permute-start(bf16[160,1536]{1,0:T(8,128)(2,1)S(1)} %pad_maximum_fusion.18), channel_id=1, source_target_pairs={{0,2},{2,0},{4,6},{6,4},{8,10},{10,8},{12,14},{14,12},{16,18},{18,... | collective-permute-start | bytes 1474568 | tf_op jit(solution)/shard_map/ppermute | solution.py:119
  232.2 26.1 %collective-permute-start.6 = (bf16[320,1536]{1,0:T(8,128)(2,1)S(1)}, bf16[320,1536]{1,0:T(8,128)(2,1)S(1)}, u32[]{:S(2)}, u32[]{:S(2)}) collective-permute-start(bf16[320,1536]{1,0:T(8,128)(2,1)S(1)} %pad_maximum_fusion.3), channel_id=1, source_target_pairs={{0,2},{2,0},{4,6},{6,4},{8,10},{10,8},{12,14},{14,12},{16,18},{18,... | collective-permute-start | bytes 2949128 | tf_op jit(solution)/shard_map/ppermute | solution.py:119
  233.9 27.6 %collective-permute-start.9 = (bf16[320,1536]{1,0:T(8,128)(2,1)S(1)}, bf16[320,1536]{1,0:T(8,128)(2,1)S(1)}, u32[]{:S(2)}, u32[]{:S(2)}) collective-permute-start(bf16[320,1536]{1,0:T(8,128)(2,1)S(1)} %pad_maximum_fusion.4), channel_id=1, source_target_pairs={{0,4},{2,6},{4,0},{6,2},{8,12},{10,14},{12,8},{14,10},{16,20},{18,... | collective-permute-start | bytes 2949128 | tf_op jit(solution)/shard_map/ppermute | solution.py:119
  241.8 35.3 %collective-permute-start.37 = (bf16[320,1536]{1,0:T(8,128)(2,1)S(1)}, bf16[320,1536]{1,0:T(8,128)(2,1)S(1)}, u32[]{:S(2)}, u32[]{:S(2)}) collective-permute-start(bf16[320,1536]{1,0:T(8,128)(2,1)S(1)} %pad_maximum_fusion.6), channel_id=1, source_target_pairs={{0,4},{2,6},{4,0},{6,2},{8,12},{10,14},{12,8},{14,10},{16,20},{18,... | collective-permute-start | bytes 2949128 | tf_op jit(solution)/shard_map/ppermute | solution.py:119
  375.6 32.3 %collective-permute-start.47 = (f32[4,16,256]{2,1,0:T(8,128)S(1)}, f32[4,16,256]{2,1,0:T(8,128)S(1)}, u32[]{:S(2)}, u32[]{:S(2)}) collective-permute-start(f32[4,16,256]{2,1,0:T(8,128)S(1)} %slice.871), channel_id=1, source_target_pairs={{0,8},{2,10},{4,12},{6,14},{8,0},{10,2},{12,4},{14,6},{16,24},{18,... | collective-permute-start | bytes 196616 | tf_op jit(solution)/shard_map/ppermute | solution.py:119
  378.6 183.1 %collective-permute-start.119 = (bf16[256,1536]{1,0:T(8,128)(2,1)}, bf16[256,1536]{1,0:T(8,128)(2,1)S(1)}, u32[]{:S(2)}, u32[]{:S(2)}) collective-permute-start(bf16[256,1536]{1,0:T(8,128)(2,1)} %dynamic-slice_convert_fusion), channel_id=1, source_target_pairs={{0,1},{1,0},{2,3},{3,2},{4,5},{5,4},{6,7},{7,6},{8,9},{9,8},{10,11... | collective-permute-start | bytes 2359304 | tf_op jit(solution)/shard_map/ppermute | solution.py:119
  418.8 24.7 %collective-permute-start.41 = (bf16[320,1536]{1,0:T(8,128)(2,1)S(1)}, bf16[320,1536]{1,0:T(8,128)(2,1)S(1)}, u32[]{:S(2)}, u32[]{:S(2)}) collective-permute-start(bf16[320,1536]{1,0:T(8,128)(2,1)S(1)} %get-tuple-element.76), channel_id=1, source_target_pairs={{0,2},{2,0},{4,6},{6,4},{8,10},{10,8},{12,14},{14,12},{16,18},{18,... | collective-permute-start | bytes 2949128 | tf_op jit(solution)/shard_map/ppermute | solution.py:119
  420.6 24.7 %collective-permute-start.44 = (bf16[320,1536]{1,0:T(8,128)(2,1)S(1)}, bf16[320,1536]{1,0:T(8,128)(2,1)S(1)}, u32[]{:S(2)}, u32[]{:S(2)}) collective-permute-start(bf16[320,1536]{1,0:T(8,128)(2,1)S(1)} %get-tuple-element.77), channel_id=1, source_target_pairs={{0,4},{2,6},{4,0},{6,2},{8,12},{10,14},{12,8},{14,10},{16,20},{18,... | collective-permute-start | bytes 2949128 | tf_op jit(solution)/shard_map/ppermute | solution.py:119
  422.8 39.9 %collective-permute-start.22 = (bf16[320,1536]{1,0:T(8,128)(2,1)S(1)}, bf16[320,1536]{1,0:T(8,128)(2,1)S(1)}, u32[]{:S(2)}, u32[]{:S(2)}) collective-permute-start(bf16[320,1536]{1,0:T(8,128)(2,1)S(1)} %get-tuple-element.80), channel_id=1, source_target_pairs={{0,2},{2,0},{4,6},{6,4},{8,10},{10,8},{12,14},{14,12},{16,18},{18,... | collective-permute-start | bytes 2949128 | tf_op jit(solution)/shard_map/ppermute | solution.py:119
  424.5 39.7 %collective-permute-start.25 = (bf16[320,1536]{1,0:T(8,128)(2,1)S(1)}, bf16[320,1536]{1,0:T(8,128)(2,1)S(1)}, u32[]{:S(2)}, u32[]{:S(2)}) collective-permute-start(bf16[320,1536]{1,0:T(8,128)(2,1)S(1)} %get-tuple-element.81), channel_id=1, source_target_pairs={{0,4},{2,6},{4,0},{6,2},{8,12},{10,14},{12,8},{14,10},{16,20},{18,... | collective-permute-start | bytes 2949128 | tf_op jit(solution)/shard_map/ppermute | solution.py:119
  443.5 240.8 %collective-permute-start.111 = (bf16[1536,256]{0,1:T(8,128)(2,1)}, bf16[1536,256]{0,1:T(8,128)(2,1)S(1)}, u32[]{:S(2)}, u32[]{:S(2)}) collective-permute-start(bf16[1536,256]{0,1:T(8,128)(2,1)} %dynamic-slice_convert_fusion.2), channel_id=1, source_target_pairs={{0,1},{1,0},{2,3},{3,2},{4,5},{5,4},{6,7},{7,6},{8,9},{9,8},{10,11... | collective-permute-start | bytes 2359304 | tf_op jit(solution)/shard_map/ppermute | solution.py:119
  445.3 28.9 %collective-permute-start.38 = (bf16[384,1536]{1,0:T(8,128)(2,1)S(1)}, bf16[384,1536]{1,0:T(8,128)(2,1)S(1)}, u32[]{:S(2)}, u32[]{:S(2)}) collective-permute-start(bf16[384,1536]{1,0:T(8,128)(2,1)S(1)} %slice.805), channel_id=1, source_target_pairs={{0,8},{2,10},{4,12},{6,14},{8,0},{10,2},{12,4},{14,6},{16,24},{18,... | collective-permute-start | bytes 3538952 | tf_op jit(solution)/shard_map/ppermute | solution.py:119
  462.7 101.8 %collective-permute-start.115 = (bf16[1536,256]{0,1:T(8,128)(2,1)}, bf16[1536,256]{0,1:T(8,128)(2,1)S(1)}, u32[]{:S(2)}, u32[]{:S(2)}) collective-permute-start(bf16[1536,256]{0,1:T(8,128)(2,1)} %dynamic-slice_convert_fusion.1), channel_id=1, source_target_pairs={{0,1},{1,0},{2,3},{3,2},{4,5},{5,4},{6,7},{7,6},{8,9},{9,8},{10,11... | collective-permute-start | bytes 2359304 | tf_op jit(solution)/shard_map/ppermute | solution.py:119
  464.2 49.8 %collective-permute-start.19 = (bf16[384,1536]{1,0:T(8,128)(2,1)S(1)}, bf16[384,1536]{1,0:T(8,128)(2,1)S(1)}, u32[]{:S(2)}, u32[]{:S(2)}) collective-permute-start(bf16[384,1536]{1,0:T(8,128)(2,1)S(1)} %slice.787), channel_id=1, source_target_pairs={{0,8},{2,10},{4,12},{6,14},{8,0},{10,2},{12,4},{14,6},{16,24},{18,... | collective-permute-start | bytes 3538952 | tf_op jit(solution)/shard_map/ppermute | solution.py:119
  474.2 87.6 %collective-permute-start.121 = (bf16[256,1536]{1,0:T(8,128)(2,1)}, bf16[256,1536]{1,0:T(8,128)(2,1)S(1)}, u32[]{:S(2)}, u32[]{:S(2)}) collective-permute-start(bf16[256,1536]{1,0:T(8,128)(2,1)} %fusion.26), channel_id=1, source_target_pairs={{0,16},{2,18},{4,20},{6,22},{8,24},{10,26},{12,28},{14,30},{16,0},... | collective-permute-start | bytes 2359304 | tf_op jit(solution)/shard_map/ppermute | solution.py:119
  556.7 52.4 %collective-permute-start.117 = (bf16[1536,256]{0,1:T(8,128)(2,1)S(1)}, bf16[1536,256]{0,1:T(8,128)(2,1)S(1)}, u32[]{:S(2)}, u32[]{:S(2)}) collective-permute-start(bf16[1536,256]{0,1:T(8,128)(2,1)S(1)} %copy-done.44), channel_id=1, source_target_pairs={{0,16},{2,18},{4,20},{6,22},{8,24},{10,26},{12,28},{14,30},{16,0},... | collective-permute-start | bytes 2359304 | tf_op jit(solution)/shard_map/ppermute | solution.py:119
  561.7 124.6 %collective-permute-start.113 = (bf16[1536,256]{0,1:T(8,128)(2,1)S(1)}, bf16[1536,256]{0,1:T(8,128)(2,1)S(1)}, u32[]{:S(2)}, u32[]{:S(2)}) collective-permute-start(bf16[1536,256]{0,1:T(8,128)(2,1)S(1)} %copy-done.43), channel_id=1, source_target_pairs={{0,16},{2,18},{4,20},{6,22},{8,24},{10,26},{12,28},{14,30},{16,0},... | collective-permute-start | bytes 2359304 | tf_op jit(solution)/shard_map/ppermute | solution.py:119
  561.8 82.2 %collective-permute-start.39 = (bf16[192,1536]{1,0:T(8,128)(2,1)S(1)}, bf16[192,1536]{1,0:T(8,128)(2,1)S(1)}, u32[]{:S(2)}, u32[]{:S(2)}) collective-permute-start(bf16[192,1536]{1,0:T(8,128)(2,1)S(1)} %slice.1019), channel_id=1, source_target_pairs={{0,4},{2,6},{4,0},{6,2},{8,12},{10,14},{12,8},{14,10},{16,20},{18,... | collective-permute-start | bytes 1769480 | tf_op jit(solution)/shard_map/ppermute | solution.py:119
  564.5 92.1 %collective-permute-start.20 = (bf16[192,1536]{1,0:T(8,128)(2,1)S(1)}, bf16[192,1536]{1,0:T(8,128)(2,1)S(1)}, u32[]{:S(2)}, u32[]{:S(2)}) collective-permute-start(bf16[192,1536]{1,0:T(8,128)(2,1)S(1)} %slice.1020), channel_id=1, source_target_pairs={{0,4},{2,6},{4,0},{6,2},{8,12},{10,14},{12,8},{14,10},{16,20},{18,... | collective-permute-start | bytes 1769480 | tf_op jit(solution)/shard_map/ppermute | solution.py:119
  609.1 18.9 %collective-permute-start.46 = (bf16[80,1536]{1,0:T(8,128)(2,1)S(1)}, bf16[80,1536]{1,0:T(8,128)(2,1)S(1)}, u32[]{:S(2)}, u32[]{:S(2)}) collective-permute-start(bf16[80,1536]{1,0:T(8,128)(2,1)S(1)} %slice.1027), channel_id=1, source_target_pairs={{0,8},{2,10},{4,12},{6,14},{8,0},{10,2},{12,4},{14,6},{16,24},{18,... | collective-permute-start | bytes 737288 | tf_op jit(solution)/shard_map/ppermute | solution.py:119
  644.0 123.0 %collective-permute-start.122 = (f32[256,1536]{1,0:T(8,128)}, f32[256,1536]{1,0:T(8,128)}, u32[]{:S(2)}, u32[]{:S(2)}) collective-permute-start(f32[256,1536]{1,0:T(8,128)} %convert_add_fusion.7), channel_id=1, source_target_pairs={{0,1},{1,0},{2,3},{3,2},{4,5},{5,4},{6,7},{7,6},{8,9},{9,8},{10,11... | collective-permute-start | bytes 4718600 | tf_op jit(solution)/shard_map/ppermute | solution.py:119
  655.8 91.9 %collective-permute-start.118 = (f32[1536,256]{0,1:T(8,128)}, f32[1536,256]{0,1:T(8,128)}, u32[]{:S(2)}, u32[]{:S(2)}) collective-permute-start(f32[1536,256]{0,1:T(8,128)} %convert_add_fusion.8), channel_id=1, source_target_pairs={{0,1},{1,0},{2,3},{3,2},{4,5},{5,4},{6,7},{7,6},{8,9},{9,8},{10,11... | collective-permute-start | bytes 4718600 | tf_op jit(solution)/shard_map/ppermute | solution.py:119
  687.8 66.5 %collective-permute-start.114 = (f32[1536,256]{0,1:T(8,128)}, f32[1536,256]{0,1:T(8,128)}, u32[]{:S(2)}, u32[]{:S(2)}) collective-permute-start(f32[1536,256]{0,1:T(8,128)} %convert_add_fusion.9), channel_id=1, source_target_pairs={{0,1},{1,0},{2,3},{3,2},{4,5},{5,4},{6,7},{7,6},{8,9},{9,8},{10,11... | collective-permute-start | bytes 4718600 | tf_op jit(solution)/shard_map/ppermute | solution.py:119
  694.7 49.4 %collective-permute-start.28 = (bf16[256,1536]{1,0:T(8,128)(2,1)}, bf16[256,1536]{1,0:T(8,128)(2,1)}, u32[]{:S(2)}, u32[]{:S(2)}) collective-permute-start(bf16[256,1536]{1,0:T(8,128)(2,1)} %get-tuple-element.91), channel_id=1, source_target_pairs={{0,1},{1,0},{2,3},{3,2},{4,5},{5,4},{6,7},{7,6},{8,9},{9,8},{10,11... | collective-permute-start | bytes 2359304 | tf_op jit(solution)/shard_map/ppermute | solution.py:119
  737.6 35.7 %collective-permute-start.90 = (bf16[128,1536]{1,0:T(8,128)(2,1)}, bf16[128,1536]{1,0:T(8,128)(2,1)}, u32[]{:S(2)}, u32[]{:S(2)}) collective-permute-start(bf16[128,1536]{1,0:T(8,128)(2,1)} %dynamic-slice_convert_fusion.7), channel_id=1, source_target_pairs={{0,4},{2,6},{4,0},{6,2},{8,12},{10,14},{12,8},{14,10},{16,20},{18,... | collective-permute-start | bytes 1179656 | tf_op jit(solution)/shard_map/ppermute | solution.py:119
  744.1 32.3 %collective-permute-start.98 = (bf16[128,1536]{1,0:T(8,128)(2,1)}, bf16[128,1536]{1,0:T(8,128)(2,1)}, u32[]{:S(2)}, u32[]{:S(2)}) collective-permute-start(bf16[128,1536]{1,0:T(8,128)(2,1)} %dynamic-slice_convert_fusion.6), channel_id=1, source_target_pairs={{0,8},{2,10},{4,12},{6,14},{8,0},{10,2},{12,4},{14,6},{16,24},{18,... | collective-permute-start | bytes 1179656 | tf_op jit(solution)/shard_map/ppermute | solution.py:119
  747.7 30.7 %collective-permute-start.82 = (bf16[128,1536]{1,0:T(8,128)(2,1)S(1)}, bf16[128,1536]{1,0:T(8,128)(2,1)}, u32[]{:S(2)}, u32[]{:S(2)}) collective-permute-start(bf16[128,1536]{1,0:T(8,128)(2,1)S(1)} %dynamic-slice_convert_fusion.8), channel_id=1, source_target_pairs={{0,2},{2,0},{4,6},{6,4},{8,10},{10,8},{12,14},{14,12},{16,18},{18,... | collective-permute-start | bytes 1179656 | tf_op jit(solution)/shard_map/ppermute | solution.py:119
  754.2 176.7 %collective-permute-start.51 = (f32[256,1536]{1,0:T(8,128)}, f32[256,1536]{1,0:T(8,128)}, u32[]{:S(2)}, u32[]{:S(2)}) collective-permute-start(f32[256,1536]{1,0:T(8,128)} %constant_dynamic-slice_fusion.3), channel_id=1, source_target_pairs={{0,1},{1,0},{2,3},{3,2},{4,5},{5,4},{6,7},{7,6},{8,9},{9,8},{10,11... | collective-permute-start | bytes 4718600 | tf_op jit(solution)/shard_map/ppermute | solution.py:119
  767.0 40.5 %collective-permute-start.66 = (bf16[256,1280]{1,0:T(8,128)(2,1)}, bf16[256,1280]{1,0:T(8,128)(2,1)S(1)}, u32[]{:S(2)}, u32[]{:S(2)}) collective-permute-start(bf16[256,1280]{1,0:T(8,128)(2,1)} %dynamic-slice_convert_fusion.4), channel_id=1, source_target_pairs={{0,4},{2,6},{4,0},{6,2},{8,12},{10,14},{12,8},{14,10},{16,20},{18,... | collective-permute-start | bytes 1966088 | tf_op jit(solution)/shard_map/ppermute | solution.py:119
  773.3 35.5 %collective-permute-start.74 = (bf16[256,1280]{1,0:T(8,128)(2,1)S(1)}, bf16[256,1280]{1,0:T(8,128)(2,1)S(1)}, u32[]{:S(2)}, u32[]{:S(2)}) collective-permute-start(bf16[256,1280]{1,0:T(8,128)(2,1)S(1)} %copy-done.47), channel_id=1, source_target_pairs={{0,8},{2,10},{4,12},{6,14},{8,0},{10,2},{12,4},{14,6},{16,24},{18,... | collective-permute-start | bytes 1966088 | tf_op jit(solution)/shard_map/ppermute | solution.py:119
  776.4 34.3 %collective-permute-start.58 = (bf16[256,1280]{1,0:T(8,128)(2,1)S(1)}, bf16[256,1280]{1,0:T(8,128)(2,1)S(1)}, u32[]{:S(2)}, u32[]{:S(2)}) collective-permute-start(bf16[256,1280]{1,0:T(8,128)(2,1)S(1)} %dynamic-slice_convert_fusion.5), channel_id=1, source_target_pairs={{0,2},{2,0},{4,6},{6,4},{8,10},{10,8},{12,14},{14,12},{16,18},{18,... | collective-permute-start | bytes 1966088 | tf_op jit(solution)/shard_map/ppermute | solution.py:119
  778.4 16.2 %collective-permute-start.91 = (bf16[64,1536]{1,0:T(8,128)(2,1)S(1)}, bf16[64,1536]{1,0:T(8,128)(2,1)S(1)}, u32[]{:S(2)}, u32[]{:S(2)}) collective-permute-start(bf16[64,1536]{1,0:T(8,128)(2,1)S(1)} %dynamic-slice_convert_fusion.13), channel_id=1, source_target_pairs={{0,8},{2,10},{4,12},{6,14},{8,0},{10,2},{12,4},{14,6},{16,24},{18,... | collective-permute-start | bytes 589832 | tf_op jit(solution)/shard_map/ppermute | solution.py:119
  810.7 53.7 %collective-permute-start.67 = (bf16[128,1280]{1,0:T(8,128)(2,1)S(1)}, bf16[128,1280]{1,0:T(8,128)(2,1)S(1)}, u32[]{:S(2)}, u32[]{:S(2)}) collective-permute-start(bf16[128,1280]{1,0:T(8,128)(2,1)S(1)} %dynamic-slice_convert_fusion.10), channel_id=1, source_target_pairs={{0,8},{2,10},{4,12},{6,14},{8,0},{10,2},{12,4},{14,6},{16,24},{18,... | collective-permute-start | bytes 983048 | tf_op jit(solution)/shard_map/ppermute | solution.py:119
  811.9 53.7 %collective-permute-start.75 = (bf16[128,1280]{1,0:T(8,128)(2,1)S(1)}, bf16[128,1280]{1,0:T(8,128)(2,1)S(1)}, u32[]{:S(2)}, u32[]{:S(2)}) collective-permute-start(bf16[128,1280]{1,0:T(8,128)(2,1)S(1)} %dynamic-slice_convert_fusion.9), channel_id=1, source_target_pairs={{0,2},{2,0},{4,6},{6,4},{8,10},{10,8},{12,14},{14,12},{16,18},{18,... | collective-permute-start | bytes 983048 | tf_op jit(solution)/shard_map/ppermute | solution.py:119
  812.8 54.0 %collective-permute-start.59 = (bf16[128,1280]{1,0:T(8,128)(2,1)S(1)}, bf16[128,1280]{1,0:T(8,128)(2,1)S(1)}, u32[]{:S(2)}, u32[]{:S(2)}) collective-permute-start(bf16[128,1280]{1,0:T(8,128)(2,1)S(1)} %dynamic-slice_convert_fusion.11), channel_id=1, source_target_pairs={{0,4},{2,6},{4,0},{6,2},{8,12},{10,14},{12,8},{14,10},{16,20},{18,... | collective-permute-start | bytes 983048 | tf_op jit(solution)/shard_map/ppermute | solution.py:119
  871.9 57.2 %collective-permute-start.97 = (bf16[128,1536]{1,0:T(8,128)(2,1)S(1)}, bf16[128,1536]{1,0:T(8,128)(2,1)S(1)}, u32[]{:S(2)}, u32[]{:S(2)}) collective-permute-start(bf16[128,1536]{1,0:T(8,128)(2,1)S(1)} %maximum_select_fusion.16), channel_id=1, source_target_pairs={{0,4},{2,6},{4,0},{6,2},{8,12},{10,14},{12,8},{14,10},{16,20},{18,... | collective-permute-start | bytes 1179656 | tf_op jit(solution)/shard_map/ppermute | solution.py:119
  873.2 56.4 %collective-permute-start.105 = (bf16[128,1536]{1,0:T(8,128)(2,1)S(1)}, bf16[128,1536]{1,0:T(8,128)(2,1)S(1)}, u32[]{:S(2)}, u32[]{:S(2)}) collective-permute-start(bf16[128,1536]{1,0:T(8,128)(2,1)S(1)} %maximum_select_fusion.17), channel_id=1, source_target_pairs={{0,8},{2,10},{4,12},{6,14},{8,0},{10,2},{12,4},{14,6},{16,24},{18,... | collective-permute-start | bytes 1179656 | tf_op jit(solution)/shard_map/ppermute | solution.py:119
  874.4 58.6 %collective-permute-start.89 = (bf16[128,1536]{1,0:T(8,128)(2,1)S(1)}, bf16[128,1536]{1,0:T(8,128)(2,1)S(1)}, u32[]{:S(2)}, u32[]{:S(2)}) collective-permute-start(bf16[128,1536]{1,0:T(8,128)(2,1)S(1)} %maximum_select_fusion.15), channel_id=1, source_target_pairs={{0,2},{2,0},{4,6},{6,4},{8,10},{10,8},{12,14},{14,12},{16,18},{18,... | collective-permute-start | bytes 1179656 | tf_op jit(solution)/shard_map/ppermute | solution.py:119
  926.9 15.9 %collective-permute-start.72 = (bf16[128,1280]{1,0:T(8,128)(2,1)S(1)}, bf16[128,1280]{1,0:T(8,128)(2,1)S(1)}, u32[]{:S(2)}, u32[]{:S(2)}) collective-permute-start(bf16[128,1280]{1,0:T(8,128)(2,1)S(1)} %maximum_select_fusion.19), channel_id=1, source_target_pairs={{0,8},{2,10},{4,12},{6,14},{8,0},{10,2},{12,4},{14,6},{16,24},{18,... | collective-permute-start | bytes 983048 | tf_op jit(solution)/shard_map/ppermute | solution.py:119
  929.0 14.7 %collective-permute-start.80 = (bf16[128,1280]{1,0:T(8,128)(2,1)S(1)}, bf16[128,1280]{1,0:T(8,128)(2,1)S(1)}, u32[]{:S(2)}, u32[]{:S(2)}) collective-permute-start(bf16[128,1280]{1,0:T(8,128)(2,1)S(1)} %maximum_select_fusion.20), channel_id=1, source_target_pairs={{0,2},{2,0},{4,6},{6,4},{8,10},{10,8},{12,14},{14,12},{16,18},{18,... | collective-permute-start | bytes 983048 | tf_op jit(solution)/shard_map/ppermute | solution.py:119
  929.6 19.0 %collective-permute-start.64 = (bf16[128,1280]{1,0:T(8,128)(2,1)S(1)}, bf16[128,1280]{1,0:T(8,128)(2,1)S(1)}, u32[]{:S(2)}, u32[]{:S(2)}) collective-permute-start(bf16[128,1280]{1,0:T(8,128)(2,1)S(1)} %maximum_select_fusion.18), channel_id=1, source_target_pairs={{0,4},{2,6},{4,0},{6,2},{8,12},{10,14},{12,8},{14,10},{16,20},{18,... | collective-permute-start | bytes 983048 | tf_op jit(solution)/shard_map/ppermute | solution.py:119
  943.0 16.0 %collective-permute-start.73 = (bf16[256,1280]{1,0:T(8,128)(2,1)S(1)}, bf16[256,1280]{1,0:T(8,128)(2,1)S(1)}, u32[]{:S(2)}, u32[]{:S(2)}) collective-permute-start(bf16[256,1280]{1,0:T(8,128)(2,1)S(1)} %maximum_select_fusion.13), channel_id=1, source_target_pairs={{0,4},{2,6},{4,0},{6,2},{8,12},{10,14},{12,8},{14,10},{16,20},{18,... | collective-permute-start | bytes 1966088 | tf_op jit(solution)/shard_map/ppermute | solution.py:119
  943.8 15.7 %collective-permute-start.81 = (bf16[256,1280]{1,0:T(8,128)(2,1)S(1)}, bf16[256,1280]{1,0:T(8,128)(2,1)S(1)}, u32[]{:S(2)}, u32[]{:S(2)}) collective-permute-start(bf16[256,1280]{1,0:T(8,128)(2,1)S(1)} %maximum_select_fusion.14), channel_id=1, source_target_pairs={{0,8},{2,10},{4,12},{6,14},{8,0},{10,2},{12,4},{14,6},{16,24},{18,... | collective-permute-start | bytes 1966088 | tf_op jit(solution)/shard_map/ppermute | solution.py:119
  946.4 24.7 %collective-permute-start.52 = (f32[256,1536]{1,0:T(8,128)S(1)}, f32[256,1536]{1,0:T(8,128)S(1)}, u32[]{:S(2)}, u32[]{:S(2)}) collective-permute-start(f32[256,1536]{1,0:T(8,128)S(1)} %fusion.22), channel_id=1, source_target_pairs={{0,1},{1,0},{2,3},{3,2},{4,5},{5,4},{6,7},{7,6},{8,9},{9,8},{10,11... | collective-permute-start | bytes 4718600 | tf_op jit(solution)/shard_map/ppermute | solution.py:119
  948.7 16.9 %collective-permute-start.65 = (bf16[256,1280]{1,0:T(8,128)(2,1)S(1)}, bf16[256,1280]{1,0:T(8,128)(2,1)S(1)}, u32[]{:S(2)}, u32[]{:S(2)}) collective-permute-start(bf16[256,1280]{1,0:T(8,128)(2,1)S(1)} %maximum_select_fusion.12), channel_id=1, source_target_pairs={{0,2},{2,0},{4,6},{6,4},{8,10},{10,8},{12,14},{14,12},{16,18},{18,... | collective-permute-start | bytes 1966088 | tf_op jit(solution)/shard_map/ppermute | solution.py:119
  (168 other events, 1582.0 us)

commit v2 on v1

--- a/solution.py
+++ b/solution.py
@@ -1,6 +1,10 @@
+import functools
+
 import jax
 import jax.numpy as jnp
 from jax import lax
+from jax.experimental import pallas as pl
+from jax.experimental.pallas import tpu as pltpu
 from jax.sharding import PartitionSpec as P
 
 HEAD_DIM = 64
@@ -181,25 +185,252 @@
     return orders
 
 
-def cube_gather(x, masks):
-    bufs = [x[s : s + n] for s, n in row_parts(x.shape[0], len(masks))]
+def peer_of(mask):
+    me = lax.axis_index("dp")
+    bit = (me // mask) % 2
+    return me + mask * (1 - 2 * bit), bit
+
+
+def remote(src, dst, send, recv, mask):
+    return pltpu.make_async_remote_copy(
+        src_ref=src,
+        dst_ref=dst,
+        send_sem=send,
+        recv_sem=recv,
+        device_id={"dp": peer_of(mask)[0]},
+        device_id_type=pl.DeviceIdType.MESH,
+    )
+
+
+def greet(masks):
+    barrier = pltpu.get_barrier_semaphore()
+    for mask in masks:
+        pl.semaphore_signal(
+            barrier,
+            inc=1,
+            device_id={"dp": peer_of(mask)[0]},
+            device_id_type=pl.DeviceIdType.MESH,
+        )
+    pl.semaphore_wait(barrier, len(masks))
+
+
+def gather_kernel(masks, parts, n, *refs):
+    ins, outs = refs[:n], refs[n:2 * n]
+    local, send, recv = refs[2 * n:]
+    greet(masks)
+    size = 2 ** len(masks)
+    locals_ = []
+    for a in range(n):
+        for j, (s, m) in enumerate(parts):
+            c = pltpu.make_async_copy(ins[a].at[pl.ds(s, m)], outs[a].at[pl.ds(size * s, m)], local.at[a, j])
+            c.start()
+            locals_.append(c)
+    sent = []
+    copies = {}
     for phase in range(len(masks)):
-        got = [swap(b, "dp", rotated(masks, j)[phase]) for j, b in enumerate(bufs)]
-        bufs = [jnp.concatenate([b, g], 0) for b, g in zip(bufs, got)]
-    return jnp.concatenate(bufs, 0)
-
-
-def cube_scatter_sum(x, masks):
-    devices = 2 ** len(masks)
-    parts = row_parts(x.shape[0] // devices, len(masks))
-    bufs = [x[devices * s : devices * (s + n)] for s, n in parts]
-    for phase in reversed(range(len(masks))):
-        got = [
-            swap(b[b.shape[0] // 2 :].astype(bf16), "dp", rotated(masks, j)[phase])
-            for j, b in enumerate(bufs)
-        ]
-        bufs = [b[: b.shape[0] // 2].astype(f32) + g.astype(f32) for b, g in zip(bufs, got)]
-    return jnp.concatenate(bufs, 0)
+        for a in range(n):
+            for j, (s, m) in enumerate(parts):
+                mask = rotated(masks, j)[phase]
+                count = 2 ** phase * m
+                if phase == 0:
+                    src = ins[a].at[pl.ds(s, m)]
+                else:
+                    copies[a, j, phase - 1].wait_recv()
+                    if phase == 1:
+                        locals_[a * len(parts) + j].wait()
+                    src = outs[a].at[pl.ds(size * s, count)]
+                c = remote(src, outs[a].at[pl.ds(size * s + count, count)],
+                           send.at[a, j, phase], recv.at[a, j, phase], mask)
+                c.start()
+                copies[a, j, phase] = c
+    for (a, j, phase), c in copies.items():
+        if phase == len(masks) - 1:
+            c.wait_recv()
+    for c in copies.values():
+        c.wait_send()
+
+def cube_gather(arrays, masks, collective_id, mult=1, space=pl.ANY):
+    n = len(arrays)
+    rows = arrays[0].shape[0]
+    parts = row_parts(rows, mult*len(masks))
+    size = 2 ** len(masks)
+    return pl.pallas_call(
+        functools.partial(gather_kernel, masks, parts, n),
+        out_shape=[jax.ShapeDtypeStruct((size * rows,) + x.shape[1:], x.dtype) for x in arrays],
+        in_specs=[pl.BlockSpec(memory_space=pl.ANY)] * n,
+        out_specs=[pl.BlockSpec(memory_space=space)] * n,
+        scratch_shapes=[pltpu.SemaphoreType.DMA((n, len(parts))),
+                        pltpu.SemaphoreType.DMA((n, len(parts), len(masks))),
+                        pltpu.SemaphoreType.DMA((n, len(parts), len(masks)))],
+        compiler_params=pltpu.CompilerParams(collective_id=collective_id, has_side_effects=True, vmem_limit_bytes=40<<20),
+    )(*arrays)
+
+def tiles(rows):
+    return 16
+
+def add_rows(dst, dst0, a, a0, b, b0, rows, out_dtype):
+    step = 16
+    def body(i, _):
+        r = pl.multiple_of(i * step, step)
+        x = a[pl.ds(a0 + r, step), :].astype(f32) + b[pl.ds(b0 + r, step), :].astype(f32)
+        dst[pl.ds(dst0 + r, step), :] = x.astype(out_dtype)
+        return 0
+    lax.fori_loop(0, rows // step, body, 0, unroll=False)
+
+def scatter_kernel(masks, parts, n, *refs):
+    ins, outs = refs[:n], refs[n:2 * n]
+    lows, gots, local, send, recv = refs[2 * n:]
+    k = len(masks)
+    size = 2 ** k
+    half = size // 2
+    rows = sum(m for _, m in parts)
+    for a in range(n):
+        for j, (s, m) in enumerate(parts):
+            pltpu.make_async_copy(ins[a].at[pl.ds(size * s, half * m)], lows.at[a, pl.ds(half * s, half * m)], local.at[a, j]).start()
+    greet(masks)
+    copies = {}
+    def got_at(a, j, phase):
+        s, m = parts[j]
+        count = 2 ** phase * m
+        base = rows * (size - 2 ** (phase + 1))
+        return base + 2 ** phase * s, count
+    for phase in reversed(range(k)):
+        for a in range(n):
+            for j, (s, m) in enumerate(parts):
+                count = 2 ** phase * m
+                mask = rotated(masks, j)[phase]
+                if phase == k - 1:
+                    src = ins[a].at[pl.ds(size * s + count, count)]
+                else:
+                    g0, c0 = got_at(a, j, phase + 1)
+                    copies[a, j, phase + 1].wait_recv()
+                    if phase == k - 2:
+                        pltpu.make_async_copy(ins[a].at[pl.ds(size * s, half * m)], lows.at[a, pl.ds(half * s, half * m)], local.at[a, j]).wait()
+                    low = lows.at[a]
+                    got = gots.at[a]
+                    add_rows(low, half * s + count, low, half * s + count, got, g0 + count, count, bf16)
+                    src = lows.at[a, pl.ds(half * s + count, count)]
+                o0, _ = got_at(a, j, phase)
+                c = remote(src, gots.at[a, pl.ds(o0, count)], send.at[a, j, phase], recv.at[a, j, phase], mask)
+                c.start()
+                copies[a, j, phase] = c
+                if phase < k - 1:
+                    add_rows(low, half * s, low, half * s, got, g0, count, bf16)
+    for a in range(n):
+        for j, (s, m) in enumerate(parts):
+            copies[a, j, 0].wait_recv()
+            g0, _ = got_at(a, j, 0)
+            add_rows(outs[a], s, lows.at[a], half * s, gots.at[a], g0, m, f32)
+    for c in copies.values():
+        c.wait_send()
+
+def cube_scatter(arrays, masks, collective_id, mult=1):
+    n = len(arrays)
+    size = 2 ** len(masks)
+    rows, width = arrays[0].shape[0] // size, arrays[0].shape[1]
+    parts = row_parts(rows, mult*len(masks))
+    k = len(masks)
+    return pl.pallas_call(
+        functools.partial(scatter_kernel, masks, parts, n),
+        out_shape=[jax.ShapeDtypeStruct((rows, width), f32) for x in arrays],
+        in_specs=[pl.BlockSpec(memory_space=pl.ANY)] * n,
+        out_specs=[pl.BlockSpec(memory_space=pltpu.VMEM)] * n,
+        scratch_shapes=[pltpu.VMEM((n, size // 2 * rows, width), bf16),
+                        pltpu.VMEM((n, (size - 1) * rows, width), bf16),
+                        pltpu.SemaphoreType.DMA((n, len(parts))),
+                        pltpu.SemaphoreType.DMA((n, len(parts), k)),
+                        pltpu.SemaphoreType.DMA((n, len(parts), k))],
+        compiler_params=pltpu.CompilerParams(collective_id=collective_id, has_side_effects=True,
+                                             vmem_limit_bytes=40 << 20),
+    )(*arrays)
+
+def reduce_kernel(orders, x_ref, small_ref, out_ref, small_out, acc, got, small_got, load, send, recv, small_send, small_recv):
+    k = len(orders[0])
+    nparts = len(orders)
+    size = x_ref.shape[0] // nparts
+    width = x_ref.shape[1]
+    for j in range(nparts):
+        pltpu.make_async_copy(x_ref.at[pl.ds(j * size, size)], acc.at[pl.ds(j * size, size)], load.at[j]).start()
+    greet(sorted(orders[0]))
+    small_out[...] = small_ref[...]
+    copies = {}
+    where = [j * size for j in range(nparts)]
+    small_copies = []
+    for step in range(k):
+        count = size >> (step + 1)
+        for j in range(nparts):
+            mask = orders[j][step]
+            _, bit = peer_of(mask)
+            if step == 0:
+                pltpu.make_async_copy(x_ref.at[pl.ds(j * size, size)], acc.at[pl.ds(j * size, size)], load.at[j]).wait()
+            keep = pl.multiple_of(where[j] + bit * count, 16)
+            give = pl.multiple_of(where[j] + (1 - bit) * count, 16)
+            if step > 0:
+                prev = copies[j, step - 1]
+                prev.wait_recv()
+                p0 = j * size + (size - (size >> (step - 1)))
+                add_rows(acc, give, acc, give, got, p0 + pl.multiple_of((1 - bit) * count, 16), count, bf16)
+            g0 = j * size + (size - (size >> step))
+            c = remote(acc.at[pl.ds(give, count)], got.at[pl.ds(g0, count)], send.at[j, step], recv.at[j, step], mask)
+            c.start()
+            copies[j, step] = c
+            if step > 0:
+                add_rows(acc, keep, acc, keep, got, p0 + pl.multiple_of(bit * count, 16), count, bf16)
+            where[j] = keep
+        mask = orders[0][step]
+        if step > 0:
+            small_copies[-1].wait_send()
+            small_copies[-1].wait_recv()
+            small_out[...] += small_got[step - 1]
+        c = remote(small_out, small_got.at[step], small_send.at[step], small_recv.at[step], mask)
+        c.start()
+        small_copies.append(c)
+    back = {}
+    for step in reversed(range(k)):
+        count = size >> (step + 1)
+        for j in range(nparts):
+            mask = orders[j][step]
+            _, bit = peer_of(mask)
+            if step == k - 1:
+                copies[j, step].wait_recv()
+                p0 = j * size + (size - (size >> step))
+                add_rows(out_ref, where[j], acc, where[j], got, p0, count, bf16)
+            else:
+                back[j, step + 1].wait_recv()
+            here = where[j]
+            c = remote(out_ref.at[pl.ds(here, count)], out_ref.at[pl.ds(here, count)], send.at[j, k + step], recv.at[j, k + step], mask)
+            c.start()
+            back[j, step] = c
+            where[j] = pl.multiple_of(here - bit * count, 16)
+    small_copies[-1].wait_send()
+    small_copies[-1].wait_recv()
+    small_out[...] += small_got[k - 1]
+    for j in range(nparts):
+        back[j, 0].wait_recv()
+    for c in copies.values():
+        c.wait_send()
+    for c in back.values():
+        c.wait_send()
+
+def all_reduce(x, small, masks, collective_id, nparts=3):
+    inner, last = masks[:-1], masks[-1:]
+    orders = [rotated(inner, j) + last for j in range(nparts)]
+    k = len(masks)
+    rows, width = x.shape
+    vm = pl.BlockSpec(memory_space=pltpu.VMEM)
+    return pl.pallas_call(
+        functools.partial(reduce_kernel, orders),
+        out_shape=[jax.ShapeDtypeStruct(x.shape, bf16), jax.ShapeDtypeStruct(small.shape, f32)],
+        in_specs=[pl.BlockSpec(memory_space=pl.ANY), vm],
+        out_specs=[vm, vm],
+        scratch_shapes=[pltpu.VMEM(x.shape, bf16), pltpu.VMEM(x.shape, bf16),
+                        pltpu.VMEM((k,) + small.shape, f32),
+                        pltpu.SemaphoreType.DMA((nparts,)),
+                        pltpu.SemaphoreType.DMA((nparts, 2 * k)), pltpu.SemaphoreType.DMA((nparts, 2 * k)),
+                        pltpu.SemaphoreType.DMA((k,)), pltpu.SemaphoreType.DMA((k,))],
+        compiler_params=pltpu.CompilerParams(collective_id=collective_id, has_side_effects=True,
+                                             vmem_limit_bytes=40 << 20),
+    )(x, small)
 
 
 def vector_gather(x, masks):
@@ -217,8 +448,8 @@
 
 
 def to_cube_rows(x, masks):
-    parts = row_parts(x.shape[1], len(masks))
-    orders = cube_orders(masks, len(masks))
+    parts = row_parts(x.shape[1], 2 * len(masks))
+    orders = cube_orders(masks, 2 * len(masks))
     return jnp.concatenate(
         [x[o, s : s + n] for (s, n), order in zip(parts, orders) for o in order]
     )
@@ -226,15 +457,15 @@
 
 def from_cube_rows(x, masks):
     devices = 2 ** len(masks)
-    parts = row_parts(x.shape[0] // devices, len(masks))
-    orders = cube_orders(masks, len(masks))
+    parts = row_parts(x.shape[0] // devices, 2 * len(masks))
+    orders = cube_orders(masks, 2 * len(masks))
     found = {}
     for j, ((s, n), order) in enumerate(zip(parts, orders)):
         for place, o in enumerate(order):
             first = devices * s + place * n
             found[o, j] = x[first : first + n]
     return jnp.stack(
-        [jnp.concatenate([found[o, j] for j in range(len(masks))]) for o in range(devices)]
+        [jnp.concatenate([found[o, j] for j in range(2 * len(masks))]) for o in range(devices)]
     )
 
 
@@ -257,19 +488,6 @@
     )
     up_low = (down_in * silu_gate).astype(bf16)
     return weighted_low, gate_deriv, gate_low, up_low
-
-
-def summed_over_dp(x, kind):
-    masks = bit_masks(lax.axis_size("dp"))
-    inner, last = masks[:-1], masks[-1:]
-    count = 3
-    size = x.shape[0] // count
-    outs = []
-    for j in range(count):
-        order = rotated(inner, j) + last
-        part = scatter_sum(x[j * size : (j + 1) * size], "dp", order, kind)
-        outs.append(gather_blocks(part.astype(kind), "dp", order))
-    return jnp.concatenate(outs, 0).astype(f32)
 
 
 def per_device(
@@ -328,7 +546,6 @@
     far_down = relative_gather(swap(my_units(w_down[0], 0), "dp", pair), 0)
 
     grad_mine = my_rows(out_grad)
-    grads = cube_gather(grad_mine, cube)
 
     inputs = hidden_in.astype(f32)
     scale_in = lax.rsqrt(jnp.mean(inputs * inputs, axis=-1, keepdims=True) + epsilon)
@@ -346,7 +563,7 @@
     middle = inputs_mine + residual_scale * attn_total
     scale_mid = lax.rsqrt(jnp.mean(middle * middle, axis=-1, keepdims=True) + epsilon)
     routed_low = (middle * scale_mid * moe_gain).astype(bf16)
-    rows = cube_gather(routed_low, cube)
+    rows, grads = cube_gather([routed_low, grad_mine], cube, 0, 2)
 
     logits = dot(w_router, routed_low, "de,td->et")
     ids_mine = my_rows(expert_ids).T
@@ -371,7 +588,6 @@
         rows, grads, column_of(far), *far_set
     )
     moe_part = dot(near_low, w_down[0], "tf,fd->td") + dot(far_low, far_down, "tf,fd->td")
-    moe_total = cube_scatter_sum(moe_part.astype(bf16), cube)
 
     one_near = (expert_range == near).astype(f32)[None, :, None]
     one_far = (expert_range == far).astype(f32)[None, :, None]
@@ -387,7 +603,9 @@
         + dot(far_gate_low, far_gate, "tf,df->td")
         + dot(far_up_low, far_up, "tf,df->td")
     )
-    routed_grad = cube_scatter_sum(routed_part.astype(bf16), cube)
+    moe_total, routed_grad = cube_scatter(
+        [moe_part.astype(bf16), routed_part.astype(bf16)], cube, 1, 2
+    )
 
     far_gate_grad = relative_scatter(dot(rows, far_gate_low, "td,tf->df"), 1)
     far_up_grad = relative_scatter(dot(rows, far_up_low, "td,tf->df"), 1)
@@ -430,14 +648,20 @@
     branch_low = gather_blocks(
         (residual_scale * middle_grad).astype(bf16), "tensor", tensor_down
     )
-    w_output_grad = summed_over_dp(dot(heads_flat, branch_low, "tc,td->cd"), bf16)
     heads_grad = dot(branch_low, w_output, "td,cd->tc").astype(bf16)
     query_low, key_low, value_low = attend_backward(
         query_heads, key_heads, value_heads, log_sums, heads_grad, segment, tables
     )
     width_q, width_k = query_low.shape[1], key_low.shape[1]
     qkv_low = jnp.concatenate([query_low, key_low, value_low], axis=1)
-    qkv_grad = summed_over_dp(dot(normed_low, qkv_low, "td,tc->dc"), bf16)
+    heads_width = heads_flat.shape[1]
+    w_output_part = [
+        dot(heads_flat, branch_low[:, i : i + heads_width], "tc,td->cd")
+        for i in range(0, model_width, heads_width)
+    ]
+    attention_part = jnp.concatenate(
+        [dot(normed_low, qkv_low, "td,tc->dc"), jnp.concatenate(w_output_part, 0)], 1
+    ).astype(bf16)
     qkv_weight = jnp.concatenate([w_query, key_weight, value_weight], axis=1)
     normed_part = dot(qkv_low, qkv_weight, "tc,dc->td")
     normed_grad = scatter_sum(normed_part, "tensor", tensor_down, f32)
@@ -452,20 +676,31 @@
     )
     input_grad = gather_blocks(input_mine, "tensor", tensor_down)
 
-    early = sum_all(
-        sum_all(jnp.concatenate([router_part, moe_gain_part[None]], 0), "tensor"), "dp"
-    )
-    attn_gain_grad = sum_all(sum_all(attn_gain_part[None], "tensor"), "dp")[0]
+    small = jnp.concatenate([router_part, moe_gain_part[None], attn_gain_part[None]], 0)
+    small = jnp.pad(small, ((0, -small.shape[0] % 8), (0, 0)))
+    for mask in tensor_masks:
+        small = small + swap(small, "tensor", mask)
+    attention_grad, small = all_reduce(attention_part, small, masks, 2)
+    attention_grad = attention_grad.astype(f32)
+    qkv_width = qkv_low.shape[1]
+    qkv_grad = attention_grad[:, :qkv_width]
+    w_output_grad = jnp.concatenate(
+        [
+            attention_grad[i : i + heads_width, qkv_width:]
+            for i in range(0, model_width, heads_width)
+        ],
+        1,
+    )
     return (
         block_out,
         input_grad,
-        attn_gain_grad,
+        small[experts + 1],
         qkv_grad[:, :width_q],
         qkv_grad[:, width_q : width_q + width_k],
         qkv_grad[:, width_q + width_k :],
         w_output_grad,
-        early[experts],
-        early[:experts].T,
+        small[experts],
+        small[:experts].T,
         gate_grad,
         up_grad,
         down_grad,

time: 982 us -> 761 us (0.77)
  waiting for transfers between devices: 476 us -> 128 us
  Pallas kernels: 0 us -> 297 us
  starting transfers between devices: 156 us -> 23.5 us
  local copies, waits for them, and re-layouts: 78.8 us -> 56.7 us
  other arithmetic: 78.8 us -> 68.5 us
    ppermute x123 -> x30, waiting for transfers between devices: 476 us -> 128 us  [swap(): lax.ppermute(x, axis, [(i, i ^ mask) for i in range(lax.axis_size(axis))])]
    pallas_call x0 -> x3, Pallas kernels: none -> 297 us  [the longest x1 123 us: all_reduce(): pl.pallas_call(functools.partial(reduce_kernel, orders), out_shape=[jax.S...]
    ppermute x123 -> x30, starting transfers between devices: 156 us -> 23.5 us  [swap(): lax.ppermute(x, axis, [(i, i ^ mask) for i in range(lax.axis_size(axis))])]
    unnamed x244 -> x206, local copies, waits for them, and re-layouts: 43.9 us -> 27 us
    dot_general x25 -> x26, matrix products: 147 us -> 143 us  [dot(): return jnp.einsum(spec, a, b, preferred_element_type=f32)]
    select_n x29 -> x6, other arithmetic: 24.4 us -> 22.4 us  [join_by_bit(): jnp.where(bit_of(axis, mask) == 0, jnp.concatenate([mine, other], dim), j...]
  transfers between devices with their start and end apart: 123 -> 30, of which waited for: 66 -> 8; matrix products, arithmetic and copies ran while one was open for 23% -> 27% of each run, Pallas kernels for 0% -> 39%
where the time goes in v2:
time: 761 us; the launch traced here: 753 us
  Pallas kernels  297 us (39%)
  matrix products  176 us (23%)
  waiting for transfers between devices  128 us (17%)
  other arithmetic  68.5 us (9%)
  local copies, waits for them, and re-layouts  56.7 us (7%)
  starting transfers between devices  23.5 us (3%)
    dot_general x26, matrix products, dot(): return jnp.einsum(spec, a, b, preferred_element_type=f32)  143 us
    ppermute x30, waiting for transfers between devices, swap(): lax.ppermute(x, axis, [(i, i ^ mask) for i in range(lax.axis_size(axis))])  128 us
    pallas_call x1, Pallas kernels, all_reduce(): pl.pallas_call(functools.partial(reduce_kernel, orders), out_shape=[jax.S...  123 us
    pallas_call x1, Pallas kernels, cube_gather(): pl.pallas_call(functools.partial(gather_kernel, masks, parts, n), out_sha...  87.9 us
    pallas_call x1, Pallas kernels, cube_scatter(): pl.pallas_call(functools.partial(scatter_kernel, masks, parts, n), out_sh...  85.6 us
    unnamed x206, local copies, waits for them, and re-layouts  27 us
    ppermute x30, starting transfers between devices, swap(): lax.ppermute(x, axis, [(i, i ^ mask) for i in range(lax.axis_size(axis))])  23.5 us
    select_n x6, other arithmetic, join_by_bit(): jnp.where(bit_of(axis, mask) == 0, jnp.concatenate([mine, other], dim), j...  22.4 us
  transfers between devices with their start and end apart: 30, of which 8 were waited for; matrix products, arithmetic and copies ran while one was open for 27% of the time, Pallas kernels for 39%

profile of v2, /device:TPU:0, one launch (start us, length us, event | category | flops | bytes accessed | tf_op | source)
XLA Modules:
  0.0 752.9 jit_solution(14788583637659141255)
XLA Ops:
  0.7 2.2 dynamic-slice_bitcast_fusion
  2.9 4.0 collective-permute-start.8
  7.0 2.1 dynamic-slice_bitcast_fusion.1
  10.0 2.9 collective-permute-start.4
  17.0 3.2 convolution_convert_fusion.4
  25.3 3.1 fusion.9
  28.5 2.6 fusion.3
  33.2 4.0 fusion.41
  44.3 31.9 %collective-permute-done.8 = bf16[256,1536]{1,0:T(8,128)(2,1)} collective-permute-done((bf16[256,1536]{1,0:T(8,128)(2,1)}, bf16[256,1536]{1,0:T(8,128)(2,1)}, u32[]{:S(2)}, u32[]{:S(2)}) %collective-permute-start.8) | collective-permute-done | bytes 786464 | tf_op jit(solution)/shard_map/ppermute | solution.py:123
  76.2 16.8 %collective-permute-done.6 = bf16[1536,256]{1,0:T(8,128)(2,1)} collective-permute-done((bf16[1536,256]{1,0:T(8,128)(2,1)}, bf16[1536,256]{1,0:T(8,128)(2,1)}, u32[]{:S(2)}, u32[]{:S(2)}) %collective-permute-start.6) | collective-permute-done | bytes 786464 | tf_op jit(solution)/shard_map/ppermute | solution.py:123
  93.1 16.0 %collective-permute-done.4 = bf16[1536,256]{1,0:T(8,128)(2,1)} collective-permute-done((bf16[1536,256]{1,0:T(8,128)(2,1)}, bf16[1536,256]{1,0:T(8,128)(2,1)}, u32[]{:S(2)}, u32[]{:S(2)}) %collective-permute-start.4) | collective-permute-done | bytes 786464 | tf_op jit(solution)/shard_map/ppermute | solution.py:123
  109.1 2.1 constant_dynamic-update-slice_fusion.1
  119.9 87.9 %shard_map.229 = (bf16[2048,1536]{1,0:T(8,128)(2,1)S(1)}, bf16[2048,1536]{1,0:T(8,128)(2,1)S(1)}) custom-call(bf16[256,1536]{1,0:T(8,128)(2,1)S(1)} %multiply_convert_fusion.7.refs_0_, bf16[256,1536]{1,0:T(8,128)(2,1)S(1)} %constant_dynamic-slice_fusion.3.refs_1_), custom_call_target="tpu_custom_call" | custom-call | tf_op jit(solution)/shard_map/pallas_call | solution.py:257
  207.9 5.7 fusion.35
  213.7 5.0 fusion.39
  218.8 5.0 fusion.88
  225.4 5.1 fusion.87
  232.5 2.4 collective-permute-done.3
  235.5 11.4 %multiply_reduce_fusion = (f32[2048]{0:T(1024)S(1)}, bf16[2048,512]{0,1:T(8,128)(2,1)}, bf16[2048,512]{0,1:T(8,128)(2,1)}, bf16[2048,512]{0,1:T(8,128)(2,1)}) fusion(f32[2048,512]{0,1:T(8,128)} %fusion.88, f32[2048,512]{0,1:T(8,128)} %fusion.87, f32[2048]{0:T(1024)S(1)} %broadcast_multiply_fusion, f32[2048]{0:T(1024)S(1)} %concatenate.222, ...), kind=kOutput, calls=%fused_computation.20 | convolution fusion | flops 3242194944 | bytes 22568960 | tf_op jit(solution)/shard_map/td,fd->tf/dot_general | solution.py:473
  247.4 9.9 %multiply_reduce_fusion.1 = (f32[2048]{0:T(1024)S(1)}, bf16[2048,512]{0,1:T(8,128)(2,1)S(1)}, bf16[2048,512]{0,1:T(8,128)(2,1)S(1)}, bf16[2048,512]{0,1:T(8,128)(2,1)S(1)}) fusion(f32[2048,512]{0,1:T(8,128)} %fusion.35, f32[2048,512]{0,1:T(8,128)} %fusion.39, f32[2048]{0:T(1024)S(1)} %broadcast_multiply_fusion.1, f32[2048]{0:T(1024)S(1)} %concatenate.219, ...), kind=kOutput, calls=%fused_computation.21 | convolution fusion | flops 3242194944 | bytes 22568960 | tf_op jit(solution)/shard_map/td,fd->tf/dot_general | solution.py:473
  257.6 5.7 fusion.92
  263.3 6.5 fusion.89
  269.8 8.0 %fusion.93 = f32[1536,512]{0,1:T(8,128)} fusion(bf16[2048,512]{0,1:T(8,128)(2,1)S(1)} %get-tuple-element.76, bf16[2048,1536]{1,0:T(8,128)(2,1)} %copy-done.5), kind=kOutput, calls=%fused_computation.309 | convolution fusion | flops 3221225472 | bytes 11534336 | tf_op jit(solution)/shard_map/td,tf->df/dot_general | solution.py:473
  277.9 6.7 fusion.33
  284.6 5.1 fusion.91
  289.7 6.5 fusion.37
  296.2 5.1 convolution_multiply_fusion.1
  301.3 6.8 fusion.31
  309.1 3.4 fusion.94
  314.5 3.4 convolution_multiply_fusion
  322.4 2.4 dynamic-slice_convert_fusion
  324.8 11.7 %add_convert_fusion.1.refs_0_ = bf16[2048,1536]{1,0:T(8,128)(2,1)} fusion(f32[2048,1536]{1,0:T(8,128)} %fusion.31, bf16[2048,512]{0,1:T(8,128)(2,1)} %get-tuple-element.78, bf16[512,1536]{1,0:T(8,128)(2,1)} %copy-done.56), kind=kOutput, calls=%fused_computation.8 | convolution fusion | flops 3227516928 | bytes 22544384 | tf_op jit(solution)/shard_map/tf,fd->td/dot_general | solution.py:473
  336.5 17.5 %add_convert_fusion.refs_1_ = bf16[2048,1536]{1,0:T(8,128)(2,1)} fusion(f32[2048,1536]{1,0:T(8,128)} %fusion.89, f32[2048,1536]{1,0:T(8,128)} %fusion.37, f32[2048,1536]{1,0:T(8,128)} %fusion.33, bf16[2048,512]{0,1:T(8,128)(2,1)} %get-tuple-element.75, bf16[1536,512]{1,0:T(8,128)(2,1)} %copy-done.17), kind=kOutput, calls=%fused_computation.7 | convolution fusion | flops 3233808384 | bytes 47710208 | tf_op jit(solution)/shard_map/tf,df->td/dot_general | solution.py:473
  355.5 2.4 dynamic-slice_convert_fusion.1
  359.5 2.4 dynamic-slice_convert_fusion.2
  361.9 2.8 copy-done.3
  364.7 85.6 %shard_map.230 = (f32[256,1536]{1,0:T(8,128)S(1)}, f32[256,1536]{1,0:T(8,128)S(1)}) custom-call(bf16[2048,1536]{1,0:T(8,128)(2,1)S(1)} %copy-done.3, bf16[2048,1536]{1,0:T(8,128)(2,1)} %add_convert_fusion.refs_1_), custom_call_target="tpu_custom_call" | custom-call | tf_op jit(solution)/shard_map/pallas_call | solution.py:333
  451.7 2.1 multiply_convert_fusion.6
  454.8 2.4 fusion.28
  457.7 2.3 fusion.27
  460.0 2.3 fusion.26
  462.3 3.4 collective-permute-start.28
  466.3 2.3 convolution_convert_fusion.3
  473.6 6.4 fusion.47
  480.1 9.6 %fusion = (f32[4,3,512]{2,1,0:T(4,128)S(1)}, f32[4,512,512,3]{2,1,3,0:T(8,128)}) fusion(f32[4,3,512]{2,1,0:T(4,128)S(1)} %copy-done.49, f32[4,512,512,3]{2,1,3,0:T(8,128)} %copy-done.6, pred[512,512]{0,1:T(8,128)(4,1)S(1)} %copy-done.15, bf16[512,4,64,1]{0,2,3,1:T(8,128)(2,1)S(1)} %bitcast.421, bf16[512,4,3,64]{0,3,2,1:T(8,128)(2,1)S(1)} %bitcast.408), kind=kOutput, calls=%fused_computation.2 | convolution fusion | flops 418375680 | bytes 26525696 | tf_op jit(solution)/shard_map/qhgd,khd->hgqk/dot_general | solution.py:91
  489.7 7.1 fusion.2
  496.9 2.0 fusion.46
  502.2 2.2 fusion.12
  504.5 4.4 convolution_convert_fusion
  510.8 6.1 maximum_maximum_fusion.x_ref
  516.8 3.7 maximum_select_fusion.4
  520.5 2.9 collective-permute-start.20
  523.5 2.9 convert_add_fusion.1
  526.9 44.6 %collective-permute-done.24 = bf16[1536,256]{0,1:T(8,128)(2,1)S(1)} collective-permute-done((bf16[1536,256]{0,1:T(8,128)(2,1)}, bf16[1536,256]{0,1:T(8,128)(2,1)S(1)}, u32[]{:S(2)}, u32[]{:S(2)}) %collective-permute-start.24) | collective-permute-done | bytes 786464 | tf_op jit(solution)/shard_map/ppermute | solution.py:123
  573.2 15.0 %collective-permute-done.20 = bf16[1536,256]{0,1:T(8,128)(2,1)S(1)} collective-permute-done((bf16[1536,256]{0,1:T(8,128)(2,1)}, bf16[1536,256]{0,1:T(8,128)(2,1)S(1)}, u32[]{:S(2)}, u32[]{:S(2)}) %collective-permute-start.20) | collective-permute-done | bytes 786464 | tf_op jit(solution)/shard_map/ppermute | solution.py:123
  588.2 2.7 convert_add_fusion.3
  594.6 123.5 %shard_map.231 = (bf16[1536,2048]{1,0:T(8,128)(2,1)S(1)}, f32[24,1536]{1,0:T(8,128)S(1)}) custom-call(bf16[1536,2048]{1,0:T(8,128)(2,1)S(1)} %bitcast.398, f32[24,1536]{1,0:T(8,128)S(1)} %fusion.71.small_ref), custom_call_target="tpu_custom_call" | custom-call | tf_op jit(solution)/shard_map/pallas_call | solution.py:421
  719.2 2.9 pad_maximum_fusion
  722.8 2.7 slice.1125
  729.4 3.5 copy.73
  732.9 5.3 maximum_select_fusion.1
  738.2 3.5 copy.72
  741.7 5.4 maximum_select_fusion.3
  747.2 5.4 maximum_select_fusion
  (366 shorter events, 67.5 us)
Async XLA Ops:
  0.6 36.6 %copy-start = (bf16[768,1536]{1,0:T(8,128)(2,1)S(1)}, bf16[768,1536]{1,0:T(8,128)(2,1)}, u32[]{:S(2)}) copy-start(bf16[768,1536]{1,0:T(8,128)(2,1)} %param.19) | copy-start | bytes 7077892
  0.7 12.2 %copy-start.70 = (s32[1,512]{1,0:T(1,128)S(1)}, s32[1,512]{1,0:T(1,128)}, u32[]{:S(2)}) copy-start(s32[1,512]{1,0:T(1,128)} %param.26) | copy-start | bytes 6148
  0.7 8.4 %copy-start.52 = (bf16[1,1536,512]{2,1,0:T(8,128)(2,1)S(1)}, bf16[1,1536,512]{2,1,0:T(8,128)(2,1)}, u32[]{:S(2)}) copy-start(bf16[1,1536,512]{2,1,0:T(8,128)(2,1)} %param.22) | copy-start | bytes 4718596
  2.9 14.0 %copy-start.68 = (f32[1536]{0:T(1024)S(1)}, f32[1536]{0:T(1024)}, u32[]{:S(2)}) copy-start(f32[1536]{0:T(1024)} %param.15) | copy-start | bytes 18436
  2.9 73.3 %collective-permute-start.8 = (bf16[256,1536]{1,0:T(8,128)(2,1)}, bf16[256,1536]{1,0:T(8,128)(2,1)}, u32[]{:S(2)}, u32[]{:S(2)}) collective-permute-start(bf16[256,1536]{1,0:T(8,128)(2,1)} %dynamic-slice_bitcast_fusion), channel_id=1, source_target_pairs={{0,16},{2,18},{4,20},{6,22},{8,24},{10,26},{12,28},{14,30},{16,0},... | collective-permute-start | bytes 2359304 | tf_op jit(solution)/shard_map/ppermute | solution.py:123
  9.0 84.0 %collective-permute-start.6 = (bf16[1536,256]{1,0:T(8,128)(2,1)}, bf16[1536,256]{1,0:T(8,128)(2,1)}, u32[]{:S(2)}, u32[]{:S(2)}) collective-permute-start(bf16[1536,256]{1,0:T(8,128)(2,1)} %dynamic-slice_bitcast_fusion.1), channel_id=1, source_target_pairs={{0,16},{2,18},{4,20},{6,22},{8,24},{10,26},{12,28},{14,30},{16,0},... | collective-permute-start | bytes 2359304 | tf_op jit(solution)/shard_map/ppermute | solution.py:123
  10.0 99.1 %collective-permute-start.4 = (bf16[1536,256]{1,0:T(8,128)(2,1)}, bf16[1536,256]{1,0:T(8,128)(2,1)}, u32[]{:S(2)}, u32[]{:S(2)}) collective-permute-start(bf16[1536,256]{1,0:T(8,128)(2,1)} %dynamic-slice_bitcast_fusion.2), channel_id=1, source_target_pairs={{0,16},{2,18},{4,20},{6,22},{8,24},{10,26},{12,28},{14,30},{16,0},... | collective-permute-start | bytes 2359304 | tf_op jit(solution)/shard_map/ppermute | solution.py:123
  16.7 25.0 %copy-start.79 = (f32[512]{0:T(512)}, f32[512]{0:T(512)S(1)}, u32[]{:S(2)}) copy-start(f32[512]{0:T(512)S(1)} %add_rsqrt_fusion) | copy-start | bytes 6148
  16.9 14.1 %copy-start.14 = (pred[512,512]{0,1:T(8,128)(4,1)}, pred[512,512]{0,1:T(8,128)(4,1)S(1)}, u32[]{:S(2)}) copy-start(pred[512,512]{0,1:T(8,128)(4,1)S(1)} %fusion.50) | copy-start | bytes 786436
  41.6 72.0 %collective-permute-start = (f32[256,1536]{1,0:T(8,128)}, f32[256,1536]{1,0:T(8,128)}, u32[]{:S(2)}, u32[]{:S(2)}) collective-permute-start(f32[256,1536]{1,0:T(8,128)} %constant_dynamic-slice_fusion.4), channel_id=1, source_target_pairs={{0,1},{1,0},{2,3},{3,2},{4,5},{5,4},{6,7},{7,6},{8,9},{9,8},{10,11... | collective-permute-start | bytes 4718600 | tf_op jit(solution)/shard_map/ppermute | solution.py:123
  41.7 75.5 %copy-start.62 = (pred[16,256]{1,0:T(8,128)(4,1)}, pred[16,256]{1,0:T(8,128)(4,1)S(1)}, u32[]{:S(2)}) copy-start(pred[16,256]{1,0:T(8,128)(4,1)S(1)} %fusion.54) | copy-start | bytes 12292
  41.8 71.7 %copy-start.75 = (f32[256]{0:T(256)}, f32[256]{0:T(256)S(1)}, u32[]{:S(2)}) copy-start(f32[256]{0:T(256)S(1)} %dynamic-slice.6) | copy-start | bytes 3076
  42.9 70.6 %copy-start.12 = (bf16[512,1536]{1,0:T(8,128)(2,1)S(1)}, bf16[512,1536]{1,0:T(8,128)(2,1)}, u32[]{:S(2)}) copy-start(bf16[512,1536]{1,0:T(8,128)(2,1)} %param.14) | copy-start | bytes 4718596
  44.2 69.3 %copy-start.10 = (f32[512,1536]{1,0:T(8,128)S(1)}, f32[512,1536]{1,0:T(8,128)}, u32[]{:S(2)}) copy-start(f32[512,1536]{1,0:T(8,128)} %copy-done.9) | copy-start | bytes 9437188
  76.2 155.0 %collective-permute-start.9 = (bf16[256,1536]{1,0:T(8,128)(2,1)}, bf16[256,1536]{1,0:T(8,128)(2,1)S(1)}, u32[]{:S(2)}, u32[]{:S(2)}) collective-permute-start(bf16[256,1536]{1,0:T(8,128)(2,1)} %collective-permute-done.8), channel_id=1, source_target_pairs={{0,1},{1,0},{2,3},{3,2},{4,5},{5,4},{6,7},{7,6},{8,9},{9,8},{10,11... | collective-permute-start | bytes 2359304 | tf_op jit(solution)/shard_map/ppermute | solution.py:123
  93.1 125.7 %collective-permute-start.7 = (bf16[1536,256]{1,0:T(8,128)(2,1)}, bf16[1536,256]{1,0:T(8,128)(2,1)S(1)}, u32[]{:S(2)}, u32[]{:S(2)}) collective-permute-start(bf16[1536,256]{1,0:T(8,128)(2,1)} %collective-permute-done.6), channel_id=1, source_target_pairs={{0,1},{1,0},{2,3},{3,2},{4,5},{5,4},{6,7},{7,6},{8,9},{9,8},{10,11... | collective-permute-start | bytes 2359304 | tf_op jit(solution)/shard_map/ppermute | solution.py:123
  109.1 114.7 %collective-permute-start.5 = (bf16[1536,256]{1,0:T(8,128)(2,1)}, bf16[1536,256]{1,0:T(8,128)(2,1)S(1)}, u32[]{:S(2)}, u32[]{:S(2)}) collective-permute-start(bf16[1536,256]{1,0:T(8,128)(2,1)} %collective-permute-done.4), channel_id=1, source_target_pairs={{0,1},{1,0},{2,3},{3,2},{4,5},{5,4},{6,7},{7,6},{8,9},{9,8},{10,11... | collective-permute-start | bytes 2359304 | tf_op jit(solution)/shard_map/ppermute | solution.py:123
  115.4 92.5 %copy-start.50 = (bf16[1,1536,512]{2,1,0:T(8,128)(2,1)S(1)}, bf16[1,1536,512]{2,1,0:T(8,128)(2,1)}, u32[]{:S(2)}) copy-start(bf16[1,1536,512]{2,1,0:T(8,128)(2,1)} %param.23) | copy-start | bytes 4718596
  116.8 96.8 %copy-start.1 = (bf16[256,1536]{1,0:T(8,128)(2,1)}, bf16[256,1536]{1,0:T(8,128)(2,1)S(1)}, u32[]{:S(2)}) copy-start(bf16[256,1536]{1,0:T(8,128)(2,1)S(1)} %multiply_convert_fusion.7.refs_0_) | copy-start | bytes 2359300
  118.3 105.6 %collective-permute-start.1 = (f32[1,16,256]{2,1,0:T(8,128)S(1)}, f32[1,16,256]{2,1,0:T(8,128)S(1)}, u32[]{:S(2)}, u32[]{:S(2)}) collective-permute-start(f32[1,16,256]{2,1,0:T(8,128)S(1)} %fusion.70), channel_id=1, source_target_pairs={{0,2},{2,0},{4,6},{6,4},{8,10},{10,8},{12,14},{14,12},{16,18},{18,... | collective-permute-start | bytes 49160 | tf_op jit(solution)/shard_map/ppermute | solution.py:123
  207.9 17.5 %copy-start.5 = (bf16[2048,1536]{1,0:T(8,128)(2,1)}, bf16[2048,1536]{1,0:T(8,128)(2,1)S(1)}, u32[]{:S(2)}) copy-start(bf16[2048,1536]{1,0:T(8,128)(2,1)S(1)} %get-tuple-element.18) | copy-start | bytes 18874372
  223.9 6.6 collective-permute-start.2
  230.5 4.3 collective-permute-start.3
  247.4 10.2 %copy-start.89 = (bf16[2048,512]{0,1:T(8,128)(2,1)S(1)}, bf16[2048,512]{0,1:T(8,128)(2,1)}, u32[]{:S(2)}) copy-start(bf16[2048,512]{0,1:T(8,128)(2,1)} %get-tuple-element.74) | copy-start | bytes 6291460
  263.3 44.9 %copy-start.24 = (f32[1536,512]{0,1:T(8,128)}, f32[1536,512]{0,1:T(8,128)S(1)}, u32[]{:S(2)}) copy-start(f32[1536,512]{0,1:T(8,128)S(1)} %fusion.92) | copy-start | bytes 9437188
  263.3 21.3 %slice-start.4 = ((s8[6291456]{0:T(1024)(128)(4,1)}), s8[4194304]{0:T(1024)(128)(4,1)S(1)}, s32[]{:S(2)}) async-start(s8[6291456]{0:T(1024)(128)(4,1)} %bitcast.401), calls=%async_computation.4 | async-start | bytes 8388608
  269.8 14.7 %slice-start.5 = ((s8[6291456]{0:T(1024)(128)(4,1)}), s8[2097152]{0:T(1024)(128)(4,1)S(1)}, s32[]{:S(2)}) async-start(s8[6291456]{0:T(1024)(128)(4,1)} %bitcast.401), calls=%async_computation.5 | async-start | bytes 4194304
  277.9 18.3 %slice-start.2 = ((s8[6291456]{0:T(1024)(128)(4,1)}), s8[4194304]{0:T(1024)(128)(4,1)S(1)}, s32[]{:S(2)}) async-start(s8[6291456]{0:T(1024)(128)(4,1)} %bitcast.399), calls=%async_computation.2 | async-start | bytes 8388608
  284.6 11.6 %slice-start.3 = ((s8[6291456]{0:T(1024)(128)(4,1)}), s8[2097152]{0:T(1024)(128)(4,1)S(1)}, s32[]{:S(2)}) async-start(s8[6291456]{0:T(1024)(128)(4,1)} %bitcast.399), calls=%async_computation.3 | async-start | bytes 4194304
  309.1 145.6 %collective-permute-start.19 = (bf16[1536,256]{0,1:T(8,128)(2,1)}, bf16[1536,256]{0,1:T(8,128)(2,1)}, u32[]{:S(2)}, u32[]{:S(2)}) collective-permute-start(bf16[1536,256]{0,1:T(8,128)(2,1)} %slice.1279), channel_id=1, source_target_pairs={{0,1},{1,0},{2,3},{3,2},{4,5},{5,4},{6,7},{7,6},{8,9},{9,8},{10,11... | collective-permute-start | bytes 2359304 | tf_op jit(solution)/shard_map/ppermute | solution.py:123
  313.7 143.5 %collective-permute-start.23 = (bf16[1536,256]{0,1:T(8,128)(2,1)}, bf16[1536,256]{0,1:T(8,128)(2,1)}, u32[]{:S(2)}, u32[]{:S(2)}) collective-permute-start(bf16[1536,256]{0,1:T(8,128)(2,1)} %slice.1278), channel_id=1, source_target_pairs={{0,1},{1,0},{2,3},{3,2},{4,5},{5,4},{6,7},{7,6},{8,9},{9,8},{10,11... | collective-permute-start | bytes 2359304 | tf_op jit(solution)/shard_map/ppermute | solution.py:123
  319.7 140.3 %collective-permute-start.27 = (bf16[256,1536]{1,0:T(8,128)(2,1)S(1)}, bf16[256,1536]{1,0:T(8,128)(2,1)}, u32[]{:S(2)}, u32[]{:S(2)}) collective-permute-start(bf16[256,1536]{1,0:T(8,128)(2,1)S(1)} %slice.1277), channel_id=1, source_target_pairs={{0,1},{1,0},{2,3},{3,2},{4,5},{5,4},{6,7},{7,6},{8,9},{9,8},{10,11... | collective-permute-start | bytes 2359304 | tf_op jit(solution)/shard_map/ppermute | solution.py:123
  321.7 32.3 %collective-permute-start.11 = (f32[4,16,256]{2,1,0:T(8,128)S(1)}, f32[4,16,256]{2,1,0:T(8,128)S(1)}, u32[]{:S(2)}, u32[]{:S(2)}) collective-permute-start(f32[4,16,256]{2,1,0:T(8,128)S(1)} %slice.1114), channel_id=1, source_target_pairs={{0,8},{2,10},{4,12},{6,14},{8,0},{10,2},{12,4},{14,6},{16,24},{18,... | collective-permute-start | bytes 196616 | tf_op jit(solution)/shard_map/ppermute | solution.py:123
  324.8 195.7 %collective-permute-start.26 = (bf16[256,1536]{1,0:T(8,128)(2,1)}, bf16[256,1536]{1,0:T(8,128)(2,1)}, u32[]{:S(2)}, u32[]{:S(2)}) collective-permute-start(bf16[256,1536]{1,0:T(8,128)(2,1)} %dynamic-slice_convert_fusion), channel_id=1, source_target_pairs={{0,1},{1,0},{2,3},{3,2},{4,5},{5,4},{6,7},{7,6},{8,9},{9,8},{10,11... | collective-permute-start | bytes 2359304 | tf_op jit(solution)/shard_map/ppermute | solution.py:123
  354.1 4.0 collective-permute-start.12
  358.1 92.3 %collective-permute-start.13 = (f32[1,16,256]{2,1,0:T(8,128)S(1)}, f32[1,16,256]{2,1,0:T(8,128)S(1)}, u32[]{:S(2)}, u32[]{:S(2)}) collective-permute-start(f32[1,16,256]{2,1,0:T(8,128)S(1)} %slice.1118), channel_id=1, source_target_pairs={{0,2},{2,0},{4,6},{6,4},{8,10},{10,8},{12,14},{14,12},{16,18},{18,... | collective-permute-start | bytes 49160 | tf_op jit(solution)/shard_map/ppermute | solution.py:123
  364.6 85.8 %copy-start.48 = (f32[16,256]{1,0:T(8,128)S(1)}, f32[16,256]{1,0:T(8,128)}, u32[]{:S(2)}) copy-start(f32[16,256]{1,0:T(8,128)} %copy-done.47) | copy-start | bytes 49156
  364.6 85.8 %copy-start.63 = (pred[16,256]{1,0:T(8,128)(4,1)S(1)}, pred[16,256]{1,0:T(8,128)(4,1)}, u32[]{:S(2)}) copy-start(pred[16,256]{1,0:T(8,128)(4,1)} %copy-done.62) | copy-start | bytes 12292
  364.6 85.8 %copy-start.72 = (f32[256]{0:T(256)S(1)}, f32[256]{0:T(256)}, u32[]{:S(2)}) copy-start(f32[256]{0:T(256)} %copy-done.71) | copy-start | bytes 3076
  364.6 85.8 %copy-start.74 = (f32[256]{0:T(256)S(1)}, f32[256]{0:T(256)}, u32[]{:S(2)}) copy-start(f32[256]{0:T(256)} %copy-done.73) | copy-start | bytes 3076
  364.7 85.9 %copy-start.8 = (f32[256,1536]{1,0:T(8,128)S(1)}, f32[256,1536]{1,0:T(8,128)}, u32[]{:S(2)}) copy-start(f32[256,1536]{1,0:T(8,128)} %copy-done.7) | copy-start | bytes 4718596
  364.7 85.9 %copy-start.61 = (bf16[1536,16]{0,1:T(8,128)(2,1)S(1)}, bf16[1536,16]{0,1:T(8,128)(2,1)}, u32[]{:S(2)}) copy-start(bf16[1536,16]{0,1:T(8,128)(2,1)} %param.21) | copy-start | bytes 147460
  364.7 85.9 %copy-start.67 = (f32[1536]{0:T(1024)S(1)}, f32[1536]{0:T(1024)}, u32[]{:S(2)}) copy-start(f32[1536]{0:T(1024)} %param.20) | copy-start | bytes 18436
  364.7 85.9 %copy-start.78 = (f32[256]{0:T(256)S(1)}, f32[256]{0:T(256)}, u32[]{:S(2)}) copy-start(f32[256]{0:T(256)} %copy-done.77) | copy-start | bytes 3076
  450.3 122.8 %collective-permute-start.18 = (bf16[1536,256]{0,1:T(8,128)(2,1)}, bf16[1536,256]{0,1:T(8,128)(2,1)}, u32[]{:S(2)}, u32[]{:S(2)}) collective-permute-start(bf16[1536,256]{0,1:T(8,128)(2,1)} %dynamic-slice_convert_fusion.2), channel_id=1, source_target_pairs={{0,1},{1,0},{2,3},{3,2},{4,5},{5,4},{6,7},{7,6},{8,9},{9,8},{10,11... | collective-permute-start | bytes 2359304 | tf_op jit(solution)/shard_map/ppermute | solution.py:123
  454.7 71.7 %collective-permute-start.22 = (bf16[1536,256]{0,1:T(8,128)(2,1)}, bf16[1536,256]{0,1:T(8,128)(2,1)}, u32[]{:S(2)}, u32[]{:S(2)}) collective-permute-start(bf16[1536,256]{0,1:T(8,128)(2,1)} %dynamic-slice_convert_fusion.1), channel_id=1, source_target_pairs={{0,1},{1,0},{2,3},{3,2},{4,5},{5,4},{6,7},{7,6},{8,9},{9,8},{10,11... | collective-permute-start | bytes 2359304 | tf_op jit(solution)/shard_map/ppermute | solution.py:123
  457.1 5.1 collective-permute-start.14
  460.0 56.8 %collective-permute-start.10 = (bf16[256,1536]{1,0:T(8,128)(2,1)}, bf16[256,1536]{1,0:T(8,128)(2,1)}, u32[]{:S(2)}, u32[]{:S(2)}) collective-permute-start(bf16[256,1536]{1,0:T(8,128)(2,1)} %get-tuple-element.87), channel_id=1, source_target_pairs={{0,1},{1,0},{2,3},{3,2},{4,5},{5,4},{6,7},{7,6},{8,9},{9,8},{10,11... | collective-permute-start | bytes 2359304 | tf_op jit(solution)/shard_map/ppermute | solution.py:123
  462.3 61.2 %collective-permute-start.28 = (bf16[256,1536]{1,0:T(8,128)(2,1)}, bf16[256,1536]{1,0:T(8,128)(2,1)}, u32[]{:S(2)}, u32[]{:S(2)}) collective-permute-start(bf16[256,1536]{1,0:T(8,128)(2,1)} %fusion.26), channel_id=1, source_target_pairs={{0,16},{2,18},{4,20},{6,22},{8,24},{10,26},{12,28},{14,30},{16,0},... | collective-permute-start | bytes 2359304 | tf_op jit(solution)/shard_map/ppermute | solution.py:123
  473.6 16.1 %slice-start.6 = ((s8[12582912]{0:T(1024)(128)(4,1)}), s8[4194304]{0:T(1024)(128)(4,1)S(1)}, s32[]{:S(2)}) async-start(s8[12582912]{0:T(1024)(128)(4,1)} %bitcast.403), calls=%async_computation.6 | async-start | bytes 8388608
  473.6 16.0 %slice-start.7 = ((s8[12582912]{0:T(1024)(128)(4,1)}), s8[4194304]{0:T(1024)(128)(4,1)S(1)}, s32[]{:S(2)}) async-start(s8[12582912]{0:T(1024)(128)(4,1)} %bitcast.403), calls=%async_computation.7 | async-start | bytes 8388608
  480.1 9.6 %slice-start.8 = ((s8[12582912]{0:T(1024)(128)(4,1)}), s8[4194304]{0:T(1024)(128)(4,1)S(1)}, s32[]{:S(2)}) async-start(s8[12582912]{0:T(1024)(128)(4,1)} %bitcast.403), calls=%async_computation.8 | async-start | bytes 8388608
  516.8 54.7 %collective-permute-start.24 = (bf16[1536,256]{0,1:T(8,128)(2,1)}, bf16[1536,256]{0,1:T(8,128)(2,1)S(1)}, u32[]{:S(2)}, u32[]{:S(2)}) collective-permute-start(bf16[1536,256]{0,1:T(8,128)(2,1)} %fusion.27), channel_id=1, source_target_pairs={{0,16},{2,18},{4,20},{6,22},{8,24},{10,26},{12,28},{14,30},{16,0},... | collective-permute-start | bytes 2359304 | tf_op jit(solution)/shard_map/ppermute | solution.py:123
  520.5 51.0 %copy-start.22 = (f32[1536,512]{0,1:T(8,128)S(1)}, f32[1536,512]{0,1:T(8,128)}, u32[]{:S(2)}) copy-start(f32[1536,512]{0,1:T(8,128)} %fusion.93) | copy-start | bytes 9437188
  520.5 67.7 %collective-permute-start.20 = (bf16[1536,256]{0,1:T(8,128)(2,1)}, bf16[1536,256]{0,1:T(8,128)(2,1)S(1)}, u32[]{:S(2)}, u32[]{:S(2)}) collective-permute-start(bf16[1536,256]{0,1:T(8,128)(2,1)} %fusion.28), channel_id=1, source_target_pairs={{0,16},{2,18},{4,20},{6,22},{8,24},{10,26},{12,28},{14,30},{16,0},... | collective-permute-start | bytes 2359304 | tf_op jit(solution)/shard_map/ppermute | solution.py:123
  523.4 67.5 %collective-permute-start.15 = (f32[256,1536]{1,0:T(8,128)}, f32[256,1536]{1,0:T(8,128)S(1)}, u32[]{:S(2)}, u32[]{:S(2)}) collective-permute-start(f32[256,1536]{1,0:T(8,128)} %constant_dynamic-slice_fusion), channel_id=1, source_target_pairs={{0,1},{1,0},{2,3},{3,2},{4,5},{5,4},{6,7},{7,6},{8,9},{9,8},{10,11... | collective-permute-start | bytes 4718600 | tf_op jit(solution)/shard_map/ppermute | solution.py:123
  526.4 61.8 %copy-start.21 = (f32[1536,512]{0,1:T(8,128)S(1)}, f32[1536,512]{0,1:T(8,128)}, u32[]{:S(2)}) copy-start(f32[1536,512]{0,1:T(8,128)} %fusion.91) | copy-start | bytes 9437188
  526.4 215.4 %collective-permute-start.29 = (f32[256,1536]{1,0:T(8,128)}, f32[256,1536]{1,0:T(8,128)}, u32[]{:S(2)}, u32[]{:S(2)}) collective-permute-start(f32[256,1536]{1,0:T(8,128)} %convert_add_fusion.1), channel_id=1, source_target_pairs={{0,1},{1,0},{2,3},{3,2},{4,5},{5,4},{6,7},{7,6},{8,9},{9,8},{10,11... | collective-permute-start | bytes 4718600 | tf_op jit(solution)/shard_map/ppermute | solution.py:123
  571.5 19.5 %copy-start.19 = (f32[512,1536]{1,0:T(8,128)S(1)}, f32[512,1536]{1,0:T(8,128)}, u32[]{:S(2)}) copy-start(f32[512,1536]{1,0:T(8,128)} %copy-done.18) | copy-start | bytes 9437188
  573.1 17.9 %copy-start.76 = (f32[256]{0:T(256)S(1)}, f32[256]{0:T(256)}, u32[]{:S(2)}) copy-start(f32[256]{0:T(256)} %copy-done.75) | copy-start | bytes 3076
  573.1 154.3 %collective-permute-start.25 = (f32[1536,256]{0,1:T(8,128)S(1)}, f32[1536,256]{0,1:T(8,128)S(1)}, u32[]{:S(2)}, u32[]{:S(2)}) collective-permute-start(f32[1536,256]{0,1:T(8,128)S(1)} %convert_add_fusion.2), channel_id=1, source_target_pairs={{0,1},{1,0},{2,3},{3,2},{4,5},{5,4},{6,7},{7,6},{8,9},{9,8},{10,11... | collective-permute-start | bytes 4718600 | tf_op jit(solution)/shard_map/ppermute | solution.py:123
  590.9 142.0 %collective-permute-start.21 = (f32[1536,256]{0,1:T(8,128)}, f32[1536,256]{0,1:T(8,128)}, u32[]{:S(2)}, u32[]{:S(2)}) collective-permute-start(f32[1536,256]{0,1:T(8,128)} %convert_add_fusion.3), channel_id=1, source_target_pairs={{0,1},{1,0},{2,3},{3,2},{4,5},{5,4},{6,7},{7,6},{8,9},{9,8},{10,11... | collective-permute-start | bytes 4718600 | tf_op jit(solution)/shard_map/ppermute | solution.py:123
  591.8 2.8 collective-permute-start.17
  594.0 153.2 %collective-permute-start.16 = (f32[256,1536]{1,0:T(8,128)}, f32[256,1536]{1,0:T(8,128)}, u32[]{:S(2)}, u32[]{:S(2)}) collective-permute-start(f32[256,1536]{1,0:T(8,128)} %fusion.22), channel_id=1, source_target_pairs={{0,1},{1,0},{2,3},{3,2},{4,5},{5,4},{6,7},{7,6},{8,9},{9,8},{10,11... | collective-permute-start | bytes 4718600 | tf_op jit(solution)/shard_map/ppermute | solution.py:123
  (66 other events, 220.4 us)

commit v3 on v1

v3 whole, which is shorter than its diff:
```python
import functools

import jax
import jax.numpy as jnp
from jax import lax
from jax.experimental import pallas as pl
from jax.experimental.pallas import tpu as pltpu
from jax.sharding import PartitionSpec as P

HEAD_DIM = 64

bf16 = jnp.bfloat16
f32 = jnp.float32
MESH = pl.DeviceIdType.MESH
epsilon = 1e-06
residual_scale = 0.22
attn_scale = 0.015625
rope_base = 10000.0
masked_score = -1e30


def positions_of(segment):
    position_index = jnp.arange(segment.shape[0], dtype=jnp.int32)
    earlier = jnp.concatenate([segment[:1] - 1, segment[:-1]])
    starts = lax.cummax(jnp.where(segment != earlier, position_index, 0), axis=0)
    return position_index - starts


def rope_tables(segment, head_size):
    position = positions_of(segment).astype(f32)
    frequency = rope_base ** (-jnp.arange(head_size // 2, dtype=f32) * 2.0 / head_size)
    angle = position[:, None] * frequency[None, :]
    return (jnp.cos(angle)[:, None, :], jnp.sin(angle)[:, None, :])


def apply_rotation(heads_in, cosine_table, sine_values):
    middle_index = heads_in.shape[-1] // 2
    first_half = heads_in[..., :middle_index]
    second_half = heads_in[..., middle_index:]
    return jnp.concatenate(
        [
            first_half * cosine_table - second_half * sine_values,
            second_half * cosine_table + first_half * sine_values,
        ],
        axis=-1,
    )


def block_scores(query_heads, key_heads, segment):
    kv_count = key_heads.shape[1]
    length = query_heads.shape[0]
    grouped = query_heads.reshape(length, kv_count, -1, query_heads.shape[2])
    raw_scores = (
        jnp.einsum("qhgd,khd->hgqk", grouped, key_heads, preferred_element_type=f32) * attn_scale
    )
    index = jnp.arange(length, dtype=jnp.int32)
    allowed = (index[:, None] >= index[None, :]) & (segment[:, None] == segment[None, :])
    return (jnp.where(allowed, raw_scores, masked_score), grouped)


def attend_forward(normed, segment, tables, w_query, key_weight, value_weight, head_size):
    length = normed.shape[0]

    def heads(weight):
        return jnp.dot(normed, weight, preferred_element_type=f32).reshape(length, -1, head_size)

    query_heads = apply_rotation(heads(w_query), *tables).astype(bf16)
    key_heads = apply_rotation(heads(key_weight), *tables).astype(bf16)
    value_heads = heads(value_weight).astype(bf16)
    scores, _ = block_scores(query_heads, key_heads, segment)
    largest = jnp.max(scores, axis=-1, keepdims=True)
    weights_raw = jnp.exp(scores - largest)
    totals = jnp.sum(weights_raw, axis=-1, keepdims=True)
    probs_low = (weights_raw / totals).astype(bf16)
    head_out = jnp.einsum("hgqk,khd->qhgd", probs_low, value_heads, preferred_element_type=f32)
    return (
        head_out.reshape(length, -1).astype(bf16),
        query_heads,
        key_heads,
        value_heads,
        (largest + jnp.log(totals))[..., 0],
    )


def attend_backward(query_heads, key_heads, value_heads, log_sums, heads_grad, segment, tables):
    length = query_heads.shape[0]
    cosine_table, sine_values = tables
    scores, grouped = block_scores(query_heads, key_heads, segment)
    probability = jnp.exp(scores - log_sums[..., None])
    probs_low = probability.astype(bf16)
    grad_grouped = heads_grad.reshape(grouped.shape)
    prob_grad = jnp.einsum(
        "qhgd,khd->hgqk", grad_grouped, value_heads, preferred_element_type=f32
    )
    weighted = jnp.sum(probability * prob_grad, axis=-1, keepdims=True)
    score_low = (probability * (prob_grad - weighted)).astype(bf16)
    query_part = (
        jnp.einsum("hgqk,khd->qhgd", score_low, key_heads, preferred_element_type=f32) * attn_scale
    ).reshape(query_heads.shape)
    key_sum = (
        jnp.einsum("hgqk,qhgd->khd", score_low, grouped, preferred_element_type=f32) * attn_scale
    )
    value_sum = jnp.einsum(
        "hgqk,qhgd->khd", probs_low, grad_grouped, preferred_element_type=f32
    )
    query_low = apply_rotation(query_part, cosine_table, -sine_values).astype(bf16)
    key_low = apply_rotation(key_sum, cosine_table, -sine_values).astype(bf16)
    return (
        query_low.reshape(length, -1),
        key_low.reshape(length, -1),
        value_sum.astype(bf16).reshape(length, -1),
    )


def bit_masks(size):
    masks = []
    while size > 1:
        size //= 2
        masks.append(size)
    return masks[::-1]


def swap(x, axis, mask):
    return lax.ppermute(x, axis, [(i, i ^ mask) for i in range(lax.axis_size(axis))])


def bit_of(axis, mask):
    return (lax.axis_index(axis) // mask) % 2


def halves_by_bit(x, axis, mask, dim=0):
    half = x.shape[dim] // 2
    bit = bit_of(axis, mask)
    mine = lax.dynamic_slice_in_dim(x, bit * half, half, dim)
    other = lax.dynamic_slice_in_dim(x, (1 - bit) * half, half, dim)
    return mine, other


def join_by_bit(mine, other, axis, mask, dim=0):
    return jnp.where(
        bit_of(axis, mask) == 0,
        jnp.concatenate([mine, other], dim),
        jnp.concatenate([other, mine], dim),
    )


def scatter_sum(x, axis, masks, kind, dim=0):
    x = x.astype(f32)
    for mask in masks:
        mine, other = halves_by_bit(x, axis, mask, dim)
        x = mine + swap(other.astype(kind), axis, mask).astype(f32)
    return x


def gather_blocks(x, axis, masks, dim=0):
    for mask in reversed(masks):
        x = join_by_bit(x, swap(x, axis, mask), axis, mask, dim)
    return x


def rotated(masks, j):
    j = j % len(masks)
    return masks[j:] + masks[:j]


def peer_of(mask):
    me = lax.axis_index("dp")
    bit = (me // mask) % 2
    return me + mask * (1 - 2 * bit), bit


def greet(masks):
    barrier = pltpu.get_barrier_semaphore()
    for mask in masks:
        pl.semaphore_signal(
            barrier, inc=1, device_id={"dp": peer_of(mask)[0]}, device_id_type=MESH
        )
    pl.semaphore_wait(barrier, len(masks))


def remote(src, dst, send, recv, mask):
    return remote_to(src, dst, send, recv, peer_of(mask)[0])


def add_rows(dst, dst0, a, a0, b, b0, rows, out_dtype):
    step = 16

    def body(i, _):
        r = pl.multiple_of(i * step, step)
        x = a[pl.ds(a0 + r, step), :].astype(f32) + b[pl.ds(b0 + r, step), :].astype(f32)
        dst[pl.ds(dst0 + r, step), :] = x.astype(out_dtype)
        return 0

    lax.fori_loop(0, rows // step, body, 0)


def group_sizes(dp_size):
    a = 4
    return a, dp_size // (2 * a)


class Spot:
    def __init__(self, a, b):
        me = lax.axis_index("dp")
        self.a, self.b = a, b
        self.n = a * b
        self.me = me
        self.A = me // (2 * b)
        self.B = (me // 2) % b
        self.block = me // 2
        self.pair = me % 2
        self.devices = (me + 2 * b, me - 2 * b, me + 2, me - 2)
        self.exists = (self.A < a - 1, self.A > 0, self.B < b - 1, self.B > 0)
        self.some = me + 2 * (1 - 2 * (self.B % 2))

    def greet(self):
        barrier = pltpu.get_barrier_semaphore()
        for device, there in zip(self.devices, self.exists):

            @pl.when(there)
            def _(device=device):
                pl.semaphore_signal(
                    barrier, inc=1, device_id={"dp": device}, device_id_type=MESH
                )

        a, b = self.a, self.b
        ups = 2 - (self.A + 1) // a - (self.B + 1) // b
        downs = (self.A + a - 1) // a + (self.B + b - 1) // b
        pl.semaphore_wait(barrier, ups + downs)


def is_at(x, value):
    return 1 // (1 + (x - value) * (x - value))


def by_distance(size, place, k):
    found = 0
    for p in range(size):
        order = sorted(range(size), key=lambda q: (abs(q - p), q))
        for j, q in enumerate(order):
            if q > 0:
                found = found + q * is_at(place, p) * is_at(k, j)
    return found


def visit_order(a, b):
    pairs = [(k, l) for k in range(a) for l in range(b)]
    return sorted(pairs, key=lambda kl: kl[0] + (2 * kl[1] + 0.5 if kl[1] else 0))


def remote_to(src, dst, send, recv, device):
    return pltpu.make_async_remote_copy(
        src_ref=src,
        dst_ref=dst,
        send_sem=send,
        recv_sem=recv,
        device_id={"dp": device},
        device_id_type=MESH,
    )


PIECES = 2
SUM_PIECES = 4


class LineGather:
    def __init__(self, spot, buf, rows, send, recv):
        self.spot, self.buf, self.rows, self.send, self.recv = spot, buf, rows, send, recv

    def coords(self, i):
        s = self.spot
        visits = visit_order(s.a, s.b)
        k = sum(v[0] * is_at(i, j) for j, v in enumerate(visits) if v[0])
        l = sum(v[1] * is_at(i, j) for j, v in enumerate(visits) if v[1])
        return by_distance(s.a, s.A, k), by_distance(s.b, s.B, l)

    def row0(self, i):
        A, B = self.coords(i)
        return pl.multiple_of((A * self.spot.b + B) * self.rows, 16)

    def copies(self, block, way, device):
        size = self.rows // PIECES
        return [
            remote_to(there, there, self.send.at[block, way, p], self.recv.at[block, p], device)
            for p in range(PIECES)
            for there in [self.buf.at[pl.ds(pl.multiple_of(block * self.rows + p * size, 16), size)]]
        ]

    def each_way(self, i, act):
        s = self.spot
        A, B = self.coords(i)
        block = A * s.b + B
        same = B == s.B
        conditions = (
            same & (A <= s.A) & s.exists[0],
            same & (A >= s.A) & s.exists[1],
            (B <= s.B) & s.exists[2],
            (B >= s.B) & s.exists[3],
        )
        for way, (condition, device) in enumerate(zip(conditions, s.devices)):

            @pl.when(condition)
            def _(way=way, device=device):
                for c in self.copies(block, way, device):
                    act(c)

    def wait(self, i):
        A, B = self.coords(i)
        for c in self.copies(A * self.spot.b + B, 0, self.spot.some):
            c.wait_recv()

    def forward(self, i):
        self.each_way(i, lambda c: c.start())

    def finish(self):
        def one(i, _):
            self.each_way(i, lambda c: c.wait_send())
            return 0

        lax.fori_loop(0, self.spot.n, one, 0)


def add_into(dst, d0, src, s0, rows, step=16):
    def body(i, _):
        r = pl.multiple_of(i * step, step)
        total = dst[pl.ds(d0 + r, step), :].astype(f32) + src[pl.ds(s0 + r, step), :].astype(f32)
        dst[pl.ds(d0 + r, step), :] = total.astype(dst.dtype)
        return 0

    lax.fori_loop(0, rows // step, body, 0)


class LineSum:
    def __init__(self, size, place, up, down, part, row_of, rows, got, send, recv, some):
        self.size, self.place, self.up, self.down = size, place, up, down
        self.part, self.row_of, self.rows, self.got = part, row_of, rows, got
        self.send, self.recv, self.some = send, recv, some

    def up_slot(self, place, c):
        return c - place

    def down_slot(self, place, c):
        return c + (self.size - place) * ((place + self.size - 1) // self.size)

    def copies(self, c, slot, send, device):
        size = self.rows // SUM_PIECES
        return [
            remote_to(
                self.part.at[pl.ds(pl.multiple_of(self.row_of(c) + p * size, 16), size)],
                self.got.at[pl.ds(pl.multiple_of(slot * self.rows + p * size, 16), size)],
                send.at[p],
                self.recv.at[slot, p],
                device,
            )
            for p in range(SUM_PIECES)
        ]

    def take(self, c, slot, p, dst=None, d0=None):
        if dst is None:
            dst, d0 = self.part, self.row_of(c)
        size = self.rows // SUM_PIECES
        self.copies(c, slot, self.send.at[0, 0], self.some)[p].wait_recv()
        from_row = pl.multiple_of(slot * self.rows + p * size, 16)
        add_into(dst, d0 + p * size, self.got, from_row, size)

    def up_copies(self, k):
        c = self.size - 1 - k
        return self.copies(c, self.up_slot(self.place + 1, c), self.send.at[k, 0], self.up)

    def down_copies(self, k):
        return self.copies(k, self.down_slot(self.place - 1, k), self.send.at[k, 1], self.down)

    def step_up(self, k):
        c = self.size - 1 - k

        @pl.when(c > self.place)
        def _():
            for p, copy in enumerate(self.up_copies(k)):

                @pl.when(self.place > 0)
                def _(p=p):
                    self.take(c, self.up_slot(self.place, c), p)

                copy.start()

    def step_down(self, k):
        @pl.when(k < self.place)
        def _():
            for p, copy in enumerate(self.down_copies(k)):

                @pl.when(self.place < self.size - 1)
                def _(p=p):
                    self.take(k, self.down_slot(self.place, k), p)

                copy.start()

    def step(self, k):
        self.step_up(k)
        self.step_down(k)

    def end(self, out=None):
        p = self.place
        d0 = None
        if out is not None:
            out[...] = self.part[pl.ds(self.row_of(p), self.rows), :].astype(out.dtype)
            d0 = 0

        @pl.when(p > 0)
        def _():
            for j in range(SUM_PIECES):
                self.take(p, self.up_slot(p, p), j, out, d0)

        @pl.when(p < self.size - 1)
        def _():
            for j in range(SUM_PIECES):
                self.take(p, self.down_slot(p, p), j, out, d0)

        for k in range(self.size - 1):

            @pl.when(self.size - 1 - k > p)
            def _(k=k):
                for c in self.up_copies(k):
                    c.wait_send()

            @pl.when(k < p)
            def _(k=k):
                for c in self.down_copies(k):
                    c.wait_send()


def slots_of(size):
    return 1 if size == 2 else size + 1


class GroupSum:
    def __init__(self, spot, part, rows, got_b, got_a, send_b, recv_b, send_a, recv_a):
        self.spot, self.part, self.rows = spot, part, rows
        a, b = spot.a, spot.b
        slots_b = slots_of(b)

        def b_line(A):
            return LineSum(
                b, spot.B, spot.devices[2], spot.devices[3], part,
                lambda B: pl.multiple_of((A * b + B) * rows, 16), rows,
                got_b.at[pl.ds(pl.multiple_of(A * slots_b * rows, 16), slots_b * rows)],
                send_b.at[A], recv_b.at[A], spot.some,
            )

        self.b_line = b_line
        self.a_line = LineSum(
            a, spot.A, spot.devices[0], spot.devices[1], part,
            lambda A: pl.multiple_of((A * b + spot.B) * rows, 16), rows,
            got_a, send_a, recv_a, spot.some,
        )

    def ready(self, A, B):
        if self.spot.b == 2:
            line = self.b_line(A)

            @pl.when(B != self.spot.B)
            def _():
                line.step(0)

    def along_b(self):
        if self.spot.b > 2:

            def one(A, _):
                for k in range(self.spot.b - 1):
                    self.b_line(A).step(k)
                return 0

            lax.fori_loop(0, self.spot.a, one, 0)

    def flow(self, fills):
        a, line = self.spot.a, self.a_line
        fills = list(fills)

        def fill():
            if fills:
                fills.pop(0)()

        for k in range(a - 1):
            if 2 * k < a:
                self.b_line(a - 1 - k).end()
            line.step_up(k)
            fill()
            if 2 * k < a and a - 1 - k != k:
                self.b_line(k).end()
            line.step_down(k)
            fill()
        while fills:
            fill()

    def order(self, j):
        a = self.spot.a
        places = sorted(range(a), key=lambda c: (min(c, a - 1 - c), -c))
        return sum(c * is_at(j, i) for i, c in enumerate(places) if c)

    def steps_a(self):
        return self.spot.a - 1

    @staticmethod
    def scratch(a, b, rows, width):
        return [
            pltpu.VMEM((a * slots_of(b) * rows, width), bf16),
            pltpu.VMEM((slots_of(a) * rows, width), bf16),
            pltpu.SemaphoreType.DMA((a, b - 1, 2, SUM_PIECES)),
            pltpu.SemaphoreType.DMA((a, slots_of(b), SUM_PIECES)),
            pltpu.SemaphoreType.DMA((a - 1, 2, SUM_PIECES)),
            pltpu.SemaphoreType.DMA((slots_of(a), SUM_PIECES)),
        ]


def sum_kernel(a, b, rows, x_ref, out_ref, part, load, *scratch):
    spot = Spot(a, b)
    n = spot.n
    total = GroupSum(spot, part, rows, *scratch)

    def loading(A, B):
        at = pl.ds(pl.multiple_of((A * b + B) * rows, 16), rows)
        return pltpu.make_async_copy(x_ref.at[at], part.at[at], load.at[A * b + B])

    order = sorted(range(a), key=lambda c: (min(c, a - 1 - c), -c))
    for A in order:
        for B in range(b):
            loading(A, B).start()
    spot.greet()
    for A in order:
        for B in range(b):
            loading(A, B).wait()
            total.ready(A, B)
    total.along_b()
    total.flow([])
    total.a_line.end(out_ref)


def group_sum(x, dp_size, collective_id):
    a, b = group_sizes(dp_size)
    n = a * b
    rows, width = x.shape[0] // n, x.shape[1]
    return pl.pallas_call(
        functools.partial(sum_kernel, a, b, rows),
        out_shape=jax.ShapeDtypeStruct((rows, width), f32),
        in_specs=[pl.BlockSpec(memory_space=pl.ANY)],
        out_specs=pl.BlockSpec(memory_space=pltpu.VMEM),
        scratch_shapes=[pltpu.VMEM(x.shape, bf16), pltpu.SemaphoreType.DMA((n,))]
        + GroupSum.scratch(a, b, rows, width),
        compiler_params=pltpu.CompilerParams(
            collective_id=collective_id, has_side_effects=True, vmem_limit_bytes=40 << 20
        ),
    )(x)


LANES = 128
LOW_AT = 64


def mm(x, y, dims):
    return lax.dot_general(x, y, (dims, ((), ())), preferred_element_type=f32)


NN, NT, TN = ((1,), (0,)), ((1,), (1,)), ((0,), (0,))


def experts_kernel(
    a, b, rows, width,
    x_ref, grads_ref, picked_ref, router_ref, near_gate, near_up, near_down, far_gate, far_up, far_down,
    moe_ref, out_ref, o_near_gate, o_near_up, o_near_down, o_far_gate, o_far_up, o_far_down,
    xs, gs, weights, downs, lows, part, extras, stage, local, load, send, recv, stage_sem, store, *scratch,
):
    spot = Spot(a, b)
    n = spot.n
    gather = LineGather(spot, xs, rows, send, recv)
    total = GroupSum(spot, part, rows, *scratch)
    mine = pltpu.make_async_copy(
        x_ref, xs.at[pl.ds(pl.multiple_of(spot.block * rows, 16), rows)], local.at[0]
    )
    mine.start()
    sources = (near_gate, near_up, far_gate, far_up)
    arriving = [
        pltpu.make_async_copy(src, weights.at[k], local.at[1 + k]) for k, src in enumerate(sources)
    ] + [
        pltpu.make_async_copy(src, downs.at[k], local.at[5 + k])
        for k, src in enumerate((near_down, far_down))
    ]

    def grads_copy(i):
        at = pl.ds(gather.row0(i), rows)
        return pltpu.make_async_copy(grads_ref.at[at], gs.at[at], load.at[i])

    grads_copy(0).start()
    for c in arriving:
        c.start()
    for i in range(1, n):
        grads_copy(i).start()
    spot.greet()
    mine.wait()
    gather.forward(0)
    for c in arriving:
        c.wait()
    lane = lax.broadcasted_iota(jnp.int32, (rows, LANES), 1)
    near, far = spot.me, spot.me + 1 - 2 * spot.pair

    def block(i, _):
        at = pl.ds(gather.row0(i), rows)
        grads_copy(i).wait()
        x = xs[at, :]
        chosen = picked_ref[at, :] > 0
        logits = jnp.where(chosen, mm(x, router_ref[...], NN), masked_score)
        raised = jnp.where(chosen, jnp.exp(logits - jnp.max(logits, axis=1, keepdims=True)), 0.0)
        gates = raised / jnp.sum(raised, axis=1, keepdims=True)
        extra = jnp.zeros((rows, LANES), f32)
        for e, expert in enumerate((near, far)):
            if e == 1:

                @pl.when(i + 1 < n)
                def _():
                    gather.wait(i + 1)
                    gather.forward(i + 1)

            column = jnp.sum(jnp.where(lane == expert, gates, 0.0), axis=1, keepdims=True)
            x = xs[at, :]
            gate_act = mm(x, weights[2 * e], NN)
            up_act = mm(x, weights[2 * e + 1], NN)
            down_in = residual_scale * mm(gs[at, :], downs[e], NT)
            sigmoid_gate = jax.nn.sigmoid(gate_act)
            silu_gate = gate_act * sigmoid_gate
            hidden = silu_gate * up_act
            deriv = jnp.sum(hidden * down_in, axis=1, keepdims=True)
            high = deriv.astype(bf16).astype(f32)
            extra += jnp.where(lane == expert, high, 0.0)
            extra += jnp.where(lane == expert + LOW_AT, deriv - high, 0.0)
            down_in = down_in * column
            lows[3 * e, at, :] = (hidden * column).astype(bf16)
            lows[3 * e + 1, at, :] = (
                down_in * up_act * sigmoid_gate * (1.0 + gate_act * (1.0 - sigmoid_gate))
            ).astype(bf16)
            lows[3 * e + 2, at, :] = (down_in * silu_gate).astype(bf16)

        extras[at, :] = extra.astype(bf16)
        return 0

    lax.fori_loop(0, n, block, 0)

    def rows_of(A, B):
        return pl.ds(pl.multiple_of((A * b + B) * rows, 16), rows)

    def back_block(A, B):
        at = rows_of(A, B)
        back = mm(lows[1, at, :], weights[0], NT) + mm(lows[2, at, :], weights[1], NT)
        back += mm(lows[4, at, :], weights[2], NT) + mm(lows[5, at, :], weights[3], NT)
        part[at, pl.ds(0, width)] = back.astype(bf16)
        part[at, pl.ds(width, LANES)] = extras[at, :]
        total.ready(A, B)

    def back_others(i, _):
        A = total.order(i // (b - 1))
        B = by_distance(b, spot.B, 1 + i % (b - 1))
        back_block(A, B)
        return 0

    def back_own(i, _):
        back_block(total.order(i), spot.B)
        return 0

    def stage_copy(i):
        at = pl.ds(pl.multiple_of(i * rows, 16), rows)
        return pltpu.make_async_copy(stage.at[i % 2], moe_ref.at[at], stage_sem.at[i % 2])

    def moe_block(i, _):
        at = pl.ds(pl.multiple_of(i * rows, 16), rows)

        @pl.when(i >= 2)
        def _():
            stage_copy(i - 2).wait()

        stage[i % 2] = (mm(lows[0, at, :], downs[0], NN) + mm(lows[3, at, :], downs[1], NN)).astype(
            bf16
        )
        stage_copy(i).start()
        return 0

    lax.fori_loop(0, a * (b - 1), back_others, 0)
    lax.fori_loop(0, 2, back_own, 0)
    if b > 2:
        lax.fori_loop(2, a, back_own, 0)
    total.along_b()
    tile = 256

    def weight_grads(e):
        def wide(k, _):
            at = pl.ds(pl.multiple_of(k * tile, tile), tile)
            x = xs[:, at]
            weights[2 * e, at, :] = mm(x, lows[3 * e + 1], TN).astype(bf16)
            weights[2 * e + 1, at, :] = mm(x, lows[3 * e + 2], TN).astype(bf16)
            downs[e, :, at] = (residual_scale * mm(lows[3 * e], gs[:, at], TN)).astype(bf16)
            return 0

        lax.fori_loop(0, width // tile, wide, 0)
        outs = (o_near_gate, o_near_up, o_near_down) if e == 0 else (o_far_gate, o_far_up, o_far_down)
        copies = [
            pltpu.make_async_copy(weights.at[2 * e], outs[0], store.at[3 * e]),
            pltpu.make_async_copy(weights.at[2 * e + 1], outs[1], store.at[3 * e + 1]),
            pltpu.make_async_copy(downs.at[e], outs[2], store.at[3 * e + 2]),
        ]
        for c in copies:
            c.start()
        return copies

    stored = []

    def moe_all():
        lax.fori_loop(0, n, moe_block, 0)

    total.flow(
        [
            (lambda: lax.fori_loop(2, a, back_own, 0)) if b == 2 else (lambda: None),
            moe_all,
            lambda: stored.extend(weight_grads(1)),
            lambda: stored.extend(weight_grads(0)),
        ]
    )
    line = total.a_line
    line.end(out_ref)
    gather.finish()
    stage_copy(n - 2).wait()
    stage_copy(n - 1).wait()
    for c in stored:
        c.wait()


def experts_call(rows_low, grads, picked, router, near, far, dp_size, collective_id):
    a, b = group_sizes(dp_size)
    n = a * b
    rows, width = rows_low.shape
    units = near[0].shape[1]
    hbm, vmem = pl.BlockSpec(memory_space=pl.ANY), pl.BlockSpec(memory_space=pltpu.VMEM)
    outs = [
        jax.ShapeDtypeStruct((n * rows, width), bf16),
        jax.ShapeDtypeStruct((rows, width + LANES), f32),
    ] + [jax.ShapeDtypeStruct(x.shape, bf16) for x in near + far]
    return pl.pallas_call(
        functools.partial(experts_kernel, a, b, rows, width),
        out_shape=outs,
        in_specs=[hbm, hbm, vmem, vmem] + [hbm] * 6,
        out_specs=[hbm, vmem] + [hbm] * 6,
        scratch_shapes=[
            pltpu.VMEM((n * rows, width), bf16),
            pltpu.VMEM((n * rows, width), bf16),
            pltpu.VMEM((4, width, units), bf16),
            pltpu.VMEM((2, units, width), bf16),
            pltpu.VMEM((6, n * rows, units), bf16),
            pltpu.VMEM((n * rows, width + LANES), bf16),
            pltpu.VMEM((n * rows, LANES), bf16),
            pltpu.VMEM((2, rows, width), bf16),
            pltpu.SemaphoreType.DMA((7,)),
            pltpu.SemaphoreType.DMA((n,)),
            pltpu.SemaphoreType.DMA((n, 4, PIECES)),
            pltpu.SemaphoreType.DMA((n, PIECES)),
            pltpu.SemaphoreType.DMA((2,)),
            pltpu.SemaphoreType.DMA((6,)),
        ]
        + GroupSum.scratch(a, b, rows, width + LANES),
        compiler_params=pltpu.CompilerParams(
            collective_id=collective_id, has_side_effects=True, vmem_limit_bytes=60 << 20
        ),
    )(rows_low, grads, picked, router, *near, *far)


def reduce_schedule(steps, groups):
    sums = [("sum", s) for s in range(steps)]
    backs = [("back", s) for s in reversed(range(steps))]
    lines = [[(g,) + e for e in sums + backs] for g in range(groups)]
    if groups == 1:
        return lines[0]
    first, second = lines
    order = first[: steps - 1]
    first = first[steps - 1 :]
    while first or second:
        if second:
            order.append(second.pop(0))
        if first:
            order.append(first.pop(0))
    return order


def reduce_kernel(orders, groups, x_ref, small_ref, out_ref, small_out, acc, got, small_got, load, send, recv, small_send, small_recv):
    k = len(orders[0])
    nparts = len(orders)
    size = x_ref.shape[0] // nparts
    loads = []
    for j in range(nparts):
        c = pltpu.make_async_copy(x_ref.at[pl.ds(j * size, size)], acc.at[pl.ds(j * size, size)], load.at[j])
        c.start()
        loads.append(c)
    greet(sorted(orders[0]))
    small_out[...] = small_ref[...]
    copies, back, small_copies = {}, {}, []
    where = [j * size for j in range(nparts)]
    per_group = nparts // groups

    def sum_step(j, step):
        count = size >> (step + 1)
        mask = orders[j][step]
        _, bit = peer_of(mask)
        keep = pl.multiple_of(where[j] + bit * count, 16)
        give = pl.multiple_of(where[j] + (1 - bit) * count, 16)
        if step == 0:
            loads[j].wait()
        else:
            copies[j, step - 1].wait_recv()
            p0 = j * size + (size - (size >> (step - 1)))
            add_rows(acc, give, acc, give, got, p0 + pl.multiple_of((1 - bit) * count, 16), count, bf16)
        g0 = j * size + (size - (size >> step))
        c = remote(acc.at[pl.ds(give, count)], got.at[pl.ds(g0, count)], send.at[j, step], recv.at[j, step], mask)
        c.start()
        copies[j, step] = c
        if step > 0:
            add_rows(acc, keep, acc, keep, got, p0 + pl.multiple_of(bit * count, 16), count, bf16)
        where[j] = keep

    def back_step(j, step):
        count = size >> (step + 1)
        mask = orders[j][step]
        _, bit = peer_of(mask)
        if step == k - 1:
            copies[j, step].wait_recv()
            p0 = j * size + (size - (size >> step))
            add_rows(out_ref, where[j], acc, where[j], got, p0, count, bf16)
        else:
            back[j, step + 1].wait_recv()
        here = where[j]
        c = remote(out_ref.at[pl.ds(here, count)], out_ref.at[pl.ds(here, count)], send.at[j, k + step], recv.at[j, k + step], mask)
        c.start()
        back[j, step] = c
        where[j] = pl.multiple_of(here - bit * count, 16)

    def small_step(step):
        if step > 0:
            small_copies[-1].wait_send()
            small_copies[-1].wait_recv()
            small_out[...] += small_got[step - 1]
        if step < k:
            c = remote(small_out, small_got.at[step], small_send.at[step], small_recv.at[step], orders[0][step])
            c.start()
            small_copies.append(c)

    small_done = 0
    for g, kind, step in reduce_schedule(k, groups):
        for j in range(g * per_group, (g + 1) * per_group):
            (sum_step if kind == "sum" else back_step)(j, step)
        if g == groups - 1 and small_done <= k:
            small_step(small_done)
            small_done += 1
    for j in range(nparts):
        back[j, 0].wait_recv()
    for c in copies.values():
        c.wait_send()
    for c in back.values():
        c.wait_send()


def all_reduce(x, small, masks, collective_id):
    inner, last = masks[:-1], masks[-1:]
    groups = 2 if x.shape[0] % (6 * 16 * 2 ** len(masks)) == 0 else 1
    nparts = 3 * groups
    orders = [rotated(inner, j) + last for j in range(nparts)]
    k = len(masks)
    vm = pl.BlockSpec(memory_space=pltpu.VMEM)
    return pl.pallas_call(
        functools.partial(reduce_kernel, orders, groups),
        out_shape=[jax.ShapeDtypeStruct(x.shape, bf16), jax.ShapeDtypeStruct(small.shape, f32)],
        in_specs=[pl.BlockSpec(memory_space=pl.ANY), vm],
        out_specs=[vm, vm],
        scratch_shapes=[
            pltpu.VMEM(x.shape, bf16),
            pltpu.VMEM(x.shape, bf16),
            pltpu.VMEM((k,) + small.shape, f32),
            pltpu.SemaphoreType.DMA((nparts,)),
            pltpu.SemaphoreType.DMA((nparts, 2 * k)),
            pltpu.SemaphoreType.DMA((nparts, 2 * k)),
            pltpu.SemaphoreType.DMA((k,)),
            pltpu.SemaphoreType.DMA((k,)),
        ],
        compiler_params=pltpu.CompilerParams(
            collective_id=collective_id, has_side_effects=True, vmem_limit_bytes=40 << 20
        ),
    )(x, small)


def place_kernel(dims, *refs):
    n = len(dims)
    mine, other, outs = refs[:n], refs[n : 2 * n], refs[2 * n : 3 * n]
    bufs, sems, out_sems = refs[3 * n : 4 * n], refs[4 * n], refs[4 * n + 1]
    me = lax.axis_index("tensor")

    def copy(i, which, src):
        size = src.shape[dims[i]]
        at = pl.multiple_of((me + which - 2 * which * me) * size, size)
        window = (slice(None),) * dims[i] + (pl.ds(at, size),)
        return pltpu.make_async_copy(src, bufs[i].at[window], sems.at[i, which])

    copies = [[copy(i, w, src) for w, src in enumerate((mine[i], other[i]))] for i in range(n)]
    for pair in copies:
        for c in pair:
            c.start()
    back = []
    for i, pair in enumerate(copies):
        for c in pair:
            c.wait()
        c = pltpu.make_async_copy(bufs[i], outs[i], out_sems.at[i])
        c.start()
        back.append(c)
    for c in back:
        c.wait()


def place(mine, other, dims):
    n = len(dims)
    shapes = [x.shape[:d] + (2 * x.shape[d],) + x.shape[d + 1 :] for x, d in zip(mine, dims)]
    return pl.pallas_call(
        functools.partial(place_kernel, dims),
        out_shape=[jax.ShapeDtypeStruct(s, x.dtype) for x, s in zip(mine, shapes)],
        in_specs=[pl.BlockSpec(memory_space=pl.ANY)] * (2 * n),
        out_specs=[pl.BlockSpec(memory_space=pl.ANY)] * n,
        scratch_shapes=[pltpu.VMEM(s, x.dtype) for x, s in zip(mine, shapes)]
        + [pltpu.SemaphoreType.DMA((n, 2)), pltpu.SemaphoreType.DMA((n,))],
        compiler_params=pltpu.CompilerParams(vmem_limit_bytes=24 << 20),
    )(*mine, *other)


def dot(a, b, spec):
    return jnp.einsum(spec, a, b, preferred_element_type=f32)


def per_device(
    hidden_in,
    attn_gain,
    w_query,
    key_weight,
    value_weight,
    w_output,
    moe_gain,
    w_router,
    w_gate,
    w_up,
    w_down,
    expert_ids,
    segment_ids,
    out_grad,
):
    tokens_here, model_width = hidden_in.shape
    head_size = HEAD_DIM
    dp_size = lax.axis_size("dp")
    tensor_size = lax.axis_size("tensor")
    experts = dp_size
    tensor_index = lax.axis_index("tensor")
    masks = bit_masks(dp_size)
    tensor_masks = bit_masks(tensor_size)
    tensor_down = tensor_masks[::-1]
    rows_here = tokens_here // tensor_size
    groups = [list(range(pair, dp_size, 2)) for pair in range(2)]

    def my_rows(x):
        return lax.dynamic_slice_in_dim(x, tensor_index * rows_here, rows_here, 0)

    block = w_gate.shape[2] // tensor_size

    def my_units(x, dim):
        return lax.dynamic_slice_in_dim(x, tensor_index * block, block, dim)

    def relative_gather(x, dim):
        for mask in tensor_masks:
            x = jnp.concatenate([x, swap(x, "tensor", mask)], dim)
        return x

    def relative_scatter(x, dim):
        for mask in reversed(tensor_masks):
            half = x.shape[dim] // 2
            keep = lax.slice_in_dim(x, 0, half, axis=dim)
            give = lax.slice_in_dim(x, half, 2 * half, axis=dim)
            x = keep.astype(f32) + swap(give.astype(bf16), "tensor", mask).astype(f32)
        return x

    far_set = [
        relative_gather(swap(my_units(w_gate[0], 1), "dp", 1), 1),
        relative_gather(swap(my_units(w_up[0], 1), "dp", 1), 1),
        relative_gather(swap(my_units(w_down[0], 0), "dp", 1), 0),
    ]
    grad_mine = my_rows(out_grad)
    grads = lax.all_gather(grad_mine, "dp", axis=0, tiled=True, axis_index_groups=groups)
    ids = lax.all_gather(
        my_rows(expert_ids), "dp", axis=0, tiled=True, axis_index_groups=groups
    )
    lanes = jnp.arange(LANES, dtype=jnp.int32)
    picked = jnp.any(ids[:, :, None] == lanes[None, None, :], axis=1).astype(bf16)
    router_wide = jnp.pad(w_router, ((0, 0), (0, LANES - experts)))

    inputs = hidden_in.astype(f32)
    scale_in = lax.rsqrt(jnp.mean(inputs * inputs, axis=-1, keepdims=True) + epsilon)
    normed_low = (inputs * scale_in * attn_gain).astype(bf16)
    segment = segment_ids[0]
    tables = rope_tables(segment, head_size)
    heads_flat, query_heads, key_heads, value_heads, log_sums = attend_forward(
        normed_low, segment, tables, w_query, key_weight, value_weight, head_size
    )
    attn_part = jnp.dot(heads_flat, w_output, preferred_element_type=f32)
    attn_total = scatter_sum(attn_part, "tensor", tensor_down, f32)

    inputs_mine = my_rows(hidden_in).astype(f32)
    scale_in_mine = my_rows(scale_in)
    middle = inputs_mine + residual_scale * attn_total
    scale_mid = lax.rsqrt(jnp.mean(middle * middle, axis=-1, keepdims=True) + epsilon)
    routed_low = (middle * scale_mid * moe_gain).astype(bf16)

    near_set = [w_gate[0], w_up[0], w_down[0]]
    moe_part, back, *expert_parts = experts_call(
        routed_low, grads, picked, router_wide, near_set, far_set, dp_size, 0
    )
    moe_total = group_sum(moe_part, dp_size, 1)

    dims = (1, 1, 0)
    near_mine = [
        scatter_sum(x, "tensor", tensor_down, bf16, d) for x, d in zip(expert_parts[:3], dims)
    ]
    returning = [
        swap(relative_scatter(x, d).astype(bf16), "dp", 1) for x, d in zip(expert_parts[3:], dims)
    ]

    logits = dot(routed_low, w_router, "td,de->te")
    chosen = jnp.any(
        my_rows(expert_ids)[:, :, None] == jnp.arange(experts, dtype=jnp.int32)[None, None, :],
        axis=1,
    )
    logits = jnp.where(chosen, logits, masked_score)
    raised = jnp.where(chosen, jnp.exp(logits - jnp.max(logits, axis=1, keepdims=True)), 0.0)
    gate_weights = raised / jnp.sum(raised, axis=1, keepdims=True)
    routed_grad = back[:, :model_width]
    gate_deriv = (
        back[:, model_width : model_width + experts]
        + back[:, model_width + LOW_AT : model_width + LOW_AT + experts]
    )
    chosen_grad = gate_weights * (
        gate_deriv - jnp.sum(gate_weights * gate_deriv, axis=1, keepdims=True)
    )
    logit_grad = chosen_grad.astype(bf16)
    router_part = dot(logit_grad, routed_low, "te,td->ed")
    routed_grad = routed_grad + dot(logit_grad, w_router, "te,de->td")
    gained = moe_gain * routed_grad
    moe_gain_part = jnp.sum(routed_grad * middle * scale_mid, axis=0)
    grad_top = grad_mine.astype(f32)
    middle_grad = (
        grad_top
        + scale_mid * gained
        - middle
        * (scale_mid * scale_mid * scale_mid)
        * jnp.mean(middle * gained, axis=-1, keepdims=True)
    )
    branch_low = gather_blocks(
        (residual_scale * middle_grad).astype(bf16), "tensor", tensor_down
    )
    heads_width = heads_flat.shape[1]
    w_output_part = [
        dot(heads_flat, branch_low[:, i : i + heads_width], "tc,td->cd")
        for i in range(0, model_width, heads_width)
    ]
    heads_grad = dot(branch_low, w_output, "td,cd->tc").astype(bf16)
    query_low, key_low, value_low = attend_backward(
        query_heads, key_heads, value_heads, log_sums, heads_grad, segment, tables
    )
    width_q, width_k = query_low.shape[1], key_low.shape[1]
    qkv_low = jnp.concatenate([query_low, key_low, value_low], axis=1)
    qkv_width = qkv_low.shape[1]
    attention_part = jnp.concatenate(
        [dot(normed_low, qkv_low, "td,tc->dc"), jnp.concatenate(w_output_part, 0)], 1
    ).astype(bf16)
    qkv_weight = jnp.concatenate([w_query, key_weight, value_weight], axis=1)
    normed_part = dot(qkv_low, qkv_weight, "tc,dc->td")
    normed_grad = scatter_sum(normed_part, "tensor", tensor_down, f32)
    gained_in = attn_gain * normed_grad
    attn_gain_part = jnp.sum(normed_grad * inputs_mine * scale_in_mine, axis=0)
    input_mine = (
        middle_grad
        + scale_in_mine * gained_in
        - inputs_mine
        * (scale_in_mine * scale_in_mine * scale_in_mine)
        * jnp.mean(inputs_mine * gained_in, axis=-1, keepdims=True)
    )
    input_grad = gather_blocks(input_mine, "tensor", tensor_down)
    block_mine = (middle + residual_scale * moe_total).astype(bf16)
    block_out = gather_blocks(block_mine, "tensor", tensor_down)

    small = jnp.concatenate([router_part, moe_gain_part[None], attn_gain_part[None]], 0)
    small = jnp.pad(small, ((0, -small.shape[0] % 8), (0, 0)))
    for mask in tensor_masks:
        small = small + swap(small, "tensor", mask)
    attention_grad, small = all_reduce(attention_part, small, masks, 2)
    attention_grad, returning = lax.optimization_barrier((attention_grad, returning))
    expert_mine = [mine + away.astype(f32) for mine, away in zip(near_mine, returning)]
    if tensor_size == 2:
        expert_grads = place(expert_mine, [swap(x, "tensor", 1) for x in expert_mine], dims)
    else:
        expert_grads = [
            gather_blocks(x, "tensor", tensor_down, dim) for x, dim in zip(expert_mine, dims)
        ]
    attention_grad = attention_grad.astype(f32)
    w_output_grad = jnp.concatenate(
        [
            attention_grad[i : i + heads_width, qkv_width:]
            for i in range(0, model_width, heads_width)
        ],
        1,
    )
    return (
        block_out,
        input_grad,
        small[experts + 1],
        attention_grad[:, :width_q],
        attention_grad[:, width_q : width_q + width_k],
        attention_grad[:, width_q + width_k : qkv_width],
        w_output_grad,
        small[experts],
        small[:experts].T,
        expert_grads[0][None],
        expert_grads[1][None],
        expert_grads[2][None],
    )


def solution(mesh):
    placed = (
        P("dp", None),
        P(),
        P(None, "tensor"),
        P(None, "tensor"),
        P(None, "tensor"),
        P("tensor", None),
        P(),
        P(),
        P("dp", None, None),
        P("dp", None, None),
        P("dp", None, None),
        P("dp", None),
        P("dp", None),
        P("dp", None),
    )
    return jax.shard_map(
        per_device,
        mesh=mesh,
        in_specs=placed,
        out_specs=(
            P("dp", None),
            P("dp", None),
            P(),
            P(None, "tensor"),
            P(None, "tensor"),
            P(None, "tensor"),
            P("tensor", None),
            P(),
            P(),
            P("dp", None, None),
            P("dp", None, None),
            P("dp", None, None),
        ),
        check_vma=False,
    )
```

time: 982 us -> 668 us (0.68)
  waiting for transfers between devices: 476 us -> 5.34 us
  Pallas kernels: 0 us -> 428 us
  starting transfers between devices: 156 us -> 12.8 us
  matrix products: 180 us -> 46.1 us
  local copies, waits for them, and re-layouts: 78.8 us -> 43.3 us
  blocking collectives: 0 us -> 33.3 us
  between operations: 4.34 us -> 16 us
    ppermute x123 -> x24, waiting for transfers between devices: 476 us -> 0.91 us  [swap(): lax.ppermute(x, axis, [(i, i ^ mask) for i in range(lax.axis_size(axis))])]
    pallas_call x0 -> x4, Pallas kernels: none -> 428 us  [the longest x1 185 us: experts_call(): pl.pallas_call(functools.partial(experts_kernel, a, b, rows, width), out_...]
    ppermute x123 -> x24, starting transfers between devices: 156 us -> 12.7 us  [swap(): lax.ppermute(x, axis, [(i, i ^ mask) for i in range(lax.axis_size(axis))])]
    dot_general x25 -> x8, matrix products: 147 us -> 15 us  [dot(): return jnp.einsum(spec, a, b, preferred_element_type=f32)]
    all_gather x0 -> x1, blocking collectives: none -> 33.3 us  [per_device(): lax.all_gather(my_rows(expert_ids), 'dp', axis=0, tiled=True, axis_index_...]
    unnamed x244 -> x157, local copies, waits for them, and re-layouts: 43.9 us -> 19.6 us
    select_n x29 -> x3, other arithmetic: 24.4 us -> 6.17 us  [join_by_bit(): jnp.where(bit_of(axis, mask) == 0, jnp.concatenate([mine, other], dim), j...]
    reduce_or x1 -> x2, other arithmetic: 0.05 us -> 12.2 us  [the longest x1 12.2 us: per_device(): jnp.any(ids[:, :, None] == lanes[None, None, :], axis=1).astype(bf16)]
  transfers between devices with their start and end apart: 123 -> 25, of which waited for: 66 -> 2; matrix products, arithmetic and copies ran while one was open for 23% -> 21% of each run, Pallas kernels for 0% -> 24%
where the time goes in v3:
time: 668 us; the launch traced here: 660 us
  Pallas kernels  428 us (64%)
  other arithmetic  74.7 us (11%)
  matrix products  46.1 us (7%)
  local copies, waits for them, and re-layouts  43.3 us (6%)
  blocking collectives  33.3 us (5%)
  between operations  16 us (2%)
  starting transfers between devices  12.8 us (2%)
    pallas_call x1, Pallas kernels, experts_call(): pl.pallas_call(functools.partial(experts_kernel, a, b, rows, width), out_...  185 us
    pallas_call x1, Pallas kernels, all_reduce(): pl.pallas_call(functools.partial(reduce_kernel, orders, groups), out_shap...  155 us
    pallas_call x1, Pallas kernels, group_sum(): pl.pallas_call(functools.partial(sum_kernel, a, b, rows), out_shape=jax.S...  83.4 us
    all_gather x1, blocking collectives, per_device(): lax.all_gather(my_rows(expert_ids), 'dp', axis=0, tiled=True, axis_index_...  33.3 us
    unnamed x157, local copies, waits for them, and re-layouts  19.6 us
    dot_general x8, matrix products, dot(): return jnp.einsum(spec, a, b, preferred_element_type=f32)  15 us
  transfers between devices with their start and end apart: 25, of which 2 were waited for; matrix products, arithmetic and copies ran while one was open for 21% of the time, Pallas kernels for 24%

profile of v3, /device:TPU:0, one launch (start us, length us, event | category | flops | bytes accessed | tf_op | source)
XLA Modules:
  0.0 659.9 jit_solution(9894717650614900998)
XLA Ops:
  7.3 2.2 constant_dynamic-slice_fusion.2
  11.3 1.9 fusion.17
  13.9 2.1 fusion.57
  16.1 1.6 fusion.55
  18.8 1.5 convolution_convert_fusion.4
  20.3 2.1 fusion.10
  22.4 2.6 fusion.3
  25.0 2.0 copy-done.4
  27.1 5.0 fusion.25
  32.2 1.4 fusion.63
  33.7 1.3 constant_dynamic-slice_fusion.3
  37.2 2.9 collective-permute-start.1
  42.2 1.8 collective-permute-start.5
  44.0 33.3 %all_gather.7 = s32[2048,8]{0,1:T(8,128)} all-gather(s32[256,8]{0,1:T(8,128)S(1)} %constant_dynamic-slice_fusion.1), channel_id=1, replica_groups={{0,4,8,12,16,20,24,28},{2,6,10,14,18,22,26,30},{1,5,9,13,17,21,25,29},{..., dimensions={0}, use_global_device_ids=true | all-gather | bytes 73728 | tf_op jit(solution)/shard_map/all_gather | solution.py:992
  77.3 1.2 copy.59
  78.5 12.2 %fusion.5 = pred[2048,128]{1,0:T(8,128)(4,1)} fusion(s32[2048,8]{1,0:T(8,128)S(1)} %copy.59), kind=kLoop, calls=%fused_computation.12 | loop fusion | flops 3932160 | bytes 327680 | tf_op jit(solution)/shard_map/reduce_or | solution.py:996
  91.4 1.8 convert_element_type.162.picked_ref
  93.3 1.0 copy.60
  97.1 2.5 multiply_reduce_fusion.2
  101.7 2.4 pad_maximum_fusion.1.far_gate
  104.1 2.4 pad_maximum_fusion.2.far_up
  106.5 2.4 pad_maximum_fusion.3.far_down
  108.9 4.4 all-gather.2.cloned.1.call-done.grads_ref
  113.3 184.7 %shard_map.229 = (bf16[2048,1536]{1,0:T(8,128)(2,1)}, f32[256,1664]{1,0:T(8,128)}, bf16[1536,512]{1,0:T(8,128)(2,1)}, bf16[1536,512]{1,0:T(8,128)(2,1)}, bf16[51...) custom-call(bf16[256,1536]{1,0:T(8,128)(2,1)} %copy-done.17, ...), custom_call_target="tpu_custom_call" | custom-call | tf_op jit(solution)/shard_map/pallas_call | solution.py:742
  298.0 1.3 multiply_reduce_fusion.3
  299.3 1.2 multiply_convert_fusion.2
  300.5 2.0 multiply_reduce_fusion
  302.6 2.8 copy-done.3
  305.4 83.4 %shard_map.230 = f32[256,1536]{1,0:T(8,128)S(1)} custom-call(bf16[2048,1536]{1,0:T(8,128)(2,1)S(1)} %copy-done.3), custom_call_target="tpu_custom_call" | custom-call | tf_op jit(solution)/shard_map/pallas_call | solution.py:541
  388.8 2.1 multiply_convert_fusion
  393.5 1.1 slice.122
  395.5 1.0 dynamic-slice_convert_fusion
  396.5 1.6 copy-done.35
  400.7 1.1 fusion.64
  404.4 1.1 copy-done.32
  405.6 2.3 convolution_convert_fusion.3
  407.9 1.5 copy.64
  409.4 11.1 %fusion = (f32[4,3,512]{2,1,0:T(4,128)S(1)}, f32[4,512,512,3]{2,1,3,0:T(8,128)}) fusion(f32[4,3,512]{2,1,0:T(4,128)S(1)} %copy-done.53, f32[4,512,512,3]{2,1,3,0:T(8,128)} %copy-done.4, pred[512,512]{0,1:T(8,128)(4,1)S(1)} %copy-done.20, bf16[512,4,64,1]{0,2,3,1:T(8,128)(2,1)S(1)} %bitcast.145, bf16[512,4,3,64]{0,3,2,1:T(8,128)(2,1)S(1)} %bitcast.129), kind=kOutput, calls=%fused_computation.2 | convolution fusion | flops 418375680 | bytes 26525696 | tf_op jit(solution)/shard_map/qhgd,khd->hgqk/dot_general | solution.py:92
  420.6 1.4 slice-done.2
  422.0 6.9 %fusion.2 = bf16[4,3,512,512]{2,3,1,0:T(8,128)(2,1)S(1)} fusion(f32[4,512,512,3]{2,1,3,0:T(8,128)} %get-tuple-element.81, f32[4,3,512]{2,1,0:T(4,128)S(1)} %get-tuple-element.80, f32[4,3,512]{2,1,0:T(4,128)S(1)} %copy-done.53, f32[4,512,512,3]{2,1,3,0:T(8,128)S(1)} %bitcast.127, pred[512,512]{0,1:T(8,128)(4,1)S(1)} %copy-done.20), kind=kLoop, calls=%fused_computation.4 | loop fusion | flops 18874368 | bytes 31768576 | tf_op jit(solution)/shard_map/convert_element_type | solution.py:96
  428.9 1.2 convolution_multiply_fusion
  430.2 2.0 fusion.30
  432.2 3.1 fusion.31
  437.6 2.2 fusion.11
  439.9 1.5 copy-done.25
  442.4 2.2 add_convert_fusion.2
  444.6 2.1 collective-permute-start.13
  446.7 2.2 add_convert_fusion.1
  450.3 2.2 add_convert_fusion
  452.5 1.5 collective-permute-start.17
  454.0 3.6 maximum_select_fusion.1
  457.6 1.8 convolution_convert_fusion.2
  459.4 4.3 convolution_convert_fusion
  463.8 6.1 maximum_maximum_fusion.x_ref
  469.9 2.5 fusion.24
  474.3 155.4 %shard_map.231 = (bf16[1536,2048]{1,0:T(8,128)(2,1)S(1)}, f32[24,1536]{1,0:T(8,128)S(1)}) custom-call(bf16[1536,2048]{1,0:T(8,128)(2,1)S(1)} %copy-done.2, f32[24,1536]{1,0:T(8,128)S(1)} %fusion.53.small_ref), custom_call_target="tpu_custom_call" | custom-call | tf_op jit(solution)/shard_map/pallas_call | solution.py:870
  630.4 1.8 convert_add_fusion.1.refs_2_
  632.7 1.7 convert_add_fusion.2.refs_1_
  634.6 1.5 convert_add_fusion.3.refs_0_
  637.0 2.9 pad_maximum_fusion
  639.9 2.7 slice.140
  643.9 2.0 fusion.61
  645.8 2.0 maximum_select_fusion
  647.8 5.0 shard_map.232
  (248 shorter events, 32.0 us)
Async XLA Ops:
  7.2 25.0 %copy-start = (bf16[768,1536]{1,0:T(8,128)(2,1)S(1)}, bf16[768,1536]{1,0:T(8,128)(2,1)}, u32[]{:S(2)}) copy-start(bf16[768,1536]{1,0:T(8,128)(2,1)} %param.19) | copy-start | bytes 7077892
  7.2 106.1 %all-gather.2.cloned.1.call-start = ((), (), s32[]{:S(2)}) async-start(), calls=%async_computation | async-start | bytes 7077888 | tf_op jit(solution)/shard_map/all_gather | solution.py:991
  9.5 4.4 copy-start.61
  13.2 4.7 copy-start.65
  13.9 11.1 %copy-start.19 = (pred[512,512]{0,1:T(8,128)(4,1)}, pred[512,512]{0,1:T(8,128)(4,1)S(1)}, u32[]{:S(2)}) copy-start(pred[512,512]{0,1:T(8,128)(4,1)S(1)} %fusion.34) | copy-start | bytes 786436
  16.1 4.2 copy-start.49
  16.1 4.2 copy-start.51
  22.4 4.6 copy-start.4
  22.4 4.7 copy-start.56
  25.0 7.2 %copy-start.58 = (f32[4,3,512]{2,1,0:T(4,128)}, f32[4,3,512]{2,1,0:T(4,128)S(1)}, u32[]{:S(2)}) copy-start(f32[4,3,512]{2,1,0:T(4,128)S(1)} %fusion.3) | copy-start | bytes 73732
  35.8 4.3 copy-start.23
  35.8 5.4 copy-start.24
  35.8 61.2 %collective-permute-start = (f32[256,1536]{1,0:T(8,128)}, f32[256,1536]{1,0:T(8,128)}, u32[]{:S(2)}, u32[]{:S(2)}) collective-permute-start(f32[256,1536]{1,0:T(8,128)} %constant_dynamic-slice_fusion.3), channel_id=1, source_target_pairs={{0,1},{1,0},{2,3},{3,2},{4,5},{5,4},{6,7},{7,6},{8,9},{9,8},{10,11... | collective-permute-start | bytes 4718600 | tf_op jit(solution)/shard_map/ppermute | solution.py:124
  37.2 6.8 %copy-start.68 = (s32[512,8]{0,1:T(8,128)S(1)}, s32[512,8]{0,1:T(8,128)}, u32[]{:S(2)}) copy-start(s32[512,8]{0,1:T(8,128)} %param.25) | copy-start | bytes 49156
  37.2 59.2 %collective-permute-start.1 = (bf16[1536,256]{1,0:T(8,128)(2,1)}, bf16[1536,256]{1,0:T(8,128)(2,1)}, u32[]{:S(2)}, u32[]{:S(2)}) collective-permute-start(bf16[1536,256]{1,0:T(8,128)(2,1)} %dynamic-slice_bitcast_fusion.2), channel_id=1, source_target_pairs={{0,2},{2,0},{4,6},{6,4},{8,10},{10,8},{12,14},{14,12},{16,18},{18,... | collective-permute-start | bytes 2359304 | tf_op jit(solution)/shard_map/ppermute | solution.py:124
  41.1 55.4 %collective-permute-start.3 = (bf16[1536,256]{1,0:T(8,128)(2,1)}, bf16[1536,256]{1,0:T(8,128)(2,1)}, u32[]{:S(2)}, u32[]{:S(2)}) collective-permute-start(bf16[1536,256]{1,0:T(8,128)(2,1)} %dynamic-slice_bitcast_fusion.1), channel_id=1, source_target_pairs={{0,2},{2,0},{4,6},{6,4},{8,10},{10,8},{12,14},{14,12},{16,18},{18,... | collective-permute-start | bytes 2359304 | tf_op jit(solution)/shard_map/ppermute | solution.py:124
  42.2 54.8 %collective-permute-start.5 = (bf16[256,1536]{1,0:T(8,128)(2,1)}, bf16[256,1536]{1,0:T(8,128)(2,1)}, u32[]{:S(2)}, u32[]{:S(2)}) collective-permute-start(bf16[256,1536]{1,0:T(8,128)(2,1)} %dynamic-slice_bitcast_fusion), channel_id=1, source_target_pairs={{0,2},{2,0},{4,6},{6,4},{8,10},{10,8},{12,14},{14,12},{16,18},{18,... | collective-permute-start | bytes 2359304 | tf_op jit(solution)/shard_map/ppermute | solution.py:124
  90.6 5.2 copy-start.57
  90.6 5.2 copy-start.59
  91.4 4.4 copy-start.63
  96.5 3.7 copy-start.60
  96.5 5.2 collective-permute-start.2
  96.5 7.6 %collective-permute-start.4 = (bf16[1536,256]{1,0:T(8,128)(2,1)}, bf16[1536,256]{1,0:T(8,128)(2,1)S(1)}, u32[]{:S(2)}, u32[]{:S(2)}) collective-permute-start(bf16[1536,256]{1,0:T(8,128)(2,1)} %collective-permute-done.3), channel_id=1, source_target_pairs={{0,1},{1,0},{2,3},{3,2},{4,5},{5,4},{6,7},{7,6},{8,9},{9,8},{10,11... | collective-permute-start | bytes 2359304 | tf_op jit(solution)/shard_map/ppermute | solution.py:124
  97.0 9.5 %collective-permute-start.6 = (bf16[256,1536]{1,0:T(8,128)(2,1)}, bf16[256,1536]{1,0:T(8,128)(2,1)S(1)}, u32[]{:S(2)}, u32[]{:S(2)}) collective-permute-start(bf16[256,1536]{1,0:T(8,128)(2,1)} %collective-permute-done.5), channel_id=1, source_target_pairs={{0,1},{1,0},{2,3},{3,2},{4,5},{5,4},{6,7},{7,6},{8,9},{9,8},{10,11... | collective-permute-start | bytes 2359304 | tf_op jit(solution)/shard_map/ppermute | solution.py:124
  113.3 187.2 %copy-start.6 = (f32[256,1536]{1,0:T(8,128)S(1)}, f32[256,1536]{1,0:T(8,128)}, u32[]{:S(2)}) copy-start(f32[256,1536]{1,0:T(8,128)} %copy-done.5) | copy-start | bytes 4718596
  302.6 2.8 copy-start.3
  305.4 83.4 %copy-start.16 = (f32[256,1664]{1,0:T(8,128)S(1)}, f32[256,1664]{1,0:T(8,128)}, u32[]{:S(2)}) copy-start(f32[256,1664]{1,0:T(8,128)} %get-tuple-element.30) | copy-start | bytes 5111812
  305.4 83.4 %copy-start.41 = (bf16[512,1536]{1,0:T(8,128)(2,1)S(1)}, bf16[512,1536]{1,0:T(8,128)(2,1)}, u32[]{:S(2)}) copy-start(bf16[512,1536]{1,0:T(8,128)(2,1)} %param.27) | copy-start | bytes 4718596
  305.4 83.4 %copy-start.69 = (f32[256]{0:T(256)S(1)}, f32[256]{0:T(256)}, u32[]{:S(2)}) copy-start(f32[256]{0:T(256)} %get-tuple-element.73) | copy-start | bytes 3076
  390.9 12.9 %collective-permute-start.8 = (bf16[256,1536]{1,0:T(8,128)(2,1)S(1)}, bf16[256,1536]{1,0:T(8,128)(2,1)S(1)}, u32[]{:S(2)}, u32[]{:S(2)}) collective-permute-start(bf16[256,1536]{1,0:T(8,128)(2,1)S(1)} %get-tuple-element.53), channel_id=1, source_target_pairs={{0,1},{1,0},{2,3},{3,2},{4,5},{5,4},{6,7},{7,6},{8,9},{9,8},{10,11... | collective-permute-start | bytes 2359304 | tf_op jit(solution)/shard_map/ppermute | solution.py:124
  391.8 49.6 %collective-permute-start.12 = (bf16[1536,256]{1,0:T(8,128)(2,1)}, bf16[1536,256]{1,0:T(8,128)(2,1)}, u32[]{:S(2)}, u32[]{:S(2)}) collective-permute-start(bf16[1536,256]{1,0:T(8,128)(2,1)} %slice.118), channel_id=1, source_target_pairs={{0,1},{1,0},{2,3},{3,2},{4,5},{5,4},{6,7},{7,6},{8,9},{9,8},{10,11... | collective-permute-start | bytes 2359304 | tf_op jit(solution)/shard_map/ppermute | solution.py:124
  393.5 51.1 %collective-permute-start.14 = (bf16[1536,256]{1,0:T(8,128)(2,1)}, bf16[1536,256]{1,0:T(8,128)(2,1)}, u32[]{:S(2)}, u32[]{:S(2)}) collective-permute-start(bf16[1536,256]{1,0:T(8,128)(2,1)} %slice.120), channel_id=1, source_target_pairs={{0,1},{1,0},{2,3},{3,2},{4,5},{5,4},{6,7},{7,6},{8,9},{9,8},{10,11... | collective-permute-start | bytes 2359304 | tf_op jit(solution)/shard_map/ppermute | solution.py:124
  394.6 55.2 %collective-permute-start.16 = (bf16[256,1536]{1,0:T(8,128)(2,1)}, bf16[256,1536]{1,0:T(8,128)(2,1)}, u32[]{:S(2)}, u32[]{:S(2)}) collective-permute-start(bf16[256,1536]{1,0:T(8,128)(2,1)} %slice.122), channel_id=1, source_target_pairs={{0,1},{1,0},{2,3},{3,2},{4,5},{5,4},{6,7},{7,6},{8,9},{9,8},{10,11... | collective-permute-start | bytes 2359304 | tf_op jit(solution)/shard_map/ppermute | solution.py:124
  395.5 3.0 copy-start.14
  396.5 233.9 %collective-permute-start.20 = (bf16[256,1536]{1,0:T(8,128)(2,1)}, bf16[256,1536]{1,0:T(8,128)(2,1)}, u32[]{:S(2)}, u32[]{:S(2)}) collective-permute-start(bf16[256,1536]{1,0:T(8,128)(2,1)} %dynamic-slice_convert_fusion), channel_id=1, source_target_pairs={{0,1},{1,0},{2,3},{3,2},{4,5},{5,4},{6,7},{7,6},{8,9},{9,8},{10,11... | collective-permute-start | bytes 2359304 | tf_op jit(solution)/shard_map/ppermute | solution.py:124
  398.5 3.3 copy-start.12
  400.7 3.1 copy-start.10
  403.8 48.7 %collective-permute-start.7 = (bf16[256,1536]{1,0:T(8,128)(2,1)}, bf16[256,1536]{1,0:T(8,128)(2,1)}, u32[]{:S(2)}, u32[]{:S(2)}) collective-permute-start(bf16[256,1536]{1,0:T(8,128)(2,1)} %get-tuple-element.65), channel_id=1, source_target_pairs={{0,1},{1,0},{2,3},{3,2},{4,5},{5,4},{6,7},{7,6},{8,9},{9,8},{10,11... | collective-permute-start | bytes 2359304 | tf_op jit(solution)/shard_map/ppermute | solution.py:124
  409.4 11.2 %slice-start = ((s8[12582912]{0:T(1024)(128)(4,1)}), s8[4194304]{0:T(1024)(128)(4,1)S(1)}, s32[]{:S(2)}) async-start(s8[12582912]{0:T(1024)(128)(4,1)} %bitcast.126), calls=%async_computation.1 | async-start | bytes 8388608
  409.4 11.1 %slice-start.1 = ((s8[12582912]{0:T(1024)(128)(4,1)}), s8[4194304]{0:T(1024)(128)(4,1)S(1)}, s32[]{:S(2)}) async-start(s8[12582912]{0:T(1024)(128)(4,1)} %bitcast.126), calls=%async_computation.2 | async-start | bytes 8388608
  409.4 12.6 %slice-start.2 = ((s8[12582912]{0:T(1024)(128)(4,1)}), s8[4194304]{0:T(1024)(128)(4,1)S(1)}, s32[]{:S(2)}) async-start(s8[12582912]{0:T(1024)(128)(4,1)} %bitcast.126), calls=%async_computation.3 | async-start | bytes 8388608
  422.0 6.9 %copy-start.50 = (bf16[512,4,32]{0,2,1:T(8,128)(2,1)S(1)}, bf16[512,4,32]{0,2,1:T(8,128)(2,1)}, u32[]{:S(2)}) copy-start(bf16[512,4,32]{0,2,1:T(8,128)(2,1)} %copy-done.49) | copy-start | bytes 393220
  422.0 6.9 %copy-start.52 = (bf16[512,4,32]{0,2,1:T(8,128)(2,1)S(1)}, bf16[512,4,32]{0,2,1:T(8,128)(2,1)}, u32[]{:S(2)}) copy-start(bf16[512,4,32]{0,2,1:T(8,128)(2,1)} %copy-done.51) | copy-start | bytes 393220
  441.5 5.2 copy-start.29
  441.5 28.4 %collective-permute-start.9 = (f32[256,1536]{1,0:T(8,128)S(1)}, f32[256,1536]{1,0:T(8,128)}, u32[]{:S(2)}, u32[]{:S(2)}) collective-permute-start(f32[256,1536]{1,0:T(8,128)S(1)} %constant_dynamic-slice_fusion), channel_id=1, source_target_pairs={{0,1},{1,0},{2,3},{3,2},{4,5},{5,4},{6,7},{7,6},{8,9},{9,8},{10,11... | collective-permute-start | bytes 4718600 | tf_op jit(solution)/shard_map/ppermute | solution.py:124
  444.6 4.3 copy-start.33
  444.6 4.3 copy-start.45
  444.6 185.1 %collective-permute-start.13 = (bf16[1536,256]{1,0:T(8,128)(2,1)}, bf16[1536,256]{1,0:T(8,128)(2,1)}, u32[]{:S(2)}, u32[]{:S(2)}) collective-permute-start(bf16[1536,256]{1,0:T(8,128)(2,1)} %add_convert_fusion.2), channel_id=1, source_target_pairs={{0,2},{2,0},{4,6},{6,4},{8,10},{10,8},{12,14},{14,12},{16,18},{18,... | collective-permute-start | bytes 2359304 | tf_op jit(solution)/shard_map/ppermute | solution.py:124
  449.7 180.1 %collective-permute-start.15 = (bf16[1536,256]{1,0:T(8,128)(2,1)}, bf16[1536,256]{1,0:T(8,128)(2,1)}, u32[]{:S(2)}, u32[]{:S(2)}) collective-permute-start(bf16[1536,256]{1,0:T(8,128)(2,1)} %add_convert_fusion.1), channel_id=1, source_target_pairs={{0,2},{2,0},{4,6},{6,4},{8,10},{10,8},{12,14},{14,12},{16,18},{18,... | collective-permute-start | bytes 2359304 | tf_op jit(solution)/shard_map/ppermute | solution.py:124
  452.5 177.8 %collective-permute-start.17 = (bf16[256,1536]{1,0:T(8,128)(2,1)}, bf16[256,1536]{1,0:T(8,128)(2,1)}, u32[]{:S(2)}, u32[]{:S(2)}) collective-permute-start(bf16[256,1536]{1,0:T(8,128)(2,1)} %add_convert_fusion), channel_id=1, source_target_pairs={{0,2},{2,0},{4,6},{6,4},{8,10},{10,8},{12,14},{14,12},{16,18},{18,... | collective-permute-start | bytes 2359304 | tf_op jit(solution)/shard_map/ppermute | solution.py:124
  463.8 6.1 copy-start.64
  469.9 2.7 copy-start.21
  469.9 2.7 copy-start.67
  469.9 4.4 copy-start.2
  472.5 1.4 collective-permute-start.11
  474.3 158.0 %collective-permute-start.19 = (bf16[1536,256]{1,0:T(8,128)(2,1)S(1)}, bf16[1536,256]{1,0:T(8,128)(2,1)S(1)}, u32[]{:S(2)}, u32[]{:S(2)}) collective-permute-start(bf16[1536,256]{1,0:T(8,128)(2,1)S(1)} %copy-done.47), channel_id=1, source_target_pairs={{0,1},{1,0},{2,3},{3,2},{4,5},{5,4},{6,7},{7,6},{8,9},{9,8},{10,11... | collective-permute-start | bytes 2359304 | tf_op jit(solution)/shard_map/ppermute | solution.py:124
  474.3 155.4 %copy-start.46 = (bf16[1536,256]{1,0:T(8,128)(2,1)S(1)}, bf16[1536,256]{1,0:T(8,128)(2,1)}, u32[]{:S(2)}) copy-start(bf16[1536,256]{1,0:T(8,128)(2,1)} %dynamic-slice_convert_fusion.2) | copy-start | bytes 2359300
  474.3 156.0 %copy-start.15 = (f32[512,1536]{1,0:T(8,128)S(1)}, f32[512,1536]{1,0:T(8,128)}, u32[]{:S(2)}) copy-start(f32[512,1536]{1,0:T(8,128)} %copy-done.14) | copy-start | bytes 9437188
  629.8 4.8 collective-permute-start.18
  629.9 16.0 %collective-permute-start.10 = (f32[256,1536]{1,0:T(8,128)S(1)}, f32[256,1536]{1,0:T(8,128)S(1)}, u32[]{:S(2)}, u32[]{:S(2)}) collective-permute-start(f32[256,1536]{1,0:T(8,128)S(1)} %fusion.21), channel_id=1, source_target_pairs={{0,1},{1,0},{2,3},{3,2},{4,5},{5,4},{6,7},{7,6},{8,9},{9,8},{10,11... | collective-permute-start | bytes 4718600 | tf_op jit(solution)/shard_map/ppermute | solution.py:124
  632.2 15.6 %collective-permute-start.23 = (f32[256,1536]{1,0:T(8,128)S(1)}, f32[256,1536]{1,0:T(8,128)S(1)}, u32[]{:S(2)}, u32[]{:S(2)}) collective-permute-start(f32[256,1536]{1,0:T(8,128)S(1)} %convert_add_fusion.1.refs_2_), channel_id=1, source_target_pairs={{0,1},{1,0},{2,3},{3,2},{4,5},{5,4},{6,7},{7,6},{8,9},{9,8},{10,11... | collective-permute-start | bytes 4718600 | tf_op jit(solution)/shard_map/ppermute | solution.py:124
  634.4 13.4 %collective-permute-start.22 = (f32[1536,256]{1,0:T(8,128)S(1)}, f32[1536,256]{1,0:T(8,128)S(1)}, u32[]{:S(2)}, u32[]{:S(2)}) collective-permute-start(f32[1536,256]{1,0:T(8,128)S(1)} %convert_add_fusion.2.refs_1_), channel_id=1, source_target_pairs={{0,1},{1,0},{2,3},{3,2},{4,5},{5,4},{6,7},{7,6},{8,9},{9,8},{10,11... | collective-permute-start | bytes 4718600 | tf_op jit(solution)/shard_map/ppermute | solution.py:124
  636.0 11.8 %collective-permute-start.21 = (f32[1536,256]{1,0:T(8,128)S(1)}, f32[1536,256]{1,0:T(8,128)S(1)}, u32[]{:S(2)}, u32[]{:S(2)}) collective-permute-start(f32[1536,256]{1,0:T(8,128)S(1)} %convert_add_fusion.3.refs_0_), channel_id=1, source_target_pairs={{0,1},{1,0},{2,3},{3,2},{4,5},{5,4},{6,7},{7,6},{8,9},{9,8},{10,11... | collective-permute-start | bytes 4718600 | tf_op jit(solution)/shard_map/ppermute | solution.py:124
  647.8 5.0 copy-start.1
  (39 other events, 68.1 us)
Sparse Core Ops, SparseCore 0:
  10.8 102.4 all-gather.1

commit v4 on v3

--- a/solution.py
+++ b/solution.py
@@ -511,46 +511,6 @@
         ]
 
 
-def sum_kernel(a, b, rows, x_ref, out_ref, part, load, *scratch):
-    spot = Spot(a, b)
-    n = spot.n
-    total = GroupSum(spot, part, rows, *scratch)
-
-    def loading(A, B):
-        at = pl.ds(pl.multiple_of((A * b + B) * rows, 16), rows)
-        return pltpu.make_async_copy(x_ref.at[at], part.at[at], load.at[A * b + B])
-
-    order = sorted(range(a), key=lambda c: (min(c, a - 1 - c), -c))
-    for A in order:
-        for B in range(b):
-            loading(A, B).start()
-    spot.greet()
-    for A in order:
-        for B in range(b):
-            loading(A, B).wait()
-            total.ready(A, B)
-    total.along_b()
-    total.flow([])
-    total.a_line.end(out_ref)
-
-
-def group_sum(x, dp_size, collective_id):
-    a, b = group_sizes(dp_size)
-    n = a * b
-    rows, width = x.shape[0] // n, x.shape[1]
-    return pl.pallas_call(
-        functools.partial(sum_kernel, a, b, rows),
-        out_shape=jax.ShapeDtypeStruct((rows, width), f32),
-        in_specs=[pl.BlockSpec(memory_space=pl.ANY)],
-        out_specs=pl.BlockSpec(memory_space=pltpu.VMEM),
-        scratch_shapes=[pltpu.VMEM(x.shape, bf16), pltpu.SemaphoreType.DMA((n,))]
-        + GroupSum.scratch(a, b, rows, width),
-        compiler_params=pltpu.CompilerParams(
-            collective_id=collective_id, has_side_effects=True, vmem_limit_bytes=40 << 20
-        ),
-    )(x)
-
-
 LANES = 128
 LOW_AT = 64
 
@@ -564,7 +524,7 @@
 
 def experts_kernel(
     a, b, rows, width,
-    x_ref, grads_ref, picked_ref, router_ref, near_gate, near_up, near_down, far_gate, far_up, far_down,
+    x_ref, grads_ref, router_ref, near_gate, near_up, near_down, far_gate, far_up, far_down,
     moe_ref, out_ref, o_near_gate, o_near_up, o_near_down, o_far_gate, o_far_up, o_far_down,
     xs, gs, weights, downs, lows, part, extras, stage, local, load, send, recv, stage_sem, store, *scratch,
 ):
@@ -605,7 +565,7 @@
         at = pl.ds(gather.row0(i), rows)
         grads_copy(i).wait()
         x = xs[at, :]
-        chosen = picked_ref[at, :] > 0
+        chosen = gs[at, pl.ds(width, LANES)] > 0
         logits = jnp.where(chosen, mm(x, router_ref[...], NN), masked_score)
         raised = jnp.where(chosen, jnp.exp(logits - jnp.max(logits, axis=1, keepdims=True)), 0.0)
         gates = raised / jnp.sum(raised, axis=1, keepdims=True)
@@ -622,7 +582,7 @@
             x = xs[at, :]
             gate_act = mm(x, weights[2 * e], NN)
             up_act = mm(x, weights[2 * e + 1], NN)
-            down_in = residual_scale * mm(gs[at, :], downs[e], NT)
+            down_in = residual_scale * mm(gs[at, pl.ds(0, width)], downs[e], NT)
             sigmoid_gate = jax.nn.sigmoid(gate_act)
             silu_gate = gate_act * sigmoid_gate
             hidden = silu_gate * up_act
@@ -729,7 +689,7 @@
         c.wait()
 
 
-def experts_call(rows_low, grads, picked, router, near, far, dp_size, collective_id):
+def experts_call(rows_low, grads, router, near, far, dp_size, collective_id):
     a, b = group_sizes(dp_size)
     n = a * b
     rows, width = rows_low.shape
@@ -742,11 +702,11 @@
     return pl.pallas_call(
         functools.partial(experts_kernel, a, b, rows, width),
         out_shape=outs,
-        in_specs=[hbm, hbm, vmem, vmem] + [hbm] * 6,
+        in_specs=[hbm, hbm, vmem] + [hbm] * 6,
         out_specs=[hbm, vmem] + [hbm] * 6,
         scratch_shapes=[
             pltpu.VMEM((n * rows, width), bf16),
-            pltpu.VMEM((n * rows, width), bf16),
+            pltpu.VMEM((n * rows, width + LANES), bf16),
             pltpu.VMEM((4, width, units), bf16),
             pltpu.VMEM((2, units, width), bf16),
             pltpu.VMEM((6, n * rows, units), bf16),
@@ -764,7 +724,7 @@
         compiler_params=pltpu.CompilerParams(
             collective_id=collective_id, has_side_effects=True, vmem_limit_bytes=60 << 20
         ),
-    )(rows_low, grads, picked, router, *near, *far)
+    )(rows_low, grads, router, *near, *far)
 
 
 def reduce_schedule(steps, groups):
@@ -988,12 +948,15 @@
         relative_gather(swap(my_units(w_down[0], 0), "dp", 1), 0),
     ]
     grad_mine = my_rows(out_grad)
-    grads = lax.all_gather(grad_mine, "dp", axis=0, tiled=True, axis_index_groups=groups)
-    ids = lax.all_gather(
-        my_rows(expert_ids), "dp", axis=0, tiled=True, axis_index_groups=groups
-    )
     lanes = jnp.arange(LANES, dtype=jnp.int32)
-    picked = jnp.any(ids[:, :, None] == lanes[None, None, :], axis=1).astype(bf16)
+    picked_mine = jnp.any(my_rows(expert_ids)[:, :, None] == lanes[None, None, :], axis=1)
+    grads = lax.all_gather(
+        jnp.concatenate([grad_mine, picked_mine.astype(bf16)], 1),
+        "dp",
+        axis=0,
+        tiled=True,
+        axis_index_groups=groups,
+    )
     router_wide = jnp.pad(w_router, ((0, 0), (0, LANES - experts)))
 
     inputs = hidden_in.astype(f32)
@@ -1015,23 +978,22 @@
 
     near_set = [w_gate[0], w_up[0], w_down[0]]
     moe_part, back, *expert_parts = experts_call(
-        routed_low, grads, picked, router_wide, near_set, far_set, dp_size, 0
-    )
-    moe_total = group_sum(moe_part, dp_size, 1)
+        routed_low, grads, router_wide, near_set, far_set, dp_size, 0
+    )
+    moe_total = lax.psum_scatter(
+        moe_part, "dp", scatter_dimension=0, tiled=True, axis_index_groups=groups
+    )
 
     dims = (1, 1, 0)
     near_mine = [
         scatter_sum(x, "tensor", tensor_down, bf16, d) for x, d in zip(expert_parts[:3], dims)
     ]
-    returning = [
-        swap(relative_scatter(x, d).astype(bf16), "dp", 1) for x, d in zip(expert_parts[3:], dims)
-    ]
+    far_mine = [relative_scatter(x, d).astype(bf16) for x, d in zip(expert_parts[3:], dims)]
+    back, far_mine = lax.optimization_barrier((back, far_mine))
+    returning = [swap(x, "dp", 1) for x in far_mine]
 
     logits = dot(routed_low, w_router, "td,de->te")
-    chosen = jnp.any(
-        my_rows(expert_ids)[:, :, None] == jnp.arange(experts, dtype=jnp.int32)[None, None, :],
-        axis=1,
-    )
+    chosen = picked_mine[:, :experts]
     logits = jnp.where(chosen, logits, masked_score)
     raised = jnp.where(chosen, jnp.exp(logits - jnp.max(logits, axis=1, keepdims=True)), 0.0)
     gate_weights = raised / jnp.sum(raised, axis=1, keepdims=True)
@@ -1087,15 +1049,17 @@
         * jnp.mean(inputs_mine * gained_in, axis=-1, keepdims=True)
     )
     input_grad = gather_blocks(input_mine, "tensor", tensor_down)
-    block_mine = (middle + residual_scale * moe_total).astype(bf16)
-    block_out = gather_blocks(block_mine, "tensor", tensor_down)
 
     small = jnp.concatenate([router_part, moe_gain_part[None], attn_gain_part[None]], 0)
     small = jnp.pad(small, ((0, -small.shape[0] % 8), (0, 0)))
     for mask in tensor_masks:
         small = small + swap(small, "tensor", mask)
     attention_grad, small = all_reduce(attention_part, small, masks, 2)
-    attention_grad, returning = lax.optimization_barrier((attention_grad, returning))
+    attention_grad, returning, moe_total = lax.optimization_barrier(
+        (attention_grad, returning, moe_total)
+    )
+    block_mine = (middle + residual_scale * moe_total.astype(f32)).astype(bf16)
+    block_out = gather_blocks(block_mine, "tensor", tensor_down)
     expert_mine = [mine + away.astype(f32) for mine, away in zip(near_mine, returning)]
     if tensor_size == 2:
         expert_grads = place(expert_mine, [swap(x, "tensor", 1) for x in expert_mine], dims)

time: 668 us -> 582 us (0.87)
  the two profiles are of different devices: /device:TPU:0 before, /device:TPU:17 now
where the time goes in v4:
time: 582 us; the launch traced here: 574 us
  Pallas kernels  329 us (57%)
  other arithmetic  66.6 us (11%)
  waiting for transfers between devices  55.5 us (10%)
  matrix products  44.4 us (8%)
  local copies, waits for them, and re-layouts  36.4 us (6%)
  starting transfers between devices  26.6 us (5%)
  between operations  16.2 us (3%)
    pallas_call x1, Pallas kernels, experts_call(): pl.pallas_call(functools.partial(experts_kernel, a, b, rows, width), out_...  187 us
    pallas_call x1, Pallas kernels, all_reduce(): pl.pallas_call(functools.partial(reduce_kernel, orders, groups), out_shap...  137 us
    ppermute x24, waiting for transfers between devices, swap(): lax.ppermute(x, axis, [(i, i ^ mask) for i in range(lax.axis_size(axis))])  42.8 us
    ppermute x24, starting transfers between devices, swap(): lax.ppermute(x, axis, [(i, i ^ mask) for i in range(lax.axis_size(axis))])  26.5 us
    dot_general x8, matrix products, dot(): return jnp.einsum(spec, a, b, preferred_element_type=f32)  13.4 us
    all_gather x1, waiting for transfers between devices, per_device(): lax.all_gather(jnp.concatenate([grad_mine, picked_mine.astype(bf16)], 1),...  12.7 us
    unnamed x147, local copies, waits for them, and re-layouts  12.3 us
  transfers between devices with their start and end apart: 26, of which 4 were waited for; matrix products, arithmetic and copies ran while one was open for 23% of the time, Pallas kernels for 24%

profile of v4, /device:TPU:17, one launch (start us, length us, event | category | flops | bytes accessed | tf_op | source)
XLA Modules:
  0.0 574.3 jit_solution(4766508742841771391)
XLA Ops:
  8.7 1.2 constant_dynamic-slice_fusion.2
  12.8 1.9 fusion.16
  15.9 2.1 fusion.56
  18.1 1.6 fusion.54
  20.9 1.5 convolution_convert_fusion.4
  22.4 2.1 fusion.9
  24.5 2.6 fusion.3
  27.1 2.0 copy-done.5
  29.1 4.8 fusion.24
  33.9 1.4 fusion.62
  35.4 1.3 constant_dynamic-slice_fusion.3
  38.3 1.3 collective-permute-start.1
  42.9 14.3 %collective-permute-done.1 = bf16[1536,256]{1,0:T(8,128)(2,1)} collective-permute-done((bf16[1536,256]{1,0:T(8,128)(2,1)S(1)}, bf16[1536,256]{1,0:T(8,128)(2,1)}, u32[]{:S(2)}, u32[]{:S(2)}) %collective-permute-start.1) | collective-permute-done | bytes 786464 | tf_op jit(solution)/shard_map/ppermute | solution.py:124
  57.2 2.1 collective-permute-start.2
  60.3 13.7 %collective-permute-done.3 = bf16[1536,256]{1,0:T(8,128)(2,1)} collective-permute-done((bf16[1536,256]{1,0:T(8,128)(2,1)}, bf16[1536,256]{1,0:T(8,128)(2,1)}, u32[]{:S(2)}, u32[]{:S(2)}) %collective-permute-start.3) | collective-permute-done | bytes 786464 | tf_op jit(solution)/shard_map/ppermute | solution.py:124
  74.0 2.1 collective-permute-start.4
  76.1 14.8 %collective-permute-done.5 = bf16[256,1536]{1,0:T(8,128)(2,1)} collective-permute-done((bf16[256,1536]{1,0:T(8,128)(2,1)}, bf16[256,1536]{1,0:T(8,128)(2,1)}, u32[]{:S(2)}, u32[]{:S(2)}) %collective-permute-start.5) | collective-permute-done | bytes 786464 | tf_op jit(solution)/shard_map/ppermute | solution.py:124
  90.9 1.2 collective-permute-start.6
  92.1 2.5 multiply_reduce_fusion.2
  95.2 2.6 pad_maximum_fusion.1.far_gate
  97.8 2.4 pad_maximum_fusion.2.far_up
  100.3 2.4 pad_maximum_fusion.3.far_down
  102.6 1.1 multiply_convert_fusion.1.x_ref
  103.7 12.7 %all-gather.2.cloned.1.call-done.grads_ref = bf16[2048,1664]{1,0:T(8,128)(2,1)} async-done(((bf16[256,1664]{1,0:T(8,128)(2,1)}), bf16[2048,1664]{1,0:T(8,128)(2,1)}) %all-gather.2.cloned.1.call-update) | async-done | bytes 6815760 | tf_op jit(solution)/shard_map/all_gather | solution.py:953
  116.4 187.0 %shard_map.229 = (bf16[2048,1536]{1,0:T(8,128)(2,1)}, f32[256,1664]{1,0:T(8,128)}, bf16[1536,512]{1,0:T(8,128)(2,1)}, bf16[1536,512]{1,0:T(8,128)(2,1)}, bf16[51...) custom-call(bf16[256,1536]{1,0:T(8,128)(2,1)} %multiply_convert_fusion.1., ...), custom_call_target="tpu_custom_call" | custom-call | tf_op jit(solution)/shard_map/pallas_call | solution.py:702
  303.4 2.2 slice.111
  305.6 4.3 collective-permute-start.7
  314.2 2.6 add_convert_fusion.3
  316.8 2.4 add_convert_fusion.2
  319.2 2.4 add_convert_fusion.1
  322.1 1.3 multiply_reduce_fusion
  323.5 1.9 multiply_convert_fusion
  326.3 1.8 convert_element_type.188
  330.8 2.1 convert_element_type.192
  332.9 2.3 maximum_select_fusion.1
  335.2 1.1 copy-done.29
  336.3 2.3 convolution_convert_fusion.3
  338.6 1.5 copy.60
  340.1 11.2 %fusion = (f32[4,3,512]{2,1,0:T(4,128)S(1)}, f32[4,512,512,3]{2,1,3,0:T(8,128)}) fusion(f32[4,3,512]{2,1,0:T(4,128)S(1)} %log_add_fusion, f32[4,512,512,3]{2,1,3,0:T(8,128)} %copy-done.5, pred[512,512]{0,1:T(8,128)(4,1)S(1)} %fusion.33, bf16[512,4,64,1]{0,2,3,1:T(8,128)(2,1)S(1)} %bitcast.145, bf16[512,4,3,64]{0,3,2,1:T(8,128)(2,1)S(1)} %bitcast.129), kind=kOutput, calls=%fused_computation.2 | convolution fusion | flops 418375680 | bytes 26525696 | tf_op jit(solution)/shard_map/qhgd,khd->hgqk/dot_general | solution.py:92
  351.4 1.8 slice-done.2
  353.2 7.0 %fusion.2 = bf16[4,3,512,512]{2,3,1,0:T(8,128)(2,1)S(1)} fusion(f32[4,512,512,3]{2,1,3,0:T(8,128)} %get-tuple-element.90, f32[4,3,512]{2,1,0:T(4,128)S(1)} %get-tuple-element.89, f32[4,3,512]{2,1,0:T(4,128)S(1)} %log_add_fusion, f32[4,512,512,3]{2,1,3,0:T(8,128)S(1)} %bitcast.127, pred[512,512]{0,1:T(8,128)(4,1)S(1)} %fusion.33), kind=kLoop, calls=%fused_computation.4 | loop fusion | flops 18874368 | bytes 31768576 | tf_op jit(solution)/shard_map/convert_element_type | solution.py:96
  360.2 2.0 fusion.29
  362.4 1.2 convolution_multiply_fusion
  363.9 3.2 fusion.30
  367.1 2.2 fusion.10
  370.1 2.4 dynamic-slice_convert_fusion.1
  374.0 1.2 collective-permute-start.13
  376.8 1.8 convolution_convert_fusion.2
  378.6 4.3 convolution_convert_fusion
  385.5 6.1 %maximum_maximum_fusion.x_ref = bf16[1536,2048]{1,0:T(8,128)(2,1)} fusion(bf16[768,768]{1,0:T(8,128)(2,1)S(1)} %convolution_convert_fusion.1, bf16[768,768]{1,0:T(8,128)(2,1)} %convolution_convert_fusion.2, bf16[1536,1280]{1,0:T(8,128)(2,1)} %convolution_convert_fusion), kind=kLoop, calls=%fused_computation.13 | loop fusion | flops 18874368 | bytes 12582912 | tf_op jit(solution)/shard_map/concatenate | solution.py:1036
  391.6 1.2 collective-permute-start.15
  392.8 2.8 copy-done.4
  395.6 136.6 %shard_map.230 = (bf16[1536,2048]{1,0:T(8,128)(2,1)S(1)}, f32[24,1536]{1,0:T(8,128)S(1)}) custom-call(bf16[1536,2048]{1,0:T(8,128)(2,1)S(1)} %copy-done.4, f32[24,1536]{1,0:T(8,128)S(1)} %fusion.52.small_ref), custom_call_target="tpu_custom_call" | custom-call | tf_op jit(solution)/shard_map/pallas_call | solution.py:830
  532.9 1.2 slice_bitcast_fusion
  534.1 6.3 %collective-permute-start.19 = (bf16[1536,256]{1,0:T(8,128)(2,1)}, bf16[1536,256]{1,0:T(8,128)(2,1)}, u32[]{:S(2)}, u32[]{:S(2)}) collective-permute-start(bf16[1536,256]{1,0:T(8,128)(2,1)} %dynamic-slice_convert_fusion.1), channel_id=1, source_target_pairs={{0,1},{1,0},{2,3},{3,2},{4,5},{5,4},{6,7},{7,6},{8,9},{9,8},{10,11... | collective-permute-start | bytes 2359304 | tf_op jit(solution)/shard_map/ppermute | solution.py:124
  540.5 4.1 maximum_select_fusion
  544.8 1.5 add_convert_fusion
  546.6 2.3 convert_add_fusion.3.refs_0_
  548.9 2.7 slice.145
  551.9 1.8 convert_add_fusion.2.refs_1_
  555.3 2.9 pad_maximum_fusion
  558.2 2.0 fusion.60
  560.1 1.8 maximum_select_fusion.2
  561.9 5.0 shard_map.231
  (239 shorter events, 31.0 us)
Async XLA Ops:
  7.2 26.7 %copy-start = (bf16[768,1536]{1,0:T(8,128)(2,1)S(1)}, bf16[768,1536]{1,0:T(8,128)(2,1)}, u32[]{:S(2)}) copy-start(bf16[768,1536]{1,0:T(8,128)(2,1)} %param.19) | copy-start | bytes 7077892
  7.2 109.2 %all-gather.2.cloned.1.call-start = ((), (), s32[]{:S(2)}) async-start(), calls=%async_computation.1 | async-start | bytes 7667712 | tf_op jit(solution)/shard_map/all_gather | solution.py:953
  10.9 5.0 copy-start.53
  10.9 533.8 %reduce-scatter.2.cloned.1.call-start = ((), (), s32[]{:S(2)}) async-start(), calls=%async_computation.2 | async-start | bytes 7077888 | tf_op jit(solution)/shard_map/reduce_scatter | solution.py:983
  12.6 3.3 copy-start.10
  14.7 5.3 copy-start.62
  18.1 4.3 copy-start.43
  18.1 4.3 copy-start.45
  24.5 4.6 copy-start.5
  24.5 4.6 copy-start.48
  27.1 6.8 %copy-start.50 = (f32[4,3,512]{2,1,0:T(4,128)}, f32[4,3,512]{2,1,0:T(4,128)S(1)}, u32[]{:S(2)}) copy-start(f32[4,3,512]{2,1,0:T(4,128)S(1)} %fusion.3) | copy-start | bytes 73732
  37.5 3.7 copy-start.20
  37.5 54.6 %collective-permute-start = (f32[256,1536]{1,0:T(8,128)}, f32[256,1536]{1,0:T(8,128)}, u32[]{:S(2)}, u32[]{:S(2)}) collective-permute-start(f32[256,1536]{1,0:T(8,128)} %constant_dynamic-slice_fusion.3), channel_id=1, source_target_pairs={{0,1},{1,0},{2,3},{3,2},{4,5},{5,4},{6,7},{7,6},{8,9},{9,8},{10,11... | collective-permute-start | bytes 4718600 | tf_op jit(solution)/shard_map/ppermute | solution.py:124
  38.3 21.0 %copy-start.47 = (bf16[1536,16]{0,1:T(8,128)(2,1)S(1)}, bf16[1536,16]{0,1:T(8,128)(2,1)}, u32[]{:S(2)}) copy-start(bf16[1536,16]{0,1:T(8,128)(2,1)} %param.21) | copy-start | bytes 147460
  38.3 18.9 %collective-permute-start.1 = (bf16[1536,256]{1,0:T(8,128)(2,1)S(1)}, bf16[1536,256]{1,0:T(8,128)(2,1)}, u32[]{:S(2)}, u32[]{:S(2)}) collective-permute-start(bf16[1536,256]{1,0:T(8,128)(2,1)S(1)} %dynamic-slice_bitcast_fusion.2), channel_id=1, source_target_pairs={{0,2},{2,0},{4,6},{6,4},{8,10},{10,8},{12,14},{14,12},{16,18},{18,... | collective-permute-start | bytes 2359304 | tf_op jit(solution)/shard_map/ppermute | solution.py:124
  40.5 33.5 %collective-permute-start.3 = (bf16[1536,256]{1,0:T(8,128)(2,1)}, bf16[1536,256]{1,0:T(8,128)(2,1)}, u32[]{:S(2)}, u32[]{:S(2)}) collective-permute-start(bf16[1536,256]{1,0:T(8,128)(2,1)} %dynamic-slice_bitcast_fusion.1), channel_id=1, source_target_pairs={{0,2},{2,0},{4,6},{6,4},{8,10},{10,8},{12,14},{14,12},{16,18},{18,... | collective-permute-start | bytes 2359304 | tf_op jit(solution)/shard_map/ppermute | solution.py:124
  42.2 48.7 %collective-permute-start.5 = (bf16[256,1536]{1,0:T(8,128)(2,1)}, bf16[256,1536]{1,0:T(8,128)(2,1)}, u32[]{:S(2)}, u32[]{:S(2)}) collective-permute-start(bf16[256,1536]{1,0:T(8,128)(2,1)} %dynamic-slice_bitcast_fusion), channel_id=1, source_target_pairs={{0,2},{2,0},{4,6},{6,4},{8,10},{10,8},{12,14},{14,12},{16,18},{18,... | collective-permute-start | bytes 2359304 | tf_op jit(solution)/shard_map/ppermute | solution.py:124
  57.2 38.0 %collective-permute-start.2 = (bf16[1536,256]{1,0:T(8,128)(2,1)}, bf16[1536,256]{1,0:T(8,128)(2,1)}, u32[]{:S(2)}, u32[]{:S(2)}) collective-permute-start(bf16[1536,256]{1,0:T(8,128)(2,1)} %collective-permute-done.1), channel_id=1, source_target_pairs={{0,1},{1,0},{2,3},{3,2},{4,5},{5,4},{6,7},{7,6},{8,9},{9,8},{10,11... | collective-permute-start | bytes 2359304 | tf_op jit(solution)/shard_map/ppermute | solution.py:124
  74.0 23.8 %collective-permute-start.4 = (bf16[1536,256]{1,0:T(8,128)(2,1)}, bf16[1536,256]{1,0:T(8,128)(2,1)S(1)}, u32[]{:S(2)}, u32[]{:S(2)}) collective-permute-start(bf16[1536,256]{1,0:T(8,128)(2,1)} %collective-permute-done.3), channel_id=1, source_target_pairs={{0,1},{1,0},{2,3},{3,2},{4,5},{5,4},{6,7},{7,6},{8,9},{9,8},{10,11... | collective-permute-start | bytes 2359304 | tf_op jit(solution)/shard_map/ppermute | solution.py:124
  90.9 9.3 %collective-permute-start.6 = (bf16[256,1536]{1,0:T(8,128)(2,1)}, bf16[256,1536]{1,0:T(8,128)(2,1)S(1)}, u32[]{:S(2)}, u32[]{:S(2)}) collective-permute-start(bf16[256,1536]{1,0:T(8,128)(2,1)} %collective-permute-done.5), channel_id=1, source_target_pairs={{0,1},{1,0},{2,3},{3,2},{4,5},{5,4},{6,7},{7,6},{8,9},{9,8},{10,11... | collective-permute-start | bytes 2359304 | tf_op jit(solution)/shard_map/ppermute | solution.py:124
  94.6 8.0 %copy-start.6 = (f32[256,1536]{1,0:T(8,128)}, f32[256,1536]{1,0:T(8,128)S(1)}, u32[]{:S(2)}) copy-start(f32[256,1536]{1,0:T(8,128)S(1)} %get-tuple-element.66) | copy-start | bytes 4718596
  95.2 7.4 %copy-start.57 = (f32[256]{0:T(256)}, f32[256]{0:T(256)S(1)}, u32[]{:S(2)}) copy-start(f32[256]{0:T(256)S(1)} %get-tuple-element.83) | copy-start | bytes 3076
  303.4 6.5 %copy-start.25 = (bf16[1536,512]{1,0:T(8,128)(2,1)S(1)}, bf16[1536,512]{1,0:T(8,128)(2,1)}, u32[]{:S(2)}) copy-start(bf16[1536,512]{1,0:T(8,128)(2,1)} %get-tuple-element.36) | copy-start | bytes 4718596
  303.4 7.5 %copy-start.16 = (bf16[256,1536]{1,0:T(8,128)(2,1)S(1)}, bf16[256,1536]{1,0:T(8,128)(2,1)}, u32[]{:S(2)}) copy-start(bf16[256,1536]{1,0:T(8,128)(2,1)} %multiply_convert_fusion.1.x_ref) | copy-start | bytes 2359300
  305.6 7.1 %copy-start.23 = (bf16[512,1536]{1,0:T(8,128)(2,1)S(1)}, bf16[512,1536]{1,0:T(8,128)(2,1)}, u32[]{:S(2)}) copy-start(bf16[512,1536]{1,0:T(8,128)(2,1)} %get-tuple-element.37) | copy-start | bytes 4718596
  305.6 8.5 %collective-permute-start.7 = (bf16[1536,256]{1,0:T(8,128)(2,1)}, bf16[1536,256]{1,0:T(8,128)(2,1)}, u32[]{:S(2)}, u32[]{:S(2)}) collective-permute-start(bf16[1536,256]{1,0:T(8,128)(2,1)} %slice.111), channel_id=1, source_target_pairs={{0,1},{1,0},{2,3},{3,2},{4,5},{5,4},{6,7},{7,6},{8,9},{9,8},{10,11... | collective-permute-start | bytes 2359304 | tf_op jit(solution)/shard_map/ppermute | solution.py:124
  310.9 5.9 %collective-permute-start.8 = (bf16[1536,256]{1,0:T(8,128)(2,1)}, bf16[1536,256]{1,0:T(8,128)(2,1)}, u32[]{:S(2)}, u32[]{:S(2)}) collective-permute-start(bf16[1536,256]{1,0:T(8,128)(2,1)} %slice.113), channel_id=1, source_target_pairs={{0,1},{1,0},{2,3},{3,2},{4,5},{5,4},{6,7},{7,6},{8,9},{9,8},{10,11... | collective-permute-start | bytes 2359304 | tf_op jit(solution)/shard_map/ppermute | solution.py:124
  313.6 5.6 collective-permute-start.9
  316.8 4.8 copy-start.21
  316.8 4.8 copy-start.36
  316.8 4.8 copy-start.60
  316.8 4.8 copy-start.61
  325.4 7.4 %collective-permute-start.10 = (bf16[256,1536]{1,0:T(8,128)(2,1)}, bf16[256,1536]{1,0:T(8,128)(2,1)}, u32[]{:S(2)}, u32[]{:S(2)}) collective-permute-start(bf16[256,1536]{1,0:T(8,128)(2,1)} %get-tuple-element.63), channel_id=1, source_target_pairs={{0,1},{1,0},{2,3},{3,2},{4,5},{5,4},{6,7},{7,6},{8,9},{9,8},{10,11... | collective-permute-start | bytes 2359304 | tf_op jit(solution)/shard_map/ppermute | solution.py:124
  328.2 4.7 copy-start.13
  329.2 217.4 %collective-permute-start.18 = (bf16[1536,256]{1,0:T(8,128)(2,1)}, bf16[1536,256]{1,0:T(8,128)(2,1)}, u32[]{:S(2)}, u32[]{:S(2)}) collective-permute-start(bf16[1536,256]{1,0:T(8,128)(2,1)} %dynamic-slice_convert_fusion.2), channel_id=1, source_target_pairs={{0,1},{1,0},{2,3},{3,2},{4,5},{5,4},{6,7},{7,6},{8,9},{9,8},{10,11... | collective-permute-start | bytes 2359304 | tf_op jit(solution)/shard_map/ppermute | solution.py:124
  340.1 11.3 %slice-start = ((s8[12582912]{0:T(1024)(128)(4,1)}), s8[4194304]{0:T(1024)(128)(4,1)S(1)}, s32[]{:S(2)}) async-start(s8[12582912]{0:T(1024)(128)(4,1)} %bitcast.126), calls=%async_computation.3 | async-start | bytes 8388608
  340.1 11.3 %slice-start.1 = ((s8[12582912]{0:T(1024)(128)(4,1)}), s8[4194304]{0:T(1024)(128)(4,1)S(1)}, s32[]{:S(2)}) async-start(s8[12582912]{0:T(1024)(128)(4,1)} %bitcast.126), calls=%async_computation.4 | async-start | bytes 8388608
  340.1 13.0 %slice-start.2 = ((s8[12582912]{0:T(1024)(128)(4,1)}), s8[4194304]{0:T(1024)(128)(4,1)S(1)}, s32[]{:S(2)}) async-start(s8[12582912]{0:T(1024)(128)(4,1)} %bitcast.126), calls=%async_computation.5 | async-start | bytes 8388608
  353.2 7.0 %copy-start.32 = (bf16[512,12,32]{0,2,1:T(8,128)(2,1)S(1)}, bf16[512,12,32]{0,2,1:T(8,128)(2,1)}, u32[]{:S(2)}) copy-start(bf16[512,12,32]{0,2,1:T(8,128)(2,1)} %copy-done.31) | copy-start | bytes 1179652
  353.2 7.0 %copy-start.34 = (bf16[512,12,32]{0,2,1:T(8,128)(2,1)S(1)}, bf16[512,12,32]{0,2,1:T(8,128)(2,1)}, u32[]{:S(2)}) copy-start(bf16[512,12,32]{0,2,1:T(8,128)(2,1)} %copy-done.33) | copy-start | bytes 1179652
  363.9 3.2 copy-start.66
  363.9 3.2 copy-start.68
  363.9 3.2 copy-start.69
  369.5 3.0 copy-start.27
  369.5 13.5 %collective-permute-start.11 = (f32[256,1536]{1,0:T(8,128)S(1)}, f32[256,1536]{1,0:T(8,128)S(1)}, u32[]{:S(2)}, u32[]{:S(2)}) collective-permute-start(f32[256,1536]{1,0:T(8,128)S(1)} %constant_dynamic-slice_fusion), channel_id=1, source_target_pairs={{0,1},{1,0},{2,3},{3,2},{4,5},{5,4},{6,7},{7,6},{8,9},{9,8},{10,11... | collective-permute-start | bytes 4718600 | tf_op jit(solution)/shard_map/ppermute | solution.py:124
  372.5 3.0 copy-start.41
  372.9 3.9 copy-start.14
  373.0 3.1 copy-start.38
  374.0 170.5 %collective-permute-start.13 = (bf16[1536,256]{1,0:T(8,128)(2,1)}, bf16[1536,256]{1,0:T(8,128)(2,1)}, u32[]{:S(2)}, u32[]{:S(2)}) collective-permute-start(bf16[1536,256]{1,0:T(8,128)(2,1)} %add_convert_fusion.3), channel_id=1, source_target_pairs={{0,2},{2,0},{4,6},{6,4},{8,10},{10,8},{12,14},{14,12},{16,18},{18,... | collective-permute-start | bytes 2359304 | tf_op jit(solution)/shard_map/ppermute | solution.py:124
  375.2 169.5 %collective-permute-start.14 = (bf16[1536,256]{1,0:T(8,128)(2,1)}, bf16[1536,256]{1,0:T(8,128)(2,1)}, u32[]{:S(2)}, u32[]{:S(2)}) collective-permute-start(bf16[1536,256]{1,0:T(8,128)(2,1)} %add_convert_fusion.2), channel_id=1, source_target_pairs={{0,2},{2,0},{4,6},{6,4},{8,10},{10,8},{12,14},{14,12},{16,18},{18,... | collective-permute-start | bytes 2359304 | tf_op jit(solution)/shard_map/ppermute | solution.py:124
  383.6 8.0 %collective-permute-start.12 = (f32[24,1536]{1,0:T(8,128)S(1)}, f32[24,1536]{1,0:T(8,128)S(1)}, u32[]{:S(2)}, u32[]{:S(2)}) collective-permute-start(f32[24,1536]{1,0:T(8,128)S(1)} %select_maximum_fusion), channel_id=1, source_target_pairs={{0,1},{1,0},{2,3},{3,2},{4,5},{5,4},{6,7},{7,6},{8,9},{9,8},{10,11... | collective-permute-start | bytes 442376 | tf_op jit(solution)/shard_map/ppermute | solution.py:124
  384.9 149.2 %collective-permute-start.17 = (f32[256,1536]{1,0:T(8,128)S(1)}, f32[256,1536]{1,0:T(8,128)}, u32[]{:S(2)}, u32[]{:S(2)}) collective-permute-start(f32[256,1536]{1,0:T(8,128)S(1)} %fusion.22), channel_id=1, source_target_pairs={{0,1},{1,0},{2,3},{3,2},{4,5},{5,4},{6,7},{7,6},{8,9},{9,8},{10,11... | collective-permute-start | bytes 4718600 | tf_op jit(solution)/shard_map/ppermute | solution.py:124
  391.6 153.1 %collective-permute-start.15 = (bf16[256,1536]{1,0:T(8,128)(2,1)}, bf16[256,1536]{1,0:T(8,128)(2,1)S(1)}, u32[]{:S(2)}, u32[]{:S(2)}) collective-permute-start(bf16[256,1536]{1,0:T(8,128)(2,1)} %add_convert_fusion.1), channel_id=1, source_target_pairs={{0,2},{2,0},{4,6},{6,4},{8,10},{10,8},{12,14},{14,12},{16,18},{18,... | collective-permute-start | bytes 2359304 | tf_op jit(solution)/shard_map/ppermute | solution.py:124
  532.2 12.3 %copy-start.2 = (bf16[1536,2048]{1,0:T(8,128)(2,1)}, bf16[1536,2048]{1,0:T(8,128)(2,1)S(1)}, u32[]{:S(2)}) copy-start(bf16[1536,2048]{1,0:T(8,128)(2,1)S(1)} %get-tuple-element.46) | copy-start | bytes 18874372
  534.1 10.6 %copy-start.8 = (f32[256,1536]{1,0:T(8,128)S(1)}, f32[256,1536]{1,0:T(8,128)}, u32[]{:S(2)}) copy-start(f32[256,1536]{1,0:T(8,128)} %copy-done.6) | copy-start | bytes 4718596
  534.1 17.8 %collective-permute-start.19 = (bf16[1536,256]{1,0:T(8,128)(2,1)}, bf16[1536,256]{1,0:T(8,128)(2,1)}, u32[]{:S(2)}, u32[]{:S(2)}) collective-permute-start(bf16[1536,256]{1,0:T(8,128)(2,1)} %dynamic-slice_convert_fusion.1), channel_id=1, source_target_pairs={{0,1},{1,0},{2,3},{3,2},{4,5},{5,4},{6,7},{7,6},{8,9},{9,8},{10,11... | collective-permute-start | bytes 2359304 | tf_op jit(solution)/shard_map/ppermute | solution.py:124
  544.5 9.5 %collective-permute-start.20 = (bf16[256,1536]{1,0:T(8,128)(2,1)}, bf16[256,1536]{1,0:T(8,128)(2,1)S(1)}, u32[]{:S(2)}, u32[]{:S(2)}) collective-permute-start(bf16[256,1536]{1,0:T(8,128)(2,1)} %dynamic-slice_convert_fusion), channel_id=1, source_target_pairs={{0,1},{1,0},{2,3},{3,2},{4,5},{5,4},{6,7},{7,6},{8,9},{9,8},{10,11... | collective-permute-start | bytes 2359304 | tf_op jit(solution)/shard_map/ppermute | solution.py:124
  544.7 4.1 copy-start.3
  546.2 13.9 %collective-permute-start.16 = (bf16[256,1536]{1,0:T(8,128)(2,1)S(1)}, bf16[256,1536]{1,0:T(8,128)(2,1)S(1)}, u32[]{:S(2)}, u32[]{:S(2)}) collective-permute-start(bf16[256,1536]{1,0:T(8,128)(2,1)S(1)} %add_convert_fusion), channel_id=1, source_target_pairs={{0,1},{1,0},{2,3},{3,2},{4,5},{5,4},{6,7},{7,6},{8,9},{9,8},{10,11... | collective-permute-start | bytes 2359304 | tf_op jit(solution)/shard_map/ppermute | solution.py:124
  548.9 3.0 copy-start.12
  551.6 10.3 %collective-permute-start.21 = (f32[1536,256]{1,0:T(8,128)S(1)}, f32[1536,256]{1,0:T(8,128)S(1)}, u32[]{:S(2)}, u32[]{:S(2)}) collective-permute-start(f32[1536,256]{1,0:T(8,128)S(1)} %convert_add_fusion.3.refs_0_), channel_id=1, source_target_pairs={{0,1},{1,0},{2,3},{3,2},{4,5},{5,4},{6,7},{7,6},{8,9},{9,8},{10,11... | collective-permute-start | bytes 4718600 | tf_op jit(solution)/shard_map/ppermute | solution.py:124
  553.8 8.1 %collective-permute-start.22 = (f32[1536,256]{1,0:T(8,128)S(1)}, f32[1536,256]{1,0:T(8,128)S(1)}, u32[]{:S(2)}, u32[]{:S(2)}) collective-permute-start(f32[1536,256]{1,0:T(8,128)S(1)} %convert_add_fusion.2.refs_1_), channel_id=1, source_target_pairs={{0,1},{1,0},{2,3},{3,2},{4,5},{5,4},{6,7},{7,6},{8,9},{9,8},{10,11... | collective-permute-start | bytes 4718600 | tf_op jit(solution)/shard_map/ppermute | solution.py:124
  554.4 7.5 %collective-permute-start.23 = (f32[256,1536]{1,0:T(8,128)S(1)}, f32[256,1536]{1,0:T(8,128)S(1)}, u32[]{:S(2)}, u32[]{:S(2)}) collective-permute-start(f32[256,1536]{1,0:T(8,128)S(1)} %convert_add_fusion.1.refs_2_), channel_id=1, source_target_pairs={{0,1},{1,0},{2,3},{3,2},{4,5},{5,4},{6,7},{7,6},{8,9},{9,8},{10,11... | collective-permute-start | bytes 4718600 | tf_op jit(solution)/shard_map/ppermute | solution.py:124
  561.9 5.0 copy-start.1
  (35 other events, 68.5 us)
Sparse Core Ops, SparseCore 0:
  11.0 105.3 all-gather.1
  314.3 122.3 reduce-scatter.1

commit v5 on v4

--- a/solution.py
+++ b/solution.py
@@ -744,110 +744,6 @@
     return order
 
 
-def reduce_kernel(orders, groups, x_ref, small_ref, out_ref, small_out, acc, got, small_got, load, send, recv, small_send, small_recv):
-    k = len(orders[0])
-    nparts = len(orders)
-    size = x_ref.shape[0] // nparts
-    loads = []
-    for j in range(nparts):
-        c = pltpu.make_async_copy(x_ref.at[pl.ds(j * size, size)], acc.at[pl.ds(j * size, size)], load.at[j])
-        c.start()
-        loads.append(c)
-    greet(sorted(orders[0]))
-    small_out[...] = small_ref[...]
-    copies, back, small_copies = {}, {}, []
-    where = [j * size for j in range(nparts)]
-    per_group = nparts // groups
-
-    def sum_step(j, step):
-        count = size >> (step + 1)
-        mask = orders[j][step]
-        _, bit = peer_of(mask)
-        keep = pl.multiple_of(where[j] + bit * count, 16)
-        give = pl.multiple_of(where[j] + (1 - bit) * count, 16)
-        if step == 0:
-            loads[j].wait()
-        else:
-            copies[j, step - 1].wait_recv()
-            p0 = j * size + (size - (size >> (step - 1)))
-            add_rows(acc, give, acc, give, got, p0 + pl.multiple_of((1 - bit) * count, 16), count, bf16)
-        g0 = j * size + (size - (size >> step))
-        c = remote(acc.at[pl.ds(give, count)], got.at[pl.ds(g0, count)], send.at[j, step], recv.at[j, step], mask)
-        c.start()
-        copies[j, step] = c
-        if step > 0:
-            add_rows(acc, keep, acc, keep, got, p0 + pl.multiple_of(bit * count, 16), count, bf16)
-        where[j] = keep
-
-    def back_step(j, step):
-        count = size >> (step + 1)
-        mask = orders[j][step]
-        _, bit = peer_of(mask)
-        if step == k - 1:
-            copies[j, step].wait_recv()
-            p0 = j * size + (size - (size >> step))
-            add_rows(out_ref, where[j], acc, where[j], got, p0, count, bf16)
-        else:
-            back[j, step + 1].wait_recv()
-        here = where[j]
-        c = remote(out_ref.at[pl.ds(here, count)], out_ref.at[pl.ds(here, count)], send.at[j, k + step], recv.at[j, k + step], mask)
-        c.start()
-        back[j, step] = c
-        where[j] = pl.multiple_of(here - bit * count, 16)
-
-    def small_step(step):
-        if step > 0:
-            small_copies[-1].wait_send()
-            small_copies[-1].wait_recv()
-            small_out[...] += small_got[step - 1]
-        if step < k:
-            c = remote(small_out, small_got.at[step], small_send.at[step], small_recv.at[step], orders[0][step])
-            c.start()
-            small_copies.append(c)
-
-    small_done = 0
-    for g, kind, step in reduce_schedule(k, groups):
-        for j in range(g * per_group, (g + 1) * per_group):
-            (sum_step if kind == "sum" else back_step)(j, step)
-        if g == groups - 1 and small_done <= k:
-            small_step(small_done)
-            small_done += 1
-    for j in range(nparts):
-        back[j, 0].wait_recv()
-    for c in copies.values():
-        c.wait_send()
-    for c in back.values():
-        c.wait_send()
-
-
-def all_reduce(x, small, masks, collective_id):
-    inner, last = masks[:-1], masks[-1:]
-    groups = 2 if x.shape[0] % (6 * 16 * 2 ** len(masks)) == 0 else 1
-    nparts = 3 * groups
-    orders = [rotated(inner, j) + last for j in range(nparts)]
-    k = len(masks)
-    vm = pl.BlockSpec(memory_space=pltpu.VMEM)
-    return pl.pallas_call(
-        functools.partial(reduce_kernel, orders, groups),
-        out_shape=[jax.ShapeDtypeStruct(x.shape, bf16), jax.ShapeDtypeStruct(small.shape, f32)],
-        in_specs=[pl.BlockSpec(memory_space=pl.ANY), vm],
-        out_specs=[vm, vm],
-        scratch_shapes=[
-            pltpu.VMEM(x.shape, bf16),
-            pltpu.VMEM(x.shape, bf16),
-            pltpu.VMEM((k,) + small.shape, f32),
-            pltpu.SemaphoreType.DMA((nparts,)),
-            pltpu.SemaphoreType.DMA((nparts, 2 * k)),
-            pltpu.SemaphoreType.DMA((nparts, 2 * k)),
-            pltpu.SemaphoreType.DMA((k,)),
-            pltpu.SemaphoreType.DMA((k,)),
-        ],
-        compiler_params=pltpu.CompilerParams(
-            collective_id=collective_id, has_side_effects=True, vmem_limit_bytes=40 << 20
-        ),
-    )(x, small)
-
-
 def place_kernel(dims, *refs):
     n = len(dims)
     mine, other, outs = refs[:n], refs[n : 2 * n], refs[2 * n : 3 * n]
@@ -887,6 +783,377 @@
         + [pltpu.SemaphoreType.DMA((n, 2)), pltpu.SemaphoreType.DMA((n,))],
         compiler_params=pltpu.CompilerParams(vmem_limit_bytes=24 << 20),
     )(*mine, *other)
+
+
+class AllReduce:
+    def __init__(self, orders, groups, acc, got, out, send, recv):
+        self.orders, self.groups = orders, groups
+        self.acc, self.got, self.out, self.send, self.recv = acc, got, out, send, recv
+        self.k = len(orders[0])
+        self.size = acc.shape[0] // len(orders)
+        self.where = [j * self.size for j in range(len(orders))]
+        self.sums, self.backs = {}, {}
+
+    def sum_step(self, j, step):
+        count = self.size >> (step + 1)
+        mask = self.orders[j][step]
+        _, bit = peer_of(mask)
+        keep = pl.multiple_of(self.where[j] + bit * count, 16)
+        give = pl.multiple_of(self.where[j] + (1 - bit) * count, 16)
+        acc, got = self.acc, self.got
+        if step > 0:
+            self.sums[j, step - 1].wait_recv()
+            p0 = j * self.size + (self.size - (self.size >> (step - 1)))
+            add_rows(acc, give, acc, give, got, p0 + pl.multiple_of((1 - bit) * count, 16), count, bf16)
+        g0 = j * self.size + (self.size - (self.size >> step))
+        c = remote(
+            acc.at[pl.ds(give, count)],
+            got.at[pl.ds(g0, count)],
+            self.send.at[j, step],
+            self.recv.at[j, step],
+            mask,
+        )
+        c.start()
+        self.sums[j, step] = c
+        if step > 0:
+            add_rows(acc, keep, acc, keep, got, p0 + pl.multiple_of(bit * count, 16), count, bf16)
+        self.where[j] = keep
+
+    def back_step(self, j, step):
+        count = self.size >> (step + 1)
+        mask = self.orders[j][step]
+        _, bit = peer_of(mask)
+        here = self.where[j]
+        if step == self.k - 1:
+            self.sums[j, step].wait_recv()
+            p0 = j * self.size + (self.size - (self.size >> step))
+            add_rows(self.out, here, self.acc, here, self.got, p0, count, bf16)
+        else:
+            self.backs[j, step + 1].wait_recv()
+        there = self.out.at[pl.ds(here, count)]
+        c = remote(
+            there, there, self.send.at[j, self.k + step], self.recv.at[j, self.k + step], mask
+        )
+        c.start()
+        self.backs[j, step] = c
+        self.where[j] = pl.multiple_of(here - bit * count, 16)
+
+    def events(self):
+        per_group = len(self.orders) // self.groups
+
+        def event(g, kind, step):
+            for j in range(g * per_group, (g + 1) * per_group):
+                (self.sum_step if kind == "sum" else self.back_step)(j, step)
+
+        return [
+            functools.partial(event, *e) for e in reduce_schedule(self.k, self.groups)
+        ]
+
+    def finish(self):
+        for j in range(len(self.orders)):
+            self.backs[j, 0].wait_recv()
+        for c in list(self.sums.values()) + list(self.backs.values()):
+            c.wait_send()
+
+
+def sum_orders(dp_size, rows, most):
+    masks = bit_masks(dp_size)
+    groups = most if rows % (3 * most * 16 * dp_size) == 0 else 1
+    return [rotated(masks[:-1], j) + masks[-1:] for j in range(3 * groups)], groups
+
+
+def turn(x, cosine, sine):
+    lane = lax.broadcasted_iota(jnp.int32, x.shape, 1)
+    swapped = jnp.where(lane % HEAD_DIM < HEAD_DIM // 2, pltpu.roll(x, 128 - 32, 1), pltpu.roll(x, 32, 1))
+    return x * cosine + swapped * sine
+
+
+def mask_bias(bias, seg_col, seg_row):
+    length = bias.shape[0]
+    row = lax.broadcasted_iota(jnp.int32, bias.shape, 0)
+    col = lax.broadcasted_iota(jnp.int32, bias.shape, 1)
+    allowed = (row >= col) & (seg_col[...] == seg_row[...])
+    bias[...] = jnp.where(allowed, 0.0, masked_score)
+
+
+def attention_back_kernel(
+    dp_size, tensor_size, orders_o, groups_o, orders_q, groups_q,
+    back, middle, scale_mid, routed, grad_top, picked, router, moe_gain,
+    heads, q_ref, k_ref, v_ref, w_out, w_query, w_key, w_value, normed, cosine, sine,
+    seg_col, seg_row, hidden, gain, scale_in,
+    out_o, out_q, out_input, small_out,
+    branch, middle_grad, bias, heads_grad, qkv_low, scratch_q, scratch_k, scratch_v,
+    acc_o, got_o, acc_q, got_q, shares, got_shares, small_got,
+    send_o, recv_o, send_q, recv_q, small_send, small_recv, share_send, share_recv, in_send, in_recv, branch_send, branch_recv,
+):
+    length, width = normed.shape
+    q_width, k_width = q_ref.shape[1], k_ref.shape[1]
+    rows = hidden.shape[0]
+    per_kv = q_width // k_width
+    core = lax.axis_index("tensor")
+    tensor_masks = bit_masks(tensor_size)
+
+    def mate(m):
+        bit = (core // m) % 2
+        return core + m * (1 - 2 * bit)
+
+    barrier = pltpu.get_barrier_semaphore()
+    masks = bit_masks(dp_size)
+    others = [(core + m) % tensor_size for m in range(1, tensor_size)]
+    for mask in masks:
+        pl.semaphore_signal(
+            barrier, inc=1, device_id={"dp": peer_of(mask)[0]}, device_id_type=MESH
+        )
+    for other in others:
+        pl.semaphore_signal(barrier, inc=1, device_id={"tensor": other}, device_id_type=MESH)
+    mine = pl.ds(pl.multiple_of(core * rows, 16), rows)
+    experts = dp_size
+    x = routed[...]
+    chosen = picked[...] > 0
+    logits = jnp.where(chosen, mm(x, router[...], NN), masked_score)
+    raised = jnp.where(chosen, jnp.exp(logits - jnp.max(logits, axis=1, keepdims=True)), 0.0)
+    gates = raised / jnp.sum(raised, axis=1, keepdims=True)
+    derivs = back[:, pl.ds(width, LANES)]
+    derivs = jnp.where(chosen, derivs + pltpu.roll(derivs, LANES - LOW_AT, 1), 0.0)
+    logit_grad = (
+        gates * (derivs - jnp.sum(gates * derivs, axis=1, keepdims=True))
+    ).astype(bf16)
+    small_out[...] = jnp.zeros(small_out.shape, f32)
+    small_out[pl.ds(0, experts), :] = mm(logit_grad, x, TN)[:experts]
+    routed_grad = back[:, pl.ds(0, width)] + mm(logit_grad, router[...], NT)
+    mid = middle[...]
+    r2 = scale_mid[...]
+    small_out[pl.ds(experts, 1), :] = jnp.sum(routed_grad * mid * r2, axis=0, keepdims=True)
+    gained = moe_gain[...] * routed_grad
+    middle_grad[...] = (
+        grad_top[...].astype(f32)
+        + r2 * gained
+        - mid * (r2 * r2 * r2) * jnp.mean(mid * gained, axis=1, keepdims=True)
+    )
+    branch[mine, :] = (residual_scale * middle_grad[...]).astype(bf16)
+    pl.semaphore_wait(barrier, len(masks) + len(others))
+    branch_copies = []
+    for m, other in enumerate(others):
+        c = pltpu.make_async_remote_copy(
+            src_ref=branch.at[mine], dst_ref=branch.at[mine], send_sem=branch_send.at[m],
+            recv_sem=branch_recv.at[m], device_id={"tensor": other}, device_id_type=MESH,
+        )
+        c.start()
+        branch_copies.append(c)
+    mask_bias(bias, seg_col, seg_row)
+    for c in branch_copies:
+        c.wait()
+    for i in range(width // q_width):
+        at = pl.ds(i * q_width, q_width)
+        acc_o[at, :] = mm(heads[...], branch[:, at], TN).astype(bf16)
+    sum_o = AllReduce(orders_o, groups_o, acc_o, got_o, out_o, send_o, recv_o)
+    events_o = sum_o.events()
+    events_o.pop(0)()
+    heads_grad[...] = mm(branch[...], w_out[...], NT).astype(bf16)
+    half = length // 2
+    spans = ((0, half, half), (half, half, length))
+    count = 0
+    for pair in range(k_width // 128):
+        k_tile = k_ref[:, pair * 128 : pair * 128 + 128]
+        v_tile = v_ref[:, pair * 128 : pair * 128 + 128]
+        for g in range(2):
+            kg = k_tile[:, g * HEAD_DIM : (g + 1) * HEAD_DIM]
+            vg = v_tile[:, g * HEAD_DIM : (g + 1) * HEAD_DIM]
+            side = pl.ds(g * HEAD_DIM, HEAD_DIM)
+            for h in range(per_kv):
+                head = (pair * 2 + g) * per_kv + h
+                lanes = pl.ds(head * HEAD_DIM, HEAD_DIM)
+                for start, size, cols in spans:
+                    at = pl.ds(start, size)
+                    qh = q_ref[at, lanes]
+                    oh = heads_grad[at, lanes]
+                    scores = mm(qh, kg[:cols], NT) * attn_scale + bias[at, pl.ds(0, cols)]
+                    raised = jnp.exp(scores - jnp.max(scores, axis=1, keepdims=True))
+                    probability = raised * (1.0 / jnp.sum(raised, axis=1, keepdims=True))
+                    prob_grad = mm(oh, vg[:cols], NT)
+                    weighted = jnp.sum(probability * prob_grad, axis=1, keepdims=True)
+                    score_low = (probability * (prob_grad - weighted)).astype(bf16)
+                    probs_low = probability.astype(bf16)
+                    scratch_q[at, lanes] = mm(score_low, kg[:cols], NN) * attn_scale
+                    dk = mm(score_low, qh, TN) * attn_scale
+                    dv = mm(probs_low, oh, TN)
+                    upto = pl.ds(0, cols)
+                    if h == 0 and start == 0:
+                        scratch_k[upto, side] = dk
+                        scratch_v[upto, side] = dv
+                        scratch_k[pl.ds(cols, length - cols), side] = jnp.zeros((length - cols, HEAD_DIM), f32)
+                        scratch_v[pl.ds(cols, length - cols), side] = jnp.zeros((length - cols, HEAD_DIM), f32)
+                    else:
+                        scratch_k[upto, side] += dk
+                        scratch_v[upto, side] += dv
+                count += 1
+                if count % 2 == 0 and len(events_o) > 1:
+                    events_o.pop(0)()
+        at = pl.ds(q_width + pair * 128, 128)
+        qkv_low[:, at] = turn(scratch_k[...], cosine[...], -sine[...]).astype(bf16)
+        at = pl.ds(q_width + k_width + pair * 128, 128)
+        qkv_low[:, at] = scratch_v[...].astype(bf16)
+    for i in range(q_width // 128):
+        at = pl.ds(i * 128, 128)
+        qkv_low[:, at] = turn(scratch_q[:, at], cosine[...], -sine[...]).astype(bf16)
+    chunk = width // len(orders_q)
+    for i in range(len(orders_q)):
+        at = pl.ds(i * chunk, chunk)
+        acc_q[at, :] = mm(normed[:, at], qkv_low[...], TN).astype(bf16)
+    sum_q = AllReduce(orders_q, groups_q, acc_q, got_q, out_q, send_q, recv_q)
+    events_q = sum_q.events()
+    events_q.pop(0)()
+    while events_o:
+        events_o.pop(0)()
+
+    def shares_of(t):
+        at = pl.ds(pl.multiple_of(t * rows, 16), rows)
+        low = qkv_low[at, :]
+        return (
+            mm(low[:, :q_width], w_query[...], NT)
+            + mm(low[:, q_width : q_width + k_width], w_key[...], NT)
+            + mm(low[:, q_width + k_width :], w_value[...], NT)
+        )
+
+    share_copies = []
+    for m, other in enumerate(others):
+        shares[m] = shares_of(other)
+        slot = tensor_size - 2 - m
+        c = pltpu.make_async_remote_copy(
+            src_ref=shares.at[m], dst_ref=got_shares.at[slot], send_sem=share_send.at[m],
+            recv_sem=share_recv.at[slot], device_id={"tensor": other}, device_id_type=MESH,
+        )
+        c.start()
+        share_copies.append(c)
+    normed_grad = shares_of(core)
+    events_q.pop(0)()
+    out_input[mine, :] = normed_grad
+    for m, c in enumerate(share_copies):
+        c.wait_send()
+        slot = tensor_size - 2 - m
+        pltpu.make_async_remote_copy(
+            src_ref=shares.at[m], dst_ref=got_shares.at[slot], send_sem=share_send.at[m],
+            recv_sem=share_recv.at[slot], device_id={"tensor": others[m]}, device_id_type=MESH,
+        ).wait_recv()
+        out_input[mine, :] += got_shares[slot]
+    normed_grad = out_input[mine, :]
+    inputs = hidden[...].astype(f32)
+    r1 = scale_in[...]
+    gained = gain[...] * normed_grad
+    small_out[pl.ds(small_out.shape[0] - 1, 1), :] = jnp.sum(normed_grad * inputs * r1, axis=0, keepdims=True)
+    out_input[mine, :] = (
+        middle_grad[...]
+        + r1 * gained
+        - inputs * (r1 * r1 * r1) * jnp.mean(inputs * gained, axis=1, keepdims=True)
+    )
+    in_copies = []
+    for m, other in enumerate(others):
+        c = pltpu.make_async_remote_copy(
+            src_ref=out_input.at[mine], dst_ref=out_input.at[mine], send_sem=in_send.at[m],
+            recv_sem=in_recv.at[m], device_id={"tensor": other}, device_id_type=MESH,
+        )
+        c.start()
+        in_copies.append(c)
+    ways = [("dp", m) for m in masks] + [("tensor", m) for m in tensor_masks]
+    small_copies = []
+
+    def small_step(step):
+        if step > 0:
+            small_copies[-1].wait_send()
+            small_copies[-1].wait_recv()
+            small_out[...] += small_got[step - 1]
+        if step < len(ways):
+            axis, m = ways[step]
+            device = {"dp": peer_of(m)[0]} if axis == "dp" else {"tensor": mate(m)}
+            c = pltpu.make_async_remote_copy(
+                src_ref=small_out, dst_ref=small_got.at[step], send_sem=small_send.at[step],
+                recv_sem=small_recv.at[step], device_id=device, device_id_type=MESH,
+            )
+            c.start()
+            small_copies.append(c)
+
+    steps = len(ways) + 1
+    done = 0
+    while events_q:
+        if done < steps:
+            small_step(done)
+            done += 1
+        events_q.pop(0)()
+    while done < steps:
+        small_step(done)
+        done += 1
+    sum_o.finish()
+    sum_q.finish()
+    for c in in_copies:
+        c.wait()
+
+
+def attention_back(
+    back, middle, scale_mid, routed, grad_top, picked, router, moe_gain,
+    heads, q, k, v, w_out, w_query, w_key, w_value, normed, cosine, sine, seg,
+    hidden, gain, scale_in, dp_size, tensor_size, collective_id,
+):
+    length, width = normed.shape
+    small = jax.ShapeDtypeStruct(((dp_size + 2 + 7) // 8 * 8, width), f32)
+    q_width, k_width = q.shape[1], k.shape[1]
+    rows = hidden.shape[0]
+    orders_o, groups_o = sum_orders(dp_size, width, 1)
+    orders_q, groups_q = sum_orders(dp_size, width, 2)
+    steps = len(bit_masks(dp_size))
+    small_steps = steps + len(bit_masks(tensor_size))
+    qkv_width = q_width + 2 * k_width
+    others = tensor_size - 1
+    vmem = pl.BlockSpec(memory_space=pltpu.VMEM)
+    dma = pltpu.SemaphoreType.DMA
+    return pl.pallas_call(
+        functools.partial(
+            attention_back_kernel, dp_size, tensor_size, orders_o, groups_o, orders_q, groups_q
+        ),
+        out_shape=[
+            jax.ShapeDtypeStruct((width, q_width), bf16),
+            jax.ShapeDtypeStruct((width, qkv_width), bf16),
+            jax.ShapeDtypeStruct((length, width), f32),
+            jax.ShapeDtypeStruct(small.shape, f32),
+        ],
+        in_specs=[vmem] * 24,
+        out_specs=[vmem] * 4,
+        scratch_shapes=[
+            pltpu.VMEM((length, width), bf16),
+            pltpu.VMEM((rows, width), f32),
+            pltpu.VMEM((length, length), f32),
+            pltpu.VMEM((length, q_width), bf16),
+            pltpu.VMEM((length, qkv_width), bf16),
+            pltpu.VMEM((length, q_width), f32),
+            pltpu.VMEM((length, 128), f32),
+            pltpu.VMEM((length, 128), f32),
+            pltpu.VMEM((width, q_width), bf16),
+            pltpu.VMEM((width, q_width), bf16),
+            pltpu.VMEM((width, qkv_width), bf16),
+            pltpu.VMEM((width, qkv_width), bf16),
+            pltpu.VMEM((others, rows, width), f32),
+            pltpu.VMEM((others, rows, width), f32),
+            pltpu.VMEM((small_steps,) + small.shape, f32),
+            dma((len(orders_o), 2 * steps)),
+            dma((len(orders_o), 2 * steps)),
+            dma((len(orders_q), 2 * steps)),
+            dma((len(orders_q), 2 * steps)),
+            dma((small_steps,)),
+            dma((small_steps,)),
+            dma((others,)),
+            dma((others,)),
+            dma((others,)),
+            dma((others,)),
+            dma((others,)),
+            dma((others,)),
+        ],
+        compiler_params=pltpu.CompilerParams(
+            collective_id=collective_id, has_side_effects=True, vmem_limit_bytes=60 << 20
+        ),
+    )(
+        back, middle, scale_mid, routed, grad_top, picked, router, moe_gain[None],
+        heads, q, k, v, w_out, w_query, w_key, w_value, normed, cosine, sine,
+        seg[:, None], seg[None, :], hidden, gain[None], scale_in,
+    )
 
 
 def dot(a, b, spec):
@@ -950,8 +1217,9 @@
     grad_mine = my_rows(out_grad)
     lanes = jnp.arange(LANES, dtype=jnp.int32)
     picked_mine = jnp.any(my_rows(expert_ids)[:, :, None] == lanes[None, None, :], axis=1)
+    picked_low = picked_mine.astype(bf16)
     grads = lax.all_gather(
-        jnp.concatenate([grad_mine, picked_mine.astype(bf16)], 1),
+        jnp.concatenate([grad_mine, picked_low], 1),
         "dp",
         axis=0,
         tiled=True,
@@ -992,71 +1260,39 @@
     back, far_mine = lax.optimization_barrier((back, far_mine))
     returning = [swap(x, "dp", 1) for x in far_mine]
 
-    logits = dot(routed_low, w_router, "td,de->te")
-    chosen = picked_mine[:, :experts]
-    logits = jnp.where(chosen, logits, masked_score)
-    raised = jnp.where(chosen, jnp.exp(logits - jnp.max(logits, axis=1, keepdims=True)), 0.0)
-    gate_weights = raised / jnp.sum(raised, axis=1, keepdims=True)
-    routed_grad = back[:, :model_width]
-    gate_deriv = (
-        back[:, model_width : model_width + experts]
-        + back[:, model_width + LOW_AT : model_width + LOW_AT + experts]
-    )
-    chosen_grad = gate_weights * (
-        gate_deriv - jnp.sum(gate_weights * gate_deriv, axis=1, keepdims=True)
-    )
-    logit_grad = chosen_grad.astype(bf16)
-    router_part = dot(logit_grad, routed_low, "te,td->ed")
-    routed_grad = routed_grad + dot(logit_grad, w_router, "te,de->td")
-    gained = moe_gain * routed_grad
-    moe_gain_part = jnp.sum(routed_grad * middle * scale_mid, axis=0)
-    grad_top = grad_mine.astype(f32)
-    middle_grad = (
-        grad_top
-        + scale_mid * gained
-        - middle
-        * (scale_mid * scale_mid * scale_mid)
-        * jnp.mean(middle * gained, axis=-1, keepdims=True)
-    )
-    branch_low = gather_blocks(
-        (residual_scale * middle_grad).astype(bf16), "tensor", tensor_down
-    )
     heads_width = heads_flat.shape[1]
-    w_output_part = [
-        dot(heads_flat, branch_low[:, i : i + heads_width], "tc,td->cd")
-        for i in range(0, model_width, heads_width)
-    ]
-    heads_grad = dot(branch_low, w_output, "td,cd->tc").astype(bf16)
-    query_low, key_low, value_low = attend_backward(
-        query_heads, key_heads, value_heads, log_sums, heads_grad, segment, tables
-    )
-    width_q, width_k = query_low.shape[1], key_low.shape[1]
-    qkv_low = jnp.concatenate([query_low, key_low, value_low], axis=1)
-    qkv_width = qkv_low.shape[1]
-    attention_part = jnp.concatenate(
-        [dot(normed_low, qkv_low, "td,tc->dc"), jnp.concatenate(w_output_part, 0)], 1
-    ).astype(bf16)
-    qkv_weight = jnp.concatenate([w_query, key_weight, value_weight], axis=1)
-    normed_part = dot(qkv_low, qkv_weight, "tc,dc->td")
-    normed_grad = scatter_sum(normed_part, "tensor", tensor_down, f32)
-    gained_in = attn_gain * normed_grad
-    attn_gain_part = jnp.sum(normed_grad * inputs_mine * scale_in_mine, axis=0)
-    input_mine = (
-        middle_grad
-        + scale_in_mine * gained_in
-        - inputs_mine
-        * (scale_in_mine * scale_in_mine * scale_in_mine)
-        * jnp.mean(inputs_mine * gained_in, axis=-1, keepdims=True)
-    )
-    input_grad = gather_blocks(input_mine, "tensor", tensor_down)
-
-    small = jnp.concatenate([router_part, moe_gain_part[None], attn_gain_part[None]], 0)
-    small = jnp.pad(small, ((0, -small.shape[0] % 8), (0, 0)))
-    for mask in tensor_masks:
-        small = small + swap(small, "tensor", mask)
-    attention_grad, small = all_reduce(attention_part, small, masks, 2)
-    attention_grad, returning, moe_total = lax.optimization_barrier(
-        (attention_grad, returning, moe_total)
+    width_q, width_k = query_heads.shape[1] * head_size, key_heads.shape[1] * head_size
+    qkv_width = width_q + 2 * width_k
+    w_output_sum, qkv_grad, input_grad, small = attention_back(
+        back,
+        middle,
+        scale_mid,
+        routed_low,
+        grad_mine,
+        picked_low,
+        router_wide,
+        moe_gain,
+        heads_flat,
+        query_heads.reshape(tokens_here, -1),
+        key_heads.reshape(tokens_here, -1),
+        value_heads.reshape(tokens_here, -1),
+        w_output,
+        w_query,
+        key_weight,
+        value_weight,
+        normed_low,
+        jnp.tile(tables[0][:, 0, :], (1, 4)),
+        jnp.tile(jnp.concatenate([-tables[1][:, 0, :], tables[1][:, 0, :]], 1), (1, 2)),
+        segment,
+        my_rows(hidden_in),
+        attn_gain,
+        scale_in_mine,
+        dp_size,
+        tensor_size,
+        2,
+    )
+    w_output_sum, returning, moe_total = lax.optimization_barrier(
+        (w_output_sum, returning, moe_total)
     )
     block_mine = (middle + residual_scale * moe_total.astype(f32)).astype(bf16)
     block_out = gather_blocks(block_mine, "tensor", tensor_down)
@@ -1067,21 +1303,17 @@
         expert_grads = [
             gather_blocks(x, "tensor", tensor_down, dim) for x, dim in zip(expert_mine, dims)
         ]
-    attention_grad = attention_grad.astype(f32)
+    w_output_sum, qkv_grad = w_output_sum.astype(f32), qkv_grad.astype(f32)
     w_output_grad = jnp.concatenate(
-        [
-            attention_grad[i : i + heads_width, qkv_width:]
-            for i in range(0, model_width, heads_width)
-        ],
-        1,
+        [w_output_sum[i : i + heads_width] for i in range(0, model_width, heads_width)], 1
     )
     return (
         block_out,
         input_grad,
-        small[experts + 1],
-        attention_grad[:, :width_q],
-        attention_grad[:, width_q : width_q + width_k],
-        attention_grad[:, width_q + width_k : qkv_width],
+        small[-1],
+        qkv_grad[:, :width_q],
+        qkv_grad[:, width_q : width_q + width_k],
+        qkv_grad[:, width_q + width_k : qkv_width],
         w_output_grad,
         small[experts],
         small[:experts].T,

time: 582 us -> 581 us (level)
  the two profiles are of different devices: /device:TPU:17 before, /device:TPU:0 now
where the time goes in v5:
time: 581 us; the launch traced here: 572 us
  Pallas kernels  393 us (68%)
  waiting for transfers between devices  58.6 us (10%)
  local copies, waits for them, and re-layouts  41.3 us (7%)
  other arithmetic  32.7 us (6%)
  matrix products  18.8 us (3%)
  between operations  15.6 us (3%)
  starting transfers between devices  12.6 us (2%)
    pallas_call x1, Pallas kernels, attention_back(): pl.pallas_call(functools.partial(attention_back_kernel, dp_size, tensor_s...  203 us
    pallas_call x1, Pallas kernels, experts_call(): pl.pallas_call(functools.partial(experts_kernel, a, b, rows, width), out_...  185 us
    ppermute x20, waiting for transfers between devices, swap(): lax.ppermute(x, axis, [(i, i ^ mask) for i in range(lax.axis_size(axis))])  45.9 us
    unnamed x98, local copies, waits for them, and re-layouts  15.3 us
    all_gather x1, waiting for transfers between devices, per_device(): lax.all_gather(jnp.concatenate([grad_mine, picked_low], 1), 'dp', axis=0,...  12.7 us
    ppermute x20, starting transfers between devices, swap(): lax.ppermute(x, axis, [(i, i ^ mask) for i in range(lax.axis_size(axis))])  12.5 us
  transfers between devices with their start and end apart: 22, of which 4 were waited for; matrix products, arithmetic and copies ran while one was open for 13% of the time, Pallas kernels for 35%

profile of v5, /device:TPU:0, one launch (start us, length us, event | category | flops | bytes accessed | tf_op | source)
XLA Modules:
  0.0 572.1 jit_solution(17267723607346224130)
XLA Ops:
  7.3 1.3 copy-done
  9.9 1.0 pad_maximum_fusion.4
  13.5 0.7 copy-done.33
  14.8 0.8 copy.54
  15.8 0.9 fusion.19
  16.8 0.9 fusion.12
  17.7 1.9 fusion.35
  19.8 1.4 fusion.36
  21.5 0.7 copy-done.41
  22.2 7.4 %fusion.30 = (f32[4,3,512]{2,1,0:T(4,128)S(1)}, f32[4,3,512,512]{2,3,1,0:T(8,128)}) fusion(pred[512,512]{0,1:T(8,128)(4,1)S(1)} %copy-done.41, bf16[512,4,3,32]{0,3,2,1:T(8,128)(2,1)S(1)} %bitcast.90, bf16[512,4,3,32]{0,3,2,1:T(8,128)(2,1)S(1)} %bitcast.89, bf16[512,4,32]{0,2,1:T(8,128)(2,1)S(1)} %get-tuple-element.72, ...), kind=kOutput, calls=%fused_computation.79 | convolution fusion | flops 417333760 | bytes 13918208 | tf_op jit(solution)/shard_map/sub | solution.py:72
  29.6 6.1 %fusion.11 = bf16[4,64,3,512]{3,1,2,0:T(8,128)(2,1)S(1)} fusion(bf16[512,4,64,1]{0,2,3,1:T(8,128)(2,1)} %bitcast.94, f32[4,3,512,512]{2,3,1,0:T(8,128)} %get-tuple-element.77, f32[4,3,512]{2,1,0:T(4,128)S(1)} %get-tuple-element.76), kind=kOutput, calls=%fused_computation.33 | convolution fusion | flops 409337856 | bytes 13656064 | tf_op jit(solution)/shard_map/hgqk,khd->qhgd/dot_general | solution.py:75
  35.7 1.4 fusion.37
  37.1 1.3 constant_dynamic-slice_fusion.2
  38.4 0.9 copy-done.6
  39.8 3.0 collective-permute-start.1
  42.8 0.9 dynamic-slice_bitcast_fusion.1
  43.7 1.0 collective-permute-start.3
  44.7 0.9 dynamic-slice_bitcast_fusion
  45.6 1.1 collective-permute-start.5
  46.6 14.6 %collective-permute-done.1 = bf16[1536,256]{1,0:T(8,128)(2,1)} collective-permute-done((bf16[1536,256]{1,0:T(8,128)(2,1)S(1)}, bf16[1536,256]{1,0:T(8,128)(2,1)}, u32[]{:S(2)}, u32[]{:S(2)}) %collective-permute-start.1) | collective-permute-done | bytes 786464 | tf_op jit(solution)/shard_map/ppermute | solution.py:124
  61.2 1.0 copy.58
  62.2 0.8 pad.4.router_ref.router
  63.1 15.0 %collective-permute-done.3 = bf16[1536,256]{1,0:T(8,128)(2,1)} collective-permute-done((bf16[1536,256]{1,0:T(8,128)(2,1)}, bf16[1536,256]{1,0:T(8,128)(2,1)}, u32[]{:S(2)}, u32[]{:S(2)}) %collective-permute-start.3) | collective-permute-done | bytes 786464 | tf_op jit(solution)/shard_map/ppermute | solution.py:124
  78.1 16.3 %collective-permute-done.5 = bf16[256,1536]{1,0:T(8,128)(2,1)} collective-permute-done((bf16[256,1536]{1,0:T(8,128)(2,1)}, bf16[256,1536]{1,0:T(8,128)(2,1)}, u32[]{:S(2)}, u32[]{:S(2)}) %collective-permute-start.5) | collective-permute-done | bytes 786464 | tf_op jit(solution)/shard_map/ppermute | solution.py:124
  94.4 3.1 multiply_reduce_fusion
  97.5 3.3 pad_maximum_fusion.1.far_gate
  100.8 2.4 pad_maximum_fusion.2.far_up
  103.2 2.4 pad_maximum_fusion.3.far_down
  105.6 1.1 multiply_convert_fusion.x_ref.routed
  106.6 12.7 %all-gather.2.cloned.1.call-done.grads_ref = bf16[2048,1664]{1,0:T(8,128)(2,1)} async-done(((bf16[256,1664]{1,0:T(8,128)(2,1)}), bf16[2048,1664]{1,0:T(8,128)(2,1)}) %all-gather.2.cloned.1.call-update) | async-done | bytes 6815760 | tf_op jit(solution)/shard_map/all_gather | solution.py:1221
  119.3 184.6 %shard_map.229 = (bf16[2048,1536]{1,0:T(8,128)(2,1)}, f32[256,1664]{1,0:T(8,128)}, bf16[1536,512]{1,0:T(8,128)(2,1)}, bf16[1536,512]{1,0:T(8,128)(2,1)}, bf16[51...) custom-call(bf16[256,1536]{1,0:T(8,128)(2,1)} %multiply_convert_fusion.x_, ...), custom_call_target="tpu_custom_call" | custom-call | tf_op jit(solution)/shard_map/pallas_call | solution.py:702
  304.0 0.9 copy-done.38
  305.1 1.3 copy-done.23
  306.4 1.0 slice.85
  307.4 1.2 copy.60.heads
  309.8 1.2 copy.61.q_ref
  310.9 0.9 copy.62.k_ref
  311.8 0.8 copy.66.scale_in
  312.6 0.8 copy.64.sine
  313.5 0.8 copy.63.cosine
  314.3 0.9 copy.65.seg_col
  315.2 0.8 copy.59.scale_mid
  317.8 1.0 dynamic-slice_convert_fusion
  319.7 0.7 copy-done.26
  320.9 1.0 dynamic-slice_convert_fusion.1
  322.8 0.7 copy-done.25
  323.9 1.0 dynamic-slice_convert_fusion.2
  324.9 1.6 copy-done.24
  326.5 2.2 add_convert_fusion.1
  328.7 1.1 add_convert_fusion.2
  330.0 1.7 collective-permute-start.10
  332.1 1.6 collective-permute-start.12
  333.7 202.8 %shard_map.230 = (bf16[1536,768]{1,0:T(8,128)(2,1)}, bf16[1536,1280]{1,0:T(8,128)(2,1)}, f32[512,1536]{1,0:T(8,128)}, f32[24,1536]{1,0:T(8,128)}) custom-call(f32[256,1664]{1,0:T(8,128)} %get-tuple-element.40.back, f32[256,1536]{1,0:T(8,128)} %copy-done.2, f32[256,1]{1,0:T(8,128)} %copy.59.scale_mid, bf16[256,1536]{1,0:T(8,128)(2,1)} %multiply_convert_fusion.x_ref.routed, ...), custom_call_target="tpu_custom_call" | custom-call | tf_op jit(solution)/shard_map/pallas_call | solution.py:1108
  536.6 3.3 fusion.28
  540.7 0.8 copy-done.34
  541.5 2.3 convert_add_fusion.refs_2_
  544.4 1.7 convert_add_fusion.1.refs_1_
  546.6 1.7 convert_add_fusion.2.refs_0_
  549.8 2.5 slice.98
  552.7 2.9 pad_maximum_fusion
  555.6 1.8 maximum_select_fusion
  557.4 5.0 shard_map.231
  562.5 1.7 copy.73
  564.2 0.8 copy-done.1
  (161 shorter events, 15.2 us)
Async XLA Ops:
  7.2 1.4 copy-start
  7.2 1.5 copy-start.47
  7.2 112.1 %all-gather.2.cloned.1.call-start = ((), (), s32[]{:S(2)}) async-start(), calls=%async_computation.1 | async-start | bytes 7667712 | tf_op jit(solution)/shard_map/all_gather | solution.py:1221
  8.7 4.4 copy-start.15
  8.7 2.3 copy-start.44
  8.7 4.0 copy-start.7
  10.9 2.2 copy-start.46
  10.9 529.7 %reduce-scatter.2.cloned.1.call-start = ((), (), s32[]{:S(2)}) async-start(), calls=%async_computation.2 | async-start | bytes 7077888 | tf_op jit(solution)/shard_map/reduce_scatter | solution.py:1251
  14.2 5.5 copy-start.5
  14.8 4.8 copy-start.28
  16.8 4.4 copy-start.29
  16.8 4.4 copy-start.31
  17.7 2.0 copy-start.20
  19.7 1.8 copy-start.37
  19.7 1.8 copy-start.39
  29.6 6.1 %copy-start.13 = (bf16[768,1536]{1,0:T(8,128)(2,1)S(1)}, bf16[768,1536]{1,0:T(8,128)(2,1)}, u32[]{:S(2)}) copy-start(bf16[768,1536]{1,0:T(8,128)(2,1)} %w_out.1) | copy-start | bytes 7077892
  37.1 2.2 copy-start.6
  37.1 2.6 copy-start.16
  39.3 3.5 copy-start.17
  39.3 5.4 copy-start.18
  39.3 55.1 %collective-permute-start = (f32[256,1536]{1,0:T(8,128)}, f32[256,1536]{1,0:T(8,128)}, u32[]{:S(2)}, u32[]{:S(2)}) collective-permute-start(f32[256,1536]{1,0:T(8,128)} %constant_dynamic-slice_fusion.2), channel_id=1, source_target_pairs={{0,1},{1,0},{2,3},{3,2},{4,5},{5,4},{6,7},{7,6},{8,9},{9,8},{10,11... | collective-permute-start | bytes 4718600 | tf_op jit(solution)/shard_map/ppermute | solution.py:124
  39.8 21.4 %collective-permute-start.1 = (bf16[1536,256]{1,0:T(8,128)(2,1)S(1)}, bf16[1536,256]{1,0:T(8,128)(2,1)}, u32[]{:S(2)}, u32[]{:S(2)}) collective-permute-start(bf16[1536,256]{1,0:T(8,128)(2,1)S(1)} %dynamic-slice_bitcast_fusion.2), channel_id=1, source_target_pairs={{0,2},{2,0},{4,6},{6,4},{8,10},{10,8},{12,14},{14,12},{16,18},{18,... | collective-permute-start | bytes 2359304 | tf_op jit(solution)/shard_map/ppermute | solution.py:124
  43.7 34.4 %collective-permute-start.3 = (bf16[1536,256]{1,0:T(8,128)(2,1)}, bf16[1536,256]{1,0:T(8,128)(2,1)}, u32[]{:S(2)}, u32[]{:S(2)}) collective-permute-start(bf16[1536,256]{1,0:T(8,128)(2,1)} %dynamic-slice_bitcast_fusion.1), channel_id=1, source_target_pairs={{0,2},{2,0},{4,6},{6,4},{8,10},{10,8},{12,14},{14,12},{16,18},{18,... | collective-permute-start | bytes 2359304 | tf_op jit(solution)/shard_map/ppermute | solution.py:124
  45.6 48.8 %collective-permute-start.5 = (bf16[256,1536]{1,0:T(8,128)(2,1)}, bf16[256,1536]{1,0:T(8,128)(2,1)}, u32[]{:S(2)}, u32[]{:S(2)}) collective-permute-start(bf16[256,1536]{1,0:T(8,128)(2,1)} %dynamic-slice_bitcast_fusion), channel_id=1, source_target_pairs={{0,2},{2,0},{4,6},{6,4},{8,10},{10,8},{12,14},{14,12},{16,18},{18,... | collective-permute-start | bytes 2359304 | tf_op jit(solution)/shard_map/ppermute | solution.py:124
  61.2 36.3 %collective-permute-start.2 = (bf16[1536,256]{1,0:T(8,128)(2,1)}, bf16[1536,256]{1,0:T(8,128)(2,1)}, u32[]{:S(2)}, u32[]{:S(2)}) collective-permute-start(bf16[1536,256]{1,0:T(8,128)(2,1)} %collective-permute-done.1), channel_id=1, source_target_pairs={{0,1},{1,0},{2,3},{3,2},{4,5},{5,4},{6,7},{7,6},{8,9},{9,8},{10,11... | collective-permute-start | bytes 2359304 | tf_op jit(solution)/shard_map/ppermute | solution.py:124
  78.1 22.7 %collective-permute-start.4 = (bf16[1536,256]{1,0:T(8,128)(2,1)}, bf16[1536,256]{1,0:T(8,128)(2,1)S(1)}, u32[]{:S(2)}, u32[]{:S(2)}) collective-permute-start(bf16[1536,256]{1,0:T(8,128)(2,1)} %collective-permute-done.3), channel_id=1, source_target_pairs={{0,1},{1,0},{2,3},{3,2},{4,5},{5,4},{6,7},{7,6},{8,9},{9,8},{10,11... | collective-permute-start | bytes 2359304 | tf_op jit(solution)/shard_map/ppermute | solution.py:124
  94.3 8.8 %collective-permute-start.6 = (bf16[256,1536]{1,0:T(8,128)(2,1)}, bf16[256,1536]{1,0:T(8,128)(2,1)S(1)}, u32[]{:S(2)}, u32[]{:S(2)}) collective-permute-start(bf16[256,1536]{1,0:T(8,128)(2,1)} %collective-permute-done.5), channel_id=1, source_target_pairs={{0,1},{1,0},{2,3},{3,2},{4,5},{5,4},{6,7},{7,6},{8,9},{9,8},{10,11... | collective-permute-start | bytes 2359304 | tf_op jit(solution)/shard_map/ppermute | solution.py:124
  97.5 8.1 %copy-start.2 = (f32[256,1536]{1,0:T(8,128)}, f32[256,1536]{1,0:T(8,128)S(1)}, u32[]{:S(2)}) copy-start(f32[256,1536]{1,0:T(8,128)S(1)} %get-tuple-element.63.middle) | copy-start | bytes 4718596
  103.2 2.4 copy-start.45
  304.9 1.4 copy-start.23
  305.0 2.4 copy-start.32
  305.0 2.3 copy-start.42
  307.3 17.6 %collective-permute-start.9 = (bf16[256,1536]{1,0:T(8,128)(2,1)}, bf16[256,1536]{1,0:T(8,128)(2,1)}, u32[]{:S(2)}, u32[]{:S(2)}) collective-permute-start(bf16[256,1536]{1,0:T(8,128)(2,1)} %slice.85), channel_id=1, source_target_pairs={{0,1},{1,0},{2,3},{3,2},{4,5},{5,4},{6,7},{7,6},{8,9},{9,8},{10,11... | collective-permute-start | bytes 2359304 | tf_op jit(solution)/shard_map/ppermute | solution.py:124
  309.8 3.7 copy-start.30
  310.9 5.1 copy-start.22
  312.6 4.0 copy-start.21
  316.0 1.4 copy-start.27
  316.0 12.7 %collective-permute-start.8 = (bf16[1536,256]{1,0:T(8,128)(2,1)S(1)}, bf16[1536,256]{1,0:T(8,128)(2,1)S(1)}, u32[]{:S(2)}, u32[]{:S(2)}) collective-permute-start(bf16[1536,256]{1,0:T(8,128)(2,1)S(1)} %slice.83), channel_id=1, source_target_pairs={{0,1},{1,0},{2,3},{3,2},{4,5},{5,4},{6,7},{7,6},{8,9},{9,8},{10,11... | collective-permute-start | bytes 2359304 | tf_op jit(solution)/shard_map/ppermute | solution.py:124
  316.7 13.1 %collective-permute-start.7 = (bf16[1536,256]{1,0:T(8,128)(2,1)S(1)}, bf16[1536,256]{1,0:T(8,128)(2,1)S(1)}, u32[]{:S(2)}, u32[]{:S(2)}) collective-permute-start(bf16[1536,256]{1,0:T(8,128)(2,1)S(1)} %slice.81), channel_id=1, source_target_pairs={{0,1},{1,0},{2,3},{3,2},{4,5},{5,4},{6,7},{7,6},{8,9},{9,8},{10,11... | collective-permute-start | bytes 2359304 | tf_op jit(solution)/shard_map/ppermute | solution.py:124
  317.8 1.9 copy-start.12
  317.8 2.6 copy-start.26
  318.8 222.7 %collective-permute-start.16 = (bf16[256,1536]{1,0:T(8,128)(2,1)}, bf16[256,1536]{1,0:T(8,128)(2,1)}, u32[]{:S(2)}, u32[]{:S(2)}) collective-permute-start(bf16[256,1536]{1,0:T(8,128)(2,1)} %dynamic-slice_convert_fusion), channel_id=1, source_target_pairs={{0,1},{1,0},{2,3},{3,2},{4,5},{5,4},{6,7},{7,6},{8,9},{9,8},{10,11... | collective-permute-start | bytes 2359304 | tf_op jit(solution)/shard_map/ppermute | solution.py:124
  320.8 1.9 copy-start.10
  320.8 2.6 copy-start.25
  321.9 222.5 %collective-permute-start.15 = (bf16[1536,256]{1,0:T(8,128)(2,1)}, bf16[1536,256]{1,0:T(8,128)(2,1)}, u32[]{:S(2)}, u32[]{:S(2)}) collective-permute-start(bf16[1536,256]{1,0:T(8,128)(2,1)} %dynamic-slice_convert_fusion.1), channel_id=1, source_target_pairs={{0,1},{1,0},{2,3},{3,2},{4,5},{5,4},{6,7},{7,6},{8,9},{9,8},{10,11... | collective-permute-start | bytes 2359304 | tf_op jit(solution)/shard_map/ppermute | solution.py:124
  323.9 4.8 copy-start.8
  323.9 2.6 copy-start.24
  330.0 210.6 %collective-permute-start.10 = (bf16[1536,256]{1,0:T(8,128)(2,1)S(1)}, bf16[1536,256]{1,0:T(8,128)(2,1)S(1)}, u32[]{:S(2)}, u32[]{:S(2)}) collective-permute-start(bf16[1536,256]{1,0:T(8,128)(2,1)S(1)} %add_convert_fusion.3), channel_id=1, source_target_pairs={{0,2},{2,0},{4,6},{6,4},{8,10},{10,8},{12,14},{14,12},{16,18},{18,... | collective-permute-start | bytes 2359304 | tf_op jit(solution)/shard_map/ppermute | solution.py:124
  331.7 208.9 %collective-permute-start.11 = (bf16[1536,256]{1,0:T(8,128)(2,1)}, bf16[1536,256]{1,0:T(8,128)(2,1)S(1)}, u32[]{:S(2)}, u32[]{:S(2)}) collective-permute-start(bf16[1536,256]{1,0:T(8,128)(2,1)} %add_convert_fusion.2), channel_id=1, source_target_pairs={{0,2},{2,0},{4,6},{6,4},{8,10},{10,8},{12,14},{14,12},{16,18},{18,... | collective-permute-start | bytes 2359304 | tf_op jit(solution)/shard_map/ppermute | solution.py:124
  332.1 208.5 %collective-permute-start.12 = (bf16[256,1536]{1,0:T(8,128)(2,1)}, bf16[256,1536]{1,0:T(8,128)(2,1)S(1)}, u32[]{:S(2)}, u32[]{:S(2)}) collective-permute-start(bf16[256,1536]{1,0:T(8,128)(2,1)} %add_convert_fusion.1), channel_id=1, source_target_pairs={{0,2},{2,0},{4,6},{6,4},{8,10},{10,8},{12,14},{14,12},{16,18},{18,... | collective-permute-start | bytes 2359304 | tf_op jit(solution)/shard_map/ppermute | solution.py:124
  536.6 3.3 copy-start.43
  540.6 6.0 %collective-permute-start.14 = (bf16[1536,256]{1,0:T(8,128)(2,1)}, bf16[1536,256]{1,0:T(8,128)(2,1)}, u32[]{:S(2)}, u32[]{:S(2)}) collective-permute-start(bf16[1536,256]{1,0:T(8,128)(2,1)} %dynamic-slice_convert_fusion.2), channel_id=1, source_target_pairs={{0,1},{1,0},{2,3},{3,2},{4,5},{5,4},{6,7},{7,6},{8,9},{9,8},{10,11... | collective-permute-start | bytes 2359304 | tf_op jit(solution)/shard_map/ppermute | solution.py:124
  541.5 2.9 copy-start.11
  543.8 2.8 copy-start.9
  543.8 13.6 %collective-permute-start.19 = (f32[256,1536]{1,0:T(8,128)S(1)}, f32[256,1536]{1,0:T(8,128)S(1)}, u32[]{:S(2)}, u32[]{:S(2)}) collective-permute-start(f32[256,1536]{1,0:T(8,128)S(1)} %convert_add_fusion.refs_2_), channel_id=1, source_target_pairs={{0,1},{1,0},{2,3},{3,2},{4,5},{5,4},{6,7},{7,6},{8,9},{9,8},{10,11... | collective-permute-start | bytes 4718600 | tf_op jit(solution)/shard_map/ppermute | solution.py:124
  546.1 2.3 copy-start.3
  546.1 2.3 copy-start.35
  546.1 11.3 %collective-permute-start.18 = (f32[1536,256]{1,0:T(8,128)S(1)}, f32[1536,256]{1,0:T(8,128)S(1)}, u32[]{:S(2)}, u32[]{:S(2)}) collective-permute-start(f32[1536,256]{1,0:T(8,128)S(1)} %convert_add_fusion.1.refs_1_), channel_id=1, source_target_pairs={{0,1},{1,0},{2,3},{3,2},{4,5},{5,4},{6,7},{7,6},{8,9},{9,8},{10,11... | collective-permute-start | bytes 4718600 | tf_op jit(solution)/shard_map/ppermute | solution.py:124
  546.6 3.2 copy-start.4
  548.3 9.1 %collective-permute-start.17 = (f32[1536,256]{1,0:T(8,128)S(1)}, f32[1536,256]{1,0:T(8,128)S(1)}, u32[]{:S(2)}, u32[]{:S(2)}) collective-permute-start(f32[1536,256]{1,0:T(8,128)S(1)} %convert_add_fusion.2.refs_0_), channel_id=1, source_target_pairs={{0,1},{1,0},{2,3},{3,2},{4,5},{5,4},{6,7},{7,6},{8,9},{9,8},{10,11... | collective-permute-start | bytes 4718600 | tf_op jit(solution)/shard_map/ppermute | solution.py:124
  548.6 7.0 %collective-permute-start.13 = (bf16[256,1536]{1,0:T(8,128)(2,1)S(1)}, bf16[256,1536]{1,0:T(8,128)(2,1)S(1)}, u32[]{:S(2)}, u32[]{:S(2)}) collective-permute-start(bf16[256,1536]{1,0:T(8,128)(2,1)S(1)} %add_convert_fusion), channel_id=1, source_target_pairs={{0,1},{1,0},{2,3},{3,2},{4,5},{5,4},{6,7},{7,6},{8,9},{9,8},{10,11... | collective-permute-start | bytes 2359304 | tf_op jit(solution)/shard_map/ppermute | solution.py:124
  549.8 2.5 copy-start.14
  557.4 5.0 copy-start.19
  562.5 2.5 copy-start.1
  (6 other events, 5.5 us)
Sparse Core Ops, SparseCore 0:
  11.0 108.2 all-gather.1
  304.1 143.2 reduce-scatter.1

commit v6 on v5

--- a/solution.py
+++ b/solution.py
@@ -213,8 +213,10 @@
         self.exists = (self.A < a - 1, self.A > 0, self.B < b - 1, self.B > 0)
         self.some = me + 2 * (1 - 2 * (self.B % 2))
 
-    def greet(self):
+    def greet(self, further=()):
         barrier = pltpu.get_barrier_semaphore()
+        for device in further:
+            pl.semaphore_signal(barrier, inc=1, device_id=device, device_id_type=MESH)
         for device, there in zip(self.devices, self.exists):
 
             @pl.when(there)
@@ -226,7 +228,11 @@
         a, b = self.a, self.b
         ups = 2 - (self.A + 1) // a - (self.B + 1) // b
         downs = (self.A + a - 1) // a + (self.B + b - 1) // b
-        pl.semaphore_wait(barrier, ups + downs)
+        pl.semaphore_wait(barrier, ups + downs + len(further))
+
+
+def xor4(x, y):
+    return ((x // 2 + y // 2) % 2) * 2 + (x % 2 + y % 2) % 2
 
 
 def is_at(x, value):
@@ -523,10 +529,11 @@
 
 
 def experts_kernel(
-    a, b, rows, width,
+    a, b, rows, width, cores,
     x_ref, grads_ref, router_ref, near_gate, near_up, near_down, far_gate, far_up, far_down,
     moe_ref, out_ref, o_near_gate, o_near_up, o_near_down, o_far_gate, o_far_up, o_far_down,
-    xs, gs, weights, downs, lows, part, extras, stage, local, load, send, recv, stage_sem, store, *scratch,
+    xs, gs, weights, downs, lows, part, extras, stage, got_wide, got_down,
+    local, load, send, recv, stage_sem, store, core_send, core_recv, *scratch,
 ):
     spot = Spot(a, b)
     n = spot.n
@@ -553,7 +560,9 @@
         c.start()
     for i in range(1, n):
         grads_copy(i).start()
-    spot.greet()
+    core = lax.axis_index("tensor")
+    mates = [xor4(core, m) for m in range(1, cores)]
+    spot.greet([{"tensor": mate} for mate in mates])
     mine.wait()
     gather.forward(0)
     for c in arriving:
@@ -657,15 +666,58 @@
             return 0
 
         lax.fori_loop(0, width // tile, wide, 0)
+        give(e)
+
+    units = lows.shape[2] // cores
+
+    def blocks(e, k):
+        at = pl.ds(pl.multiple_of(k * units, units), units)
+        return (weights.at[2 * e, :, at], weights.at[2 * e + 1, :, at], downs.at[e, at, :])
+
+    def own(e):
+        return blocks(e, core if e == 0 else 0)
+
+    def gifts(e):
+        copies = []
+        for m, mate in enumerate(mates):
+            landing = (got_wide.at[e, m, 0], got_wide.at[e, m, 1], got_down.at[e, m])
+            for i, (src, dst) in enumerate(zip(blocks(e, mate if e == 0 else m + 1), landing)):
+                copies.append(
+                    pltpu.make_async_remote_copy(
+                        src_ref=src,
+                        dst_ref=dst,
+                        send_sem=core_send.at[e, m, i],
+                        recv_sem=core_recv.at[e, m, i],
+                        device_id={"tensor": mate},
+                        device_id_type=MESH,
+                    )
+                )
+        return copies
+
+    def give(e):
+        for c in gifts(e):
+            c.start()
+
+    def collect(e):
+        for c in gifts(e):
+            c.wait()
         outs = (o_near_gate, o_near_up, o_near_down) if e == 0 else (o_far_gate, o_far_up, o_far_down)
-        copies = [
-            pltpu.make_async_copy(weights.at[2 * e], outs[0], store.at[3 * e]),
-            pltpu.make_async_copy(weights.at[2 * e + 1], outs[1], store.at[3 * e + 1]),
-            pltpu.make_async_copy(downs.at[e], outs[2], store.at[3 * e + 2]),
-        ]
-        for c in copies:
+        for i, (view, out) in enumerate(zip(own(e), outs)):
+
+            def chunk(k, _, i=i, view=view):
+                size = view.shape[0] // 8
+                at = pl.ds(pl.multiple_of(k * size, 16), size)
+                total = view[at, :].astype(f32)
+                for m in range(len(mates)):
+                    got = got_wide[e, m, i, at, :] if i < 2 else got_down[e, m, at, :]
+                    total += got.astype(f32)
+                view[at, :] = total.astype(bf16)
+                return 0
+
+            lax.fori_loop(0, 8, chunk, 0)
+            c = pltpu.make_async_copy(view, out, store.at[3 * e + i])
             c.start()
-        return copies
+            stored.append(c)
 
     stored = []
 
@@ -676,8 +728,10 @@
         [
             (lambda: lax.fori_loop(2, a, back_own, 0)) if b == 2 else (lambda: None),
             moe_all,
-            lambda: stored.extend(weight_grads(1)),
-            lambda: stored.extend(weight_grads(0)),
+            lambda: weight_grads(1),
+            lambda: weight_grads(0),
+            lambda: collect(1),
+            lambda: collect(0),
         ]
     )
     line = total.a_line
@@ -689,7 +743,7 @@
         c.wait()
 
 
-def experts_call(rows_low, grads, router, near, far, dp_size, collective_id):
+def experts_call(rows_low, grads, router, near, far, dp_size, cores, collective_id):
     a, b = group_sizes(dp_size)
     n = a * b
     rows, width = rows_low.shape
@@ -698,9 +752,12 @@
     outs = [
         jax.ShapeDtypeStruct((n * rows, width), bf16),
         jax.ShapeDtypeStruct((rows, width + LANES), f32),
-    ] + [jax.ShapeDtypeStruct(x.shape, bf16) for x in near + far]
+    ] + [
+        jax.ShapeDtypeStruct(shape, bf16)
+        for shape in 2 * [(width, units // cores), (width, units // cores), (units // cores, width)]
+    ]
     return pl.pallas_call(
-        functools.partial(experts_kernel, a, b, rows, width),
+        functools.partial(experts_kernel, a, b, rows, width, cores),
         out_shape=outs,
         in_specs=[hbm, hbm, vmem] + [hbm] * 6,
         out_specs=[hbm, vmem] + [hbm] * 6,
@@ -713,16 +770,20 @@
             pltpu.VMEM((n * rows, width + LANES), bf16),
             pltpu.VMEM((n * rows, LANES), bf16),
             pltpu.VMEM((2, rows, width), bf16),
+            pltpu.VMEM((2, cores - 1, 2, width, units // cores), bf16),
+            pltpu.VMEM((2, cores - 1, units // cores, width), bf16),
             pltpu.SemaphoreType.DMA((7,)),
             pltpu.SemaphoreType.DMA((n,)),
             pltpu.SemaphoreType.DMA((n, 4, PIECES)),
             pltpu.SemaphoreType.DMA((n, PIECES)),
             pltpu.SemaphoreType.DMA((2,)),
             pltpu.SemaphoreType.DMA((6,)),
+            pltpu.SemaphoreType.DMA((2, cores - 1, 3)),
+            pltpu.SemaphoreType.DMA((2, cores - 1, 3)),
         ]
         + GroupSum.scratch(a, b, rows, width + LANES),
         compiler_params=pltpu.CompilerParams(
-            collective_id=collective_id, has_side_effects=True, vmem_limit_bytes=60 << 20
+            collective_id=collective_id, has_side_effects=True, vmem_limit_bytes=62 << 20
         ),
     )(rows_low, grads, router, *near, *far)
 
@@ -1201,14 +1262,6 @@
             x = jnp.concatenate([x, swap(x, "tensor", mask)], dim)
         return x
 
-    def relative_scatter(x, dim):
-        for mask in reversed(tensor_masks):
-            half = x.shape[dim] // 2
-            keep = lax.slice_in_dim(x, 0, half, axis=dim)
-            give = lax.slice_in_dim(x, half, 2 * half, axis=dim)
-            x = keep.astype(f32) + swap(give.astype(bf16), "tensor", mask).astype(f32)
-        return x
-
     far_set = [
         relative_gather(swap(my_units(w_gate[0], 1), "dp", 1), 1),
         relative_gather(swap(my_units(w_up[0], 1), "dp", 1), 1),
@@ -1246,20 +1299,15 @@
 
     near_set = [w_gate[0], w_up[0], w_down[0]]
     moe_part, back, *expert_parts = experts_call(
-        routed_low, grads, router_wide, near_set, far_set, dp_size, 0
+        routed_low, grads, router_wide, near_set, far_set, dp_size, tensor_size, 0
     )
     moe_total = lax.psum_scatter(
         moe_part, "dp", scatter_dimension=0, tiled=True, axis_index_groups=groups
     )
 
+    near_mine = expert_parts[:3]
+    returning = [swap(x, "dp", 1) for x in expert_parts[3:]]
     dims = (1, 1, 0)
-    near_mine = [
-        scatter_sum(x, "tensor", tensor_down, bf16, d) for x, d in zip(expert_parts[:3], dims)
-    ]
-    far_mine = [relative_scatter(x, d).astype(bf16) for x, d in zip(expert_parts[3:], dims)]
-    back, far_mine = lax.optimization_barrier((back, far_mine))
-    returning = [swap(x, "dp", 1) for x in far_mine]
-
     heads_width = heads_flat.shape[1]
     width_q, width_k = query_heads.shape[1] * head_size, key_heads.shape[1] * head_size
     qkv_width = width_q + 2 * width_k
@@ -1296,7 +1344,9 @@
     )
     block_mine = (middle + residual_scale * moe_total.astype(f32)).astype(bf16)
     block_out = gather_blocks(block_mine, "tensor", tensor_down)
-    expert_mine = [mine + away.astype(f32) for mine, away in zip(near_mine, returning)]
+    expert_mine = [
+        mine.astype(f32) + away.astype(f32) for mine, away in zip(near_mine, returning)
+    ]
     if tensor_size == 2:
         expert_grads = place(expert_mine, [swap(x, "tensor", 1) for x in expert_mine], dims)
     else:

time: 581 us -> 570 us (0.981)
  other arithmetic: 32.7 us -> 24.6 us
  local copies, waits for them, and re-layouts: 41.3 us -> 33.8 us
  Pallas kernels: 393 us -> 399 us
    pallas_call x1, Pallas kernels: 203 us -> 209 us  [attention_back(): pl.pallas_call(functools.partial(attention_back_kernel, dp_size, tensor_s...]
    unnamed x98 -> x96, local copies, waits for them, and re-layouts: 15.3 us -> 11 us
    ppermute x20 -> x14, starting transfers between devices: 12.5 us -> 10.6 us  [swap(): lax.ppermute(x, axis, [(i, i ^ mask) for i in range(lax.axis_size(axis))])]
    ppermute x20 -> x14, waiting for transfers between devices: 45.9 us -> 47.5 us  [swap(): lax.ppermute(x, axis, [(i, i ^ mask) for i in range(lax.axis_size(axis))])]
  transfers between devices with their start and end apart: 22 -> 16, of which waited for: 4 -> 4; matrix products, arithmetic and copies ran while one was open for 13% -> 11% of each run, Pallas kernels for 35% -> 37%
where the time goes in v6:
time: 570 us; the launch traced here: 562 us
  Pallas kernels  399 us (70%)
  waiting for transfers between devices  59 us (10%)
  local copies, waits for them, and re-layouts  33.8 us (6%)
  other arithmetic  24.6 us (4%)
  matrix products  18.7 us (3%)
  between operations  15.7 us (3%)
  starting transfers between devices  10.7 us (2%)
    pallas_call x1, Pallas kernels, attention_back(): pl.pallas_call(functools.partial(attention_back_kernel, dp_size, tensor_s...  209 us
    pallas_call x1, Pallas kernels, experts_call(): pl.pallas_call(functools.partial(experts_kernel, a, b, rows, width, cores...  185 us
    ppermute x14, waiting for transfers between devices, swap(): lax.ppermute(x, axis, [(i, i ^ mask) for i in range(lax.axis_size(axis))])  47.5 us
    all_gather x1, waiting for transfers between devices, per_device(): lax.all_gather(jnp.concatenate([grad_mine, picked_low], 1), 'dp', axis=0,...  11.5 us
  transfers between devices with their start and end apart: 16, of which 4 were waited for; matrix products, arithmetic and copies ran while one was open for 11% of the time, Pallas kernels for 37%

profile of v6, /device:TPU:0, one launch (start us, length us, event | category | flops | bytes accessed | tf_op | source)
XLA Modules:
  0.0 561.6 jit_solution(12004660439708697430)
XLA Ops:
  7.3 1.3 copy-done
  9.3 0.6 copy-done.30
  9.9 1.0 pad_maximum_fusion.4
  11.0 0.5 slice.54
  13.1 0.6 copy-done.44
  14.1 0.7 copy-done.23
  14.8 0.6 convolution_convert_fusion.v_ref
  15.4 0.8 copy.54
  16.4 1.0 fusion.19
  17.4 0.9 fusion.12
  18.3 1.9 fusion.35
  20.2 0.8 multiply_subtract_fusion
  21.0 1.4 fusion.36
  22.8 0.6 copy-done.31
  23.5 7.4 %fusion.30 = (f32[4,3,512]{2,1,0:T(4,128)S(1)}, f32[4,3,512,512]{2,3,1,0:T(8,128)}) fusion(pred[512,512]{0,1:T(8,128)(4,1)S(1)} %copy-done.36, bf16[512,4,3,32]{0,3,2,1:T(8,128)(2,1)S(1)} %bitcast.90, bf16[512,4,3,32]{0,3,2,1:T(8,128)(2,1)S(1)} %bitcast.89, bf16[512,4,32]{0,2,1:T(8,128)(2,1)S(1)} %copy-done.33, bf16[512,4,32]{0,2,1:T(8,128)(2,1)S(1)} %copy-done.31), kind=kOutput, calls=%fused_computation.73 | convolution fusion | flops 417333760 | bytes 13918208 | tf_op jit(solution)/shard_map/sub | solution.py:72
  30.9 6.0 %fusion.11 = bf16[4,64,3,512]{3,1,2,0:T(8,128)(2,1)S(1)} fusion(bf16[512,4,64,1]{0,2,3,1:T(8,128)(2,1)S(1)} %bitcast.94, f32[4,3,512,512]{2,3,1,0:T(8,128)} %get-tuple-element.69, f32[4,3,512]{2,1,0:T(4,128)S(1)} %get-tuple-element.68), kind=kOutput, calls=%fused_computation.27 | convolution fusion | flops 409337856 | bytes 13656064 | tf_op jit(solution)/shard_map/hgqk,khd->qhgd/dot_general | solution.py:75
  37.0 1.4 fusion.37
  38.4 1.3 constant_dynamic-slice_fusion.2
  39.7 0.9 copy-done.6
  41.1 2.9 collective-permute-start.1
  44.0 0.9 dynamic-slice_bitcast_fusion.1
  45.0 1.0 collective-permute-start.3
  46.0 1.1 collective-permute-start.5
  47.1 15.4 %collective-permute-done.1 = bf16[1536,256]{1,0:T(8,128)(2,1)} collective-permute-done((bf16[1536,256]{1,0:T(8,128)(2,1)S(1)}, bf16[1536,256]{1,0:T(8,128)(2,1)}, u32[]{:S(2)}, u32[]{:S(2)}) %collective-permute-start.1) | collective-permute-done | bytes 786464 | tf_op jit(solution)/shard_map/ppermute | solution.py:124
  62.7 0.8 pad.4.router_ref.router
  63.6 15.8 %collective-permute-done.3 = bf16[1536,256]{1,0:T(8,128)(2,1)} collective-permute-done((bf16[1536,256]{1,0:T(8,128)(2,1)}, bf16[1536,256]{1,0:T(8,128)(2,1)}, u32[]{:S(2)}, u32[]{:S(2)}) %collective-permute-start.3) | collective-permute-done | bytes 786464 | tf_op jit(solution)/shard_map/ppermute | solution.py:124
  79.3 16.3 %collective-permute-done.5 = bf16[256,1536]{1,0:T(8,128)(2,1)} collective-permute-done((bf16[256,1536]{1,0:T(8,128)(2,1)S(1)}, bf16[256,1536]{1,0:T(8,128)(2,1)}, u32[]{:S(2)}, u32[]{:S(2)}) %collective-permute-start.5) | collective-permute-done | bytes 786464 | tf_op jit(solution)/shard_map/ppermute | solution.py:124
  95.7 3.1 multiply_reduce_fusion
  98.8 3.2 pad_maximum_fusion.1.far_gate
  102.0 2.4 pad_maximum_fusion.2.far_up
  104.4 2.4 pad_maximum_fusion.3.far_down
  106.8 1.1 multiply_convert_fusion.x_ref.routed
  107.9 11.5 %all-gather.2.cloned.1.call-done.grads_ref = bf16[2048,1664]{1,0:T(8,128)(2,1)} async-done(((bf16[256,1664]{1,0:T(8,128)(2,1)}), bf16[2048,1664]{1,0:T(8,128)(2,1)}) %all-gather.2.cloned.1.call-update) | async-done | bytes 6815760 | tf_op jit(solution)/shard_map/all_gather | solution.py:1274
  119.3 184.8 %shard_map.229 = (bf16[2048,1536]{1,0:T(8,128)(2,1)}, f32[256,1664]{1,0:T(8,128)}, bf16[1536,256]{1,0:T(8,128)(2,1)}, bf16[1536,256]{1,0:T(8,128)(2,1)}, bf16[25...) custom-call(bf16[256,1536]{1,0:T(8,128)(2,1)} %multiply_convert_fusion.x_, ...), custom_call_target="tpu_custom_call" | custom-call | tf_op jit(solution)/shard_map/pallas_call | solution.py:759
  304.2 1.1 copy-done.15
  305.3 1.2 copy.60.heads
  306.6 0.6 broadcast_in_dim.44.moe_gain
  307.2 0.6 broadcast_in_dim.45.gain
  307.8 1.2 copy.61.q_ref
  309.0 0.8 copy.62.k_ref
  309.9 0.8 copy.66.scale_in
  310.7 0.8 copy.64.sine
  311.6 0.8 copy.63.cosine
  312.4 0.9 copy.65.seg_col
  313.3 0.8 copy.59.scale_mid
  314.1 1.4 collective-permute-start.7
  315.5 0.6 collective-permute-start.8
  316.1 1.4 collective-permute-start.9
  317.6 209.4 %shard_map.230 = (bf16[1536,768]{1,0:T(8,128)(2,1)}, bf16[1536,1280]{1,0:T(8,128)(2,1)}, f32[512,1536]{1,0:T(8,128)}, f32[24,1536]{1,0:T(8,128)}) custom-call(f32[256,1664]{1,0:T(8,128)} %get-tuple-element.32.back, f32[256,1536]{1,0:T(8,128)} %copy-done.2, f32[256,1]{1,0:T(8,128)} %copy.59.scale_mid, bf16[256,1536]{1,0:T(8,128)(2,1)} %multiply_convert_fusion.x_ref.routed, ...), custom_call_target="tpu_custom_call" | custom-call | tf_op jit(solution)/shard_map/pallas_call | solution.py:1169
  526.9 1.5 slice_bitcast_fusion
  528.5 3.4 fusion.28
  531.9 0.8 copy-done.28
  532.7 1.5 convert_add_fusion.refs_2_
  534.5 0.5 collective-permute-start.12
  535.7 0.5 collective-permute-start.11
  536.2 0.7 copy-done.3
  537.1 0.5 collective-permute-start.10
  537.7 1.5 slice_reduce_fusion
  539.2 2.5 slice.74
  542.1 2.9 pad_maximum_fusion
  545.0 1.8 maximum_select_fusion
  546.8 5.0 shard_map.231
  551.8 1.7 copy.73
  553.5 0.8 copy-done.1
  (135 shorter events, 5.4 us)
Async XLA Ops:
  7.2 1.4 copy-start
  7.2 1.5 copy-start.46
  7.2 112.1 %all-gather.2.cloned.1.call-start = ((), (), s32[]{:S(2)}) async-start(), calls=%async_computation.1 | async-start | bytes 7667712 | tf_op jit(solution)/shard_map/all_gather | solution.py:1274
  8.7 4.4 copy-start.10
  8.7 2.3 copy-start.38
  8.7 4.0 copy-start.7
  9.3 0.6 copy-start.30
  10.9 2.7 copy-start.42
  10.9 520.9 %reduce-scatter.2.cloned.1.call-start = ((), (), s32[]{:S(2)}) async-start(), calls=%async_computation.2 | async-start | bytes 7077888 | tf_op jit(solution)/shard_map/reduce_scatter | solution.py:1304
  13.1 0.6 copy-start.44
  13.7 1.1 copy-start.23
  14.8 6.2 %copy-start.5 = (bf16[512,1536]{1,0:T(8,128)(2,1)}, bf16[512,1536]{1,0:T(8,128)(2,1)S(1)}, u32[]{:S(2)}) copy-start(bf16[512,1536]{1,0:T(8,128)(2,1)S(1)} %fusion.8.normed) | copy-start | bytes 4718596
  15.4 4.8 copy-start.20
  17.4 5.1 copy-start.21
  18.3 2.7 copy-start.17
  22.4 0.9 copy-start.31
  22.4 1.0 copy-start.33
  22.5 1.1 copy-start.36
  22.7 8.2 %copy-start.18 = (bf16[512,12,32]{0,2,1:T(8,128)(2,1)}, bf16[512,12,32]{0,2,1:T(8,128)(2,1)S(1)}, u32[]{:S(2)}) copy-start(bf16[512,12,32]{0,2,1:T(8,128)(2,1)S(1)} %get-tuple-element.62) | copy-start | bytes 1179652
  23.5 7.4 %copy-start.35 = (bf16[512,256]{0,1:T(8,128)(2,1)S(1)}, bf16[512,256]{0,1:T(8,128)(2,1)}, u32[]{:S(2)}) copy-start(bf16[512,256]{0,1:T(8,128)(2,1)} %copy.54) | copy-start | bytes 786436
  30.9 6.0 %copy-start.8 = (bf16[768,1536]{1,0:T(8,128)(2,1)S(1)}, bf16[768,1536]{1,0:T(8,128)(2,1)}, u32[]{:S(2)}) copy-start(bf16[768,1536]{1,0:T(8,128)(2,1)} %w_out.1) | copy-start | bytes 7077892
  36.9 1.4 copy-start.14
  38.4 2.2 copy-start.6
  38.4 2.7 copy-start.11
  40.6 3.5 copy-start.12
  40.6 5.3 copy-start.13
  40.6 55.1 %collective-permute-start = (f32[256,1536]{1,0:T(8,128)}, f32[256,1536]{1,0:T(8,128)}, u32[]{:S(2)}, u32[]{:S(2)}) collective-permute-start(f32[256,1536]{1,0:T(8,128)} %constant_dynamic-slice_fusion.2), channel_id=1, source_target_pairs={{0,1},{1,0},{2,3},{3,2},{4,5},{5,4},{6,7},{7,6},{8,9},{9,8},{10,11... | collective-permute-start | bytes 4718600 | tf_op jit(solution)/shard_map/ppermute | solution.py:124
  41.1 21.4 %copy-start.40 = (bf16[1536,16]{0,1:T(8,128)(2,1)S(1)}, bf16[1536,16]{0,1:T(8,128)(2,1)}, u32[]{:S(2)}) copy-start(bf16[1536,16]{0,1:T(8,128)(2,1)} %param.21) | copy-start | bytes 147460
  41.1 21.3 %collective-permute-start.1 = (bf16[1536,256]{1,0:T(8,128)(2,1)S(1)}, bf16[1536,256]{1,0:T(8,128)(2,1)}, u32[]{:S(2)}, u32[]{:S(2)}) collective-permute-start(bf16[1536,256]{1,0:T(8,128)(2,1)S(1)} %dynamic-slice_bitcast_fusion.2), channel_id=1, source_target_pairs={{0,2},{2,0},{4,6},{6,4},{8,10},{10,8},{12,14},{14,12},{16,18},{18,... | collective-permute-start | bytes 2359304 | tf_op jit(solution)/shard_map/ppermute | solution.py:124
  45.0 34.4 %collective-permute-start.3 = (bf16[1536,256]{1,0:T(8,128)(2,1)}, bf16[1536,256]{1,0:T(8,128)(2,1)}, u32[]{:S(2)}, u32[]{:S(2)}) collective-permute-start(bf16[1536,256]{1,0:T(8,128)(2,1)} %dynamic-slice_bitcast_fusion.1), channel_id=1, source_target_pairs={{0,2},{2,0},{4,6},{6,4},{8,10},{10,8},{12,14},{14,12},{16,18},{18,... | collective-permute-start | bytes 2359304 | tf_op jit(solution)/shard_map/ppermute | solution.py:124
  46.0 49.7 %collective-permute-start.5 = (bf16[256,1536]{1,0:T(8,128)(2,1)S(1)}, bf16[256,1536]{1,0:T(8,128)(2,1)}, u32[]{:S(2)}, u32[]{:S(2)}) collective-permute-start(bf16[256,1536]{1,0:T(8,128)(2,1)S(1)} %dynamic-slice_bitcast_fusion), channel_id=1, source_target_pairs={{0,2},{2,0},{4,6},{6,4},{8,10},{10,8},{12,14},{14,12},{16,18},{18,... | collective-permute-start | bytes 2359304 | tf_op jit(solution)/shard_map/ppermute | solution.py:124
  62.5 36.3 %collective-permute-start.2 = (bf16[1536,256]{1,0:T(8,128)(2,1)}, bf16[1536,256]{1,0:T(8,128)(2,1)}, u32[]{:S(2)}, u32[]{:S(2)}) collective-permute-start(bf16[1536,256]{1,0:T(8,128)(2,1)} %collective-permute-done.1), channel_id=1, source_target_pairs={{0,1},{1,0},{2,3},{3,2},{4,5},{5,4},{6,7},{7,6},{8,9},{9,8},{10,11... | collective-permute-start | bytes 2359304 | tf_op jit(solution)/shard_map/ppermute | solution.py:124
  79.3 22.7 %collective-permute-start.4 = (bf16[1536,256]{1,0:T(8,128)(2,1)}, bf16[1536,256]{1,0:T(8,128)(2,1)S(1)}, u32[]{:S(2)}, u32[]{:S(2)}) collective-permute-start(bf16[1536,256]{1,0:T(8,128)(2,1)} %collective-permute-done.3), channel_id=1, source_target_pairs={{0,1},{1,0},{2,3},{3,2},{4,5},{5,4},{6,7},{7,6},{8,9},{9,8},{10,11... | collective-permute-start | bytes 2359304 | tf_op jit(solution)/shard_map/ppermute | solution.py:124
  95.7 8.7 %collective-permute-start.6 = (bf16[256,1536]{1,0:T(8,128)(2,1)}, bf16[256,1536]{1,0:T(8,128)(2,1)S(1)}, u32[]{:S(2)}, u32[]{:S(2)}) collective-permute-start(bf16[256,1536]{1,0:T(8,128)(2,1)} %collective-permute-done.5), channel_id=1, source_target_pairs={{0,1},{1,0},{2,3},{3,2},{4,5},{5,4},{6,7},{7,6},{8,9},{9,8},{10,11... | collective-permute-start | bytes 2359304 | tf_op jit(solution)/shard_map/ppermute | solution.py:124
  98.8 8.0 %copy-start.2 = (f32[256,1536]{1,0:T(8,128)}, f32[256,1536]{1,0:T(8,128)S(1)}, u32[]{:S(2)}) copy-start(f32[256,1536]{1,0:T(8,128)S(1)} %get-tuple-element.55.middle) | copy-start | bytes 4718596
  104.4 2.4 copy-start.41
  304.2 1.1 copy-start.15
  305.3 1.2 copy-start.45
  305.3 1.8 copy-start.43
  305.3 2.4 copy-start.19
  307.8 1.2 copy-start.32
  307.8 1.2 copy-start.34
  307.8 2.8 copy-start.22
  307.8 2.8 copy-start.37
  309.0 3.4 copy-start.39
  314.1 217.7 %collective-permute-start.7 = (bf16[1536,256]{1,0:T(8,128)(2,1)}, bf16[1536,256]{1,0:T(8,128)(2,1)S(1)}, u32[]{:S(2)}, u32[]{:S(2)}) collective-permute-start(bf16[1536,256]{1,0:T(8,128)(2,1)} %get-tuple-element.34), channel_id=1, source_target_pairs={{0,2},{2,0},{4,6},{6,4},{8,10},{10,8},{12,14},{14,12},{16,18},{18,... | collective-permute-start | bytes 2359304 | tf_op jit(solution)/shard_map/ppermute | solution.py:124
  315.5 216.3 %collective-permute-start.8 = (bf16[1536,256]{1,0:T(8,128)(2,1)}, bf16[1536,256]{1,0:T(8,128)(2,1)S(1)}, u32[]{:S(2)}, u32[]{:S(2)}) collective-permute-start(bf16[1536,256]{1,0:T(8,128)(2,1)} %get-tuple-element.35), channel_id=1, source_target_pairs={{0,2},{2,0},{4,6},{6,4},{8,10},{10,8},{12,14},{14,12},{16,18},{18,... | collective-permute-start | bytes 2359304 | tf_op jit(solution)/shard_map/ppermute | solution.py:124
  316.1 215.7 %collective-permute-start.9 = (bf16[256,1536]{1,0:T(8,128)(2,1)}, bf16[256,1536]{1,0:T(8,128)(2,1)}, u32[]{:S(2)}, u32[]{:S(2)}) collective-permute-start(bf16[256,1536]{1,0:T(8,128)(2,1)} %get-tuple-element.36), channel_id=1, source_target_pairs={{0,2},{2,0},{4,6},{6,4},{8,10},{10,8},{12,14},{14,12},{16,18},{18,... | collective-permute-start | bytes 2359304 | tf_op jit(solution)/shard_map/ppermute | solution.py:124
  528.5 4.3 copy-start.27
  531.8 0.9 copy-start.28
  532.7 1.6 copy-start.26
  532.7 1.6 copy-start.29
  534.2 12.6 %collective-permute-start.13 = (f32[256,1536]{1,0:T(8,128)S(1)}, f32[256,1536]{1,0:T(8,128)S(1)}, u32[]{:S(2)}, u32[]{:S(2)}) collective-permute-start(f32[256,1536]{1,0:T(8,128)S(1)} %convert_add_fusion.refs_2_), channel_id=1, source_target_pairs={{0,1},{1,0},{2,3},{3,2},{4,5},{5,4},{6,7},{7,6},{8,9},{9,8},{10,11... | collective-permute-start | bytes 4718600 | tf_op jit(solution)/shard_map/ppermute | solution.py:124
  534.3 1.1 copy-start.24
  534.3 1.9 copy-start.25
  534.5 12.3 %collective-permute-start.12 = (f32[1536,256]{1,0:T(8,128)S(1)}, f32[1536,256]{1,0:T(8,128)S(1)}, u32[]{:S(2)}, u32[]{:S(2)}) collective-permute-start(f32[1536,256]{1,0:T(8,128)S(1)} %convert_add_fusion.1.refs_1_), channel_id=1, source_target_pairs={{0,1},{1,0},{2,3},{3,2},{4,5},{5,4},{6,7},{7,6},{8,9},{9,8},{10,11... | collective-permute-start | bytes 4718600 | tf_op jit(solution)/shard_map/ppermute | solution.py:124
  535.5 1.5 copy-start.3
  535.5 3.7 copy-start.4
  535.7 11.1 %collective-permute-start.11 = (f32[1536,256]{1,0:T(8,128)S(1)}, f32[1536,256]{1,0:T(8,128)S(1)}, u32[]{:S(2)}, u32[]{:S(2)}) collective-permute-start(f32[1536,256]{1,0:T(8,128)S(1)} %convert_add_fusion.2.refs_0_), channel_id=1, source_target_pairs={{0,1},{1,0},{2,3},{3,2},{4,5},{5,4},{6,7},{7,6},{8,9},{9,8},{10,11... | collective-permute-start | bytes 4718600 | tf_op jit(solution)/shard_map/ppermute | solution.py:124
  537.1 7.8 %collective-permute-start.10 = (bf16[256,1536]{1,0:T(8,128)(2,1)S(1)}, bf16[256,1536]{1,0:T(8,128)(2,1)S(1)}, u32[]{:S(2)}, u32[]{:S(2)}) collective-permute-start(bf16[256,1536]{1,0:T(8,128)(2,1)S(1)} %add_convert_fusion), channel_id=1, source_target_pairs={{0,1},{1,0},{2,3},{3,2},{4,5},{5,4},{6,7},{7,6},{8,9},{9,8},{10,11... | collective-permute-start | bytes 2359304 | tf_op jit(solution)/shard_map/ppermute | solution.py:124
  539.2 2.5 copy-start.9
  546.8 5.0 copy-start.16
  551.8 2.5 copy-start.1
Sparse Core Ops, SparseCore 0:
  11.1 108.2 all-gather.1
  304.3 168.6 reduce-scatter.1

commit v7 on v6

--- a/solution.py
+++ b/solution.py
@@ -17,99 +17,6 @@
 attn_scale = 0.015625
 rope_base = 10000.0
 masked_score = -1e30
-
-
-def positions_of(segment):
-    position_index = jnp.arange(segment.shape[0], dtype=jnp.int32)
-    earlier = jnp.concatenate([segment[:1] - 1, segment[:-1]])
-    starts = lax.cummax(jnp.where(segment != earlier, position_index, 0), axis=0)
-    return position_index - starts
-
-
-def rope_tables(segment, head_size):
-    position = positions_of(segment).astype(f32)
-    frequency = rope_base ** (-jnp.arange(head_size // 2, dtype=f32) * 2.0 / head_size)
-    angle = position[:, None] * frequency[None, :]
-    return (jnp.cos(angle)[:, None, :], jnp.sin(angle)[:, None, :])
-
-
-def apply_rotation(heads_in, cosine_table, sine_values):
-    middle_index = heads_in.shape[-1] // 2
-    first_half = heads_in[..., :middle_index]
-    second_half = heads_in[..., middle_index:]
-    return jnp.concatenate(
-        [
-            first_half * cosine_table - second_half * sine_values,
-            second_half * cosine_table + first_half * sine_values,
-        ],
-        axis=-1,
-    )
-
-
-def block_scores(query_heads, key_heads, segment):
-    kv_count = key_heads.shape[1]
-    length = query_heads.shape[0]
-    grouped = query_heads.reshape(length, kv_count, -1, query_heads.shape[2])
-    raw_scores = (
-        jnp.einsum("qhgd,khd->hgqk", grouped, key_heads, preferred_element_type=f32) * attn_scale
-    )
-    index = jnp.arange(length, dtype=jnp.int32)
-    allowed = (index[:, None] >= index[None, :]) & (segment[:, None] == segment[None, :])
-    return (jnp.where(allowed, raw_scores, masked_score), grouped)
-
-
-def attend_forward(normed, segment, tables, w_query, key_weight, value_weight, head_size):
-    length = normed.shape[0]
-
-    def heads(weight):
-        return jnp.dot(normed, weight, preferred_element_type=f32).reshape(length, -1, head_size)
-
-    query_heads = apply_rotation(heads(w_query), *tables).astype(bf16)
-    key_heads = apply_rotation(heads(key_weight), *tables).astype(bf16)
-    value_heads = heads(value_weight).astype(bf16)
-    scores, _ = block_scores(query_heads, key_heads, segment)
-    largest = jnp.max(scores, axis=-1, keepdims=True)
-    weights_raw = jnp.exp(scores - largest)
-    totals = jnp.sum(weights_raw, axis=-1, keepdims=True)
-    probs_low = (weights_raw / totals).astype(bf16)
-    head_out = jnp.einsum("hgqk,khd->qhgd", probs_low, value_heads, preferred_element_type=f32)
-    return (
-        head_out.reshape(length, -1).astype(bf16),
-        query_heads,
-        key_heads,
-        value_heads,
-        (largest + jnp.log(totals))[..., 0],
-    )
-
-
-def attend_backward(query_heads, key_heads, value_heads, log_sums, heads_grad, segment, tables):
-    length = query_heads.shape[0]
-    cosine_table, sine_values = tables
-    scores, grouped = block_scores(query_heads, key_heads, segment)
-    probability = jnp.exp(scores - log_sums[..., None])
-    probs_low = probability.astype(bf16)
-    grad_grouped = heads_grad.reshape(grouped.shape)
-    prob_grad = jnp.einsum(
-        "qhgd,khd->hgqk", grad_grouped, value_heads, preferred_element_type=f32
-    )
-    weighted = jnp.sum(probability * prob_grad, axis=-1, keepdims=True)
-    score_low = (probability * (prob_grad - weighted)).astype(bf16)
-    query_part = (
-        jnp.einsum("hgqk,khd->qhgd", score_low, key_heads, preferred_element_type=f32) * attn_scale
-    ).reshape(query_heads.shape)
-    key_sum = (
-        jnp.einsum("hgqk,qhgd->khd", score_low, grouped, preferred_element_type=f32) * attn_scale
-    )
-    value_sum = jnp.einsum(
-        "hgqk,qhgd->khd", probs_low, grad_grouped, preferred_element_type=f32
-    )
-    query_low = apply_rotation(query_part, cosine_table, -sine_values).astype(bf16)
-    key_low = apply_rotation(key_sum, cosine_table, -sine_values).astype(bf16)
-    return (
-        query_low.reshape(length, -1),
-        key_low.reshape(length, -1),
-        value_sum.astype(bf16).reshape(length, -1),
-    )
 
 
 def bit_masks(size):
@@ -265,13 +172,14 @@
     )
 
 
-PIECES = 2
 SUM_PIECES = 4
 
 
 class LineGather:
     def __init__(self, spot, buf, rows, send, recv):
         self.spot, self.buf, self.rows, self.send, self.recv = spot, buf, rows, send, recv
+        few = max(16, rows * 3 // 16 // 16 * 16)
+        self.parts = ((0, rows - few, False), (rows - few, few, True))
 
     def coords(self, i):
         s = self.spot
@@ -284,43 +192,45 @@
         A, B = self.coords(i)
         return pl.multiple_of((A * self.spot.b + B) * self.rows, 16)
 
-    def copies(self, block, way, device):
-        size = self.rows // PIECES
-        return [
-            remote_to(there, there, self.send.at[block, way, p], self.recv.at[block, p], device)
-            for p in range(PIECES)
-            for there in [self.buf.at[pl.ds(pl.multiple_of(block * self.rows + p * size, 16), size)]]
-        ]
-
-    def each_way(self, i, act):
+    def copy(self, p, block, way, device):
+        start, size, _ = self.parts[p]
+        there = self.buf.at[pl.ds(pl.multiple_of(block * self.rows + start, 16), size)]
+        return remote_to(there, there, self.send.at[block, way, p], self.recv.at[block, p], device)
+
+    def each_way(self, i, p, act):
         s = self.spot
         A, B = self.coords(i)
         block = A * s.b + B
-        same = B == s.B
+        if self.parts[p][2]:
+            along_a, along_b = True, A == s.A
+        else:
+            along_a, along_b = B == s.B, True
         conditions = (
-            same & (A <= s.A) & s.exists[0],
-            same & (A >= s.A) & s.exists[1],
-            (B <= s.B) & s.exists[2],
-            (B >= s.B) & s.exists[3],
+            along_a & (A <= s.A) & s.exists[0],
+            along_a & (A >= s.A) & s.exists[1],
+            along_b & (B <= s.B) & s.exists[2],
+            along_b & (B >= s.B) & s.exists[3],
         )
         for way, (condition, device) in enumerate(zip(conditions, s.devices)):
 
             @pl.when(condition)
             def _(way=way, device=device):
-                for c in self.copies(block, way, device):
-                    act(c)
-
-    def wait(self, i):
+                act(self.copy(p, block, way, device))
+
+    def arrive(self, i):
         A, B = self.coords(i)
-        for c in self.copies(A * self.spot.b + B, 0, self.spot.some):
-            c.wait_recv()
-
-    def forward(self, i):
-        self.each_way(i, lambda c: c.start())
+        for p in range(len(self.parts)):
+            self.copy(p, A * self.spot.b + B, 0, self.spot.some).wait_recv()
+            self.each_way(i, p, lambda c: c.start())
+
+    def begin(self):
+        for p in range(len(self.parts)):
+            self.each_way(0, p, lambda c: c.start())
 
     def finish(self):
         def one(i, _):
-            self.each_way(i, lambda c: c.wait_send())
+            for p in range(len(self.parts)):
+                self.each_way(i, p, lambda c: c.wait_send())
             return 0
 
         lax.fori_loop(0, self.spot.n, one, 0)
@@ -564,7 +474,7 @@
     mates = [xor4(core, m) for m in range(1, cores)]
     spot.greet([{"tensor": mate} for mate in mates])
     mine.wait()
-    gather.forward(0)
+    gather.begin()
     for c in arriving:
         c.wait()
     lane = lax.broadcasted_iota(jnp.int32, (rows, LANES), 1)
@@ -584,8 +494,7 @@
 
                 @pl.when(i + 1 < n)
                 def _():
-                    gather.wait(i + 1)
-                    gather.forward(i + 1)
+                    gather.arrive(i + 1)
 
             column = jnp.sum(jnp.where(lane == expert, gates, 0.0), axis=1, keepdims=True)
             x = xs[at, :]
@@ -774,8 +683,8 @@
             pltpu.VMEM((2, cores - 1, units // cores, width), bf16),
             pltpu.SemaphoreType.DMA((7,)),
             pltpu.SemaphoreType.DMA((n,)),
-            pltpu.SemaphoreType.DMA((n, 4, PIECES)),
-            pltpu.SemaphoreType.DMA((n, PIECES)),
+            pltpu.SemaphoreType.DMA((n, 4, 2)),
+            pltpu.SemaphoreType.DMA((n, 2)),
             pltpu.SemaphoreType.DMA((2,)),
             pltpu.SemaphoreType.DMA((6,)),
             pltpu.SemaphoreType.DMA((2, cores - 1, 3)),
@@ -855,16 +764,16 @@
         self.where = [j * self.size for j in range(len(orders))]
         self.sums, self.backs = {}, {}
 
-    def sum_step(self, j, step):
+    def sum_send(self, j, step):
         count = self.size >> (step + 1)
         mask = self.orders[j][step]
         _, bit = peer_of(mask)
         keep = pl.multiple_of(self.where[j] + bit * count, 16)
         give = pl.multiple_of(self.where[j] + (1 - bit) * count, 16)
         acc, got = self.acc, self.got
+        p0 = j * self.size + (self.size - (self.size >> max(step - 1, 0)))
         if step > 0:
             self.sums[j, step - 1].wait_recv()
-            p0 = j * self.size + (self.size - (self.size >> (step - 1)))
             add_rows(acc, give, acc, give, got, p0 + pl.multiple_of((1 - bit) * count, 16), count, bf16)
         g0 = j * self.size + (self.size - (self.size >> step))
         c = remote(
@@ -876,9 +785,13 @@
         )
         c.start()
         self.sums[j, step] = c
-        if step > 0:
-            add_rows(acc, keep, acc, keep, got, p0 + pl.multiple_of(bit * count, 16), count, bf16)
         self.where[j] = keep
+
+        def stay():
+            if step > 0:
+                add_rows(acc, keep, acc, keep, got, p0 + pl.multiple_of(bit * count, 16), count, bf16)
+
+        return stay
 
     def back_step(self, j, step):
         count = self.size >> (step + 1)
@@ -903,8 +816,13 @@
         per_group = len(self.orders) // self.groups
 
         def event(g, kind, step):
-            for j in range(g * per_group, (g + 1) * per_group):
-                (self.sum_step if kind == "sum" else self.back_step)(j, step)
+            members = range(g * per_group, (g + 1) * per_group)
+            if kind == "sum":
+                for stay in [self.sum_send(j, step) for j in members]:
+                    stay()
+            else:
+                for j in members:
+                    self.back_step(j, step)
 
         return [
             functools.partial(event, *e) for e in reduce_schedule(self.k, self.groups)
@@ -939,9 +857,9 @@
 
 def attention_back_kernel(
     dp_size, tensor_size, orders_o, groups_o, orders_q, groups_q,
-    back, middle, scale_mid, routed, grad_top, picked, router, moe_gain,
+    back, middle, routed, grad_top, picked, router, moe_gain,
     heads, q_ref, k_ref, v_ref, w_out, w_query, w_key, w_value, normed, cosine, sine,
-    seg_col, seg_row, hidden, gain, scale_in,
+    seg_col, seg_row, hidden, gain,
     out_o, out_q, out_input, small_out,
     branch, middle_grad, bias, heads_grad, qkv_low, scratch_q, scratch_k, scratch_v,
     acc_o, got_o, acc_q, got_q, shares, got_shares, small_got,
@@ -983,7 +901,7 @@
     small_out[pl.ds(0, experts), :] = mm(logit_grad, x, TN)[:experts]
     routed_grad = back[:, pl.ds(0, width)] + mm(logit_grad, router[...], NT)
     mid = middle[...]
-    r2 = scale_mid[...]
+    r2 = lax.rsqrt(jnp.mean(mid * mid, axis=1, keepdims=True) + epsilon)
     small_out[pl.ds(experts, 1), :] = jnp.sum(routed_grad * mid * r2, axis=0, keepdims=True)
     gained = moe_gain[...] * routed_grad
     middle_grad[...] = (
@@ -1099,7 +1017,7 @@
         out_input[mine, :] += got_shares[slot]
     normed_grad = out_input[mine, :]
     inputs = hidden[...].astype(f32)
-    r1 = scale_in[...]
+    r1 = lax.rsqrt(jnp.mean(inputs * inputs, axis=1, keepdims=True) + epsilon)
     gained = gain[...] * normed_grad
     small_out[pl.ds(small_out.shape[0] - 1, 1), :] = jnp.sum(normed_grad * inputs * r1, axis=0, keepdims=True)
     out_input[mine, :] = (
@@ -1150,9 +1068,9 @@
 
 
 def attention_back(
-    back, middle, scale_mid, routed, grad_top, picked, router, moe_gain,
+    back, middle, routed, grad_top, picked, router, moe_gain,
     heads, q, k, v, w_out, w_query, w_key, w_value, normed, cosine, sine, seg,
-    hidden, gain, scale_in, dp_size, tensor_size, collective_id,
+    hidden, gain, dp_size, tensor_size, collective_id,
 ):
     length, width = normed.shape
     small = jax.ShapeDtypeStruct(((dp_size + 2 + 7) // 8 * 8, width), f32)
@@ -1176,7 +1094,7 @@
             jax.ShapeDtypeStruct((length, width), f32),
             jax.ShapeDtypeStruct(small.shape, f32),
         ],
-        in_specs=[vmem] * 24,
+        in_specs=[vmem] * 22,
         out_specs=[vmem] * 4,
         scratch_shapes=[
             pltpu.VMEM((length, width), bf16),
@@ -1211,9 +1129,205 @@
             collective_id=collective_id, has_side_effects=True, vmem_limit_bytes=60 << 20
         ),
     )(
-        back, middle, scale_mid, routed, grad_top, picked, router, moe_gain[None],
+        back, middle, routed, grad_top, picked, router, moe_gain[None],
         heads, q, k, v, w_out, w_query, w_key, w_value, normed, cosine, sine,
-        seg[:, None], seg[None, :], hidden, gain[None], scale_in,
+        seg[:, None], seg[None, :], hidden, gain[None],
+    )
+
+
+def attention_kernel(
+    a, b, tensor_size,
+    w_gate, w_up, w_down,
+    payload, hidden, gain, w_query, w_key, w_value, w_out, seg_col, seg_row, frequency, moe_gain,
+    grads, cosine, sine, heads, q_ref, k_ref, v_ref, normed, middle, routed, far_gate, far_up, far_down,
+    bias, shares, got_shares, own_gate, own_up, own_down, local, send, recv, share_send, share_recv,
+    own_load, pair_send, pair_recv, mate_send, mate_recv,
+):
+    spot = Spot(a, b)
+    length, width = hidden.shape
+    rows = payload.shape[0]
+    q_width, k_width = q_ref.shape[1], k_ref.shape[1]
+    per_kv = q_width // k_width
+    core = lax.axis_index("tensor")
+    others = [(core + m) % tensor_size for m in range(1, tensor_size)]
+    own = pl.ds(pl.multiple_of(spot.block * rows, 16), rows)
+    mine_copy = pltpu.make_async_copy(payload, grads.at[own], local)
+    mine_copy.start()
+    units = own_gate.shape[1]
+    unit_at = pl.ds(pl.multiple_of(core * units, units), units)
+    loads = [
+        pltpu.make_async_copy(src, dst, own_load.at[i])
+        for i, (src, dst) in enumerate(
+            ((w_gate.at[:, unit_at], own_gate), (w_up.at[:, unit_at], own_up), (w_down.at[unit_at, :], own_down))
+        )
+    ]
+    for c in loads:
+        c.start()
+
+    def far_blocks(m):
+        at = pl.ds(m * units, units)
+        return (far_gate.at[:, at], far_up.at[:, at], far_down.at[at, :])
+
+    partner = spot.me + 1 - 2 * spot.pair
+    to_pair = [
+        remote_to(src, dst, pair_send.at[i], pair_recv.at[i], partner)
+        for i, (src, dst) in enumerate(zip((own_gate, own_up, own_down), far_blocks(0)))
+    ]
+    to_mates = [
+        pltpu.make_async_remote_copy(
+            src_ref=src, dst_ref=dst, send_sem=mate_send.at[m - 1, i], recv_sem=mate_recv.at[m - 1, i],
+            device_id={"tensor": xor4(core, m)}, device_id_type=MESH,
+        )
+        for m in range(1, tensor_size)
+        for i, (src, dst) in enumerate(zip(far_blocks(0), far_blocks(m)))
+    ]
+    spot.greet([{"tensor": other} for other in others] + [{"dp": partner}])
+    mine_copy.wait()
+    gather = LineGather(spot, grads, rows, send, recv)
+    gather.begin()
+    for load, c in zip(loads, to_pair):
+        load.wait()
+        c.start()
+    earlier = jnp.sum(jnp.where(seg_row[...] < seg_col[...], 1.0, 0.0), axis=1, keepdims=True)
+    lane = lax.broadcasted_iota(jnp.int32, (length, 128), 1)
+    position = lax.broadcasted_iota(jnp.int32, (length, 128), 0).astype(f32) - earlier
+    angle = position * frequency[...]
+    cosine[...] = jnp.cos(angle)
+    sine[...] = jnp.where(lane % HEAD_DIM < HEAD_DIM // 2, -1.0, 1.0) * jnp.sin(angle)
+    mask_bias(bias, seg_col, seg_row)
+    inputs = hidden[...].astype(f32)
+    r1 = lax.rsqrt(jnp.mean(inputs * inputs, axis=1, keepdims=True) + epsilon)
+    normed[...] = (inputs * r1 * gain[...]).astype(bf16)
+    for out, weight, turned in ((q_ref, w_query, True), (k_ref, w_key, True), (v_ref, w_value, False)):
+        tile = min(256, out.shape[1])
+        for i in range(out.shape[1] // tile):
+            product = mm(normed[...], weight[:, i * tile : (i + 1) * tile], NN)
+            for j in range(tile // 128):
+                piece = product[:, j * 128 : (j + 1) * 128]
+                if turned:
+                    piece = turn(piece, cosine[...], sine[...])
+                at = i * tile + j * 128
+                out[:, at : at + 128] = piece.astype(bf16)
+    arrivals = list(range(1, spot.n))
+
+    def arrive(count):
+        for _ in range(count):
+            gather.arrive(arrivals.pop(0))
+
+    half = length // 2
+    spans = ((0, half, half), (half, half, length))
+    kv_count = k_width // HEAD_DIM
+    for g in range(kv_count):
+        kg = k_ref[:, g * HEAD_DIM : (g + 1) * HEAD_DIM]
+        vg = v_ref[:, g * HEAD_DIM : (g + 1) * HEAD_DIM]
+        for h in range(per_kv):
+            lanes = pl.ds((g * per_kv + h) * HEAD_DIM, HEAD_DIM)
+            for start, size, cols in spans:
+                at = pl.ds(start, size)
+                scores = mm(q_ref[at, lanes], kg[:cols], NT) * attn_scale + bias[at, pl.ds(0, cols)]
+                raised = jnp.exp(scores - jnp.max(scores, axis=1, keepdims=True))
+                probs_low = (raised * (1.0 / jnp.sum(raised, axis=1, keepdims=True))).astype(bf16)
+                heads[at, lanes] = mm(probs_low, vg[:cols], NN).astype(bf16)
+        if g == kv_count // 2 - 1:
+            arrive(2)
+
+    def part_of(t):
+        at = pl.ds(pl.multiple_of(t * rows, 16), rows)
+        return mm(heads[at, :], w_out[...], NN)
+
+    def share_copy(m):
+        slot = tensor_size - 2 - m
+        return pltpu.make_async_remote_copy(
+            src_ref=shares.at[m], dst_ref=got_shares.at[slot], send_sem=share_send.at[m],
+            recv_sem=share_recv.at[slot], device_id={"tensor": others[m]}, device_id_type=MESH,
+        )
+
+    for m, other in enumerate(others):
+        shares[m] = part_of(other)
+        share_copy(m).start()
+    arrive(1)
+    mine = pl.ds(pl.multiple_of(core * rows, 16), rows)
+    total = part_of(core)
+    for m in range(len(others)):
+        share_copy(m).wait_send()
+        share_copy(m).wait_recv()
+    for m in range(len(others)):
+        total += got_shares[m]
+    mid = hidden[mine, :].astype(f32) + residual_scale * total
+    middle[...] = mid
+    r2 = lax.rsqrt(jnp.mean(mid * mid, axis=1, keepdims=True) + epsilon)
+    routed[...] = (mid * r2 * moe_gain[...]).astype(bf16)
+    arrive(max(0, len(arrivals) - 2))
+    for c in to_pair:
+        c.wait_recv()
+    for c in to_mates:
+        c.start()
+    arrive(len(arrivals))
+    for c in to_mates:
+        c.wait()
+    for c in to_pair:
+        c.wait_send()
+    gather.finish()
+
+
+def attention_forward(
+    w_gate, w_up, w_down, payload, hidden, gain, w_query, w_key, w_value, w_out, seg, moe_gain, dp_size, tensor_size, collective_id
+):
+    a, b = group_sizes(dp_size)
+    n = a * b
+    length, width = hidden.shape
+    rows = payload.shape[0]
+    q_width, k_width = w_query.shape[1], w_key.shape[1]
+    others = tensor_size - 1
+    units = w_gate.shape[1] // tensor_size
+    half = HEAD_DIM // 2
+    frequency = rope_base ** (-jnp.arange(half, dtype=f32) * 2.0 / HEAD_DIM)
+    vmem = pl.BlockSpec(memory_space=pltpu.VMEM)
+    dma = pltpu.SemaphoreType.DMA
+    struct = jax.ShapeDtypeStruct
+    return pl.pallas_call(
+        functools.partial(attention_kernel, a, b, tensor_size),
+        out_shape=[
+            struct((n * rows, payload.shape[1]), bf16),
+            struct((length, 128), f32),
+            struct((length, 128), f32),
+            struct((length, q_width), bf16),
+            struct((length, q_width), bf16),
+            struct((length, k_width), bf16),
+            struct((length, k_width), bf16),
+            struct((length, width), bf16),
+            struct((rows, width), f32),
+            struct((rows, width), bf16),
+            struct(w_gate.shape, bf16),
+            struct(w_up.shape, bf16),
+            struct(w_down.shape, bf16),
+        ],
+        in_specs=[pl.BlockSpec(memory_space=pl.ANY)] * 3 + [vmem] * 11,
+        out_specs=[vmem] * 13,
+        scratch_shapes=[
+            pltpu.VMEM((length, length), f32),
+            pltpu.VMEM((others, rows, width), f32),
+            pltpu.VMEM((others, rows, width), f32),
+            pltpu.VMEM((width, units), bf16),
+            pltpu.VMEM((width, units), bf16),
+            pltpu.VMEM((units, width), bf16),
+            dma(()),
+            dma((n, 4, 2)),
+            dma((n, 2)),
+            dma((others,)),
+            dma((others,)),
+            dma((3,)),
+            dma((3,)),
+            dma((3,)),
+            dma((others, 3)),
+            dma((others, 3)),
+        ],
+        compiler_params=pltpu.CompilerParams(
+            collective_id=collective_id, has_side_effects=True, vmem_limit_bytes=52 << 20
+        ),
+    )(
+        w_gate, w_up, w_down, payload, hidden, gain[None], w_query, w_key, w_value, w_out,
+        seg[:, None], seg[None, :], jnp.tile(frequency, 4)[None], moe_gain[None],
     )
 
 
@@ -1238,7 +1352,6 @@
     out_grad,
 ):
     tokens_here, model_width = hidden_in.shape
-    head_size = HEAD_DIM
     dp_size = lax.axis_size("dp")
     tensor_size = lax.axis_size("tensor")
     experts = dp_size
@@ -1252,50 +1365,32 @@
     def my_rows(x):
         return lax.dynamic_slice_in_dim(x, tensor_index * rows_here, rows_here, 0)
 
-    block = w_gate.shape[2] // tensor_size
-
-    def my_units(x, dim):
-        return lax.dynamic_slice_in_dim(x, tensor_index * block, block, dim)
-
-    def relative_gather(x, dim):
-        for mask in tensor_masks:
-            x = jnp.concatenate([x, swap(x, "tensor", mask)], dim)
-        return x
-
-    far_set = [
-        relative_gather(swap(my_units(w_gate[0], 1), "dp", 1), 1),
-        relative_gather(swap(my_units(w_up[0], 1), "dp", 1), 1),
-        relative_gather(swap(my_units(w_down[0], 0), "dp", 1), 0),
-    ]
     grad_mine = my_rows(out_grad)
     lanes = jnp.arange(LANES, dtype=jnp.int32)
     picked_mine = jnp.any(my_rows(expert_ids)[:, :, None] == lanes[None, None, :], axis=1)
     picked_low = picked_mine.astype(bf16)
-    grads = lax.all_gather(
-        jnp.concatenate([grad_mine, picked_low], 1),
-        "dp",
-        axis=0,
-        tiled=True,
-        axis_index_groups=groups,
-    )
     router_wide = jnp.pad(w_router, ((0, 0), (0, LANES - experts)))
 
-    inputs = hidden_in.astype(f32)
-    scale_in = lax.rsqrt(jnp.mean(inputs * inputs, axis=-1, keepdims=True) + epsilon)
-    normed_low = (inputs * scale_in * attn_gain).astype(bf16)
     segment = segment_ids[0]
-    tables = rope_tables(segment, head_size)
-    heads_flat, query_heads, key_heads, value_heads, log_sums = attend_forward(
-        normed_low, segment, tables, w_query, key_weight, value_weight, head_size
-    )
-    attn_part = jnp.dot(heads_flat, w_output, preferred_element_type=f32)
-    attn_total = scatter_sum(attn_part, "tensor", tensor_down, f32)
-
-    inputs_mine = my_rows(hidden_in).astype(f32)
-    scale_in_mine = my_rows(scale_in)
-    middle = inputs_mine + residual_scale * attn_total
-    scale_mid = lax.rsqrt(jnp.mean(middle * middle, axis=-1, keepdims=True) + epsilon)
-    routed_low = (middle * scale_mid * moe_gain).astype(bf16)
+    grads, cosine, sine, heads_flat, query_heads, key_heads, value_heads, normed_low, middle, routed_low, *far_set = (
+        attention_forward(
+            w_gate[0],
+            w_up[0],
+            w_down[0],
+            jnp.concatenate([grad_mine, picked_low], 1),
+            hidden_in,
+            attn_gain,
+            w_query,
+            key_weight,
+            value_weight,
+            w_output,
+            segment,
+            moe_gain,
+            dp_size,
+            tensor_size,
+            3,
+        )
+    )
 
     near_set = [w_gate[0], w_up[0], w_down[0]]
     moe_part, back, *expert_parts = experts_call(
@@ -1309,32 +1404,30 @@
     returning = [swap(x, "dp", 1) for x in expert_parts[3:]]
     dims = (1, 1, 0)
     heads_width = heads_flat.shape[1]
-    width_q, width_k = query_heads.shape[1] * head_size, key_heads.shape[1] * head_size
+    width_q, width_k = query_heads.shape[1], key_heads.shape[1]
     qkv_width = width_q + 2 * width_k
     w_output_sum, qkv_grad, input_grad, small = attention_back(
         back,
         middle,
-        scale_mid,
         routed_low,
         grad_mine,
         picked_low,
         router_wide,
         moe_gain,
         heads_flat,
-        query_heads.reshape(tokens_here, -1),
-        key_heads.reshape(tokens_here, -1),
-        value_heads.reshape(tokens_here, -1),
+        query_heads,
+        key_heads,
+        value_heads,
         w_output,
         w_query,
         key_weight,
         value_weight,
         normed_low,
-        jnp.tile(tables[0][:, 0, :], (1, 4)),
-        jnp.tile(jnp.concatenate([-tables[1][:, 0, :], tables[1][:, 0, :]], 1), (1, 2)),
+        cosine,
+        sine,
         segment,
         my_rows(hidden_in),
         attn_gain,
-        scale_in_mine,
         dp_size,
         tensor_size,
         2,

time: 570 us -> 553 us (0.970)
  Pallas kernels: 399 us -> 486 us
  waiting for transfers between devices: 59 us -> 0.06 us
  matrix products: 18.7 us -> 0 us
  other arithmetic: 24.6 us -> 13.2 us
  local copies, waits for them, and re-layouts: 33.8 us -> 24.6 us
  starting transfers between devices: 10.7 us -> 4.25 us
    pallas_call x0 -> x1, Pallas kernels: none -> 86.9 us  [attention_forward(): pl.pallas_call(functools.partial(attention_kernel, a, b, tensor_size), ou...]
    ppermute x14 -> x7, waiting for transfers between devices: 47.5 us -> 0.02 us  [swap(): lax.ppermute(x, axis, [(i, i ^ mask) for i in range(lax.axis_size(axis))])]
    all_gather x1 -> x0, waiting for transfers between devices: 11.5 us -> none  [per_device(): lax.all_gather(jnp.concatenate([grad_mine, picked_low], 1), 'dp', axis=0,...]
    dot_general x5 -> x0, matrix products: 11.3 us -> none  [the longest x1 6 us: attend_forward(): jnp.einsum('hgqk,khd->qhgd', probs_low, value_heads, preferred_element_ty...]
    concatenate x5 -> x0, other arithmetic: 8.05 us -> none  [the longest x3 7.98 us: relative_gather(): x = jnp.concatenate([x, swap(x, 'tensor', mask)], dim)]
    sub x1 -> x0, matrix products: 7.37 us -> none  [attend_forward(): weights_raw = jnp.exp(scores - largest)]
    ppermute x14 -> x7, starting transfers between devices: 10.6 us -> 4.22 us  [swap(): lax.ppermute(x, axis, [(i, i ^ mask) for i in range(lax.axis_size(axis))])]
  transfers between devices with their start and end apart: 16 -> 8, of which waited for: 4 -> 0; matrix products, arithmetic and copies ran while one was open for 11% -> 4% of each run, Pallas kernels for 37% -> 39%
where the time goes in v7:
time: 553 us; the launch traced here: 543 us
  Pallas kernels  486 us (88%)
  local copies, waits for them, and re-layouts  24.6 us (4%)
  between operations  14.8 us (3%)
  other arithmetic  13.2 us (2%)
    pallas_call x1, Pallas kernels, attention_back(): pl.pallas_call(functools.partial(attention_back_kernel, dp_size, tensor_s...  214 us
    pallas_call x1, Pallas kernels, experts_call(): pl.pallas_call(functools.partial(experts_kernel, a, b, rows, width, cores...  179 us
    pallas_call x1, Pallas kernels, attention_forward(): pl.pallas_call(functools.partial(attention_kernel, a, b, tensor_size), ou...  86.9 us
  transfers between devices with their start and end apart: 8, of which 0 were waited for; matrix products, arithmetic and copies ran while one was open for 4% of the time, Pallas kernels for 39%

profile of v7, /device:TPU:0, one launch (start us, length us, event | category | flops | bytes accessed | tf_op | source)
XLA Modules:
  0.0 542.7 jit_solution(8497848682301496919)
XLA Ops:
  7.2 0.0 copy-start
  7.2 0.0 copy-start.12
  7.2 0.0 reduce-scatter.2.cloned.1.call-start
  7.3 0.1 broadcast_in_dim_tile.3.frequency
  7.4 0.8 broadcast_in_dim.19.gain
  8.2 0.7 broadcast_in_dim.20.moe_gain
  8.9 0.0 copy-done
  8.9 0.1 copy.32
  9.0 0.4 fusion
  9.5 0.0 copy-start.18
  9.5 0.8 copy.33.seg_col
  10.4 0.0 copy-start.2
  10.4 1.1 copy.34
  11.5 0.8 pad.4.router_ref.router
  12.3 0.0 copy-done.12
  12.3 2.1 constant_dynamic-slice_fusion
  14.4 0.0 copy-done.18
  14.4 1.1 pad_maximum_fusion.1.payload
  15.5 0.0 copy-done.7
  15.5 0.0 copy-done.8
  15.5 0.0 copy-done.2
  15.5 0.0 copy-done.9
  15.5 86.9 %shard_map.229 = (bf16[2048,1664]{1,0:T(8,128)(2,1)}, f32[512,128]{1,0:T(8,128)S(1)}, f32[512,128]{1,0:T(8,128)S(1)}, bf16[512,768]{1,0:T(8,128)(2,1)}, bf16[512...) custom-call(bf16[1536,512]{1,0:T(8,128)(2,1)} %bitcast.10, ...), custom_call_target="tpu_custom_call" | custom-call | tf_op jit(solution)/shard_map/pallas_call | solution.py:1288
  102.4 0.0 copy-done.10
  102.4 0.0 copy-start.3
  102.4 0.7 copy-done.3
  103.1 0.7 copy-done.4
  103.8 0.7 copy-done.5
  104.5 0.7 copy-done.6
  105.2 179.3 %shard_map.230 = (bf16[2048,1536]{1,0:T(8,128)(2,1)}, f32[256,1664]{1,0:T(8,128)}, bf16[1536,256]{1,0:T(8,128)(2,1)}, bf16[1536,256]{1,0:T(8,128)(2,1)}, bf16[25...) custom-call(bf16[256,1536]{1,0:T(8,128)(2,1)} %get-tuple-element.46.x_ref, ...), custom_call_target="tpu_custom_call" | custom-call | tf_op jit(solution)/shard_map/pallas_call | solution.py:668
  284.6 0.0 copy-start.20
  284.6 0.0 reduce-scatter.2.cloned.1.call-update
  284.6 1.5 collective-permute-start
  286.1 1.0 collective-permute-start.1
  287.2 1.0 collective-permute-start.2
  288.2 213.6 %shard_map.231 = (bf16[1536,768]{1,0:T(8,128)(2,1)}, bf16[1536,1280]{1,0:T(8,128)(2,1)}, f32[512,1536]{1,0:T(8,128)}, f32[24,1536]{1,0:T(8,128)}) custom-call(f32[256,1664]{1,0:T(8,128)} %get-tuple-element.51.back, f32[256,1536]{1,0:T(8,128)} %get-tuple-element.45.middle, bf16[256,1536]{1,0:T(8,128)(2,1)} %get-tuple-element.46.x_ref.routed, ...), custom_call_target="tpu_custom_call" | custom-call | tf_op jit(solution)/shard_map/pallas_call | solution.py:1087
  501.8 1.5 slice_bitcast_fusion
  503.3 3.4 fusion.1
  506.7 0.0 collective-permute-done
  506.7 0.0 collective-permute-done.1
  506.7 0.0 collective-permute-done.2
  506.7 0.0 reduce-scatter.2.cloned.1.call-done
  506.7 0.2 convert_add_fusion.refs_2_
  507.0 0.1 collective-permute-start.6
  507.0 0.8 copy-done.16
  507.9 1.4 convert_add_fusion.1.refs_1_
  509.2 0.1 collective-permute-start.5
  509.3 2.6 convert_add_fusion.2.refs_0_
  511.9 0.5 collective-permute-start.4
  512.4 0.0 copy-done.11
  512.4 1.1 add_convert_fusion
  513.5 0.0 collective-permute-start.3
  513.5 1.5 slice_reduce_fusion
  515.0 4.2 slice.32
  519.2 2.0 fusion.2
  521.2 2.9 pad_maximum_fusion
  524.1 0.0 collective-permute-done.3
  524.1 3.5 maximum_select_fusion
  527.6 0.0 collective-permute-done.6.refs_5_
  527.6 0.0 collective-permute-done.5.refs_4_
  527.6 0.0 collective-permute-done.4.refs_3_
  527.6 6.1 %shard_map.232 = (f32[1536,512]{1,0:T(8,128)}, f32[1536,512]{1,0:T(8,128)}, f32[512,1536]{1,0:T(8,128)}) custom-call(f32[1536,256]{1,0:T(8,128)} %convert_add_fusion.2.refs_0_, f32[1536,256]{1,0:T(8,128)S(1)} %convert_add_fusion.1.refs_1_, f32[256,1536]{1,0:T(8,128)S(1)} %convert_add_fusion.refs_2_, f32[1536,256]{1,0:T(8,128)} %collective-permute-done.4.refs_3_, ...), custom_call_target="tpu_custom_call" | custom-call | tf_op jit(solution)/shard_map/pallas_call | solution.py:747
  533.7 0.0 copy-start.1
  533.7 1.7 copy.37
  (25 shorter events, 0.1 us)
Async XLA Ops:
  7.2 1.7 copy-start
  7.2 5.1 copy-start.12
  7.2 499.5 %reduce-scatter.2.cloned.1.call-start = ((), (), s32[]{:S(2)}) async-start(), calls=%async_computation.1 | async-start | bytes 7077888 | tf_op jit(solution)/shard_map/reduce_scatter | solution.py:1399
  8.2 7.3 %copy-start.7 = (f32[1,1536]{1,0:T(1,128)}, f32[1,1536]{1,0:T(1,128)S(1)}, u32[]{:S(2)}) copy-start(f32[1,1536]{1,0:T(1,128)S(1)} %broadcast_in_dim.19.gain) | copy-start | bytes 18436
  8.9 6.6 %copy-start.8 = (f32[1,1536]{1,0:T(1,128)}, f32[1,1536]{1,0:T(1,128)S(1)}, u32[]{:S(2)}) copy-start(f32[1,1536]{1,0:T(1,128)S(1)} %broadcast_in_dim.20.moe_gain) | copy-start | bytes 18436
  9.5 4.9 copy-start.18
  10.4 5.1 copy-start.2
  14.4 88.0 %copy-start.10 = (bf16[256,1536]{1,0:T(8,128)(2,1)}, bf16[256,1536]{1,0:T(8,128)(2,1)S(1)}, u32[]{:S(2)}) copy-start(bf16[256,1536]{1,0:T(8,128)(2,1)S(1)} %get-tuple-element.85.grad_top) | copy-start | bytes 2359300
  14.4 1.1 copy-start.9
  102.4 0.7 copy-start.3
  103.1 0.7 copy-start.4
  103.8 0.7 copy-start.5
  104.5 0.7 copy-start.6
  284.6 1.6 copy-start.20
  284.6 2.6 copy-start.19
  284.6 222.1 %collective-permute-start = (bf16[1536,256]{1,0:T(8,128)(2,1)}, bf16[1536,256]{1,0:T(8,128)(2,1)}, u32[]{:S(2)}, u32[]{:S(2)}) collective-permute-start(bf16[1536,256]{1,0:T(8,128)(2,1)} %get-tuple-element.60), channel_id=1, source_target_pairs={{0,2},{2,0},{4,6},{6,4},{8,10},{10,8},{12,14},{14,12},{16,18},{18,... | collective-permute-start | bytes 2359304 | tf_op jit(solution)/shard_map/ppermute | solution.py:31
  286.1 220.5 %collective-permute-start.1 = (bf16[1536,256]{1,0:T(8,128)(2,1)S(1)}, bf16[1536,256]{1,0:T(8,128)(2,1)}, u32[]{:S(2)}, u32[]{:S(2)}) collective-permute-start(bf16[1536,256]{1,0:T(8,128)(2,1)S(1)} %copy-done.20), channel_id=1, source_target_pairs={{0,2},{2,0},{4,6},{6,4},{8,10},{10,8},{12,14},{14,12},{16,18},{18,... | collective-permute-start | bytes 2359304 | tf_op jit(solution)/shard_map/ppermute | solution.py:31
  287.2 219.5 %collective-permute-start.2 = (bf16[256,1536]{1,0:T(8,128)(2,1)S(1)}, bf16[256,1536]{1,0:T(8,128)(2,1)S(1)}, u32[]{:S(2)}, u32[]{:S(2)}) collective-permute-start(bf16[256,1536]{1,0:T(8,128)(2,1)S(1)} %copy-done.19), channel_id=1, source_target_pairs={{0,2},{2,0},{4,6},{6,4},{8,10},{10,8},{12,14},{14,12},{16,18},{18,... | collective-permute-start | bytes 2359304 | tf_op jit(solution)/shard_map/ppermute | solution.py:31
  503.3 3.4 copy-start.17
  506.7 1.1 copy-start.16
  507.0 20.6 %collective-permute-start.6 = (f32[256,1536]{1,0:T(8,128)S(1)}, f32[256,1536]{1,0:T(8,128)}, u32[]{:S(2)}, u32[]{:S(2)}) collective-permute-start(f32[256,1536]{1,0:T(8,128)S(1)} %convert_add_fusion.refs_2_), channel_id=1, source_target_pairs={{0,1},{1,0},{2,3},{3,2},{4,5},{5,4},{6,7},{7,6},{8,9},{9,8},{10,11... | collective-permute-start | bytes 4718600 | tf_op jit(solution)/shard_map/ppermute | solution.py:31
  507.9 1.4 copy-start.14
  509.2 18.4 %collective-permute-start.5 = (f32[1536,256]{1,0:T(8,128)S(1)}, f32[1536,256]{1,0:T(8,128)}, u32[]{:S(2)}, u32[]{:S(2)}) collective-permute-start(f32[1536,256]{1,0:T(8,128)S(1)} %convert_add_fusion.1.refs_1_), channel_id=1, source_target_pairs={{0,1},{1,0},{2,3},{3,2},{4,5},{5,4},{6,7},{7,6},{8,9},{9,8},{10,11... | collective-permute-start | bytes 4718600 | tf_op jit(solution)/shard_map/ppermute | solution.py:31
  509.3 3.1 copy-start.11
  509.3 3.1 copy-start.15
  511.9 15.7 %collective-permute-start.4 = (f32[1536,256]{1,0:T(8,128)}, f32[1536,256]{1,0:T(8,128)}, u32[]{:S(2)}, u32[]{:S(2)}) collective-permute-start(f32[1536,256]{1,0:T(8,128)} %convert_add_fusion.2.refs_0_), channel_id=1, source_target_pairs={{0,1},{1,0},{2,3},{3,2},{4,5},{5,4},{6,7},{7,6},{8,9},{9,8},{10,11... | collective-permute-start | bytes 4718600 | tf_op jit(solution)/shard_map/ppermute | solution.py:31
  513.5 10.7 %collective-permute-start.3 = (bf16[256,1536]{1,0:T(8,128)(2,1)}, bf16[256,1536]{1,0:T(8,128)(2,1)}, u32[]{:S(2)}, u32[]{:S(2)}) collective-permute-start(bf16[256,1536]{1,0:T(8,128)(2,1)} %add_convert_fusion), channel_id=1, source_target_pairs={{0,1},{1,0},{2,3},{3,2},{4,5},{5,4},{6,7},{7,6},{8,9},{9,8},{10,11... | collective-permute-start | bytes 2359304 | tf_op jit(solution)/shard_map/ppermute | solution.py:31
  527.6 6.1 %copy-start.13 = (f32[512,1536]{1,0:T(8,128)S(1)}, f32[512,1536]{1,0:T(8,128)}, u32[]{:S(2)}) copy-start(f32[512,1536]{1,0:T(8,128)} %get-tuple-element.99) | copy-start | bytes 9437188
  533.7 1.7 copy-start.1
Sparse Core Ops, SparseCore 0:
  284.7 160.9 reduce-scatter.1

commit v8 on v7

--- a/solution.py
+++ b/solution.py
@@ -98,7 +98,7 @@
         dst[pl.ds(dst0 + r, step), :] = x.astype(out_dtype)
         return 0
 
-    lax.fori_loop(0, rows // step, body, 0)
+    lax.fori_loop(0, rows // step, body, 0, unroll=rows // step <= 4)
 
 
 def group_sizes(dp_size):
@@ -243,7 +243,7 @@
         dst[pl.ds(d0 + r, step), :] = total.astype(dst.dtype)
         return 0
 
-    lax.fori_loop(0, rows // step, body, 0)
+    lax.fori_loop(0, rows // step, body, 0, unroll=rows // step <= 4)
 
 
 class LineSum:
@@ -841,6 +841,74 @@
     return [rotated(masks[:-1], j) + masks[-1:] for j in range(3 * groups)], groups
 
 
+class OutputSum:
+    def __init__(self, spot, src, own, rows, got_b, got_a, load, send_b, recv_b, send_a, recv_a):
+        self.spot, self.src, self.own, self.rows, self.got_b = spot, src, own, rows, got_b
+        self.load, self.send_b, self.recv_b = load, send_b, recv_b
+        self.line = LineSum(
+            spot.a, spot.A, spot.devices[0], spot.devices[1], own, lambda A: A * rows, rows,
+            got_a, send_a, recv_a, spot.some,
+        )
+
+    def block(self, A, B):
+        return pl.multiple_of((A * 2 + B) * self.rows, 16)
+
+    def own_copy(self, A):
+        src = self.src.at[pl.ds(self.block(A, self.spot.B), self.rows)]
+        return pltpu.make_async_copy(src, self.own.at[pl.ds(A * self.rows, self.rows)], self.load.at[A])
+
+    def start(self):
+        for A in range(self.spot.a):
+            self.own_copy(A).start()
+
+    def b_copies(self, A):
+        size = self.rows // SUM_PIECES
+        return [
+            remote_to(
+                self.src.at[pl.ds(pl.multiple_of(self.block(A, 1 - self.spot.B) + p * size, 16), size)],
+                self.got_b.at[pl.ds(A * self.rows + p * size, size)],
+                self.send_b.at[A, p],
+                self.recv_b.at[A, p],
+                self.spot.some,
+            )
+            for p in range(SUM_PIECES)
+        ]
+
+    def b_send(self, A):
+        for c in self.b_copies(A):
+            c.start()
+
+    def b_end(self, A):
+        self.own_copy(A).wait()
+        size = self.rows // SUM_PIECES
+        for p, c in enumerate(self.b_copies(A)):
+            c.wait_recv()
+            at = A * self.rows + p * size
+            add_into(self.own, at, self.got_b, at, size)
+
+    def events(self):
+        a, line = self.spot.a, self.line
+        sends = [functools.partial(self.b_send, A) for k in range(a // 2) for A in (a - 1 - k, k)]
+
+        def up(k):
+            if 2 * k < a:
+                self.b_end(a - 1 - k)
+            line.step_up(k)
+
+        def down(k):
+            if 2 * k < a:
+                self.b_end(k)
+            line.step_down(k)
+
+        flow = [functools.partial(f, k) for k in range(a - 1) for f in (up, down)]
+        return sends, flow
+
+    def finish(self):
+        for A in range(self.spot.a):
+            for c in self.b_copies(A):
+                c.wait_send()
+
+
 def turn(x, cosine, sine):
     lane = lax.broadcasted_iota(jnp.int32, x.shape, 1)
     swapped = jnp.where(lane % HEAD_DIM < HEAD_DIM // 2, pltpu.roll(x, 128 - 32, 1), pltpu.roll(x, 32, 1))
@@ -852,24 +920,26 @@
     row = lax.broadcasted_iota(jnp.int32, bias.shape, 0)
     col = lax.broadcasted_iota(jnp.int32, bias.shape, 1)
     allowed = (row >= col) & (seg_col[...] == seg_row[...])
-    bias[...] = jnp.where(allowed, 0.0, masked_score)
+    bias[...] = jnp.where(allowed, 0.0, masked_score).astype(bias.dtype)
 
 
 def attention_back_kernel(
-    dp_size, tensor_size, orders_o, groups_o, orders_q, groups_q,
-    back, middle, routed, grad_top, picked, router, moe_gain,
+    dp_size, tensor_size, orders_o, groups_o, orders_q, groups_q, moe_inside,
+    moe_ref, back, middle, routed, grad_top, picked, router, moe_gain,
     heads, q_ref, k_ref, v_ref, w_out, w_query, w_key, w_value, normed, cosine, sine,
     seg_col, seg_row, hidden, gain,
-    out_o, out_q, out_input, small_out,
-    branch, middle_grad, bias, heads_grad, qkv_low, scratch_q, scratch_k, scratch_v,
+    out_o, out_q, out_input, small_out, out_block,
+    middle_grad, bias, heads_grad, qkv_low, scratch_q, scratch_k, scratch_v,
     acc_o, got_o, acc_q, got_q, shares, got_shares, small_got,
-    send_o, recv_o, send_q, recv_q, small_send, small_recv, share_send, share_recv, in_send, in_recv, branch_send, branch_recv,
+    send_o, recv_o, send_q, recv_q, small_send, small_recv, share_send, share_recv, in_send, in_recv, branch_send, branch_recv, block_send, block_recv,
+    *moe_scratch,
 ):
     length, width = normed.shape
     q_width, k_width = q_ref.shape[1], k_ref.shape[1]
     rows = hidden.shape[0]
     per_kv = q_width // k_width
     core = lax.axis_index("tensor")
+    branch = out_block
     tensor_masks = bit_masks(tensor_size)
 
     def mate(m):
@@ -885,6 +955,26 @@
         )
     for other in others:
         pl.semaphore_signal(barrier, inc=1, device_id={"tensor": other}, device_id_type=MESH)
+    sends_m, flow_m = [], []
+    if moe_inside:
+        spot = Spot(*group_sizes(dp_size))
+        for device, there in zip(spot.devices[:2], spot.exists[:2]):
+
+            @pl.when(there)
+            def _(device=device):
+                pl.semaphore_signal(
+                    barrier, inc=1, device_id={"dp": device}, device_id_type=MESH
+                )
+
+        lines = 1 - (spot.A + 1) // spot.a + (spot.A + spot.a - 1) // spot.a
+        moe = OutputSum(spot, moe_ref, moe_scratch[0], rows, *moe_scratch[1:])
+        moe.start()
+        sends_m, flow_m = moe.events()
+    else:
+        lines = 0
+    pl.semaphore_wait(barrier, len(masks) + len(others) + lines)
+    for event in sends_m:
+        event()
     mine = pl.ds(pl.multiple_of(core * rows, 16), rows)
     experts = dp_size
     x = routed[...]
@@ -910,7 +1000,6 @@
         - mid * (r2 * r2 * r2) * jnp.mean(mid * gained, axis=1, keepdims=True)
     )
     branch[mine, :] = (residual_scale * middle_grad[...]).astype(bf16)
-    pl.semaphore_wait(barrier, len(masks) + len(others))
     branch_copies = []
     for m, other in enumerate(others):
         c = pltpu.make_async_remote_copy(
@@ -946,7 +1035,7 @@
                     at = pl.ds(start, size)
                     qh = q_ref[at, lanes]
                     oh = heads_grad[at, lanes]
-                    scores = mm(qh, kg[:cols], NT) * attn_scale + bias[at, pl.ds(0, cols)]
+                    scores = mm(qh, kg[:cols], NT) * attn_scale + bias[at, pl.ds(0, cols)].astype(f32)
                     raised = jnp.exp(scores - jnp.max(scores, axis=1, keepdims=True))
                     probability = raised * (1.0 / jnp.sum(raised, axis=1, keepdims=True))
                     prob_grad = mm(oh, vg[:cols], NT)
@@ -966,8 +1055,8 @@
                         scratch_k[upto, side] += dk
                         scratch_v[upto, side] += dv
                 count += 1
-                if count % 2 == 0 and len(events_o) > 1:
-                    events_o.pop(0)()
+                if count in BESIDE_M and flow_m:
+                    flow_m.pop(0)()
         at = pl.ds(q_width + pair * 128, 128)
         qkv_low[:, at] = turn(scratch_k[...], cosine[...], -sine[...]).astype(bf16)
         at = pl.ds(q_width + k_width + pair * 128, 128)
@@ -982,8 +1071,6 @@
     sum_q = AllReduce(orders_q, groups_q, acc_q, got_q, out_q, send_q, recv_q)
     events_q = sum_q.events()
     events_q.pop(0)()
-    while events_o:
-        events_o.pop(0)()
 
     def shares_of(t):
         at = pl.ds(pl.multiple_of(t * rows, 16), rows)
@@ -1006,6 +1093,7 @@
         share_copies.append(c)
     normed_grad = shares_of(core)
     events_q.pop(0)()
+    events_o.pop(0)()
     out_input[mine, :] = normed_grad
     for m, c in enumerate(share_copies):
         c.wait_send()
@@ -1053,22 +1141,47 @@
 
     steps = len(ways) + 1
     done = 0
-    while events_q:
+    block_copies = []
+
+    def block_end():
+        total = shares.at[0]
+        moe.line.end(total)
+        out_block[mine, :] = (middle[...] + residual_scale * total[...]).astype(bf16)
+        for m, other in enumerate(others):
+            c = pltpu.make_async_remote_copy(
+                src_ref=out_block.at[mine], dst_ref=out_block.at[mine], send_sem=block_send.at[m],
+                recv_sem=block_recv.at[m], device_id={"tensor": other}, device_id_type=MESH,
+            )
+            c.start()
+            block_copies.append(c)
+
+    if moe_inside:
+        flow_m.append(block_end)
+    else:
+        out_block[...] = jnp.zeros(out_block.shape, bf16)
+    while events_q or events_o or flow_m:
         if done < steps:
             small_step(done)
             done += 1
-        events_q.pop(0)()
+        for events in (events_q, events_o, flow_m):
+            if events:
+                events.pop(0)()
     while done < steps:
         small_step(done)
         done += 1
     sum_o.finish()
     sum_q.finish()
-    for c in in_copies:
+    for c in in_copies + block_copies:
         c.wait()
+    if moe_inside:
+        moe.finish()
+
+
+BESIDE_M = (6, 12)
 
 
 def attention_back(
-    back, middle, routed, grad_top, picked, router, moe_gain,
+    moe_part, back, middle, routed, grad_top, picked, router, moe_gain,
     heads, q, k, v, w_out, w_query, w_key, w_value, normed, cosine, sine, seg,
     hidden, gain, dp_size, tensor_size, collective_id,
 ):
@@ -1082,24 +1195,37 @@
     small_steps = steps + len(bit_masks(tensor_size))
     qkv_width = q_width + 2 * k_width
     others = tensor_size - 1
-    vmem = pl.BlockSpec(memory_space=pltpu.VMEM)
+    vmem, hbm = pl.BlockSpec(memory_space=pltpu.VMEM), pl.BlockSpec(memory_space=pl.ANY)
     dma = pltpu.SemaphoreType.DMA
+    a, b = group_sizes(dp_size)
+    moe_inside = b == 2
+    moe_scratch = [
+        pltpu.VMEM((a * rows, width), bf16),
+        pltpu.VMEM((a * rows, width), bf16),
+        pltpu.VMEM((slots_of(a) * rows, width), bf16),
+        dma((a,)),
+        dma((a, SUM_PIECES)),
+        dma((a, SUM_PIECES)),
+        dma((a - 1, 2, SUM_PIECES)),
+        dma((slots_of(a), SUM_PIECES)),
+    ]
     return pl.pallas_call(
         functools.partial(
-            attention_back_kernel, dp_size, tensor_size, orders_o, groups_o, orders_q, groups_q
+            attention_back_kernel,
+            dp_size, tensor_size, orders_o, groups_o, orders_q, groups_q, moe_inside,
         ),
         out_shape=[
             jax.ShapeDtypeStruct((width, q_width), bf16),
             jax.ShapeDtypeStruct((width, qkv_width), bf16),
             jax.ShapeDtypeStruct((length, width), f32),
             jax.ShapeDtypeStruct(small.shape, f32),
+            jax.ShapeDtypeStruct((length, width), bf16),
         ],
-        in_specs=[vmem] * 22,
-        out_specs=[vmem] * 4,
+        in_specs=[hbm] + [vmem] * 22,
+        out_specs=[vmem] * 5,
         scratch_shapes=[
-            pltpu.VMEM((length, width), bf16),
             pltpu.VMEM((rows, width), f32),
-            pltpu.VMEM((length, length), f32),
+            pltpu.VMEM((length, length), bf16),
             pltpu.VMEM((length, q_width), bf16),
             pltpu.VMEM((length, qkv_width), bf16),
             pltpu.VMEM((length, q_width), f32),
@@ -1124,12 +1250,15 @@
             dma((others,)),
             dma((others,)),
             dma((others,)),
-        ],
+            dma((others,)),
+            dma((others,)),
+        ]
+        + (moe_scratch if moe_inside else []),
         compiler_params=pltpu.CompilerParams(
-            collective_id=collective_id, has_side_effects=True, vmem_limit_bytes=60 << 20
+            collective_id=collective_id, has_side_effects=True, vmem_limit_bytes=63 << 20
         ),
     )(
-        back, middle, routed, grad_top, picked, router, moe_gain[None],
+        moe_part, back, middle, routed, grad_top, picked, router, moe_gain[None],
         heads, q, k, v, w_out, w_query, w_key, w_value, normed, cosine, sine,
         seg[:, None], seg[None, :], hidden, gain[None],
     )
@@ -1396,17 +1525,14 @@
     moe_part, back, *expert_parts = experts_call(
         routed_low, grads, router_wide, near_set, far_set, dp_size, tensor_size, 0
     )
-    moe_total = lax.psum_scatter(
-        moe_part, "dp", scatter_dimension=0, tiled=True, axis_index_groups=groups
-    )
-
     near_mine = expert_parts[:3]
     returning = [swap(x, "dp", 1) for x in expert_parts[3:]]
     dims = (1, 1, 0)
     heads_width = heads_flat.shape[1]
     width_q, width_k = query_heads.shape[1], key_heads.shape[1]
     qkv_width = width_q + 2 * width_k
-    w_output_sum, qkv_grad, input_grad, small = attention_back(
+    w_output_sum, qkv_grad, input_grad, small, block_out = attention_back(
+        moe_part,
         back,
         middle,
         routed_low,
@@ -1432,11 +1558,13 @@
         tensor_size,
         2,
     )
-    w_output_sum, returning, moe_total = lax.optimization_barrier(
-        (w_output_sum, returning, moe_total)
-    )
-    block_mine = (middle + residual_scale * moe_total.astype(f32)).astype(bf16)
-    block_out = gather_blocks(block_mine, "tensor", tensor_down)
+    w_output_sum, returning = lax.optimization_barrier((w_output_sum, returning))
+    if group_sizes(dp_size)[1] > 2:
+        moe_total = lax.psum_scatter(
+            moe_part, "dp", scatter_dimension=0, tiled=True, axis_index_groups=groups
+        )
+        block_mine = (middle + residual_scale * moe_total.astype(f32)).astype(bf16)
+        block_out = gather_blocks(block_mine, "tensor", tensor_down)
     expert_mine = [
         mine.astype(f32) + away.astype(f32) for mine, away in zip(near_mine, returning)
     ]

time: 553 us -> 545 us (0.986)
  Pallas kernels: 486 us -> 501 us
  between operations: 14.8 us -> 1.11 us
    pallas_call x1, Pallas kernels: 214 us -> 229 us  [attention_back(): pl.pallas_call(functools.partial(attention_back_kernel, dp_size, tensor_s...]
  transfers between devices with their start and end apart: 8 -> 6, of which waited for: 0 -> 0; matrix products, arithmetic and copies ran while one was open for 4% -> 2% of each run, Pallas kernels for 39% -> 43%
where the time goes in v8:
time: 545 us; the launch traced here: 535 us
  Pallas kernels  501 us (92%)
  local copies, waits for them, and re-layouts  21.2 us (4%)
  other arithmetic  7.84 us (1%)
    pallas_call x1, Pallas kernels, attention_back(): pl.pallas_call(functools.partial(attention_back_kernel, dp_size, tensor_s...  229 us
    pallas_call x1, Pallas kernels, experts_call(): pl.pallas_call(functools.partial(experts_kernel, a, b, rows, width, cores...  179 us
    pallas_call x1, Pallas kernels, attention_forward(): pl.pallas_call(functools.partial(attention_kernel, a, b, tensor_size), ou...  87 us
  transfers between devices with their start and end apart: 6, of which 0 were waited for; matrix products, arithmetic and copies ran while one was open for 2% of the time, Pallas kernels for 43%

profile of v8, /device:TPU:0, one launch (start us, length us, event | category | flops | bytes accessed | tf_op | source)
XLA Modules:
  0.0 535.0 jit_solution(7615123397816977842)
XLA Ops:
  0.6 0.0 copy-start
  0.7 0.0 copy-start.13
  0.7 0.1 broadcast_in_dim_tile.3.frequency
  0.8 0.8 broadcast_in_dim.19.gain
  1.6 0.7 broadcast_in_dim.20.moe_gain
  2.3 0.0 copy-done
  2.3 0.1 copy.32
  2.5 0.4 fusion
  2.9 0.0 copy-start.18
  2.9 0.8 copy.33.seg_col
  3.8 0.0 copy-start.2
  3.8 1.1 copy.34
  4.9 0.8 pad.4.router_ref.router
  5.7 0.0 copy-done.13
  5.7 2.1 constant_dynamic-slice_fusion
  7.8 0.0 copy-done.18
  7.8 1.1 pad_maximum_fusion.1.payload
  8.9 0.0 copy-done.7
  8.9 0.0 copy-done.8
  8.9 0.0 copy-done.2
  8.9 0.0 copy-done.9
  8.9 87.0 %shard_map.229 = (bf16[2048,1664]{1,0:T(8,128)(2,1)}, f32[512,128]{1,0:T(8,128)S(1)}, f32[512,128]{1,0:T(8,128)S(1)}, bf16[512,768]{1,0:T(8,128)(2,1)}, bf16[512...) custom-call(bf16[1536,512]{1,0:T(8,128)(2,1)} %bitcast.10, ...), custom_call_target="tpu_custom_call" | custom-call | tf_op jit(solution)/shard_map/pallas_call | solution.py:1417
  95.9 0.0 copy-done.12
  95.9 0.0 copy-start.3
  95.9 0.7 copy-done.3
  96.6 0.7 copy-done.4
  97.3 0.7 copy-done.5
  98.0 0.7 copy-done.6
  98.7 179.4 %shard_map.230 = (bf16[2048,1536]{1,0:T(8,128)(2,1)}, f32[256,1664]{1,0:T(8,128)}, bf16[1536,256]{1,0:T(8,128)(2,1)}, bf16[1536,256]{1,0:T(8,128)(2,1)}, bf16[25...) custom-call(bf16[256,1536]{1,0:T(8,128)(2,1)} %get-tuple-element.45.x_ref, ...), custom_call_target="tpu_custom_call" | custom-call | tf_op jit(solution)/shard_map/pallas_call | solution.py:668
  278.1 1.6 collective-permute-start
  279.7 0.5 collective-permute-start.1
  280.2 1.5 collective-permute-start.2
  281.7 229.2 %shard_map.231 = (bf16[1536,768]{1,0:T(8,128)(2,1)}, bf16[1536,1280]{1,0:T(8,128)(2,1)}, f32[512,1536]{1,0:T(8,128)}, f32[24,1536]{1,0:T(8,128)}, bf16[512,1536]{1,0:T(8,128)(2,1)}) custom-call(bf16[2048,1536]{1,0:T(8,128)(2,1)} %get-tuple-element.50.moe_ref, f32[256,1664]{1,0:T(8,128)} %get-tuple-element.51.back, f32[256,1536]{1,0:T(8,128)} %get-tuple-element.52.middle, ...), custom_call_target="tpu_custom_call" | custom-call | tf_op jit(solution)/shard_map/pallas_call | solution.py:1212
  510.9 0.0 collective-permute-done
  511.0 0.0 collective-permute-done.1
  511.0 0.0 collective-permute-done.2
  511.0 0.0 copy-start.17
  511.0 0.0 copy-start.16
  511.0 1.7 convert_add_fusion.refs_2_
  512.7 0.1 collective-permute-start.5
  512.8 0.0 copy-done.17
  512.8 0.0 copy-start.10
  512.8 1.5 convert_add_fusion.1.refs_1_
  514.3 0.5 collective-permute-start.4
  514.8 0.0 copy-done.16
  514.8 0.2 convert_add_fusion.2.refs_0_
  515.0 0.1 collective-permute-start.3
  515.1 0.6 copy-done.19
  515.8 0.6 slice_bitcast_fusion
  516.4 0.0 copy-done.10
  516.4 2.5 slice.32
  519.0 0.6 slice_reduce_fusion
  519.6 1.9 fusion.1
  521.5 0.9 copy-done.11
  522.4 0.4 fusion.2
  522.7 2.9 pad_maximum_fusion
  525.7 0.0 collective-permute-done.5.refs_5_
  525.7 0.0 collective-permute-done.4.refs_4_
  525.7 0.0 collective-permute-done.3.refs_3_
  525.7 5.0 shard_map.232
  530.7 0.0 copy-done.15
  530.7 1.1 copy.38
  531.9 1.3 copy-done.14
  533.2 1.7 copy.39
  (17 shorter events, 0.1 us)
Async XLA Ops:
  0.6 1.7 copy-start
  0.7 5.1 copy-start.13
  1.6 7.3 %copy-start.7 = (f32[1,1536]{1,0:T(1,128)}, f32[1,1536]{1,0:T(1,128)S(1)}, u32[]{:S(2)}) copy-start(f32[1,1536]{1,0:T(1,128)S(1)} %broadcast_in_dim.19.gain) | copy-start | bytes 18436
  2.3 6.6 %copy-start.8 = (f32[1,1536]{1,0:T(1,128)}, f32[1,1536]{1,0:T(1,128)S(1)}, u32[]{:S(2)}) copy-start(f32[1,1536]{1,0:T(1,128)S(1)} %broadcast_in_dim.20.moe_gain) | copy-start | bytes 18436
  2.9 4.9 copy-start.18
  3.8 5.1 copy-start.2
  7.8 88.1 %copy-start.12 = (bf16[256,1536]{1,0:T(8,128)(2,1)}, bf16[256,1536]{1,0:T(8,128)(2,1)S(1)}, u32[]{:S(2)}) copy-start(bf16[256,1536]{1,0:T(8,128)(2,1)S(1)} %get-tuple-element.85.grad_top) | copy-start | bytes 2359300
  7.8 1.1 copy-start.9
  95.9 0.7 copy-start.3
  96.6 0.7 copy-start.4
  97.3 0.7 copy-start.5
  98.0 0.7 copy-start.6
  278.1 232.8 %collective-permute-start = (bf16[1536,256]{1,0:T(8,128)(2,1)}, bf16[1536,256]{1,0:T(8,128)(2,1)S(1)}, u32[]{:S(2)}, u32[]{:S(2)}) collective-permute-start(bf16[1536,256]{1,0:T(8,128)(2,1)} %get-tuple-element.65), channel_id=1, source_target_pairs={{0,2},{2,0},{4,6},{6,4},{8,10},{10,8},{12,14},{14,12},{16,18},{18,... | collective-permute-start | bytes 2359304 | tf_op jit(solution)/shard_map/ppermute | solution.py:31
  279.7 231.3 %collective-permute-start.1 = (bf16[1536,256]{1,0:T(8,128)(2,1)}, bf16[1536,256]{1,0:T(8,128)(2,1)}, u32[]{:S(2)}, u32[]{:S(2)}) collective-permute-start(bf16[1536,256]{1,0:T(8,128)(2,1)} %get-tuple-element.66), channel_id=1, source_target_pairs={{0,2},{2,0},{4,6},{6,4},{8,10},{10,8},{12,14},{14,12},{16,18},{18,... | collective-permute-start | bytes 2359304 | tf_op jit(solution)/shard_map/ppermute | solution.py:31
  280.2 230.8 %collective-permute-start.2 = (bf16[256,1536]{1,0:T(8,128)(2,1)}, bf16[256,1536]{1,0:T(8,128)(2,1)}, u32[]{:S(2)}, u32[]{:S(2)}) collective-permute-start(bf16[256,1536]{1,0:T(8,128)(2,1)} %get-tuple-element.67), channel_id=1, source_target_pairs={{0,2},{2,0},{4,6},{6,4},{8,10},{10,8},{12,14},{14,12},{16,18},{18,... | collective-permute-start | bytes 2359304 | tf_op jit(solution)/shard_map/ppermute | solution.py:31
  511.0 1.8 copy-start.17
  511.0 3.9 copy-start.16
  512.7 12.9 %collective-permute-start.5 = (f32[256,1536]{1,0:T(8,128)S(1)}, f32[256,1536]{1,0:T(8,128)S(1)}, u32[]{:S(2)}, u32[]{:S(2)}) collective-permute-start(f32[256,1536]{1,0:T(8,128)S(1)} %convert_add_fusion.refs_2_), channel_id=1, source_target_pairs={{0,1},{1,0},{2,3},{3,2},{4,5},{5,4},{6,7},{7,6},{8,9},{9,8},{10,11... | collective-permute-start | bytes 4718600 | tf_op jit(solution)/shard_map/ppermute | solution.py:31
  512.8 3.6 copy-start.10
  514.3 11.4 %collective-permute-start.4 = (f32[1536,256]{1,0:T(8,128)S(1)}, f32[1536,256]{1,0:T(8,128)S(1)}, u32[]{:S(2)}, u32[]{:S(2)}) collective-permute-start(f32[1536,256]{1,0:T(8,128)S(1)} %convert_add_fusion.1.refs_1_), channel_id=1, source_target_pairs={{0,1},{1,0},{2,3},{3,2},{4,5},{5,4},{6,7},{7,6},{8,9},{9,8},{10,11... | collective-permute-start | bytes 4718600 | tf_op jit(solution)/shard_map/ppermute | solution.py:31
  514.8 0.9 copy-start.19
  515.0 10.6 %collective-permute-start.3 = (f32[1536,256]{1,0:T(8,128)S(1)}, f32[1536,256]{1,0:T(8,128)S(1)}, u32[]{:S(2)}, u32[]{:S(2)}) collective-permute-start(f32[1536,256]{1,0:T(8,128)S(1)} %convert_add_fusion.2.refs_0_), channel_id=1, source_target_pairs={{0,1},{1,0},{2,3},{3,2},{4,5},{5,4},{6,7},{7,6},{8,9},{9,8},{10,11... | collective-permute-start | bytes 4718600 | tf_op jit(solution)/shard_map/ppermute | solution.py:31
  519.6 2.8 copy-start.11
  525.6 5.1 copy-start.15
  530.7 2.5 copy-start.14
  533.2 1.7 copy-start.1
